TPU v7x, 32 devices: a whole 2x2x4 slice. The times are simulated.
32 devices in a mesh: dp: 8 (over z, core), cls: 4 (over y, x).
Axes of the slice: x: 2, y: 2, z: 4, core: 2. Of those that a mesh axis runs over, the one named last changes fastest.
Arguments:
- attended: bfloat16 [27648, 1024], P(('dp', 'cls')), may hold values from -6 to 6
- stream: bfloat16 [27648, 1024], P(('dp', 'cls')), may hold values from -6 to 6
- out_proj: bfloat16 [1024, 1024], P('dp'), may hold values from -0.1875 to 0.1875
- norm_gain: float32 [1024], replicated, may hold values from 0.25 to 1.75
- norm_shift: float32 [1024], replicated, may hold values from -0.75 to 0.75
- head_proj: bfloat16 [1024, 512], P('dp'), may hold values from -0.1875 to 0.1875
- class_weight: bfloat16 [4096, 512], P('cls'), may hold values from -6 to 6
- block_ids: int32 [8, 4, 3], P('dp', 'cls'), may hold values from 0 to 7, as said below
- block_count: int32 [8, 4], P('dp', 'cls'), may hold values from 1 to 3, as said below
- labels: int32 [192], P('dp'), may hold values from 0 to 4095, as said below
Outputs:
- sample_loss: float32 [192], P(('dp', 'cls'))
- embed_grad: float32 [192, 512], P(('dp', 'cls'))
- class_grad: float32 [4096, 512], P('cls', 'dp')
Inputs may be any that keep to these rules, and one draw needn't show every extreme that they name: `block_ids`: within one data group and class shard the 3 block numbers are all different. `block_count`: some data group and class shard has all 3 slots live, another just one. `labels`: every image's class lies in a live slot's block of its own data group.
All inputs are finite; a program needn't handle non-finite values.
Results may differ from a plain program's by a relative error of at most 0.0028.
Values may be sent and summed in bfloat16 or wider, within the bound.
No kernel may reach another device: no remote copies, remote signals or barrier semaphores. Data moves between devices by JAX's collectives and lax.ppermute only.
A program may use at most 64 MiB of HBM per device.

v0:
```python
import math

import jax
import jax.numpy as jnp
from jax import lax
from jax.sharding import PartitionSpec as P

P_SIZE = 144
BLOCK_ROWS = 128


LOGIT_SCALE = 64.0
ANGLE_MARGIN = 0.5
NORM_EPSILON = 1e-06


def per_device(
    attended,
    stream,
    out_proj,
    norm_gain,
    norm_shift,
    head_proj,
    class_weight,
    block_ids,
    block_count,
    labels,
):
    tok_rows, model_width = attended.shape
    images = tok_rows // P_SIZE
    embed_width = head_proj.shape[1]
    columns = attended
    product = jnp.dot(
        columns,
        lax.all_gather(out_proj, "dp", axis=0, tiled=True),
        preferred_element_type=jnp.float32,
    )
    mixed = stream.astype(jnp.float32) + product
    token_mean = jnp.mean(mixed, axis=1, keepdims=True)
    centred = mixed - token_mean
    variance = jnp.mean(centred * centred, axis=1, keepdims=True)
    normed = norm_gain * centred / jnp.sqrt(variance + NORM_EPSILON) + norm_shift
    pooled = jnp.mean(normed.reshape(images, P_SIZE, model_width), axis=1).astype(jnp.bfloat16)
    columns = pooled
    embedding = jnp.dot(
        columns,
        lax.all_gather(head_proj, "dp", axis=0, tiled=True),
        preferred_element_type=jnp.float32,
    )
    group_embed = lax.all_gather(embedding, "cls", axis=0, tiled=True)
    embed_norm = jnp.sqrt(jnp.sum(group_embed * group_embed, axis=1) + NORM_EPSILON)
    unit_embed = group_embed / embed_norm[:, None]
    shard_index = lax.axis_index("cls")
    own_start = shard_index * images
    slot_ids = block_ids[0, 0]
    live_count = block_count[0, 0]
    slot_total = slot_ids.shape[0]
    blocks_dev = class_weight.shape[0] // BLOCK_ROWS
    cls_dev = blocks_dev * BLOCK_ROWS
    picked = (
        class_weight.reshape(blocks_dev, BLOCK_ROWS, embed_width)[slot_ids]
        .astype(jnp.float32)
        .reshape(-1, embed_width)
    )
    weight_norm = jnp.sqrt(jnp.sum(picked * picked, axis=1) + NORM_EPSILON)
    unit_weight = picked / weight_norm[:, None]
    cosine = jnp.dot(
        unit_embed,
        unit_weight.T,
        precision=lax.Precision.HIGHEST,
        preferred_element_type=jnp.float32,
    )
    slot_range = jnp.arange(slot_total, dtype=jnp.int32)
    row_range = jnp.arange(BLOCK_ROWS, dtype=jnp.int32)
    slot_live = slot_range < live_count
    live_mask = jnp.broadcast_to(slot_live[:, None], (slot_total, BLOCK_ROWS)).reshape(-1)
    local_label = labels - shard_index * cls_dev
    inside = (local_label >= 0) & (local_label < cls_dev)
    label_block = local_label // BLOCK_ROWS
    label_row = local_label % BLOCK_ROWS
    target_mask = (
        (slot_ids[None, :, None] == label_block[:, None, None])
        & (row_range[None, None, :] == label_row[:, None, None])
        & slot_live[None, :, None]
        & inside[:, None, None]
    ).reshape(labels.shape[0], -1)
    target_cos = cosine * math.cos(ANGLE_MARGIN) - jnp.sqrt(1.0 - cosine * cosine) * math.sin(
        ANGLE_MARGIN
    )
    logits = LOGIT_SCALE * jnp.where(target_mask, target_cos, cosine)
    exponent = jnp.where(live_mask[None, :], jnp.exp(logits - LOGIT_SCALE), 0.0)
    denom_part = jnp.sum(exponent, axis=1)
    target_part = jnp.sum(jnp.where(target_mask, logits, 0.0), axis=1)
    denominator, target_logit = lax.psum((denom_part, target_part), "cls")
    target_float = target_mask.astype(jnp.float32)
    cos_grad = LOGIT_SCALE * (exponent / denominator[:, None] - target_float)
    unit_own = lax.dynamic_slice_in_dim(unit_embed, own_start, images, 0)
    norm_own = lax.dynamic_slice_in_dim(embed_norm, own_start, images, 0)
    grad_part = jnp.dot(
        cos_grad, unit_weight, precision=lax.Precision.HIGHEST, preferred_element_type=jnp.float32
    )
    unit_grad = lax.psum_scatter(grad_part, "cls", scatter_dimension=0, tiled=True)
    embed_grad = (
        unit_grad - unit_own * jnp.sum(unit_own * unit_grad, axis=1, keepdims=True)
    ) / norm_own[:, None]
    loss_group = jnp.log(denominator) + LOGIT_SCALE - target_logit
    sample_loss = lax.dynamic_slice_in_dim(loss_group, own_start, images, 0)
    weight_unit_grad = lax.dot_general(
        cos_grad,
        unit_embed,
        (((0,), (0,)), ((), ())),
        precision=lax.Precision.HIGHEST,
        preferred_element_type=jnp.float32,
    )
    weight_grad = (
        weight_unit_grad
        - unit_weight * jnp.sum(unit_weight * weight_unit_grad, axis=1, keepdims=True)
    ) / weight_norm[:, None]
    block_range = jnp.arange(blocks_dev, dtype=jnp.int32)
    placement = ((block_range[:, None] == slot_ids[None, :]) & slot_live[None, :]).astype(
        jnp.float32
    )
    dense_grad = jnp.dot(
        placement,
        weight_grad.reshape(slot_total, -1),
        precision=lax.Precision.HIGHEST,
        preferred_element_type=jnp.float32,
    ).reshape(cls_dev, embed_width)
    class_grad = lax.psum_scatter(dense_grad, "dp", scatter_dimension=1, tiled=True)
    return (sample_loss, embed_grad, class_grad)


def solution(mesh):
    placed = (
        P(("dp", "cls"), None),
        P(("dp", "cls"), None),
        P("dp", None),
        P(),
        P(),
        P("dp", None),
        P("cls", None),
        P("dp", "cls", None),
        P("dp", "cls"),
        P("dp"),
    )
    return jax.shard_map(
        per_device,
        mesh=mesh,
        in_specs=placed,
        out_specs=(P(("dp", "cls")), P(("dp", "cls"), None), P("cls", "dp")),
        check_vma=False,
    )
```

profile of v0, /device:TPU:0, one launch (start us, length us, event | category | flops | bytes accessed | tf_op | source)
XLA Modules:
  0.0 140.2 jit_solution(3663762146035174739)
XLA Ops:
  7.2 0.7 all-gather.4.cloned.1.call-update
  8.0 0.7 all-gather.6.cloned.1.call-update
  8.7 0.7 and_select_fusion.1
  9.4 0.7 compare_and_fusion
  10.0 0.7 fusion.8
  10.7 1.8 %gather_fusion = bf16[3,128,512]{2,1,0:T(8,128)(2,1)S(1)} fusion(bf16[8,128,512]{2,1,0:T(8,128)(2,1)} %bitcast.48, s32[1024]{0:T(1024)S(1)} %pad_clamp_fusion), kind=kCustom, calls=%fused_computation | custom fusion | bytes 786444 | tf_op jit(solution)/shard_map/gather | solution.py:61
  12.5 0.2 multiply_reduce_fusion.2
  12.7 0.1 bitcast_divide_fusion
  13.7 0.7 broadcast_compare_fusion
  14.5 27.0 %all-gather.4.cloned.1.call-done = bf16[1024,1024]{1,0:T(8,128)(2,1)} async-done(((bf16[128,1024]{1,0:T(8,128)(2,1)}), bf16[1024,1024]{1,0:T(8,128)(2,1)}) %all-gather.4.cloned.1.call-update) | async-done | bytes 2097168 | tf_op jit(solution)/shard_map/all_gather | solution.py:35
  41.5 4.2 %fusion.14 = (f32[864]{0:T(1024)S(1)}, f32[864,1024]{1,0:T(8,128)S(1)}) fusion(bf16[864,1024]{1,0:T(8,128)(2,1)S(1)} %copy-done, bf16[1024,1024]{1,0:T(8,128)(2,1)} %all-gather.4.cloned.1.call-done, bf16[864,1024]{1,0:T(8,128)(2,1)} %param.11), kind=kOutput, calls=%fused_computation.50 | convolution fusion | flops 1814592640 | bytes 9178496 | tf_op jit(solution)/shard_map/dot_general | solution.py:33
  45.7 0.5 multiply_reduce_fusion
  46.2 0.1 copy-done.1
  46.3 2.3 %divide_add_fusion = f32[864,1024]{1,0:T(8,128)} fusion(f32[864,1024]{1,0:T(8,128)S(1)} %get-tuple-element.10, f32[1024]{0:T(1024)S(1)} %copy-done.1, f32[864]{0:T(1024)S(1)} %add_sqrt_fusion, f32[864]{0:T(1024)S(1)} %broadcast_multiply_fusion, f32[1024]{0:T(1024)S(1)} %copy-done.2), kind=kLoop, calls=%fused_computation.1 | loop fusion | flops 3538944 | bytes 7092992 | tf_op jit(solution)/shard_map/add | solution.py:42
  48.7 2.4 %reduce_sum.83 = f32[6,1024]{1,0:T(8,128)S(1)} reduce(f32[6,144,1024]{2,1,0:T(8,128)} %bitcast.47, f32[]{:T(128)} %constant.56.clone.1), dimensions={1}, to_apply=%region_2.0 | reduce | flops 878592 | bytes 3563524 | tf_op jit(solution)/shard_map/reduce_sum | solution.py:43
  51.1 13.6 %all-gather.6.cloned.1.call-done = bf16[1024,512]{1,0:T(8,128)(2,1)} async-done(((bf16[128,512]{1,0:T(8,128)(2,1)}), bf16[1024,512]{1,0:T(8,128)(2,1)}) %all-gather.6.cloned.1.call-update) | async-done | bytes 1048592 | tf_op jit(solution)/shard_map/all_gather | solution.py:47
  64.7 1.5 %convolution_bitcast_fusion = f32[1,6,512]{2,1,0:T(8,128)S(1)} fusion(bf16[1024,512]{1,0:T(8,128)(2,1)} %all-gather.6.cloned.1.call-done, f32[6,1024]{1,0:T(8,128)S(1)} %reduce_sum.83), kind=kOutput, calls=%fused_computation.4 | convolution fusion | flops 6303744 | bytes 1085440 | tf_op jit(solution)/shard_map/dot_general | solution.py:45
  66.1 8.2 %all-gather = f32[4,6,512]{2,1,0:T(8,128)S(1)} all-gather(f32[1,6,512]{2,1,0:T(8,128)S(1)} %convolution_bitcast_fusion), channel_id=1, replica_groups=mesh['dp'=8,'cls'=4] {'cls'}, dimensions={0}, use_global_device_ids=true | all-gather | bytes 61440 | tf_op jit(solution)/shard_map/all_gather | solution.py:50
  74.5 0.9 fusion.1
  75.4 8.9 %psum.14 = f32[24]{0:T(128)S(1)} all-reduce(f32[24]{0:T(128)S(1)} %get-tuple-element.3), channel_id=1, replica_groups=mesh['dp'=8,'cls'=4] {'cls'}, use_global_device_ids=true, to_apply=%region_6.7 | all-reduce | flops 24 | bytes 192 | tf_op jit(solution)/shard_map/psum | solution.py:94
  84.4 1.0 multiply_reduce_fusion.1
  85.4 1.1 subtract_divide_fusion
  86.5 2.7 %reshape.161 = f32[3,65536]{1,0:T(4,128)} reshape(f32[384,512]{1,0:T(8,128)} %subtract_divide_fusion) | data formatting | bytes 1572864 | tf_op jit(solution)/shard_map/reshape | solution.py:125
  89.2 3.6 %fusion.4 = f32[8,65536]{1,0:T(8,128)} fusion(f32[3,65536]{1,0:T(4,128)} %reshape.161, s32[3]{0:T(128)S(1)} %bitcast.53, pred[3]{0:T(512)(128)(4,1)S(1)} %iota_compare_fusion.2), kind=kOutput, calls=%fused_computation.29 | convolution fusion | flops 18874416 | bytes 2883599 | tf_op jit(solution)/shard_map/dot_general | solution.py:123
  92.8 3.3 %reshape.162 = f32[1024,512]{1,0:T(8,128)} reshape(f32[8,65536]{1,0:T(8,128)} %fusion.4) | data formatting | bytes 4194304 | tf_op jit(solution)/shard_map/reshape | solution.py:128
  96.1 3.0 %copy.15 = f32[1024,512]{0,1:T(8,128)} copy(f32[1024,512]{1,0:T(8,128)} %reshape.162) | data formatting | bytes 4194304 | tf_op jit(solution)/shard_map/reshape | solution.py:128
  99.1 0.6 dynamic-slice
  100.3 0.5 fusion.11
  100.8 16.2 %all-reduce.1 = (f32[24]{0:T(128)S(1)}, f32[24,512]{1,0:T(8,128)S(1)}) all-reduce(f32[24]{0:T(128)S(1)} %get-tuple-element.4, f32[24,512]{1,0:T(8,128)S(1)} %fusion.11), channel_id=1, replica_groups=mesh['dp'=8,'cls'=4] {'cls'}, use_global_device_ids=true, to_apply=%region_8.9 | all-reduce | flops 12312 | bytes 98496 | tf_op jit(solution)/shard_map/psum | solution.py:94
  117.1 0.6 dynamic_slice.9
  117.9 0.7 subtract_divide_fusion.1
  118.5 15.1 %reduce-scatter.2.cloned.1.call-done = f32[1024,64]{0,1:T(8,128)} async-done(((f32[1024,512]{0,1:T(8,128)}), f32[1024,64]{0,1:T(8,128)}) %reduce-scatter.2.cloned.1.call-update) | async-done | bytes 262160 | tf_op jit(solution)/shard_map/reduce_scatter | solution.py:129
  (29 shorter events, 0.9 us)
Async XLA Ops:
  7.2 34.3 %copy-start = (bf16[864,1024]{1,0:T(8,128)(2,1)S(1)}, bf16[864,1024]{1,0:T(8,128)(2,1)}, u32[]{:S(2)}) copy-start(bf16[864,1024]{1,0:T(8,128)(2,1)} %param.10) | copy-start | bytes 5308420
  7.2 34.3 %all-gather.4.cloned.1.call-start = ((), (), s32[]{:S(2)}) async-start(), calls=%async_computation.1 | async-start | bytes 2359296 | tf_op jit(solution)/shard_map/all_gather | solution.py:35
  7.9 56.8 %all-gather.6.cloned.1.call-start = ((), (), s32[]{:S(2)}) async-start(), calls=%async_computation.2 | async-start | bytes 1179648 | tf_op jit(solution)/shard_map/all_gather | solution.py:47
  8.7 125.0 %reduce-scatter.2.cloned.1.call-start = ((), (), s32[]{:S(2)}) async-start(), calls=%async_computation.3 | async-start | bytes 2359296 | tf_op jit(solution)/shard_map/reduce_scatter | solution.py:129
  45.6 0.7 copy-start.1
  45.6 0.7 copy-start.2
  84.4 4.8 %copy-start.3 = (s32[1,1,3]{2,1,0:T(1,128)S(1)}, s32[1,1,3]{2,1,0:T(1,128)}, u32[]{:S(2)}) copy-start(s32[1,1,3]{2,1,0:T(1,128)} %param.17) | copy-start | bytes 40
  96.1 3.0 %copy-start.4 = (u32[32]{0:T(128)S(1)}, u32[32]{0:T(128)}, u32[]{:S(2)}) copy-start(u32[32]{0:T(128)} %constant.72) | copy-start | bytes 388
Sparse Core Ops, SparseCore 0:
  9.6 31.7 all-gather.3
  43.0 21.5 all-gather.5
  99.2 34.4 reduce-scatter.1
where the time goes:
time: 141 us; the launch traced here: 140 us
  waiting for transfers between devices  57.1 us (40%)
  blocking collectives  33.3 us (24%)
  between operations  15.2 us (11%)
  local copies, waits for them, and re-layouts  12.2 us (9%)
  matrix products  11.7 us (8%)
  other arithmetic  10.6 us (8%)
    all_gather x1, waiting for transfers between devices, per_device(): lax.all_gather(out_proj, 'dp', axis=0, tiled=True)  27 us
    psum x2, blocking collectives, per_device(): denominator, target_logit = lax.psum((denom_part, target_part), 'cls')  25.1 us
    reduce_scatter x1, waiting for transfers between devices, per_device(): lax.psum_scatter(dense_grad, 'dp', scatter_dimension=1, tiled=True)  15.1 us
    all_gather x1, waiting for transfers between devices, per_device(): lax.all_gather(head_proj, 'dp', axis=0, tiled=True)  13.6 us
    all_gather x1, blocking collectives, per_device(): group_embed = lax.all_gather(embedding, 'cls', axis=0, tiled=True)  8.19 us
    reshape x2, local copies, waits for them, and re-layouts, per_device(): dense_grad = jnp.dot(placement, weight_grad.reshape(slot_total, -1), prec...  6.22 us
    dot_general x1, matrix products, per_device(): jnp.dot(columns, lax.all_gather(out_proj, 'dp', axis=0, tiled=True), pref...  4.19 us
    dot_general x1, matrix products, per_device(): jnp.dot(placement, weight_grad.reshape(slot_total, -1), precision=lax.Pre...  3.61 us
  transfers between devices with their start and end apart: 3, of which 3 were waited for; matrix products, arithmetic and copies ran while one was open for 12% of the time, Pallas kernels for 0%

commit v1 on v0

v1 whole, which is shorter than its diff:
```python
import math

import jax
import jax.numpy as jnp
from jax import lax
from jax.experimental import pallas as pl
from jax.experimental.pallas import tpu as pltpu
from jax.sharding import PartitionSpec as P

P_SIZE = 144
BLOCK_ROWS = 128
CORES = 2

LOGIT_SCALE = 64.0
ANGLE_MARGIN = 0.5
NORM_EPSILON = 1e-06
HIGHEST = lax.Precision.HIGHEST


def z_swap(value, step):
    count = lax.axis_size("dp")
    return lax.ppermute(value, "dp", [(i, i ^ (step * CORES)) for i in range(count)])


def core_swap(value):
    count = lax.axis_size("dp")
    return lax.ppermute(value, "dp", [(i, i ^ 1) for i in range(count)])


def plane_swap(value, step):
    count = lax.axis_size("cls")
    return lax.ppermute(value, "cls", [(i, i ^ step) for i in range(count)])


def pool_kernel(part_ref, att_ref, own_ref, other_ref, gain_ref, shift_ref, out_ref, mixed_ref, pooled_ref):
    tokens, width = part_ref.shape
    images = tokens // P_SIZE
    depth = own_ref.shape[0]
    per = 3 if images % 3 == 0 else 1
    chunk = per * P_SIZE
    for start in range(0, tokens, chunk):
        rows = pl.ds(start, chunk)
        mixed_ref[rows, :] = (
            part_ref[rows, :]
            + jnp.dot(att_ref[rows, pl.ds(0, depth)], own_ref[...], preferred_element_type=jnp.float32)
            + jnp.dot(att_ref[rows, pl.ds(depth, depth)], other_ref[...], preferred_element_type=jnp.float32)
        )
    step = 24
    for image in range(images):
        total = jnp.zeros((8, width), jnp.float32)
        for r in range(0, P_SIZE, step):
            x = mixed_ref[pl.ds(image * P_SIZE + r, step), :]
            centred = x - jnp.mean(x, axis=1, keepdims=True)
            variance = jnp.mean(centred * centred, axis=1, keepdims=True)
            scaled = centred * lax.rsqrt(variance + NORM_EPSILON)
            total = total + jnp.sum(scaled.reshape(step // 8, 8, width), axis=0)
        mean = jnp.sum(total, axis=0, keepdims=True) * (1.0 / P_SIZE)
        pooled_ref[pl.ds(image, 1), :] = gain_ref[...] * mean + shift_ref[...]
    out_ref[...] = pooled_ref[...].astype(out_ref.dtype)


def pool_tokens(part, att, own, other, gain, shift):
    tokens, width = part.shape
    images = tokens // P_SIZE
    vmem = pl.BlockSpec(memory_space=pltpu.VMEM)
    return pl.pallas_call(
        pool_kernel,
        out_shape=jax.ShapeDtypeStruct((images, width), jnp.bfloat16),
        in_specs=[vmem] * 6,
        out_specs=vmem,
        scratch_shapes=[
            pltpu.VMEM((tokens, width), jnp.float32),
            pltpu.VMEM((images, width), jnp.float32),
        ],
        compiler_params=pltpu.CompilerParams(vmem_limit_bytes=24 * 1024 * 1024),
        cost_estimate=pl.CostEstimate(
            flops=4 * tokens * width * own.shape[0], bytes_accessed=8 * tokens * width, transcendentals=tokens
        ),
    )(part, att, own, other, gain.reshape(1, width), shift.reshape(1, width))


def per_device(
    attended,
    stream,
    out_proj,
    norm_gain,
    norm_shift,
    head_proj,
    class_weight,
    block_ids,
    block_count,
    labels,
):
    n_dp, n_cls = lax.axis_size("dp"), lax.axis_size("cls")
    n_z = n_dp // CORES
    dp, cls = lax.axis_index("dp"), lax.axis_index("cls")
    z, core = dp // CORES, dp % CORES
    tokens, width = attended.shape
    images = tokens // P_SIZE
    rows = out_proj.shape[0]
    slice_rows = rows // n_cls

    own_slice = lax.dynamic_slice_in_dim(out_proj, cls * slice_rows, slice_rows, 0)
    far = [z_swap(own_slice, step) for step in range(n_z - 1, 1, -1)]
    near = z_swap(out_proj, 1)
    far = jnp.stack(far)
    whole_far = jnp.zeros((n_z - 2, n_cls, slice_rows, width), out_proj.dtype)
    whole_far = lax.dynamic_update_slice_in_dim(whole_far, far[:, None], cls, 1)
    for step in range(n_cls - 1, 0, -1):
        whole_far = lax.dynamic_update_slice_in_dim(
            whole_far, plane_swap(far, step)[:, None], cls ^ step, 1
        )
    whole_far = whole_far.reshape((n_z - 2) * rows, width)
    two = jnp.concatenate([out_proj, near], axis=0)
    other_two = core_swap(two)
    other_far = core_swap(whole_far)

    def columns_of(steps):
        taken = []
        for side in (core, 1 - core):
            for step in steps:
                at = ((z ^ step) * CORES + side) * rows
                taken.append(lax.dynamic_slice_in_dim(attended, at, rows, 1))
        return jnp.concatenate(taken, axis=1)

    part = stream.astype(jnp.float32) + jnp.dot(
        columns_of((0, 1)), jnp.concatenate([two, other_two], axis=0), preferred_element_type=jnp.float32
    )
    att_far = columns_of(range(n_z - 1, 1, -1))
    pooled = pool_tokens(part, att_far, whole_far, other_far, norm_gain, norm_shift)

    heads = jnp.stack([head_proj] + [z_swap(head_proj, step) for step in range(1, n_z)])
    other_heads = core_swap(heads)
    head = jnp.zeros((n_z, CORES) + head_proj.shape, head_proj.dtype)
    for step in range(n_z):
        for k, source in ((0, heads), (1, other_heads)):
            head = lax.dynamic_update_slice(
                head, source[step][None, None], (z ^ step, core ^ k, 0, 0)
            )
    head = head.reshape(n_dp * head_proj.shape[0], -1)

    own_labels = labels.reshape(n_cls, images)
    label_rows = jnp.concatenate(
        [lax.dynamic_slice_in_dim(own_labels, cls ^ step, 1, 0) for step in range(n_cls)], axis=0
    ).reshape(-1)
    facts = jnp.concatenate(
        [block_ids[0, 0], block_count[0], label_rows // BLOCK_ROWS, label_rows % BLOCK_ROWS]
    ).astype(jnp.bfloat16)
    n_facts = facts.shape[0]
    facts = jnp.pad(facts, (0, width - n_facts))[None]
    group = jnp.concatenate(
        [pooled] + [plane_swap(pooled, step) for step in range(1, n_cls)] + [facts], axis=0
    )
    groups = jnp.stack([group] + [z_swap(group, step) for step in range(1, n_z)])
    groups = jnp.concatenate([groups, core_swap(groups)], axis=0)
    size = n_cls * images
    pooled_all = groups[:, :size].reshape(n_dp * size, width)
    slots = block_ids.shape[2]
    facts_all = groups[:, size, :n_facts].astype(jnp.int32)
    ids = facts_all[:, :slots]
    count = facts_all[:, slots]
    label_block = facts_all[:, slots + 1 : slots + 1 + size].reshape(-1)
    label_row = facts_all[:, slots + 1 + size :].reshape(-1)

    classes, embed = class_weight.shape
    weight = class_weight.astype(jnp.float32)
    weight_norm = jnp.sqrt(jnp.sum(weight * weight, axis=1) + NORM_EPSILON)
    unit_weight = weight / weight_norm[:, None]

    embedding = jnp.dot(pooled_all, head, preferred_element_type=jnp.float32)
    embed_norm = jnp.sqrt(jnp.sum(embedding * embedding, axis=1) + NORM_EPSILON)
    unit_embed = embedding / embed_norm[:, None]
    cosine = jnp.dot(unit_embed, unit_weight.T, precision=HIGHEST, preferred_element_type=jnp.float32)

    blocks = classes // BLOCK_ROWS
    block_range = jnp.arange(blocks, dtype=jnp.int32)
    live = jnp.any(
        (ids[:, :, None] == block_range) & (jnp.arange(slots)[None, :, None] < count[:, None, None]), axis=1
    )
    live = jnp.broadcast_to(live[:, None, :, None], (n_dp, size, blocks, BLOCK_ROWS)).reshape(-1, classes)
    class_index = jnp.arange(classes, dtype=jnp.int32) + cls * classes
    label = label_block * BLOCK_ROWS + label_row
    target = (class_index[None, :] == label[:, None]) & live
    target_cos = cosine * math.cos(ANGLE_MARGIN) - jnp.sqrt(1.0 - cosine * cosine) * math.sin(ANGLE_MARGIN)
    logits = LOGIT_SCALE * jnp.where(target, target_cos, cosine)
    exponent = jnp.where(live, jnp.exp(logits), 0.0)
    denom_part = jnp.sum(exponent, axis=1)
    target_part = jnp.sum(jnp.where(target, logits, 0.0), axis=1)
    target_float = target.astype(jnp.float32)
    both = jnp.concatenate([exponent[:size], target_float[:size]], axis=0)
    sums = jnp.dot(both, unit_weight, precision=HIGHEST, preferred_element_type=jnp.float32)
    sums = sums.reshape(2, n_cls, images, embed)
    denom_part = denom_part.reshape(n_dp, n_cls, images)
    target_part = target_part[:size].reshape(n_cls, images)

    def packed(step):
        order = [k ^ step for k in range(n_cls)]
        denoms = denom_part[:, jnp.array(order)].reshape(-1)
        tail = jnp.concatenate([denoms, target_part[step]])
        lines = -(-tail.shape[0] // embed)
        tail = jnp.pad(tail, (0, lines * embed - tail.shape[0])).reshape(lines, embed)
        return jnp.concatenate([sums[0, step], sums[1, step], tail], axis=0)

    total = packed(0)
    for step in range(1, n_cls):
        total = total + plane_swap(packed(step), step)
    weighted, picked = total[:images], total[images : 2 * images]
    tail = total[2 * images :].reshape(-1)
    denominator = tail[: n_dp * size]
    target_logit = tail[n_dp * size : n_dp * size + images]
    own_denominator = denominator[:images]
    sample_loss = jnp.log(own_denominator) - target_logit
    unit_grad = LOGIT_SCALE * (weighted / own_denominator[:, None] - picked)
    unit_own = unit_embed[:images]
    embed_grad = (
        unit_grad - unit_own * jnp.sum(unit_own * unit_grad, axis=1, keepdims=True)
    ) / embed_norm[:images, None]

    cos_grad = LOGIT_SCALE * (exponent / denominator[:, None] - target_float)
    share = embed // n_dp
    unit_share = lax.dynamic_slice_in_dim(unit_embed, dp * share, share, 1)
    weight_share = lax.dynamic_slice_in_dim(unit_weight, dp * share, share, 1)
    along = jnp.sum(cos_grad * cosine, axis=0)
    grad = lax.dot_general(
        unit_share, cos_grad, (((0,), (0,)), ((), ())), precision=HIGHEST, preferred_element_type=jnp.float32
    )
    class_grad = ((grad - weight_share.T * along[None, :]) / weight_norm[None, :]).T
    return (sample_loss, embed_grad, class_grad)


def solution(mesh):
    placed = (
        P(("dp", "cls"), None),
        P(("dp", "cls"), None),
        P("dp", None),
        P(),
        P(),
        P("dp", None),
        P("cls", None),
        P("dp", "cls", None),
        P("dp", "cls"),
        P("dp"),
    )
    return jax.shard_map(
        per_device,
        mesh=mesh,
        in_specs=placed,
        out_specs=(P(("dp", "cls")), P(("dp", "cls"), None), P("cls", "dp")),
        check_vma=False,
    )
```

time: 141 us -> 74 us (0.52)
  waiting for transfers between devices: 57.1 us -> 19 us
  blocking collectives: 33.3 us -> 0 us
  starting transfers between devices: 0.11 us -> 27.4 us
  between operations: 15.2 us -> 1.89 us
  other arithmetic: 10.6 us -> 5.53 us
  local copies, waits for them, and re-layouts: 12.2 us -> 8.95 us
  matrix products: 11.7 us -> 9.26 us
  Pallas kernels: 0 us -> 1.78 us
    all_gather x2 -> x0, waiting for transfers between devices: 40.6 us -> none  [the longest x1 27 us: per_device(): lax.all_gather(out_proj, 'dp', axis=0, tiled=True)]
    ppermute x0 -> x22, starting transfers between devices: none -> 27.4 us  [the longest x9 14.6 us: z_swap(): lax.ppermute(value, 'dp', [(i, i ^ step * CORES) for i in range(count)])]
    psum x2 -> x0, blocking collectives: 25.1 us -> none  [per_device(): denominator, target_logit = lax.psum((denom_part, target_part), 'cls')]
    ppermute x0 -> x22, waiting for transfers between devices: none -> 19 us  [the longest x9 9.07 us: plane_swap(): return lax.ppermute(value, 'cls', [(i, i ^ step) for i in range(count)])]
    reduce_scatter x1 -> x0, waiting for transfers between devices: 15.1 us -> none  [per_device(): lax.psum_scatter(dense_grad, 'dp', scatter_dimension=1, tiled=True)]
    all_gather x1 -> x0, blocking collectives: 8.19 us -> none  [per_device(): group_embed = lax.all_gather(embedding, 'cls', axis=0, tiled=True)]
    reshape x3 -> x9, local copies, waits for them, and re-layouts: 8.91 us -> 1.38 us  [the longest x1 0.74 us: per_device(): own_labels = labels.reshape(n_cls, images)]
    reduce_sum x4 -> x2, other arithmetic: 3.17 us -> 0.59 us  [the longest x1 0.34 us: per_device(): along = jnp.sum(cos_grad * cosine, axis=0)]
  transfers between devices with their start and end apart: 3 -> 22, of which waited for: 3 -> 11; matrix products, arithmetic and copies ran while one was open for 12% -> 15% of each run, Pallas kernels for 0% -> 0%
where the time goes in v1:
time: 74 us; the launch traced here: 73.7 us
  starting transfers between devices  27.4 us (37%)
  waiting for transfers between devices  19 us (26%)
  matrix products  9.26 us (13%)
  local copies, waits for them, and re-layouts  8.95 us (12%)
  other arithmetic  5.53 us (7%)
  between operations  1.89 us (3%)
  Pallas kernels  1.78 us (2%)
    ppermute x9, starting transfers between devices, z_swap(): lax.ppermute(value, 'dp', [(i, i ^ step * CORES) for i in range(count)])  14.6 us
    ppermute x9, starting transfers between devices, plane_swap(): return lax.ppermute(value, 'cls', [(i, i ^ step) for i in range(count)])  12 us
    ppermute x9, waiting for transfers between devices, plane_swap(): return lax.ppermute(value, 'cls', [(i, i ^ step) for i in range(count)])  9.07 us
    ppermute x9, waiting for transfers between devices, z_swap(): lax.ppermute(value, 'dp', [(i, i ^ step * CORES) for i in range(count)])  6.52 us
    ppermute x4, waiting for transfers between devices, core_swap(): return lax.ppermute(value, 'dp', [(i, i ^ 1) for i in range(count)])  3.37 us
    dot_general x1, matrix products, per_device(): jnp.dot(unit_embed, unit_weight.T, precision=HIGHEST, preferred_element_t...  3.09 us
    dot_general x1, matrix products, per_device(): lax.dot_general(unit_share, cos_grad, (((0,), (0,)), ((), ())), precision...  2.57 us
    gather x8, local copies, waits for them, and re-layouts, packed(): denoms = denom_part[:, jnp.array(order)].reshape(-1)  2.22 us
  transfers between devices with their start and end apart: 22, of which 11 were waited for; matrix products, arithmetic and copies ran while one was open for 15% of the time, Pallas kernels for 0%

profile of v1, /device:TPU:0, one launch (start us, length us, event | category | flops | bytes accessed | tf_op | source)
XLA Modules:
  0.0 73.7 jit_solution(14469686926996983918)
XLA Ops:
  0.6 3.1 %collective-permute-start = (bf16[128,1024]{1,0:T(8,128)(2,1)}, bf16[128,1024]{1,0:T(8,128)(2,1)S(1)}, u32[]{:S(2)}, u32[]{:S(2)}) collective-permute-start(bf16[128,1024]{1,0:T(8,128)(2,1)} %param.16), channel_id=1, source_target_pairs={{0,8},{4,12},{8,0},{12,4},{16,24},{20,28},{24,16},{28,20},{1,9},{5... | collective-permute-start | bytes 786440 | tf_op jit(solution)/shard_map/ppermute | solution.py:22
  3.7 0.9 %constant_dynamic-slice_fusion.4 = bf16[32,1024]{1,0:T(8,128)(2,1)S(1)} fusion(bf16[128,1024]{1,0:T(8,128)(2,1)} %param.16, s32[]{:T(128)S(6)} %select_n.130), kind=kLoop, calls=%fused_computation.88 | loop fusion | bytes 131076 | tf_op jit(solution)/shard_map/dynamic_slice | solution.py:103
  4.6 2.6 %collective-permute-start.3 = (bf16[32,1024]{1,0:T(8,128)(2,1)S(1)}, bf16[32,1024]{1,0:T(8,128)(2,1)S(1)}, u32[]{:S(2)}, u32[]{:S(2)}) collective-permute-start(bf16[32,1024]{1,0:T(8,128)(2,1)S(1)} %constant_dynamic-slice_fusion.4), channel_id=1, source_target_pairs={{0,16},{4,20},{8,24},{12,28},{16,0},{20,4},{24,8},{28,12},{1,17},{... | collective-permute-start | bytes 196616 | tf_op jit(solution)/shard_map/ppermute | solution.py:22
  7.2 3.8 %collective-permute-start.17 = (bf16[128,512]{1,0:T(8,128)(2,1)}, bf16[128,512]{1,0:T(8,128)(2,1)S(1)}, u32[]{:S(2)}, u32[]{:S(2)}) collective-permute-start(bf16[128,512]{1,0:T(8,128)(2,1)} %param.19), channel_id=1, source_target_pairs={{0,24},{4,28},{8,16},{12,20},{16,8},{20,12},{24,0},{28,4},{1,25},{... | collective-permute-start | bytes 393224 | tf_op jit(solution)/shard_map/ppermute | solution.py:22
  11.0 0.7 reshape.145
  12.6 0.7 convert_bitcast_fusion
  13.3 1.5 %copy.40 = bf16[1024,512]{0,1:T(8,128)(2,1)S(1)} copy(bf16[1024,512]{1,0:T(8,128)(2,1)} %param.20) | data formatting | bytes 2097152 | tf_op args[6]
  15.1 1.6 %convert_divide_fusion = f32[1024,512]{0,1:T(8,128)} fusion(bf16[1024,512]{0,1:T(8,128)(2,1)S(1)} %copy.40, f32[1024]{0:T(1024)S(1)} %add_sqrt_fusion), kind=kLoop, calls=%fused_computation.5 | loop fusion | flops 1048576 | bytes 3149824 | tf_op jit(solution)/shard_map/div | solution.py:168
  16.9 1.7 %constant_dynamic-slice_fusion.8 = (bf16[864,128]{1,0:T(8,128)(2,1)S(1)}, bf16[864,128]{1,0:T(8,128)(2,1)S(1)}, bf16[864,128]{1,0:T(8,128)(2,1)S(1)}, bf16[864,1...) fusion(bf16[864,1024]{1,0:T(8,128)(2,1)} %param.14, ...), kind=kLoop, calls=%fused_computation.92 | loop fusion | bytes 3538976 | tf_op jit(solution)/shard_map/dynamic_slice | solution.py:123
  19.5 2.7 %collective-permute-start.4 = (bf16[2,32,1024]{2,1,0:T(8,128)(2,1)S(1)}, bf16[2,32,1024]{2,1,0:T(8,128)(2,1)S(1)}, u32[]{:S(2)}, u32[]{:S(2)}) collective-permute-start(bf16[2,32,1024]{2,1,0:T(8,128)(2,1)S(1)} %pad_maximum_fusion.4), channel_id=1, source_target_pairs={{0,3},{1,2},{2,1},{3,0},{4,7},{5,6},{6,5},{7,4},{8,11},{9,10},{10,... | collective-permute-start | bytes 393224 | tf_op jit(solution)/shard_map/ppermute | solution.py:32
  22.8 2.4 %collective-permute-done.16 = bf16[128,512]{1,0:T(8,128)(2,1)S(1)} collective-permute-done((bf16[128,512]{1,0:T(8,128)(2,1)}, bf16[128,512]{1,0:T(8,128)(2,1)S(1)}, u32[]{:S(2)}, u32[]{:S(2)}) %collective-permute-start.16) | collective-permute-done | bytes 131104 | tf_op jit(solution)/shard_map/ppermute | solution.py:22
  25.2 1.5 %collective-permute-start.6 = (bf16[2,32,1024]{2,1,0:T(8,128)(2,1)S(1)}, bf16[2,32,1024]{2,1,0:T(8,128)(2,1)S(1)}, u32[]{:S(2)}, u32[]{:S(2)}) collective-permute-start(bf16[2,32,1024]{2,1,0:T(8,128)(2,1)S(1)} %pad_maximum_fusion.4), channel_id=1, source_target_pairs={{0,1},{1,0},{2,3},{3,2},{4,5},{5,4},{6,7},{7,6},{8,9},{9,8},{10,11... | collective-permute-start | bytes 393224 | tf_op jit(solution)/shard_map/ppermute | solution.py:32
  27.3 2.9 %collective-permute-done.6 = bf16[2,32,1024]{2,1,0:T(8,128)(2,1)S(1)} collective-permute-done((bf16[2,32,1024]{2,1,0:T(8,128)(2,1)S(1)}, bf16[2,32,1024]{2,1,0:T(8,128)(2,1)S(1)}, u32[]{:S(2)}, u32[]{:S(2)}) %collective-permute-start.6) | collective-permute-done | bytes 131104 | tf_op jit(solution)/shard_map/ppermute | solution.py:32
  31.0 1.9 %collective-permute-done.1 = bf16[256,1024]{1,0:T(8,128)(2,1)S(1)} collective-permute-done((bf16[256,1024]{1,0:T(8,128)(2,1)S(1)}, bf16[256,1024]{1,0:T(8,128)(2,1)S(1)}, u32[]{:S(2)}, u32[]{:S(2)}) %collective-permute-start.1) | collective-permute-done | bytes 524320 | tf_op jit(solution)/shard_map/ppermute | solution.py:27
  32.9 1.1 %convert_add_fusion.part_ref = f32[864,1024]{1,0:T(8,128)S(1)} fusion(bf16[864,1024]{1,0:T(8,128)(2,1)S(1)} %copy-done.8, bf16[256,1024]{1,0:T(8,128)(2,1)S(1)} %collective-permute-done.1, bf16[128,1024]{1,0:T(8,128)(2,1)S(1)} %collective-permute-done, bf16[128,1024]{1,0:T(8,128)(2,1)S(1)} %copy-done.4, bf16[864,128]{1,0:T(8,128)(2,1)S(1)} %get-tuple-element.7, ...), kind=kOutput, calls=%fused_computation.4 | convolution fusion | flops 914423808 | bytes 7241728 | tf_op jit(solution)/shard_map/dot_general | solution.py:126
  34.1 1.8 %shard_map.157 = bf16[6,1024]{1,0:T(8,128)(2,1)S(1)} custom-call(f32[864,1024]{1,0:T(8,128)S(1)} %convert_add_fusion.part_ref, bf16[864,512]{1,0:T(8,128)(2,1)S(1)} %pad_maximum_fusion.att_ref, bf16[256,1024]{1,0:T(8,128)(2,1)S(1)} %bitcast.118, bf16[256,1024]{1,0:T(8,128)(2,1)S(1)} %collective-permute-done.7.other_ref, f32[1,1024]{1,0:T(1,128)S(1)} %bitcast.119, ...), custom_call_target="tpu_custom_call" | custom-call | flops 905969664 | bytes 7077888 | tf_op jit(solution)/shard_map/pallas_call | solution.py:66
  35.8 1.6 %collective-permute-start.8 = (bf16[6,1024]{1,0:T(8,128)(2,1)S(1)}, bf16[6,1024]{1,0:T(8,128)(2,1)S(1)}, u32[]{:S(2)}, u32[]{:S(2)}) collective-permute-start(bf16[6,1024]{1,0:T(8,128)(2,1)S(1)} %shard_map.157), channel_id=1, source_target_pairs={{0,1},{1,0},{2,3},{3,2},{4,5},{5,4},{6,7},{7,6},{8,9},{9,8},{10,11... | collective-permute-start | bytes 36872 | tf_op jit(solution)/shard_map/ppermute | solution.py:32
  37.4 1.5 %collective-permute-start.9 = (bf16[6,1024]{1,0:T(8,128)(2,1)S(1)}, bf16[6,1024]{1,0:T(8,128)(2,1)S(1)}, u32[]{:S(2)}, u32[]{:S(2)}) collective-permute-start(bf16[6,1024]{1,0:T(8,128)(2,1)S(1)} %shard_map.157), channel_id=1, source_target_pairs={{0,2},{1,3},{2,0},{3,1},{4,6},{5,7},{6,4},{7,5},{8,10},{9,11},{10,... | collective-permute-start | bytes 36872 | tf_op jit(solution)/shard_map/ppermute | solution.py:32
  39.6 1.5 %collective-permute-done.9 = bf16[6,1024]{1,0:T(8,128)(2,1)S(1)} collective-permute-done((bf16[6,1024]{1,0:T(8,128)(2,1)S(1)}, bf16[6,1024]{1,0:T(8,128)(2,1)S(1)}, u32[]{:S(2)}, u32[]{:S(2)}) %collective-permute-start.9) | collective-permute-done | bytes 12320 | tf_op jit(solution)/shard_map/ppermute | solution.py:32
  41.1 2.4 %collective-permute-done.10 = bf16[6,1024]{1,0:T(8,128)(2,1)S(1)} collective-permute-done((bf16[6,1024]{1,0:T(8,128)(2,1)S(1)}, bf16[6,1024]{1,0:T(8,128)(2,1)S(1)}, u32[]{:S(2)}, u32[]{:S(2)}) %collective-permute-start.10) | collective-permute-done | bytes 12320 | tf_op jit(solution)/shard_map/ppermute | solution.py:32
  43.9 2.5 %collective-permute-start.12 = (bf16[25,1024]{1,0:T(8,128)(2,1)S(1)}, bf16[25,1024]{1,0:T(8,128)(2,1)S(1)}, u32[]{:S(2)}, u32[]{:S(2)}) collective-permute-start(bf16[25,1024]{1,0:T(8,128)(2,1)S(1)} %concatenate.60), channel_id=1, source_target_pairs={{0,16},{4,20},{8,24},{12,28},{16,0},{20,4},{24,8},{28,12},{1,17},{... | collective-permute-start | bytes 153608 | tf_op jit(solution)/shard_map/ppermute | solution.py:22
  46.3 1.9 %collective-permute-start.13 = (bf16[25,1024]{1,0:T(8,128)(2,1)S(1)}, bf16[25,1024]{1,0:T(8,128)(2,1)S(1)}, u32[]{:S(2)}, u32[]{:S(2)}) collective-permute-start(bf16[25,1024]{1,0:T(8,128)(2,1)S(1)} %concatenate.60), channel_id=1, source_target_pairs={{0,24},{4,28},{8,16},{12,20},{16,8},{20,12},{24,0},{28,4},{1,25},{... | collective-permute-start | bytes 153608 | tf_op jit(solution)/shard_map/ppermute | solution.py:22
  48.2 2.2 %collective-permute-done.12 = bf16[25,1024]{1,0:T(8,128)(2,1)S(1)} collective-permute-done((bf16[25,1024]{1,0:T(8,128)(2,1)S(1)}, bf16[25,1024]{1,0:T(8,128)(2,1)S(1)}, u32[]{:S(2)}, u32[]{:S(2)}) %collective-permute-start.12) | collective-permute-done | bytes 51232 | tf_op jit(solution)/shard_map/ppermute | solution.py:22
  50.5 1.9 %collective-permute-done.13 = bf16[25,1024]{1,0:T(8,128)(2,1)S(1)} collective-permute-done((bf16[25,1024]{1,0:T(8,128)(2,1)S(1)}, bf16[25,1024]{1,0:T(8,128)(2,1)S(1)}, u32[]{:S(2)}, u32[]{:S(2)}) %collective-permute-start.13) | collective-permute-done | bytes 51232 | tf_op jit(solution)/shard_map/ppermute | solution.py:22
  52.5 1.5 %collective-permute-done.14 = bf16[4,25,1024]{2,1,0:T(8,128)(2,1)S(1)} collective-permute-done((bf16[4,25,1024]{2,1,0:T(8,128)(2,1)S(1)}, bf16[4,25,1024]{2,1,0:T(8,128)(2,1)S(1)}, u32[]{:S(2)}, u32[]{:S(2)}) %collective-permute-start.14) | collective-permute-done | bytes 204832 | tf_op jit(solution)/shard_map/ppermute | solution.py:27
  55.5 3.1 %fusion.43 = (f32[192]{0:T(256)S(1)}, f32[192,1024]{1,0:T(8,128)S(1)}, f32[192]{0:T(256)S(1)}, f32[192,1024]{1,0:T(8,128)}) fusion(s32[192]{0:T(256)S(1)} %add.216, s32[1024]{0:T(1024)S(1)} %iota_add_fusion, pred[24,8,8,128]{3,2,1,0:T(8,128)(4,1)S(1)} %bitcast.123, f32[192,512]{1,0:T(8,128)S(1)} %broadcast_divide_fusion, bf16[1024,512]{0,1:T(8,128)(2,1)S(1)} %copy.40, ...), kind=kOutput, calls=%fused_computation.137 | convolution fusion | flops 1211563648 | bytes 3221760 | tf_op jit(solution)/shard_map/dot_general | solution.py:173
  60.2 2.0 %fusion.14 = f32[48,512]{1,0:T(8,128)S(1)} fusion(f32[24,1024]{1,0:T(8,128)S(1)} %slice.164, f32[24,1024]{1,0:T(8,128)S(1)} %slice.163, bf16[1024,512]{0,1:T(8,128)(2,1)S(1)} %copy.40, f32[1024]{0:T(1024)S(1)} %add_sqrt_fusion), kind=kOutput, calls=%fused_computation.33 | convolution fusion | flops 303087616 | bytes 1347584 | tf_op jit(solution)/shard_map/dot_general | solution.py:191
  63.0 1.6 %collective-permute-start.20 = (f32[13,512]{1,0:T(8,128)S(1)}, f32[13,512]{1,0:T(8,128)S(1)}, u32[]{:S(2)}, u32[]{:S(2)}) collective-permute-start(f32[13,512]{1,0:T(8,128)S(1)} %pad_maximum_fusion.6), channel_id=1, source_target_pairs={{0,2},{1,3},{2,0},{3,1},{4,6},{5,7},{6,4},{7,5},{8,10},{9,11},{10,... | collective-permute-start | bytes 79880 | tf_op jit(solution)/shard_map/ppermute | solution.py:32
  65.3 1.5 %collective-permute-start.19 = (f32[13,512]{1,0:T(8,128)S(1)}, f32[13,512]{1,0:T(8,128)S(1)}, u32[]{:S(2)}, u32[]{:S(2)}) collective-permute-start(f32[13,512]{1,0:T(8,128)S(1)} %pad_maximum_fusion.5), channel_id=1, source_target_pairs={{0,1},{1,0},{2,3},{3,2},{4,5},{5,4},{6,7},{7,6},{8,9},{9,8},{10,11... | collective-permute-start | bytes 79880 | tf_op jit(solution)/shard_map/ppermute | solution.py:32
  67.7 1.7 %collective-permute-done.19 = f32[13,512]{1,0:T(8,128)S(1)} collective-permute-done((f32[13,512]{1,0:T(8,128)S(1)}, f32[13,512]{1,0:T(8,128)S(1)}, u32[]{:S(2)}, u32[]{:S(2)}) %collective-permute-start.19) | collective-permute-done | bytes 26656 | tf_op jit(solution)/shard_map/ppermute | solution.py:32
  70.1 0.7 subtract_divide_fusion
  71.2 2.6 %fusion.1 = f32[1024,64]{0,1:T(8,128)} fusion(f32[1024,512]{0,1:T(8,128)} %convert_divide_fusion, s32[]{:T(128)S(6)} %select_n.150, f32[1024]{0:T(1024)S(1)} %add_sqrt_fusion, f32[1024]{0:T(1024)S(1)} %multiply_reduce_fusion, f32[192,512]{1,0:T(8,128)S(1)} %broadcast_divide_fusion, f32[192,1024]{1,0:T(8,128)S(1)} %get-tuple-element.4, f32[192]{0:T(256)S(1)} %bitcast.151, ...), kind=kOutput, calls=%fused_computation.9 | convolution fusion | flops 152371200 | bytes 1620992 | tf_op jit(solution)/shard_map/dot_general | solution.py:224
  (125 shorter events, 10.9 us)
Async XLA Ops:
  0.6 14.5 %copy-start.7 = (s32[4]{0:T(128)S(1)}, s32[4]{0:T(128)}, u32[]{:S(2)}) copy-start(s32[4]{0:T(128)} %constant.134) | copy-start | bytes 52
  0.6 29.6 %collective-permute-start = (bf16[128,1024]{1,0:T(8,128)(2,1)}, bf16[128,1024]{1,0:T(8,128)(2,1)S(1)}, u32[]{:S(2)}, u32[]{:S(2)}) collective-permute-start(bf16[128,1024]{1,0:T(8,128)(2,1)} %param.16), channel_id=1, source_target_pairs={{0,8},{4,12},{8,0},{12,4},{16,24},{20,28},{24,16},{28,20},{1,9},{5... | collective-permute-start | bytes 786440 | tf_op jit(solution)/shard_map/ppermute | solution.py:22
  4.6 14.2 %collective-permute-start.3 = (bf16[32,1024]{1,0:T(8,128)(2,1)S(1)}, bf16[32,1024]{1,0:T(8,128)(2,1)S(1)}, u32[]{:S(2)}, u32[]{:S(2)}) collective-permute-start(bf16[32,1024]{1,0:T(8,128)(2,1)S(1)} %constant_dynamic-slice_fusion.4), channel_id=1, source_target_pairs={{0,16},{4,20},{8,24},{12,28},{16,0},{20,4},{24,8},{28,12},{1,17},{... | collective-permute-start | bytes 196616 | tf_op jit(solution)/shard_map/ppermute | solution.py:22
  7.2 12.2 %collective-permute-start.2 = (bf16[32,1024]{1,0:T(8,128)(2,1)S(1)}, bf16[32,1024]{1,0:T(8,128)(2,1)S(1)}, u32[]{:S(2)}, u32[]{:S(2)}) collective-permute-start(bf16[32,1024]{1,0:T(8,128)(2,1)S(1)} %constant_dynamic-slice_fusion.4), channel_id=1, source_target_pairs={{0,24},{4,28},{8,16},{12,20},{16,8},{20,12},{24,0},{28,4},{1,25},{... | collective-permute-start | bytes 196616 | tf_op jit(solution)/shard_map/ppermute | solution.py:22
  7.2 15.0 %collective-permute-start.17 = (bf16[128,512]{1,0:T(8,128)(2,1)}, bf16[128,512]{1,0:T(8,128)(2,1)S(1)}, u32[]{:S(2)}, u32[]{:S(2)}) collective-permute-start(bf16[128,512]{1,0:T(8,128)(2,1)} %param.19), channel_id=1, source_target_pairs={{0,24},{4,28},{8,16},{12,20},{16,8},{20,12},{24,0},{28,4},{1,25},{... | collective-permute-start | bytes 393224 | tf_op jit(solution)/shard_map/ppermute | solution.py:22
  11.0 14.2 %collective-permute-start.16 = (bf16[128,512]{1,0:T(8,128)(2,1)}, bf16[128,512]{1,0:T(8,128)(2,1)S(1)}, u32[]{:S(2)}, u32[]{:S(2)}) collective-permute-start(bf16[128,512]{1,0:T(8,128)(2,1)} %param.19), channel_id=1, source_target_pairs={{0,16},{4,20},{8,24},{12,28},{16,0},{20,4},{24,8},{28,12},{1,17},{... | collective-permute-start | bytes 393224 | tf_op jit(solution)/shard_map/ppermute | solution.py:22
  14.8 1.9 %copy-start.6 = (s32[4]{0:T(128)S(1)}, s32[4]{0:T(128)}, u32[]{:S(2)}) copy-start(s32[4]{0:T(128)} %constant.132) | copy-start | bytes 52
  15.1 1.8 %copy-start.3 = (bf16[128,512]{1,0:T(8,128)(2,1)S(1)}, bf16[128,512]{1,0:T(8,128)(2,1)}, u32[]{:S(2)}) copy-start(bf16[128,512]{1,0:T(8,128)(2,1)} %param.19) | copy-start | bytes 393220
  16.9 1.9 %copy-start.5 = (s32[4]{0:T(128)S(1)}, s32[4]{0:T(128)}, u32[]{:S(2)}) copy-start(s32[4]{0:T(128)} %constant.133) | copy-start | bytes 52
  18.6 11.7 %copy-start.4 = (bf16[128,1024]{1,0:T(8,128)(2,1)S(1)}, bf16[128,1024]{1,0:T(8,128)(2,1)}, u32[]{:S(2)}) copy-start(bf16[128,1024]{1,0:T(8,128)(2,1)} %param.16) | copy-start | bytes 786436
  18.8 7.9 %collective-permute-start.15 = (bf16[128,512]{1,0:T(8,128)(2,1)S(1)}, bf16[128,512]{1,0:T(8,128)(2,1)S(1)}, u32[]{:S(2)}, u32[]{:S(2)}) collective-permute-start(bf16[128,512]{1,0:T(8,128)(2,1)S(1)} %copy-done.3), channel_id=1, source_target_pairs={{0,8},{4,12},{8,0},{12,4},{16,24},{20,28},{24,16},{28,20},{1,9},{5... | collective-permute-start | bytes 393224 | tf_op jit(solution)/shard_map/ppermute | solution.py:22
  19.5 7.4 %collective-permute-start.4 = (bf16[2,32,1024]{2,1,0:T(8,128)(2,1)S(1)}, bf16[2,32,1024]{2,1,0:T(8,128)(2,1)S(1)}, u32[]{:S(2)}, u32[]{:S(2)}) collective-permute-start(bf16[2,32,1024]{2,1,0:T(8,128)(2,1)S(1)} %pad_maximum_fusion.4), channel_id=1, source_target_pairs={{0,3},{1,2},{2,1},{3,0},{4,7},{5,6},{6,5},{7,4},{8,11},{9,10},{10,... | collective-permute-start | bytes 393224 | tf_op jit(solution)/shard_map/ppermute | solution.py:32
  22.3 5.0 %collective-permute-start.5 = (bf16[2,32,1024]{2,1,0:T(8,128)(2,1)S(1)}, bf16[2,32,1024]{2,1,0:T(8,128)(2,1)S(1)}, u32[]{:S(2)}, u32[]{:S(2)}) collective-permute-start(bf16[2,32,1024]{2,1,0:T(8,128)(2,1)S(1)} %pad_maximum_fusion.4), channel_id=1, source_target_pairs={{0,2},{1,3},{2,0},{3,1},{4,6},{5,7},{6,4},{7,5},{8,10},{9,11},{10,... | collective-permute-start | bytes 393224 | tf_op jit(solution)/shard_map/ppermute | solution.py:32
  25.2 5.0 %collective-permute-start.6 = (bf16[2,32,1024]{2,1,0:T(8,128)(2,1)S(1)}, bf16[2,32,1024]{2,1,0:T(8,128)(2,1)S(1)}, u32[]{:S(2)}, u32[]{:S(2)}) collective-permute-start(bf16[2,32,1024]{2,1,0:T(8,128)(2,1)S(1)} %pad_maximum_fusion.4), channel_id=1, source_target_pairs={{0,1},{1,0},{2,3},{3,2},{4,5},{5,4},{6,7},{7,6},{8,9},{9,8},{10,11... | collective-permute-start | bytes 393224 | tf_op jit(solution)/shard_map/ppermute | solution.py:32
  26.7 6.2 %copy-start.8 = (bf16[864,1024]{1,0:T(8,128)(2,1)S(1)}, bf16[864,1024]{1,0:T(8,128)(2,1)}, u32[]{:S(2)}) copy-start(bf16[864,1024]{1,0:T(8,128)(2,1)} %param.15) | copy-start | bytes 5308420
  26.8 4.1 %collective-permute-start.18 = (bf16[4,128,512]{2,1,0:T(8,128)(2,1)S(1)}, bf16[4,128,512]{2,1,0:T(8,128)(2,1)S(1)}, u32[]{:S(2)}, u32[]{:S(2)}) collective-permute-start(bf16[4,128,512]{2,1,0:T(8,128)(2,1)S(1)} %pad_maximum_fusion.2), channel_id=1, source_target_pairs={{0,4},{4,0},{8,12},{12,8},{16,20},{20,16},{24,28},{28,24},{1,5},{5... | collective-permute-start | bytes 1572872 | tf_op jit(solution)/shard_map/ppermute | solution.py:27
  30.2 3.8 %collective-permute-start.7 = (bf16[256,1024]{1,0:T(8,128)(2,1)S(1)}, bf16[256,1024]{1,0:T(8,128)(2,1)S(1)}, u32[]{:S(2)}, u32[]{:S(2)}) collective-permute-start(bf16[256,1024]{1,0:T(8,128)(2,1)S(1)} %bitcast.117), channel_id=1, source_target_pairs={{0,4},{4,0},{8,12},{12,8},{16,20},{20,16},{24,28},{28,24},{1,5},{5... | collective-permute-start | bytes 1572872 | tf_op jit(solution)/shard_map/ppermute | solution.py:27
  30.3 2.6 %collective-permute-start.1 = (bf16[256,1024]{1,0:T(8,128)(2,1)S(1)}, bf16[256,1024]{1,0:T(8,128)(2,1)S(1)}, u32[]{:S(2)}, u32[]{:S(2)}) collective-permute-start(bf16[256,1024]{1,0:T(8,128)(2,1)S(1)} %pad_maximum_fusion.1), channel_id=1, source_target_pairs={{0,4},{4,0},{8,12},{12,8},{16,20},{20,16},{24,28},{28,24},{1,5},{5... | collective-permute-start | bytes 1572872 | tf_op jit(solution)/shard_map/ppermute | solution.py:27
  32.9 1.1 %copy-start = (f32[1024]{0:T(1024)S(1)}, f32[1024]{0:T(1024)}, u32[]{:S(2)}) copy-start(f32[1024]{0:T(1024)} %param.17) | copy-start | bytes 12292
  32.9 1.1 %copy-start.1 = (f32[1024]{0:T(1024)S(1)}, f32[1024]{0:T(1024)}, u32[]{:S(2)}) copy-start(f32[1024]{0:T(1024)} %param.18) | copy-start | bytes 12292
  35.8 3.8 %collective-permute-start.8 = (bf16[6,1024]{1,0:T(8,128)(2,1)S(1)}, bf16[6,1024]{1,0:T(8,128)(2,1)S(1)}, u32[]{:S(2)}, u32[]{:S(2)}) collective-permute-start(bf16[6,1024]{1,0:T(8,128)(2,1)S(1)} %shard_map.157), channel_id=1, source_target_pairs={{0,1},{1,0},{2,3},{3,2},{4,5},{5,4},{6,7},{7,6},{8,9},{9,8},{10,11... | collective-permute-start | bytes 36872 | tf_op jit(solution)/shard_map/ppermute | solution.py:32
  37.4 3.7 %collective-permute-start.9 = (bf16[6,1024]{1,0:T(8,128)(2,1)S(1)}, bf16[6,1024]{1,0:T(8,128)(2,1)S(1)}, u32[]{:S(2)}, u32[]{:S(2)}) collective-permute-start(bf16[6,1024]{1,0:T(8,128)(2,1)S(1)} %shard_map.157), channel_id=1, source_target_pairs={{0,2},{1,3},{2,0},{3,1},{4,6},{5,7},{6,4},{7,5},{8,10},{9,11},{10,... | collective-permute-start | bytes 36872 | tf_op jit(solution)/shard_map/ppermute | solution.py:32
  38.9 4.6 %collective-permute-start.10 = (bf16[6,1024]{1,0:T(8,128)(2,1)S(1)}, bf16[6,1024]{1,0:T(8,128)(2,1)S(1)}, u32[]{:S(2)}, u32[]{:S(2)}) collective-permute-start(bf16[6,1024]{1,0:T(8,128)(2,1)S(1)} %shard_map.157), channel_id=1, source_target_pairs={{0,3},{1,2},{2,1},{3,0},{4,7},{5,6},{6,5},{7,4},{8,11},{9,10},{10,... | collective-permute-start | bytes 36872 | tf_op jit(solution)/shard_map/ppermute | solution.py:32
  43.8 4.5 %collective-permute-start.11 = (bf16[25,1024]{1,0:T(8,128)(2,1)S(1)}, bf16[25,1024]{1,0:T(8,128)(2,1)S(1)}, u32[]{:S(2)}, u32[]{:S(2)}) collective-permute-start(bf16[25,1024]{1,0:T(8,128)(2,1)S(1)} %concatenate.60), channel_id=1, source_target_pairs={{0,8},{4,12},{8,0},{12,4},{16,24},{20,28},{24,16},{28,20},{1,9},{5... | collective-permute-start | bytes 153608 | tf_op jit(solution)/shard_map/ppermute | solution.py:22
  43.9 6.6 %collective-permute-start.12 = (bf16[25,1024]{1,0:T(8,128)(2,1)S(1)}, bf16[25,1024]{1,0:T(8,128)(2,1)S(1)}, u32[]{:S(2)}, u32[]{:S(2)}) collective-permute-start(bf16[25,1024]{1,0:T(8,128)(2,1)S(1)} %concatenate.60), channel_id=1, source_target_pairs={{0,16},{4,20},{8,24},{12,28},{16,0},{20,4},{24,8},{28,12},{1,17},{... | collective-permute-start | bytes 153608 | tf_op jit(solution)/shard_map/ppermute | solution.py:22
  46.3 6.1 %collective-permute-start.13 = (bf16[25,1024]{1,0:T(8,128)(2,1)S(1)}, bf16[25,1024]{1,0:T(8,128)(2,1)S(1)}, u32[]{:S(2)}, u32[]{:S(2)}) collective-permute-start(bf16[25,1024]{1,0:T(8,128)(2,1)S(1)} %concatenate.60), channel_id=1, source_target_pairs={{0,24},{4,28},{8,16},{12,20},{16,8},{20,12},{24,0},{28,4},{1,25},{... | collective-permute-start | bytes 153608 | tf_op jit(solution)/shard_map/ppermute | solution.py:22
  52.4 1.6 %collective-permute-start.14 = (bf16[4,25,1024]{2,1,0:T(8,128)(2,1)S(1)}, bf16[4,25,1024]{2,1,0:T(8,128)(2,1)S(1)}, u32[]{:S(2)}, u32[]{:S(2)}) collective-permute-start(bf16[4,25,1024]{2,1,0:T(8,128)(2,1)S(1)} %pad_maximum_fusion.3), channel_id=1, source_target_pairs={{0,4},{4,0},{8,12},{12,8},{16,20},{20,16},{24,28},{28,24},{1,5},{5... | collective-permute-start | bytes 614408 | tf_op jit(solution)/shard_map/ppermute | solution.py:27
  60.2 10.6 %copy-start.2 = (f32[192,1024]{1,0:T(8,128)S(1)}, f32[192,1024]{1,0:T(8,128)}, u32[]{:S(2)}) copy-start(f32[192,1024]{1,0:T(8,128)} %get-tuple-element.34) | copy-start | bytes 2359300
  62.4 5.2 %collective-permute-start.21 = (f32[13,512]{1,0:T(8,128)S(1)}, f32[13,512]{1,0:T(8,128)S(1)}, u32[]{:S(2)}, u32[]{:S(2)}) collective-permute-start(f32[13,512]{1,0:T(8,128)S(1)} %pad_maximum_fusion.7), channel_id=1, source_target_pairs={{0,3},{1,2},{2,1},{3,0},{4,7},{5,6},{6,5},{7,4},{8,11},{9,10},{10,... | collective-permute-start | bytes 79880 | tf_op jit(solution)/shard_map/ppermute | solution.py:32
  63.0 4.7 %collective-permute-start.20 = (f32[13,512]{1,0:T(8,128)S(1)}, f32[13,512]{1,0:T(8,128)S(1)}, u32[]{:S(2)}, u32[]{:S(2)}) collective-permute-start(f32[13,512]{1,0:T(8,128)S(1)} %pad_maximum_fusion.6), channel_id=1, source_target_pairs={{0,2},{1,3},{2,0},{3,1},{4,6},{5,7},{6,4},{7,5},{8,10},{9,11},{10,... | collective-permute-start | bytes 79880 | tf_op jit(solution)/shard_map/ppermute | solution.py:32
  65.3 4.0 %collective-permute-start.19 = (f32[13,512]{1,0:T(8,128)S(1)}, f32[13,512]{1,0:T(8,128)S(1)}, u32[]{:S(2)}, u32[]{:S(2)}) collective-permute-start(f32[13,512]{1,0:T(8,128)S(1)} %pad_maximum_fusion.5), channel_id=1, source_target_pairs={{0,1},{1,0},{2,3},{3,2},{4,5},{5,4},{6,7},{7,6},{8,9},{9,8},{10,11... | collective-permute-start | bytes 79880 | tf_op jit(solution)/shard_map/ppermute | solution.py:32

commit v2 on v1

v2 whole, which is shorter than its diff:
```python
import functools
import math

import jax
import jax.numpy as jnp
from jax import lax
from jax.experimental import pallas as pl
from jax.experimental.pallas import tpu as pltpu
from jax.sharding import PartitionSpec as P

P_SIZE = 144
BLOCK_ROWS = 128
CORES = 2

LOGIT_SCALE = 64.0
ANGLE_MARGIN = 0.5
NORM_EPSILON = 1e-06


def z_swap(value, step):
    count = lax.axis_size("dp")
    return lax.ppermute(value, "dp", [(i, i ^ (step * CORES)) for i in range(count)])


def core_swap(value):
    count = lax.axis_size("dp")
    return lax.ppermute(value, "dp", [(i, i ^ 1) for i in range(count)])


def plane_swap(value, step):
    count = lax.axis_size("cls")
    return lax.ppermute(value, "cls", [(i, i ^ step) for i in range(count)])


def pool_kernel(part_ref, att_ref, own_ref, other_ref, gain_ref, shift_ref, out_ref, mixed_ref, pooled_ref):
    tokens, width = part_ref.shape
    images = tokens // P_SIZE
    depth = own_ref.shape[0]
    per = 3 if images % 3 == 0 else 1
    chunk = per * P_SIZE
    for start in range(0, tokens, chunk):
        rows = pl.ds(start, chunk)
        mixed_ref[rows, :] = (
            part_ref[rows, :]
            + jnp.dot(att_ref[rows, pl.ds(0, depth)], own_ref[...], preferred_element_type=jnp.float32)
            + jnp.dot(att_ref[rows, pl.ds(depth, depth)], other_ref[...], preferred_element_type=jnp.float32)
        )
    step = 24
    for image in range(images):
        total = jnp.zeros((8, width), jnp.float32)
        for r in range(0, P_SIZE, step):
            x = mixed_ref[pl.ds(image * P_SIZE + r, step), :]
            centred = x - jnp.mean(x, axis=1, keepdims=True)
            variance = jnp.mean(centred * centred, axis=1, keepdims=True)
            scaled = centred * lax.rsqrt(variance + NORM_EPSILON)
            total = total + jnp.sum(scaled.reshape(step // 8, 8, width), axis=0)
        mean = jnp.sum(total, axis=0, keepdims=True) * (1.0 / P_SIZE)
        pooled_ref[pl.ds(image, 1), :] = gain_ref[...] * mean + shift_ref[...]
    out_ref[...] = pooled_ref[...].astype(out_ref.dtype)


def pool_tokens(part, att, own, other, gain, shift):
    tokens, width = part.shape
    images = tokens // P_SIZE
    vmem = pl.BlockSpec(memory_space=pltpu.VMEM)
    return pl.pallas_call(
        pool_kernel,
        out_shape=jax.ShapeDtypeStruct((images, width), jnp.bfloat16),
        in_specs=[vmem] * 6,
        out_specs=vmem,
        scratch_shapes=[
            pltpu.VMEM((tokens, width), jnp.float32),
            pltpu.VMEM((images, width), jnp.float32),
        ],
        compiler_params=pltpu.CompilerParams(vmem_limit_bytes=24 * 1024 * 1024),
        cost_estimate=pl.CostEstimate(
            flops=4 * tokens * width * own.shape[0], bytes_accessed=8 * tokens * width, transcendentals=tokens
        ),
    )(part, att, own, other, gain.reshape(1, width), shift.reshape(1, width))


def split(value):
    high = value.astype(jnp.bfloat16)
    return high, (value - high.astype(jnp.float32)).astype(jnp.bfloat16)


def as_row(column):
    return jnp.broadcast_to(column, (column.shape[0], 128)).T[0:1]


def class_kernel(own, pooled_ref, head_ref, code_ref, weight_ref, scale_ref,
                 exp_ref, cos_ref, unit_ref, sums_ref, denom_ref):
    images = pooled_ref.shape[0]
    classes, embed = weight_ref.shape
    embedding = jnp.dot(pooled_ref[...], head_ref[...], preferred_element_type=jnp.float32)
    norm = jnp.sqrt(jnp.sum(embedding * embedding, axis=1, keepdims=True) + NORM_EPSILON)
    unit = embedding * (1.0 / norm)
    unit_ref[:, :embed] = unit
    unit_ref[:, embed:] = jnp.broadcast_to(norm, (images, 128))
    terms = jnp.concatenate(split(unit), axis=0)
    denom = jnp.zeros((images, 128), jnp.float32)
    picked = jnp.zeros((own, 128), jnp.float32)
    wide = 256
    for start in range(0, classes, wide):
        cols = pl.ds(start, wide)
        both = lax.dot_general(
            terms, weight_ref[cols, :], (((1,), (1,)), ((), ())), preferred_element_type=jnp.float32
        )
        cosine = (both[:images] + both[images:]) * scale_ref[:, cols]
        cos_ref[:, cols] = cosine
        code = code_ref[:, cols]
        target = code > 1.5
        sine = jnp.sqrt(jnp.maximum(1.0 - cosine * cosine, 0.0))
        margin = cosine * math.cos(ANGLE_MARGIN) - sine * math.sin(ANGLE_MARGIN)
        logits = LOGIT_SCALE * jnp.where(target, margin, cosine)
        exponent = jnp.where(code > 0.5, jnp.exp(logits), 0.0)
        exp_ref[:, cols] = exponent
        labelled = jnp.where(target, logits, 0.0)[:own]
        for k in range(0, wide, 128):
            denom = denom + exponent[:, k : k + 128]
            picked = picked + labelled[:, k : k + 128]
    denom = jnp.sum(denom, axis=1, keepdims=True)
    denom_ref[...] = as_row(denom)
    scale = scale_ref[...]
    weighted = split(exp_ref[:own, :] * scale)
    chosen = split(jnp.where(code_ref[:own, :] > 1.5, scale, 0.0))
    sums = jnp.dot(
        jnp.concatenate(weighted + chosen, axis=0), weight_ref[...], preferred_element_type=jnp.float32
    )
    sums_ref[:, :embed] = sums[:own] + sums[own : 2 * own]
    sums_ref[:, embed : 2 * embed] = sums[2 * own : 3 * own] + sums[3 * own :]
    sums_ref[:, 2 * embed : 2 * embed + 128] = jnp.broadcast_to(denom[:own], (own, 128))
    sums_ref[:, 2 * embed + 128 :] = jnp.broadcast_to(jnp.sum(picked, axis=1, keepdims=True), (own, 128))


def class_parts(own, pooled, head, code, weight, scale):
    images = pooled.shape[0]
    classes, embed = weight.shape
    vmem = pl.BlockSpec(memory_space=pltpu.VMEM)
    f32 = jnp.float32
    return pl.pallas_call(
        functools.partial(class_kernel, own),
        out_shape=(
            jax.ShapeDtypeStruct((images, classes), f32),
            jax.ShapeDtypeStruct((images, classes), f32),
            jax.ShapeDtypeStruct((images, embed + 128), f32),
            jax.ShapeDtypeStruct((own, 2 * embed + 256), f32),
            jax.ShapeDtypeStruct((1, images), f32),
        ),
        in_specs=[vmem] * 5,
        out_specs=(vmem,) * 5,
        compiler_params=pltpu.CompilerParams(vmem_limit_bytes=24 * 1024 * 1024),
        cost_estimate=pl.CostEstimate(
            flops=6 * images * embed * classes, bytes_accessed=16 * images * classes, transcendentals=images * classes
        ),
    )(pooled, head, code, weight, scale)


def grad_kernel(denom_ref, exp_ref, cos_ref, code_ref, unit_ref, weight_ref, scale_ref, grad_ref):
    ratio = LOGIT_SCALE / denom_ref[...]
    unit = unit_ref[...]
    share, images = unit.shape
    left = jnp.concatenate(split(unit * ratio), axis=0)
    exponent = exp_ref[...]
    high, low = split(exponent)
    dot = functools.partial(jnp.dot, preferred_element_type=jnp.float32)
    first = dot(left, high)
    grad = first[:share] + first[share:] + dot(left[:share], low)
    target = code_ref[...] > 1.5
    second = dot(jnp.concatenate(split(unit * LOGIT_SCALE), axis=0), jnp.where(target, 1.0, 0.0).astype(jnp.bfloat16))
    grad = grad - second[:share] - second[share:]
    cosine = cos_ref[...]
    column = jnp.broadcast_to(ratio, (128, images)).T
    along = jnp.zeros((1, cosine.shape[1]), jnp.float32)
    weighted = exponent * column[:, 0:1] - jnp.where(target, LOGIT_SCALE, 0.0)
    along = jnp.sum(weighted * cosine, axis=0, keepdims=True)
    scale = scale_ref[...]
    grad_ref[...] = (grad - weight_ref[...] * (along * scale)) * scale


def class_grad_part(denom, exponent, cosine, code, unit_share, weight_share, scale):
    share, images = unit_share.shape
    classes = exponent.shape[1]
    vmem = pl.BlockSpec(memory_space=pltpu.VMEM)
    return pl.pallas_call(
        grad_kernel,
        out_shape=jax.ShapeDtypeStruct((share, classes), jnp.float32),
        in_specs=[vmem] * 7,
        out_specs=vmem,
        compiler_params=pltpu.CompilerParams(vmem_limit_bytes=24 * 1024 * 1024),
        cost_estimate=pl.CostEstimate(
            flops=10 * images * share * classes, bytes_accessed=12 * images * classes, transcendentals=0
        ),
    )(denom, exponent, cosine, code, unit_share, weight_share, scale)


def per_device(
    attended,
    stream,
    out_proj,
    norm_gain,
    norm_shift,
    head_proj,
    class_weight,
    block_ids,
    block_count,
    labels,
):
    n_dp, n_cls = lax.axis_size("dp"), lax.axis_size("cls")
    n_z = n_dp // CORES
    dp, cls = lax.axis_index("dp"), lax.axis_index("cls")
    z, core = dp // CORES, dp % CORES
    tokens, width = attended.shape
    images = tokens // P_SIZE
    rows = out_proj.shape[0]
    slice_rows = rows // n_cls

    size = n_cls * images
    slots = block_ids.shape[2]
    classes, embed = class_weight.shape

    facts = jnp.concatenate(
        [block_ids[0, 0], block_count[0], labels // BLOCK_ROWS, labels % BLOCK_ROWS]
    ).astype(jnp.bfloat16)
    n_facts = facts.shape[0]
    facts = jnp.pad(facts, (0, 16 * embed - n_facts)).reshape(16, embed)

    own_slice = lax.dynamic_slice_in_dim(out_proj, cls * slice_rows, slice_rows, 0)
    far = [z_swap(own_slice, step) for step in range(n_z - 1, 1, -1)]
    far = jnp.stack(far)
    late_out, far_first = lax.optimization_barrier((out_proj, own_slice))
    near = z_swap(late_out, 1)
    two = jnp.concatenate([out_proj, near], axis=0)
    attended, stream, class_weight, head_proj, far = lax.optimization_barrier(
        (attended, stream, class_weight, head_proj, far)
    )
    from_plane = [plane_swap(far, step) for step in range(n_cls - 1, 0, -1)]
    whole_far = jnp.zeros((n_z - 2, n_cls, slice_rows, width), out_proj.dtype)
    whole_far = lax.dynamic_update_slice_in_dim(whole_far, far[:, None], cls, 1)
    for step, got in zip(range(n_cls - 1, 0, -1), from_plane):
        whole_far = lax.dynamic_update_slice_in_dim(whole_far, got[:, None], cls ^ step, 1)
    whole_far = whole_far.reshape((n_z - 2) * rows, width)
    other_two = core_swap(two)
    other_far = core_swap(whole_far)

    def columns_of(steps):
        taken = []
        for side in (core, 1 - core):
            for step in steps:
                at = ((z ^ step) * CORES + side) * rows
                taken.append(lax.dynamic_slice_in_dim(attended, at, rows, 1))
        return jnp.concatenate(taken, axis=1)

    part = stream.astype(jnp.float32) + jnp.dot(
        columns_of((0, 1)), jnp.concatenate([two, other_two], axis=0), preferred_element_type=jnp.float32
    )
    att_far = columns_of(range(n_z - 1, 1, -1))

    pooled = pool_tokens(part, att_far, whole_far, other_far, norm_gain, norm_shift)

    head_rows = head_proj.shape[0]
    head_own = jnp.concatenate([head_proj, facts], axis=0)
    heads = jnp.stack([head_own] + [z_swap(head_own, step) for step in range(1, n_z)])
    other_heads = core_swap(heads)
    head = jnp.zeros((n_z, CORES, head_rows, embed), head_proj.dtype)
    for step in range(n_z):
        for k, source in ((0, heads), (1, other_heads)):
            head = lax.dynamic_update_slice(
                head, source[step, :head_rows][None, None], (z ^ step, core ^ k, 0, 0)
            )
    head = head.reshape(n_dp * head_rows, embed)
    all_facts = jnp.concatenate([heads[:, head_rows:], other_heads[:, head_rows:]], axis=0)
    all_facts = all_facts.reshape(n_dp, 16 * embed)[:, :n_facts].astype(jnp.int32)

    block_of = jnp.arange(classes, dtype=jnp.int32) // BLOCK_ROWS
    code = jnp.zeros((n_dp, 1, classes), jnp.float32)
    for slot in range(slots):
        used = (all_facts[:, slot, None] == block_of) & (slot < all_facts[:, slots, None])
        code = jnp.where(used[:, None, :], 1.0, code)
    label = all_facts[:, slots + 1 : slots + 1 + size] * BLOCK_ROWS + all_facts[:, slots + 1 + size :]
    hit = (label - cls * classes)[:, :, None] == jnp.arange(classes, dtype=jnp.int32)
    code = jnp.where(hit & (code > 0.5), 2.0, jnp.broadcast_to(code, hit.shape)).reshape(-1, classes)

    scale = lax.rsqrt(
        jnp.sum(jnp.square(class_weight.astype(jnp.float32)), axis=1) + NORM_EPSILON
    )[None, :]
    share = embed // n_dp
    weight_share = lax.dynamic_slice_in_dim(class_weight, dp * share, share, 1).T.astype(jnp.float32)

    group = jnp.zeros((n_cls, images, width), pooled.dtype)
    for step, got in [(0, pooled)] + [(step, plane_swap(pooled, step)) for step in range(n_cls - 1, 0, -1)]:
        group = lax.dynamic_update_slice_in_dim(group, got[None], cls ^ step, 0)
    group = group.reshape(size, width)
    groups = jnp.stack([group] + [z_swap(group, step) for step in range(1, n_z)])
    groups = jnp.concatenate([groups, core_swap(groups)], axis=0)
    pooled_all = groups.reshape(n_dp * size, width)

    piece = size * max(1, min(n_dp, 192 // size))
    own = -(-size // 16) * 16
    parts = [
        class_parts(own, pooled_all[at : at + piece], head, code[at : at + piece], class_weight, scale)
        for at in range(0, n_dp * size, piece)
    ]
    denoms = jnp.concatenate([p[4] for p in parts], axis=1)
    sums = parts[0][3]
    lines = -(-denoms.shape[1] // sums.shape[1])
    denoms = jnp.pad(denoms, ((0, 0), (0, lines * sums.shape[1] - denoms.shape[1]))).reshape(lines, -1)

    def packed(step):
        return jnp.concatenate(
            [lax.dynamic_slice_in_dim(sums, (cls ^ step) * images, images, 0), denoms], axis=0
        )

    total = packed(0)
    for step in range(n_cls - 1, 0, -1):
        total = total + plane_swap(packed(step), step)
    denominator = total[images:].reshape(1, -1)[:, : n_dp * size]
    class_grad = jnp.zeros((share, classes), jnp.float32)
    for k, (exponent, cosine, unit, _, _) in enumerate(parts):
        at = k * piece
        unit_share = lax.dynamic_slice_in_dim(unit, dp * share, share, 1).T
        grad = class_grad_part(
            denominator[:, at : at + piece], exponent, cosine, code[at : at + piece], unit_share, weight_share, scale
        )
        class_grad = grad if k == 0 else class_grad + grad

    weighted, picked = total[:images, :embed], total[:images, embed : 2 * embed]
    own_denominator = total[:images, 2 * embed]
    target_logit = total[:images, 2 * embed + 128]
    sample_loss = jnp.log(own_denominator) - target_logit
    unit_grad = LOGIT_SCALE * (weighted / own_denominator[:, None] - picked)
    own_unit = lax.dynamic_slice_in_dim(parts[0][2], cls * images, images, 0)
    unit_own, norm_own = own_unit[:, :embed], own_unit[:, embed : embed + 1]
    embed_grad = (
        unit_grad - unit_own * jnp.sum(unit_own * unit_grad, axis=1, keepdims=True)
    ) / norm_own
    return (sample_loss, embed_grad, class_grad.T)


def solution(mesh):
    placed = (
        P(("dp", "cls"), None),
        P(("dp", "cls"), None),
        P("dp", None),
        P(),
        P(),
        P("dp", None),
        P("cls", None),
        P("dp", "cls", None),
        P("dp", "cls"),
        P("dp"),
    )
    return jax.shard_map(
        per_device,
        mesh=mesh,
        in_specs=placed,
        out_specs=(P(("dp", "cls")), P(("dp", "cls"), None), P("cls", "dp")),
        check_vma=False,
    )
```

time: 74 us -> 80 us (1.081); the launches traced: 73.7 us -> 78.9 us
  local copies, waits for them, and re-layouts: 8.95 us -> 23.9 us
  waiting for transfers between devices: 19 us -> 7.4 us
  other arithmetic: 5.53 us -> 13 us
  matrix products: 9.26 us -> 2.13 us
  Pallas kernels: 1.78 us -> 4.58 us
  starting transfers between devices: 27.4 us -> 25.9 us
    dot_general x4 -> x0, matrix products: 8.17 us -> none  [the longest x1 3.09 us: per_device(): jnp.dot(unit_embed, unit_weight.T, precision=HIGHEST, preferred_element_t...]
    dynamic_update_slice x11 -> x16, local copies, waits for them, and re-layouts: 0.17 us -> 6.54 us  [the longest x8 3.76 us: per_device(): lax.dynamic_update_slice(head, source[step, :head_rows][None, None], (z ^...]
    ppermute x9, waiting for transfers between devices: 9.07 us -> 3.19 us  [plane_swap(): return lax.ppermute(value, 'cls', [(i, i ^ step) for i in range(count)])]
    unnamed x23 -> x50, local copies, waits for them, and re-layouts: 1.56 us -> 6.56 us
    ppermute x4, waiting for transfers between devices: 3.37 us -> 0.01 us  [core_swap(): return lax.ppermute(value, 'dp', [(i, i ^ 1) for i in range(count)])]
    pallas_call x0 -> x2, Pallas kernels: none -> 2.81 us  [the longest x1 1.58 us: class_parts(): pl.pallas_call(functools.partial(class_kernel, own), out_shape=(jax.Shape...]
    slice x9 -> x6, local copies, waits for them, and re-layouts: 0.39 us -> 2.93 us  [the longest x1 0.88 us: per_device(): unit_own, norm_own = (own_unit[:, :embed], own_unit[:, embed:embed + 1])]
    ppermute x9, waiting for transfers between devices: 6.52 us -> 4.19 us  [z_swap(): lax.ppermute(value, 'dp', [(i, i ^ step * CORES) for i in range(count)])]
  transfers between devices with their start and end apart: 22 -> 22, of which waited for: 11 -> 5; matrix products, arithmetic and copies ran while one was open for 15% -> 39% of each run, Pallas kernels for 0% -> 2%
where the time goes in v2:
time: 80 us; the launch traced here: 78.9 us
  starting transfers between devices  25.9 us (32%)
  local copies, waits for them, and re-layouts  23.9 us (30%)
  other arithmetic  13 us (16%)
  waiting for transfers between devices  7.4 us (9%)
  Pallas kernels  4.58 us (6%)
  matrix products  2.13 us (3%)
  between operations  1.95 us (2%)
    ppermute x9, starting transfers between devices, z_swap(): lax.ppermute(value, 'dp', [(i, i ^ step * CORES) for i in range(count)])  14.6 us
    ppermute x9, starting transfers between devices, plane_swap(): return lax.ppermute(value, 'cls', [(i, i ^ step) for i in range(count)])  10.7 us
    unnamed x50, local copies, waits for them, and re-layouts  6.56 us
    ppermute x9, waiting for transfers between devices, z_swap(): lax.ppermute(value, 'dp', [(i, i ^ step * CORES) for i in range(count)])  4.19 us
    dynamic_update_slice x8, local copies, waits for them, and re-layouts, per_device(): lax.dynamic_update_slice(head, source[step, :head_rows][None, None], (z ^...  3.76 us
    ppermute x9, waiting for transfers between devices, plane_swap(): return lax.ppermute(value, 'cls', [(i, i ^ step) for i in range(count)])  3.19 us
    dynamic_update_slice x3, local copies, waits for them, and re-layouts, per_device(): lax.dynamic_update_slice_in_dim(whole_far, got[:, None], cls ^ step, 1)  2.75 us
    dot_general x1, matrix products, per_device(): jnp.dot(columns_of((0, 1)), jnp.concatenate([two, other_two], axis=0), pr...  2.13 us
  transfers between devices with their start and end apart: 22, of which 5 were waited for; matrix products, arithmetic and copies ran while one was open for 39% of the time, Pallas kernels for 2%

profile of v2, /device:TPU:0, one launch (start us, length us, event | category | flops | bytes accessed | tf_op | source)
XLA Modules:
  0.0 78.9 jit_solution(16171465042452098054)
XLA Ops:
  1.5 4.0 %collective-permute-start.1 = (bf16[32,1024]{1,0:T(8,128)(2,1)S(1)}, bf16[32,1024]{1,0:T(8,128)(2,1)S(1)}, u32[]{:S(2)}, u32[]{:S(2)}) collective-permute-start(bf16[32,1024]{1,0:T(8,128)(2,1)S(1)} %constant_dynamic-slice_fusion.12), channel_id=1, source_target_pairs={{0,16},{4,20},{8,24},{12,28},{16,0},{20,4},{24,8},{28,12},{1,17},{... | collective-permute-start | bytes 196616 | tf_op jit(solution)/shard_map/ppermute | solution.py:22
  5.5 1.3 %collective-permute-start = (bf16[32,1024]{1,0:T(8,128)(2,1)S(1)}, bf16[32,1024]{1,0:T(8,128)(2,1)S(1)}, u32[]{:S(2)}, u32[]{:S(2)}) collective-permute-start(bf16[32,1024]{1,0:T(8,128)(2,1)S(1)} %constant_dynamic-slice_fusion.12), channel_id=1, source_target_pairs={{0,24},{4,28},{8,16},{12,20},{16,8},{20,12},{24,0},{28,4},{1,25},{... | collective-permute-start | bytes 196616 | tf_op jit(solution)/shard_map/ppermute | solution.py:22
  9.3 3.0 %collective-permute-done = bf16[32,1024]{1,0:T(8,128)(2,1)S(1)} collective-permute-done((bf16[32,1024]{1,0:T(8,128)(2,1)S(1)}, bf16[32,1024]{1,0:T(8,128)(2,1)S(1)}, u32[]{:S(2)}, u32[]{:S(2)}) %collective-permute-start) | collective-permute-done | bytes 65568 | tf_op jit(solution)/shard_map/ppermute | solution.py:22
  12.4 2.5 %collective-permute-start.4 = (bf16[2,32,1024]{2,1,0:T(8,128)(2,1)S(1)}, bf16[2,32,1024]{2,1,0:T(8,128)(2,1)}, u32[]{:S(2)}, u32[]{:S(2)}) collective-permute-start(bf16[2,32,1024]{2,1,0:T(8,128)(2,1)S(1)} %pad_maximum_fusion.4), channel_id=1, source_target_pairs={{0,3},{1,2},{2,1},{3,0},{4,7},{5,6},{6,5},{7,4},{8,11},{9,10},{10,... | collective-permute-start | bytes 393224 | tf_op jit(solution)/shard_map/ppermute | solution.py:32
  16.9 2.1 %collective-permute-start.17 = (bf16[144,512]{1,0:T(8,128)(2,1)S(1)}, bf16[144,512]{1,0:T(8,128)(2,1)S(1)}, u32[]{:S(2)}, u32[]{:S(2)}) collective-permute-start(bf16[144,512]{1,0:T(8,128)(2,1)S(1)} %constant_dynamic-update-slice_fusion.5), channel_id=1, source_target_pairs={{0,24},{4,28},{8,16},{12,20},{16,8},{20,12},{24,0},{28,4},{1,25},{... | collective-permute-start | bytes 442376 | tf_op jit(solution)/shard_map/ppermute | solution.py:22
  19.0 1.5 %multiply_reduce_fusion = f32[1024]{0:T(1024)S(1)} fusion(bf16[1024,512]{1,0:T(8,128)(2,1)} %weight_ref), kind=kLoop, calls=%fused_computation.1 | loop fusion | flops 1571840 | bytes 1052672 | tf_op jit(solution)/shard_map/reduce_sum | solution.py:285
  20.7 1.2 %constant_dynamic-slice_fusion.7 = (bf16[864,128]{1,0:T(8,128)(2,1)S(1)}, bf16[864,128]{1,0:T(8,128)(2,1)S(1)}, bf16[864,128]{1,0:T(8,128)(2,1)S(1)}, bf16[864,1...) fusion(bf16[864,1024]{1,0:T(8,128)(2,1)S(1)} %copy-done.9, ...), kind=kLoop, calls=%fused_computation.90 | loop fusion | bytes 3538976 | tf_op jit(solution)/shard_map/dynamic_slice | solution.py:251
  21.9 1.0 %pad_maximum_fusion.att_ref = bf16[864,512]{1,0:T(8,128)(2,1)} fusion(bf16[864,128]{1,0:T(8,128)(2,1)S(1)} %get-tuple-element.34, bf16[864,128]{1,0:T(8,128)(2,1)S(1)} %get-tuple-element.35, bf16[864,128]{1,0:T(8,128)(2,1)S(1)} %get-tuple-element.36, bf16[864,128]{1,0:T(8,128)(2,1)S(1)} %get-tuple-element.33), kind=kLoop, calls=%fused_computation.14 | loop fusion | flops 3538944 | bytes 1769472 | tf_op jit(solution)/shard_map/concatenate | solution.py:252
  23.5 1.3 %copy.39 = bf16[1024,512]{0,1:T(8,128)(2,1)} copy(bf16[1024,512]{1,0:T(8,128)(2,1)S(1)} %copy-done) | data formatting | bytes 2097152 | tf_op jit(solution)/shard_map/optimization_barrier | solution.py:234
  24.8 1.1 %convert_bitcast_fusion.weight_ref = f32[64,1024]{1,0:T(8,128)S(1)} fusion(bf16[1024,512]{0,1:T(8,128)(2,1)} %copy.39, s32[]{:T(128)S(6)} %select_n.200), kind=kLoop, calls=%fused_computation.20 | loop fusion | flops 65536 | bytes 393220 | tf_op jit(solution)/shard_map/convert_element_type | solution.py:288
  27.0 2.3 %collective-permute-start.15 = (bf16[144,512]{1,0:T(8,128)(2,1)S(1)}, bf16[144,512]{1,0:T(8,128)(2,1)S(1)}, u32[]{:S(2)}, u32[]{:S(2)}) collective-permute-start(bf16[144,512]{1,0:T(8,128)(2,1)S(1)} %constant_dynamic-update-slice_fusion.5), channel_id=1, source_target_pairs={{0,8},{4,12},{8,0},{12,4},{16,24},{20,28},{24,16},{28,20},{1,9},{5... | collective-permute-start | bytes 442376 | tf_op jit(solution)/shard_map/ppermute | solution.py:22
  29.3 1.1 %pad_maximum_fusion.2 = bf16[256,1024]{1,0:T(8,128)(2,1)S(1)} fusion(bf16[128,1024]{1,0:T(8,128)(2,1)} %collective-permute-done.2, bf16[128,1024]{1,0:T(8,128)(2,1)} %param.12), kind=kLoop, calls=%fused_computation.19 | loop fusion | flops 1048576 | bytes 1048576 | tf_op jit(solution)/shard_map/concatenate | solution.py:233
  32.9 1.2 %collective-permute-done.16 = bf16[144,512]{1,0:T(8,128)(2,1)S(1)} collective-permute-done((bf16[144,512]{1,0:T(8,128)(2,1)S(1)}, bf16[144,512]{1,0:T(8,128)(2,1)S(1)}, u32[]{:S(2)}, u32[]{:S(2)}) %collective-permute-start.16) | collective-permute-done | bytes 147488 | tf_op jit(solution)/shard_map/ppermute | solution.py:22
  34.1 0.9 %pad_maximum_fusion.1 = bf16[4,144,512]{2,1,0:T(8,128)(2,1)} fusion(bf16[1,144,512]{2,1,0:T(8,128)(2,1)S(1)} %bitcast.99, bf16[1,144,512]{2,1,0:T(8,128)(2,1)S(1)} %bitcast.101, bf16[1,144,512]{2,1,0:T(8,128)(2,1)S(1)} %bitcast.103, bf16[1,144,512]{2,1,0:T(8,128)(2,1)S(1)} %bitcast.98), kind=kLoop, calls=%fused_computation.18 | loop fusion | flops 884736 | bytes 1179648 | tf_op jit(solution)/shard_map/stack | solution.py:263
  35.9 2.1 %convert_add_fusion.part_ref = f32[864,1024]{1,0:T(8,128)S(1)} fusion(bf16[864,1024]{1,0:T(8,128)(2,1)S(1)} %copy-done.21, bf16[256,1024]{1,0:T(8,128)(2,1)S(1)} %collective-permute-done.3, bf16[128,1024]{1,0:T(8,128)(2,1)} %collective-permute-done.2, bf16[128,1024]{1,0:T(8,128)(2,1)S(1)} %copy-done.17, bf16[864,128]{1,0:T(8,128)(2,1)S(1)} %get-tuple-element.37, ...), kind=kOutput, calls=%fused_computation | convolution fusion | flops 914423808 | bytes 7241728 | tf_op jit(solution)/shard_map/dot_general | solution.py:254
  38.1 1.8 %shard_map.121 = bf16[6,1024]{1,0:T(8,128)(2,1)S(1)} custom-call(f32[864,1024]{1,0:T(8,128)S(1)} %convert_add_fusion.part_ref, bf16[864,512]{1,0:T(8,128)(2,1)S(1)} %copy-done.1, bf16[256,1024]{1,0:T(8,128)(2,1)S(1)} %bitcast.91, bf16[256,1024]{1,0:T(8,128)(2,1)S(1)} %collective-permute-done.7.other_ref, f32[1,1024]{1,0:T(1,128)S(1)} %bitcast.95, ...), custom_call_target="tpu_custom_call" | custom-call | flops 905969664 | bytes 7077888 | tf_op jit(solution)/shard_map/pallas_call | solution.py:66
  39.9 2.5 %collective-permute-start.8 = (bf16[6,1024]{1,0:T(8,128)(2,1)S(1)}, bf16[6,1024]{1,0:T(8,128)(2,1)S(1)}, u32[]{:S(2)}, u32[]{:S(2)}) collective-permute-start(bf16[6,1024]{1,0:T(8,128)(2,1)S(1)} %shard_map.121), channel_id=1, source_target_pairs={{0,3},{1,2},{2,1},{3,0},{4,7},{5,6},{6,5},{7,4},{8,11},{9,10},{10,... | collective-permute-start | bytes 36872 | tf_op jit(solution)/shard_map/ppermute | solution.py:32
  43.5 1.1 %collective-permute-done.8 = bf16[6,1024]{1,0:T(8,128)(2,1)S(1)} collective-permute-done((bf16[6,1024]{1,0:T(8,128)(2,1)S(1)}, bf16[6,1024]{1,0:T(8,128)(2,1)S(1)}, u32[]{:S(2)}, u32[]{:S(2)}) %collective-permute-start.8) | collective-permute-done | bytes 12320 | tf_op jit(solution)/shard_map/ppermute | solution.py:32
  44.6 1.6 %collective-permute-done.9 = bf16[6,1024]{1,0:T(8,128)(2,1)S(1)} collective-permute-done((bf16[6,1024]{1,0:T(8,128)(2,1)S(1)}, bf16[6,1024]{1,0:T(8,128)(2,1)S(1)}, u32[]{:S(2)}, u32[]{:S(2)}) %collective-permute-start.9) | collective-permute-done | bytes 12320 | tf_op jit(solution)/shard_map/ppermute | solution.py:32
  47.7 2.5 %collective-permute-start.12 = (bf16[24,1024]{1,0:T(8,128)(2,1)}, bf16[24,1024]{1,0:T(8,128)(2,1)}, u32[]{:S(2)}, u32[]{:S(2)}) collective-permute-start(bf16[24,1024]{1,0:T(8,128)(2,1)} %reshape.290), channel_id=1, source_target_pairs={{0,16},{4,20},{8,24},{12,28},{16,0},{20,4},{24,8},{28,12},{1,17},{... | collective-permute-start | bytes 147464 | tf_op jit(solution)/shard_map/ppermute | solution.py:22
  50.2 1.6 %collective-permute-start.13 = (bf16[24,1024]{1,0:T(8,128)(2,1)}, bf16[24,1024]{1,0:T(8,128)(2,1)}, u32[]{:S(2)}, u32[]{:S(2)}) collective-permute-start(bf16[24,1024]{1,0:T(8,128)(2,1)} %reshape.290), channel_id=1, source_target_pairs={{0,24},{4,28},{8,16},{12,20},{16,8},{20,12},{24,0},{28,4},{1,25},{... | collective-permute-start | bytes 147464 | tf_op jit(solution)/shard_map/ppermute | solution.py:22
  54.9 0.9 %fusion.17 = bf16[4,2,128,512]{3,2,1,0:T(8,128)(2,1)S(1)} fusion(bf16[4,2,128,512]{3,2,1,0:T(8,128)(2,1)S(1)} %fusion.18, s32[]{:T(128)S(6)} %select_n.186, s32[]{:T(128)S(6)} %select_n.185, bf16[4,144,512]{2,1,0:T(8,128)(2,1)} %collective-permute-done.18), kind=kLoop, calls=%fused_computation.31 | loop fusion | bytes 262152 | tf_op jit(solution)/shard_map/dynamic_update_slice | solution.py:268
  55.9 0.9 %fusion.15 = bf16[4,2,128,512]{3,2,1,0:T(8,128)(2,1)S(1)} fusion(bf16[4,2,128,512]{3,2,1,0:T(8,128)(2,1)S(1)} %fusion.16, s32[]{:T(128)S(6)} %select_n.187, s32[]{:T(128)S(6)} %select_n.185, bf16[4,144,512]{2,1,0:T(8,128)(2,1)} %collective-permute-done.18), kind=kLoop, calls=%fused_computation.27 | loop fusion | bytes 262152 | tf_op jit(solution)/shard_map/dynamic_update_slice | solution.py:268
  56.9 0.9 %fusion.13 = bf16[4,2,128,512]{3,2,1,0:T(8,128)(2,1)S(1)} fusion(bf16[4,2,128,512]{3,2,1,0:T(8,128)(2,1)S(1)} %fusion.14, s32[]{:T(128)S(6)} %select_n.188, s32[]{:T(128)S(6)} %select_n.185, bf16[4,144,512]{2,1,0:T(8,128)(2,1)} %collective-permute-done.18), kind=kLoop, calls=%fused_computation.23 | loop fusion | bytes 262152 | tf_op jit(solution)/shard_map/dynamic_update_slice | solution.py:268
  58.5 1.0 %bitcast_select_fusion.code_ref = f32[192,1024]{1,0:T(8,128)S(1)} fusion(f32[8,1024]{1,0:T(8,128)} %select_select_fusion, s32[192]{0:T(256)} %eq.86, pred[8,1024]{1,0:T(8,128)(4,1)S(1)} %broadcast_compare_fusion), kind=kLoop, calls=%fused_computation.15 | loop fusion | flops 589824 | bytes 828160 | tf_op jit(solution)/shard_map/jit(_where)/select_n | solution.py:282
  62.9 1.6 %shard_map.122 = (f32[192,1024]{1,0:T(8,128)S(1)}, f32[192,1024]{1,0:T(8,128)S(1)}, f32[192,640]{1,0:T(8,128)S(1)}, f32[32,1280]{1,0:T(8,128)S(1)}, f32[1,192]{1,0:T(1,128)S(1)}) custom-call(bf16[192,1024]{1,0:T(8,128)(2,1)S(1)} %bitcast.92, bf16[1024,512]{1,0:T(8,128)(2,1)S(1)} %bitcast.89, f32[192,1024]{1,0:T(8,128)S(1)} %bitcast_select_fusion.code_ref, ...), custom_call_target="tpu_custom_call" | custom-call | flops 603979776 | bytes 3145728 | tf_op jit(solution)/shard_map/pallas_call | solution.py:141
  67.8 1.5 %collective-permute-start.20 = (f32[7,1280]{1,0:T(8,128)S(1)}, f32[7,1280]{1,0:T(8,128)S(1)}, u32[]{:S(2)}, u32[]{:S(2)}) collective-permute-start(f32[7,1280]{1,0:T(8,128)S(1)} %get-tuple-element.46), channel_id=1, source_target_pairs={{0,2},{1,3},{2,0},{3,1},{4,6},{5,7},{6,4},{7,5},{8,10},{9,11},{10,... | collective-permute-start | bytes 107528 | tf_op jit(solution)/shard_map/ppermute | solution.py:32
  69.3 1.4 %collective-permute-start.19 = (f32[7,1280]{1,0:T(8,128)S(1)}, f32[7,1280]{1,0:T(8,128)S(1)}, u32[]{:S(2)}, u32[]{:S(2)}) collective-permute-start(f32[7,1280]{1,0:T(8,128)S(1)} %get-tuple-element.45), channel_id=1, source_target_pairs={{0,3},{1,2},{2,1},{3,0},{4,7},{5,6},{6,5},{7,4},{8,11},{9,10},{10,... | collective-permute-start | bytes 107528 | tf_op jit(solution)/shard_map/ppermute | solution.py:32
  70.7 2.1 %copy.38 = f32[192,640]{0,1:T(8,128)} copy(f32[192,640]{1,0:T(8,128)} %copy-done.6) | data formatting | bytes 983040 | tf_op jit(solution)/shard_map/pallas_call | solution.py:141
  74.7 1.0 %multiply_reduce_fusion.1 = f32[6]{0:T(128)S(1)} fusion(f32[192,640]{1,0:T(8,128)} %copy-done.6, s32[]{:T(128)S(6)} %select_n.198, f32[7,1280]{1,0:T(8,128)S(1)} %fusion.27, f32[6]{0:T(128)S(1)} %get-tuple-element.25), kind=kLoop, calls=%fused_computation.78 | loop fusion | flops 15354 | bytes 36916 | tf_op jit(solution)/shard_map/reduce_sum | solution.py:335
  76.2 1.4 %subtract_divide_fusion = f32[6,512]{1,0:T(8,128)} fusion(f32[192,640]{1,0:T(8,128)} %copy-done.6, s32[]{:T(128)S(6)} %select_n.198, f32[6]{0:T(128)S(1)} %dynamic-slice_reduce_fusion, f32[6]{0:T(128)S(1)} %multiply_reduce_fusion.1, f32[7,1280]{1,0:T(8,128)S(1)} %fusion.27, f32[6]{0:T(128)S(1)} %get-tuple-element.25), kind=kLoop, calls=%fused_computation.77 | loop fusion | flops 18432 | bytes 49228 | tf_op jit(solution)/shard_map/div | solution.py:334
  77.7 1.2 %shard_map.123 = f32[64,1024]{1,0:T(8,128)} custom-call(f32[1,192]{1,0:T(1,128)S(1)} %slice.115.denom_ref, f32[192,1024]{1,0:T(8,128)S(1)} %copy-done.3, f32[192,1024]{1,0:T(8,128)S(1)} %copy-done.5, f32[192,1024]{1,0:T(8,128)S(1)} %bitcast_select_fusion.code_ref, f32[64,192]{1,0:T(8,128)S(1)} %dynamic-slice_bitcast_fusion.unit_ref, ...), custom_call_target="tpu_custom_call" | custom-call | flops 125829120 | bytes 2359296 | tf_op jit(solution)/shard_map/pallas_call | solution.py:185
  (127 shorter events, 25.2 us)
Async XLA Ops:
  1.5 7.8 %collective-permute-start.1 = (bf16[32,1024]{1,0:T(8,128)(2,1)S(1)}, bf16[32,1024]{1,0:T(8,128)(2,1)S(1)}, u32[]{:S(2)}, u32[]{:S(2)}) collective-permute-start(bf16[32,1024]{1,0:T(8,128)(2,1)S(1)} %constant_dynamic-slice_fusion.12), channel_id=1, source_target_pairs={{0,16},{4,20},{8,24},{12,28},{16,0},{20,4},{24,8},{28,12},{1,17},{... | collective-permute-start | bytes 196616 | tf_op jit(solution)/shard_map/ppermute | solution.py:22
  5.5 6.8 %collective-permute-start = (bf16[32,1024]{1,0:T(8,128)(2,1)S(1)}, bf16[32,1024]{1,0:T(8,128)(2,1)S(1)}, u32[]{:S(2)}, u32[]{:S(2)}) collective-permute-start(bf16[32,1024]{1,0:T(8,128)(2,1)S(1)} %constant_dynamic-slice_fusion.12), channel_id=1, source_target_pairs={{0,24},{4,28},{8,16},{12,20},{16,8},{20,12},{24,0},{28,4},{1,25},{... | collective-permute-start | bytes 196616 | tf_op jit(solution)/shard_map/ppermute | solution.py:22
  6.9 20.2 %collective-permute-start.2 = (bf16[128,1024]{1,0:T(8,128)(2,1)}, bf16[128,1024]{1,0:T(8,128)(2,1)}, u32[]{:S(2)}, u32[]{:S(2)}) collective-permute-start(bf16[128,1024]{1,0:T(8,128)(2,1)} %param.12), channel_id=1, source_target_pairs={{0,8},{4,12},{8,0},{12,4},{16,24},{20,28},{24,16},{28,20},{1,9},{5... | collective-permute-start | bytes 786440 | tf_op jit(solution)/shard_map/ppermute | solution.py:22
  12.4 13.5 %collective-permute-start.4 = (bf16[2,32,1024]{2,1,0:T(8,128)(2,1)S(1)}, bf16[2,32,1024]{2,1,0:T(8,128)(2,1)}, u32[]{:S(2)}, u32[]{:S(2)}) collective-permute-start(bf16[2,32,1024]{2,1,0:T(8,128)(2,1)S(1)} %pad_maximum_fusion.4), channel_id=1, source_target_pairs={{0,3},{1,2},{2,1},{3,0},{4,7},{5,6},{6,5},{7,4},{8,11},{9,10},{10,... | collective-permute-start | bytes 393224 | tf_op jit(solution)/shard_map/ppermute | solution.py:32
  14.9 15.5 %collective-permute-start.5 = (bf16[2,32,1024]{2,1,0:T(8,128)(2,1)S(1)}, bf16[2,32,1024]{2,1,0:T(8,128)(2,1)}, u32[]{:S(2)}, u32[]{:S(2)}) collective-permute-start(bf16[2,32,1024]{2,1,0:T(8,128)(2,1)S(1)} %pad_maximum_fusion.4), channel_id=1, source_target_pairs={{0,2},{1,3},{2,0},{3,1},{4,6},{5,7},{6,4},{7,5},{8,10},{9,11},{10,... | collective-permute-start | bytes 393224 | tf_op jit(solution)/shard_map/ppermute | solution.py:32
  15.4 16.0 %collective-permute-start.6 = (bf16[2,32,1024]{2,1,0:T(8,128)(2,1)S(1)}, bf16[2,32,1024]{2,1,0:T(8,128)(2,1)}, u32[]{:S(2)}, u32[]{:S(2)}) collective-permute-start(bf16[2,32,1024]{2,1,0:T(8,128)(2,1)S(1)} %pad_maximum_fusion.4), channel_id=1, source_target_pairs={{0,1},{1,0},{2,3},{3,2},{4,5},{5,4},{6,7},{7,6},{8,9},{9,8},{10,11... | collective-permute-start | bytes 393224 | tf_op jit(solution)/shard_map/ppermute | solution.py:32
  16.9 16.0 %collective-permute-start.17 = (bf16[144,512]{1,0:T(8,128)(2,1)S(1)}, bf16[144,512]{1,0:T(8,128)(2,1)S(1)}, u32[]{:S(2)}, u32[]{:S(2)}) collective-permute-start(bf16[144,512]{1,0:T(8,128)(2,1)S(1)} %constant_dynamic-update-slice_fusion.5), channel_id=1, source_target_pairs={{0,24},{4,28},{8,16},{12,20},{16,8},{20,12},{24,0},{28,4},{1,25},{... | collective-permute-start | bytes 442376 | tf_op jit(solution)/shard_map/ppermute | solution.py:22
  24.8 11.1 %copy-start.17 = (bf16[128,1024]{1,0:T(8,128)(2,1)S(1)}, bf16[128,1024]{1,0:T(8,128)(2,1)}, u32[]{:S(2)}) copy-start(bf16[128,1024]{1,0:T(8,128)(2,1)} %param.12) | copy-start | bytes 786436
  24.8 11.1 %copy-start.18 = (bf16[864,128]{1,0:T(8,128)(2,1)S(1)}, bf16[864,128]{1,0:T(8,128)(2,1)}, u32[]{:S(2)}) copy-start(bf16[864,128]{1,0:T(8,128)(2,1)} %get-tuple-element.38) | copy-start | bytes 663556
  24.8 11.1 %copy-start.19 = (bf16[864,128]{1,0:T(8,128)(2,1)S(1)}, bf16[864,128]{1,0:T(8,128)(2,1)}, u32[]{:S(2)}) copy-start(bf16[864,128]{1,0:T(8,128)(2,1)} %get-tuple-element.39) | copy-start | bytes 663556
  24.8 11.1 %copy-start.20 = (bf16[864,128]{1,0:T(8,128)(2,1)S(1)}, bf16[864,128]{1,0:T(8,128)(2,1)}, u32[]{:S(2)}) copy-start(bf16[864,128]{1,0:T(8,128)(2,1)} %get-tuple-element.40) | copy-start | bytes 663556
  24.8 11.1 %copy-start.21 = (bf16[864,1024]{1,0:T(8,128)(2,1)S(1)}, bf16[864,1024]{1,0:T(8,128)(2,1)}, u32[]{:S(2)}) copy-start(bf16[864,1024]{1,0:T(8,128)(2,1)} %param.11) | copy-start | bytes 5308420
  25.9 8.1 %collective-permute-start.16 = (bf16[144,512]{1,0:T(8,128)(2,1)S(1)}, bf16[144,512]{1,0:T(8,128)(2,1)S(1)}, u32[]{:S(2)}, u32[]{:S(2)}) collective-permute-start(bf16[144,512]{1,0:T(8,128)(2,1)S(1)} %constant_dynamic-update-slice_fusion.5), channel_id=1, source_target_pairs={{0,16},{4,20},{8,24},{12,28},{16,0},{20,4},{24,8},{28,12},{1,17},{... | collective-permute-start | bytes 442376 | tf_op jit(solution)/shard_map/ppermute | solution.py:22
  27.0 7.0 %collective-permute-start.15 = (bf16[144,512]{1,0:T(8,128)(2,1)S(1)}, bf16[144,512]{1,0:T(8,128)(2,1)S(1)}, u32[]{:S(2)}, u32[]{:S(2)}) collective-permute-start(bf16[144,512]{1,0:T(8,128)(2,1)S(1)} %constant_dynamic-update-slice_fusion.5), channel_id=1, source_target_pairs={{0,8},{4,12},{8,0},{12,4},{16,24},{20,28},{24,16},{28,20},{1,9},{5... | collective-permute-start | bytes 442376 | tf_op jit(solution)/shard_map/ppermute | solution.py:22
  30.4 5.5 %collective-permute-start.3 = (bf16[256,1024]{1,0:T(8,128)(2,1)S(1)}, bf16[256,1024]{1,0:T(8,128)(2,1)S(1)}, u32[]{:S(2)}, u32[]{:S(2)}) collective-permute-start(bf16[256,1024]{1,0:T(8,128)(2,1)S(1)} %pad_maximum_fusion.2), channel_id=1, source_target_pairs={{0,4},{4,0},{8,12},{12,8},{16,20},{20,16},{24,28},{28,24},{1,5},{5... | collective-permute-start | bytes 1572872 | tf_op jit(solution)/shard_map/ppermute | solution.py:27
  32.3 5.8 %collective-permute-start.7 = (bf16[256,1024]{1,0:T(8,128)(2,1)S(1)}, bf16[256,1024]{1,0:T(8,128)(2,1)S(1)}, u32[]{:S(2)}, u32[]{:S(2)}) collective-permute-start(bf16[256,1024]{1,0:T(8,128)(2,1)S(1)} %bitcast.90), channel_id=1, source_target_pairs={{0,4},{4,0},{8,12},{12,8},{16,20},{20,16},{24,28},{28,24},{1,5},{5... | collective-permute-start | bytes 1572872 | tf_op jit(solution)/shard_map/ppermute | solution.py:27
  35.0 16.8 %collective-permute-start.18 = (bf16[4,144,512]{2,1,0:T(8,128)(2,1)}, bf16[4,144,512]{2,1,0:T(8,128)(2,1)}, u32[]{:S(2)}, u32[]{:S(2)}) collective-permute-start(bf16[4,144,512]{2,1,0:T(8,128)(2,1)} %pad_maximum_fusion.1), channel_id=1, source_target_pairs={{0,4},{4,0},{8,12},{12,8},{16,20},{20,16},{24,28},{28,24},{1,5},{5... | collective-permute-start | bytes 1769480 | tf_op jit(solution)/shard_map/ppermute | solution.py:27
  38.1 16.8 %copy-start.15 = (bf16[144,512]{1,0:T(8,128)(2,1)S(1)}, bf16[144,512]{1,0:T(8,128)(2,1)}, u32[]{:S(2)}) copy-start(bf16[144,512]{1,0:T(8,128)(2,1)} %copy-done.14) | copy-start | bytes 442372
  39.9 15.9 %copy-start.13 = (bf16[144,512]{1,0:T(8,128)(2,1)S(1)}, bf16[144,512]{1,0:T(8,128)(2,1)}, u32[]{:S(2)}) copy-start(bf16[144,512]{1,0:T(8,128)(2,1)} %copy-done.12) | copy-start | bytes 442372
  39.9 16.9 %copy-start.11 = (bf16[144,512]{1,0:T(8,128)(2,1)S(1)}, bf16[144,512]{1,0:T(8,128)(2,1)}, u32[]{:S(2)}) copy-start(bf16[144,512]{1,0:T(8,128)(2,1)} %copy-done.10) | copy-start | bytes 442372
  39.9 4.7 %collective-permute-start.8 = (bf16[6,1024]{1,0:T(8,128)(2,1)S(1)}, bf16[6,1024]{1,0:T(8,128)(2,1)S(1)}, u32[]{:S(2)}, u32[]{:S(2)}) collective-permute-start(bf16[6,1024]{1,0:T(8,128)(2,1)S(1)} %shard_map.121), channel_id=1, source_target_pairs={{0,3},{1,2},{2,1},{3,0},{4,7},{5,6},{6,5},{7,4},{8,11},{9,10},{10,... | collective-permute-start | bytes 36872 | tf_op jit(solution)/shard_map/ppermute | solution.py:32
  42.5 3.7 %collective-permute-start.9 = (bf16[6,1024]{1,0:T(8,128)(2,1)S(1)}, bf16[6,1024]{1,0:T(8,128)(2,1)S(1)}, u32[]{:S(2)}, u32[]{:S(2)}) collective-permute-start(bf16[6,1024]{1,0:T(8,128)(2,1)S(1)} %shard_map.121), channel_id=1, source_target_pairs={{0,2},{1,3},{2,0},{3,1},{4,6},{5,7},{6,4},{7,5},{8,10},{9,11},{10,... | collective-permute-start | bytes 36872 | tf_op jit(solution)/shard_map/ppermute | solution.py:32
  43.0 3.7 %collective-permute-start.10 = (bf16[6,1024]{1,0:T(8,128)(2,1)S(1)}, bf16[6,1024]{1,0:T(8,128)(2,1)S(1)}, u32[]{:S(2)}, u32[]{:S(2)}) collective-permute-start(bf16[6,1024]{1,0:T(8,128)(2,1)S(1)} %shard_map.121), channel_id=1, source_target_pairs={{0,1},{1,0},{2,3},{3,2},{4,5},{5,4},{6,7},{7,6},{8,9},{9,8},{10,11... | collective-permute-start | bytes 36872 | tf_op jit(solution)/shard_map/ppermute | solution.py:32
  46.7 11.1 %copy-start.16 = (bf16[1,24,1024]{2,1,0:T(8,128)(2,1)}, bf16[1,24,1024]{2,1,0:T(8,128)(2,1)S(1)}, u32[]{:S(2)}) copy-start(bf16[1,24,1024]{2,1,0:T(8,128)(2,1)S(1)} %stack_reshape.3) | copy-start | bytes 147460
  47.4 12.1 %collective-permute-start.11 = (bf16[24,1024]{1,0:T(8,128)(2,1)}, bf16[24,1024]{1,0:T(8,128)(2,1)}, u32[]{:S(2)}, u32[]{:S(2)}) collective-permute-start(bf16[24,1024]{1,0:T(8,128)(2,1)} %reshape.290), channel_id=1, source_target_pairs={{0,8},{4,12},{8,0},{12,4},{16,24},{20,28},{24,16},{28,20},{1,9},{5... | collective-permute-start | bytes 147464 | tf_op jit(solution)/shard_map/ppermute | solution.py:22
  47.7 11.8 %collective-permute-start.12 = (bf16[24,1024]{1,0:T(8,128)(2,1)}, bf16[24,1024]{1,0:T(8,128)(2,1)}, u32[]{:S(2)}, u32[]{:S(2)}) collective-permute-start(bf16[24,1024]{1,0:T(8,128)(2,1)} %reshape.290), channel_id=1, source_target_pairs={{0,16},{4,20},{8,24},{12,28},{16,0},{20,4},{24,8},{28,12},{1,17},{... | collective-permute-start | bytes 147464 | tf_op jit(solution)/shard_map/ppermute | solution.py:22
  50.2 9.3 %collective-permute-start.13 = (bf16[24,1024]{1,0:T(8,128)(2,1)}, bf16[24,1024]{1,0:T(8,128)(2,1)}, u32[]{:S(2)}, u32[]{:S(2)}) collective-permute-start(bf16[24,1024]{1,0:T(8,128)(2,1)} %reshape.290), channel_id=1, source_target_pairs={{0,24},{4,28},{8,16},{12,20},{16,8},{20,12},{24,0},{28,4},{1,25},{... | collective-permute-start | bytes 147464 | tf_op jit(solution)/shard_map/ppermute | solution.py:22
  60.4 2.5 %collective-permute-start.14 = (bf16[4,24,1024]{2,1,0:T(8,128)(2,1)S(1)}, bf16[4,24,1024]{2,1,0:T(8,128)(2,1)S(1)}, u32[]{:S(2)}, u32[]{:S(2)}) collective-permute-start(bf16[4,24,1024]{2,1,0:T(8,128)(2,1)S(1)} %pad_maximum_fusion.3), channel_id=1, source_target_pairs={{0,4},{4,0},{8,12},{12,8},{16,20},{20,16},{24,28},{28,24},{1,5},{5... | collective-permute-start | bytes 589832 | tf_op jit(solution)/shard_map/ppermute | solution.py:27
  67.1 10.6 %copy-start.5 = (f32[192,1024]{1,0:T(8,128)S(1)}, f32[192,1024]{1,0:T(8,128)}, u32[]{:S(2)}) copy-start(f32[192,1024]{1,0:T(8,128)} %copy-done.4) | copy-start | bytes 2359300
  67.2 7.4 %collective-permute-start.21 = (f32[7,1280]{1,0:T(8,128)S(1)}, f32[7,1280]{1,0:T(8,128)S(1)}, u32[]{:S(2)}, u32[]{:S(2)}) collective-permute-start(f32[7,1280]{1,0:T(8,128)S(1)} %get-tuple-element.47), channel_id=1, source_target_pairs={{0,1},{1,0},{2,3},{3,2},{4,5},{5,4},{6,7},{7,6},{8,9},{9,8},{10,11... | collective-permute-start | bytes 107528 | tf_op jit(solution)/shard_map/ppermute | solution.py:32
  67.8 6.8 %collective-permute-start.20 = (f32[7,1280]{1,0:T(8,128)S(1)}, f32[7,1280]{1,0:T(8,128)S(1)}, u32[]{:S(2)}, u32[]{:S(2)}) collective-permute-start(f32[7,1280]{1,0:T(8,128)S(1)} %get-tuple-element.46), channel_id=1, source_target_pairs={{0,2},{1,3},{2,0},{3,1},{4,6},{5,7},{6,4},{7,5},{8,10},{9,11},{10,... | collective-permute-start | bytes 107528 | tf_op jit(solution)/shard_map/ppermute | solution.py:32
  69.3 5.3 %collective-permute-start.19 = (f32[7,1280]{1,0:T(8,128)S(1)}, f32[7,1280]{1,0:T(8,128)S(1)}, u32[]{:S(2)}, u32[]{:S(2)}) collective-permute-start(f32[7,1280]{1,0:T(8,128)S(1)} %get-tuple-element.45), channel_id=1, source_target_pairs={{0,3},{1,2},{2,1},{3,0},{4,7},{5,6},{6,5},{7,4},{8,11},{9,10},{10,... | collective-permute-start | bytes 107528 | tf_op jit(solution)/shard_map/ppermute | solution.py:32
  (12 other events, 38.4 us)

commit v3 on v2

v3 whole, which is shorter than its diff:
```python
import functools
import math

import jax
import jax.numpy as jnp
from jax import lax
from jax.experimental import pallas as pl
from jax.experimental.pallas import tpu as pltpu
from jax.sharding import PartitionSpec as P

P_SIZE = 144
BLOCK_ROWS = 128
CORES = 2

LOGIT_SCALE = 64.0
ANGLE_MARGIN = 0.5
NORM_EPSILON = 1e-06


def z_swap(value, step):
    count = lax.axis_size("dp")
    return lax.ppermute(value, "dp", [(i, i ^ (step * CORES)) for i in range(count)])


def core_swap(value):
    count = lax.axis_size("dp")
    return lax.ppermute(value, "dp", [(i, i ^ 1) for i in range(count)])


def plane_swap(value, step):
    count = lax.axis_size("cls")
    return lax.ppermute(value, "cls", [(i, i ^ step) for i in range(count)])


def pool_kernel(att_ref, stream_ref, own_ref, near_ref, own_other_ref, near_other_ref, far_ref, far_other_ref,
                gain_ref, shift_ref, out_ref, weight_ref, mixed_ref, pooled_ref):
    tokens, width = stream_ref.shape
    images = tokens // P_SIZE
    rows = own_ref.shape[0]
    n_cls, n_far, slice_rows, _ = far_ref.shape
    dp, cls = lax.axis_index("dp"), lax.axis_index("cls")
    z, core = dp // CORES, dp % CORES

    def place(shard, start, value):
        at = pl.multiple_of(shard * rows + start, slice_rows)
        weight_ref[pl.ds(at, value.shape[0]), :] = value

    for side, own, near, far in (
        (core, own_ref, near_ref, far_ref), (1 - core, own_other_ref, near_other_ref, far_other_ref)
    ):
        place(z * CORES + side, 0, own[...])
        place((z ^ 1) * CORES + side, 0, near[...])
        for k in range(n_far):
            for step in range(n_cls):
                start = (cls ^ step) * slice_rows if n_cls > 1 else 0
                place((z ^ (k + 2)) * CORES + side, start, far[step, k])
    per = 3 if images % 3 == 0 else 1
    chunk = per * P_SIZE
    for start in range(0, tokens, chunk):
        here = pl.ds(start, chunk)
        mixed_ref[here, :] = stream_ref[here, :].astype(jnp.float32) + jnp.dot(
            att_ref[here, :], weight_ref[...], preferred_element_type=jnp.float32
        )
    step = 24
    for image in range(images):
        total = jnp.zeros((8, width), jnp.float32)
        for r in range(0, P_SIZE, step):
            x = mixed_ref[pl.ds(image * P_SIZE + r, step), :]
            centred = x - jnp.mean(x, axis=1, keepdims=True)
            variance = jnp.mean(centred * centred, axis=1, keepdims=True)
            scaled = centred * lax.rsqrt(variance + NORM_EPSILON)
            total = total + jnp.sum(scaled.reshape(step // 8, 8, width), axis=0)
        mean = jnp.sum(total, axis=0, keepdims=True) * (1.0 / P_SIZE)
        pooled_ref[pl.ds(image, 1), :] = gain_ref[...] * mean + shift_ref[...]
    if images < pooled_ref.shape[0]:
        pooled_ref[images:, :] = jnp.zeros((pooled_ref.shape[0] - images, width), jnp.float32)
    out_ref[...] = pooled_ref[...].astype(out_ref.dtype)


def padded(images):
    return -(-images // 8) * 8


def in_vmem(kernel, outs, scratch, mib, flops, operands):
    vmem = pl.BlockSpec(memory_space=pltpu.VMEM)
    moved = sum(math.prod(x.shape) * x.dtype.itemsize for x in list(operands) + list(outs))
    return pl.pallas_call(
        kernel,
        out_shape=tuple(outs),
        in_specs=[vmem] * len(operands),
        out_specs=(vmem,) * len(outs),
        scratch_shapes=scratch,
        compiler_params=pltpu.CompilerParams(vmem_limit_bytes=mib * 1024 * 1024),
        cost_estimate=pl.CostEstimate(flops=flops, bytes_accessed=moved, transcendentals=0),
    )(*operands)


def f32(*shape):
    return jax.ShapeDtypeStruct(shape, jnp.float32)


def pool_tokens(*operands):
    tokens, width = operands[0].shape
    lines = padded(tokens // P_SIZE)
    return in_vmem(
        pool_kernel,
        [jax.ShapeDtypeStruct((lines, width), jnp.bfloat16)],
        [
            pltpu.VMEM((width, width), jnp.bfloat16),
            pltpu.VMEM((tokens, width), jnp.float32),
            pltpu.VMEM((lines, width), jnp.float32),
        ],
        12,
        2 * tokens * width * width,
        operands,
    )[0]


def split(value):
    high = value.astype(jnp.bfloat16)
    return high, (value - high.astype(jnp.float32)).astype(jnp.bfloat16)


def as_row(column):
    return jnp.broadcast_to(column, (column.shape[0], 128)).T[0:1]


def over_lanes(left, right):
    return lax.dot_general(left, right, (((1,), (1,)), ((), ())), preferred_element_type=jnp.float32)


def one_hot(rows, columns, at):
    row = lax.broadcasted_iota(jnp.int32, (rows, columns), 0)
    column = lax.broadcasted_iota(jnp.int32, (rows, columns), 1)
    return jnp.where(column == at(row), 1.0, 0.0).astype(jnp.bfloat16)


def masks(image_ref, start, wide):
    images = image_ref.shape[0]
    label, bits = image_ref[:, 0:1], image_ref[:, 1:2]
    live = [
        jnp.broadcast_to((bits & (1 << (k // BLOCK_ROWS))) != 0, (images, BLOCK_ROWS))
        for k in range(start, start + wide, BLOCK_ROWS)
    ]
    live = jnp.concatenate(live, axis=1)
    column = lax.broadcasted_iota(jnp.int32, (images, wide), 1) + start
    return live, live & (column == label)


def class_kernel(own, pooled_ref, head_ref, other_ref, image_ref, weight_ref, scale_ref,
                 exp_ref, cos_ref, unit_ref, sums_ref, denom_ref, whole_ref, chosen_ref, group_ref):
    images = pooled_ref.shape[0]
    classes, embed = weight_ref.shape
    n_z = head_ref.shape[0]
    n_cls = sums_ref.shape[0]
    rows = pooled_ref.shape[1] // (CORES * n_z)
    dp, cls = lax.axis_index("dp"), lax.axis_index("cls")
    z, core = dp // CORES, dp % CORES
    for k in range(n_z):
        for side, source in ((core, head_ref), (1 - core, other_ref)):
            at = pl.multiple_of(((z ^ k) * CORES + side) * rows, rows)
            whole_ref[pl.ds(at, rows), :] = source[k, :rows, :]
    embedding = jnp.dot(pooled_ref[...], whole_ref[...], preferred_element_type=jnp.float32)
    norm = jnp.sqrt(jnp.sum(embedding * embedding, axis=1, keepdims=True) + NORM_EPSILON)
    unit = embedding * (1.0 / norm)
    unit_ref[:, :embed] = unit
    unit_ref[:, embed:] = jnp.broadcast_to(norm, (images, 128))
    terms = jnp.concatenate(split(unit), axis=0)
    denom = jnp.zeros((images, 128), jnp.float32)
    picked = jnp.zeros((own, 128), jnp.float32)
    wide = 256
    for start in range(0, classes, wide):
        cols = pl.ds(start, wide)
        both = over_lanes(terms, weight_ref[cols, :])
        cosine = (both[:images] + both[images:]) * scale_ref[:, cols]
        cos_ref[:, cols] = cosine
        live, target = masks(image_ref, start, wide)
        sine = jnp.sqrt(jnp.maximum(1.0 - cosine * cosine, 0.0))
        margin = cosine * math.cos(ANGLE_MARGIN) - sine * math.sin(ANGLE_MARGIN)
        logits = LOGIT_SCALE * jnp.where(target, margin, cosine)
        exponent = jnp.where(live, jnp.exp(logits), 0.0)
        exp_ref[:, cols] = exponent
        labelled = jnp.where(target, logits, 0.0)[:own]
        chosen_ref[:, cols] = jnp.where(target[:own], scale_ref[:, cols], 0.0)
        for k in range(0, wide, 128):
            denom = denom + exponent[:, k : k + 128]
            picked = picked + labelled[:, k : k + 128]
    denom = jnp.sum(denom, axis=1, keepdims=True)
    denom_ref[...] = as_row(denom)
    weighted = split(exp_ref[:own, :] * scale_ref[...])
    chosen = split(chosen_ref[...])
    sums = jnp.dot(
        jnp.concatenate(weighted + chosen, axis=0), weight_ref[...], preferred_element_type=jnp.float32
    )
    sums = jnp.concatenate(
        [
            sums[:own] + sums[own : 2 * own],
            sums[2 * own : 3 * own] + sums[3 * own :],
            jnp.broadcast_to(denom[:own], (own, 128)),
            jnp.broadcast_to(jnp.sum(picked, axis=1, keepdims=True), (own, 128)),
        ],
        axis=1,
    )
    group_ref[...] = sums
    lines = sums_ref.shape[1]
    for step in range(n_cls):
        at = pl.multiple_of((cls ^ step) * lines, lines)
        sums_ref[step] = group_ref[pl.ds(at, lines), :]


def class_parts(own, n_cls, *operands):
    pooled, head, _, _, weight, _ = operands
    images, width = pooled.shape
    classes, embed = weight.shape
    return in_vmem(
        functools.partial(class_kernel, own),
        [
            f32(images, classes),
            f32(images, classes),
            f32(images, embed + 128),
            f32(n_cls, own // n_cls, 2 * embed + 256),
            f32(1, images),
        ],
        [
            pltpu.VMEM((width, embed), jnp.bfloat16),
            pltpu.VMEM((own, classes), jnp.float32),
            pltpu.VMEM((own, 2 * embed + 256), jnp.float32),
        ],
        6,
        6 * images * embed * classes,
        operands,
    )


def grad_kernel(share, total_ref, denom_ref, exp_ref, cos_ref, unit_ref, image_ref, weight_ref, scale_ref,
                grad_ref, loss_ref, embed_ref):
    images, classes = exp_ref.shape
    embed = weight_ref.shape[1]
    at = lax.axis_index("dp") * share
    block = pl.ds(pl.multiple_of(at // 128 * 128, 128), 128)
    take = one_hot(share, 128, lambda row: row + at % 128)
    high, low = split(unit_ref[:, block])
    unit = over_lanes(take, high) + over_lanes(take, low)
    weight = over_lanes(take, weight_ref[:, block])
    denom = denom_ref[...]
    ratio = jnp.where(denom > 0.0, LOGIT_SCALE / denom, 0.0)
    left = jnp.concatenate(split(unit * ratio), axis=0)
    marked = jnp.concatenate(split(unit * LOGIT_SCALE), axis=0)
    column = jnp.broadcast_to(ratio, (128, images)).T[:, 0:1]
    dot = functools.partial(jnp.dot, preferred_element_type=jnp.float32)
    wide = 256
    for start in range(0, classes, wide):
        cols = pl.ds(start, wide)
        exponent = exp_ref[:, cols]
        _, target = masks(image_ref, start, wide)
        high, low = split(exponent)
        first = dot(left, high)
        second = dot(marked, jnp.where(target, 1.0, 0.0).astype(jnp.bfloat16))
        grad = first[:share] + first[share:] + dot(left[:share], low) - second[:share] - second[share:]
        weighted = exponent * column - jnp.where(target, LOGIT_SCALE, 0.0)
        along = jnp.sum(weighted * cos_ref[:, cols], axis=0, keepdims=True)
        scale = scale_ref[:, cols]
        grad_ref[:, cols] = (grad - weight[:, start : start + wide] * (along * scale)) * scale

    lines = padded(embed_ref.shape[0])
    own = unit_ref[pl.ds(pl.multiple_of(lax.axis_index("cls") * lines, lines), lines), :][: embed_ref.shape[0]]
    total = total_ref[: embed_ref.shape[0], :]
    weighted, picked = total[:, :embed], total[:, embed : 2 * embed]
    own_denom, target_logit = total[:, 2 * embed : 2 * embed + 1], total[:, 2 * embed + 128 : 2 * embed + 129]
    loss = jnp.broadcast_to(jnp.log(own_denom) - target_logit, (loss_ref.shape[1], 128))
    loss = jnp.concatenate([loss, jnp.zeros((128 - loss_ref.shape[1], 128), jnp.float32)], axis=0)
    loss_ref[...] = loss.T[0:1, : loss_ref.shape[1]]
    unit_grad = LOGIT_SCALE * (weighted / own_denom - picked)
    own_unit = own[:, :embed]
    embed_ref[...] = (
        unit_grad - own_unit * jnp.sum(own_unit * unit_grad, axis=1, keepdims=True)
    ) / own[:, embed : embed + 1]


def class_grad_part(share, own_images, *operands):
    images, classes = operands[2].shape
    embed = operands[6].shape[1]
    return in_vmem(
        functools.partial(grad_kernel, share),
        [f32(share, classes), f32(1, own_images), f32(own_images, embed)],
        [],
        6,
        10 * images * share * classes,
        operands,
    )


def per_device(
    attended,
    stream,
    out_proj,
    norm_gain,
    norm_shift,
    head_proj,
    class_weight,
    block_ids,
    block_count,
    labels,
):
    n_dp, n_cls = lax.axis_size("dp"), lax.axis_size("cls")
    n_z = n_dp // CORES
    dp, cls = lax.axis_index("dp"), lax.axis_index("cls")
    tokens, width = attended.shape
    images = tokens // P_SIZE
    size = n_cls * images
    lines = padded(images)
    group_lines = n_cls * lines
    rows = out_proj.shape[0]
    slice_rows = rows // n_cls
    slots = block_ids.shape[2]
    classes, embed = class_weight.shape

    facts = jnp.concatenate(
        [block_ids[0, 0], block_count[0], labels // BLOCK_ROWS, labels % BLOCK_ROWS]
    ).astype(jnp.bfloat16)
    n_facts = facts.shape[0]
    facts = jnp.pad(facts, (0, 16 * embed - n_facts)).reshape(16, embed)

    own_slice = lax.dynamic_slice_in_dim(out_proj, cls * slice_rows, slice_rows, 0)
    far = jnp.stack([z_swap(own_slice, step) for step in range(2, n_z)])
    near_from, _ = lax.optimization_barrier((out_proj, own_slice))
    near = z_swap(near_from, 1)
    own_other = core_swap(near_from)
    head_rows = head_proj.shape[0]
    head_own = jnp.concatenate([head_proj, facts], axis=0)
    class_weight, head_own, far = lax.optimization_barrier((class_weight, head_own, far))
    far = jnp.stack([far] + [plane_swap(far, step) for step in range(1, n_cls)])
    if slice_rows % 16:
        ordered = jnp.zeros_like(far)
        for step in range(n_cls):
            ordered = lax.dynamic_update_index_in_dim(ordered, far[step], cls ^ step, 0)
        far = ordered.transpose(1, 0, 2, 3).reshape(1, n_z - 2, rows, width)
    near_other = core_swap(near)
    far_other = core_swap(far)
    pooled = pool_tokens(
        attended, stream, out_proj, near, own_other, near_other, far, far_other,
        norm_gain.reshape(1, width), norm_shift.reshape(1, width),
    )

    heads = [z_swap(head_own, step) for step in range(1, n_z)]
    heads, pooled = lax.optimization_barrier((heads, pooled))
    heads = jnp.stack([head_own] + heads)
    other_heads = core_swap(heads)
    all_facts = jnp.concatenate([heads[:, head_rows:], other_heads[:, head_rows:]], axis=0)
    all_facts = all_facts.reshape(n_dp, 16 * embed)[:, :n_facts].astype(jnp.int32)

    bits = jnp.zeros((n_dp,), jnp.int32)
    for slot in range(slots):
        bits = bits + jnp.where(slot < all_facts[:, slots], 1 << all_facts[:, slot], 0)
    label = all_facts[:, slots + 1 : slots + 1 + size] * BLOCK_ROWS + all_facts[:, slots + 1 + size :]
    label = (label - cls * classes).reshape(n_dp, n_cls, images)
    bits = jnp.broadcast_to(bits[:, None, None], label.shape)
    image_facts = jnp.pad(jnp.stack([label, bits], axis=-1), ((0, 0), (0, 0), (0, lines - images), (0, 0)))
    image_facts = image_facts.reshape(-1, 2)

    scale = lax.rsqrt(
        jnp.sum(jnp.square(class_weight.astype(jnp.float32)), axis=1) + NORM_EPSILON
    )[None, :]

    column = jnp.stack([pooled] + [z_swap(pooled, step) for step in range(1, n_z)])
    groups = jnp.zeros((n_z, n_cls, lines, width), pooled.dtype)
    for step, got in [(0, column)] + [(step, plane_swap(column, step)) for step in range(1, n_cls)]:
        groups = lax.dynamic_update_slice_in_dim(groups, got[:, None], cls ^ step, 1)
    groups = jnp.concatenate([groups, core_swap(groups)], axis=0)
    pooled_all = groups.reshape(n_dp * group_lines, width)

    piece = group_lines * max(1, min(n_dp, 256 // group_lines))
    total_lines = n_dp * group_lines
    parts = [
        class_parts(
            group_lines, n_cls, pooled_all[at : at + piece], heads, other_heads, image_facts[at : at + piece],
            class_weight, scale,
        )
        for at in range(0, total_lines, piece)
    ]
    denoms = jnp.concatenate([p[4] for p in parts], axis=1)
    sums = parts[0][3]
    extra = -(-total_lines // sums.shape[2])
    denoms = jnp.pad(denoms, ((0, 0), (0, extra * sums.shape[2] - total_lines))).reshape(extra, -1)

    def packed(step):
        return jnp.concatenate([sums[step, :images], denoms], axis=0)

    total = packed(0)
    for step in range(n_cls - 1, 0, -1):
        total = total + plane_swap(packed(step), step)
    denominator = total[images:].reshape(1, -1)[:, :total_lines]
    share = embed // n_dp
    for k, (exponent, cosine, unit, _, _) in enumerate(parts):
        at = k * piece
        grad, loss, embed_part = class_grad_part(
            share, images, total, denominator[:, at : at + piece], exponent, cosine, unit,
            image_facts[at : at + piece], class_weight, scale,
        )
        if k == 0:
            class_grad, sample_loss, embed_grad = grad, loss, embed_part
        else:
            class_grad = class_grad + grad
    return (sample_loss.reshape(images), embed_grad, class_grad.T)


def solution(mesh):
    placed = (
        P(("dp", "cls"), None),
        P(("dp", "cls"), None),
        P("dp", None),
        P(),
        P(),
        P("dp", None),
        P("cls", None),
        P("dp", "cls", None),
        P("dp", "cls"),
        P("dp"),
    )
    return jax.shard_map(
        per_device,
        mesh=mesh,
        in_specs=placed,
        out_specs=(P(("dp", "cls")), P(("dp", "cls"), None), P("cls", "dp")),
        check_vma=False,
    )
```

time: 80 us -> 66.3 us (0.83); the launches traced: 78.9 us -> 66 us
  local copies, waits for them, and re-layouts: 23.9 us -> 4.51 us
  waiting for transfers between devices: 7.4 us -> 24.8 us
  other arithmetic: 13 us -> 3.16 us
  Pallas kernels: 4.58 us -> 6.83 us
  matrix products: 2.13 us -> 0 us
    ppermute x9, waiting for transfers between devices: 3.19 us -> 12.6 us  [plane_swap(): return lax.ppermute(value, 'cls', [(i, i ^ step) for i in range(count)])]
    ppermute x9, waiting for transfers between devices: 4.19 us -> 10.9 us  [z_swap(): lax.ppermute(value, 'dp', [(i, i ^ step * CORES) for i in range(count)])]
    dynamic_update_slice x16 -> x3, local copies, waits for them, and re-layouts: 6.54 us -> 0.03 us  [per_device(): lax.dynamic_update_slice_in_dim(groups, got[:, None], cls ^ step, 1)]
    unnamed x50 -> x14, local copies, waits for them, and re-layouts: 6.56 us -> 3.36 us
    pallas_call x3, Pallas kernels: 4.58 us -> 6.83 us  [in_vmem(): pl.pallas_call(kernel, out_shape=tuple(outs), in_specs=[vmem] * len(opera...]
    dot_general x1 -> x0, matrix products: 2.13 us -> none  [per_device(): jnp.dot(columns_of((0, 1)), jnp.concatenate([two, other_two], axis=0), pr...]
    pallas_call x1 -> x0, local copies, waits for them, and re-layouts: 2.09 us -> none  [class_parts(): pl.pallas_call(functools.partial(class_kernel, own), out_shape=(jax.Shape...]
    select_n x3 -> x0, other arithmetic: 1.68 us -> none  [the longest x1 0.98 us: per_device(): jnp.where(hit & (code > 0.5), 2.0, jnp.broadcast_to(code, hit.shape))]
  transfers between devices with their start and end apart: 22 -> 23, of which waited for: 5 -> 13; matrix products, arithmetic and copies ran while one was open for 39% -> 4% of each run, Pallas kernels for 2% -> 4%
where the time goes in v3:
time: 66.3 us; the launch traced here: 66 us
  starting transfers between devices  25.2 us (38%)
  waiting for transfers between devices  24.8 us (37%)
  Pallas kernels  6.83 us (10%)
  local copies, waits for them, and re-layouts  4.51 us (7%)
  other arithmetic  3.16 us (5%)
  between operations  1.59 us (2%)
    ppermute x9, starting transfers between devices, z_swap(): lax.ppermute(value, 'dp', [(i, i ^ step * CORES) for i in range(count)])  13.8 us
    ppermute x9, waiting for transfers between devices, plane_swap(): return lax.ppermute(value, 'cls', [(i, i ^ step) for i in range(count)])  12.6 us
    ppermute x9, waiting for transfers between devices, z_swap(): lax.ppermute(value, 'dp', [(i, i ^ step * CORES) for i in range(count)])  10.9 us
    ppermute x9, starting transfers between devices, plane_swap(): return lax.ppermute(value, 'cls', [(i, i ^ step) for i in range(count)])  10.7 us
    pallas_call x3, Pallas kernels, in_vmem(): pl.pallas_call(kernel, out_shape=tuple(outs), in_specs=[vmem] * len(opera...  6.83 us
    unnamed x14, local copies, waits for them, and re-layouts  3.36 us
  transfers between devices with their start and end apart: 23, of which 13 were waited for; matrix products, arithmetic and copies ran while one was open for 4% of the time, Pallas kernels for 4%

profile of v3, /device:TPU:0, one launch (start us, length us, event | category | flops | bytes accessed | tf_op | source)
XLA Modules:
  0.0 66.0 jit_solution(9057951927104195446)
XLA Ops:
  0.7 0.9 %constant_dynamic-slice_fusion = bf16[32,1024]{1,0:T(8,128)(2,1)S(1)} fusion(bf16[128,1024]{1,0:T(8,128)(2,1)} %own_ref.1, s32[]{:T(128)S(6)} %select_n.45), kind=kLoop, calls=%fused_computation.40 | loop fusion | bytes 131076 | tf_op jit(solution)/shard_map/dynamic_slice | solution.py:324
  1.6 5.0 %collective-permute-start.1 = (bf16[32,1024]{1,0:T(8,128)(2,1)S(1)}, bf16[32,1024]{1,0:T(8,128)(2,1)S(1)}, u32[]{:S(2)}, u32[]{:S(2)}) collective-permute-start(bf16[32,1024]{1,0:T(8,128)(2,1)S(1)} %constant_dynamic-slice_fusion), channel_id=1, source_target_pairs={{0,24},{4,28},{8,16},{12,20},{16,8},{20,12},{24,0},{28,4},{1,25},{... | collective-permute-start | bytes 196616 | tf_op jit(solution)/shard_map/ppermute | solution.py:22
  7.3 0.7 %convert_bitcast_fusion = bf16[3]{0:T(256)(128)(2,1)S(1)} fusion(s32[1,1,3]{2,1,0:T(1,128)} %param.17), kind=kLoop, calls=%fused_computation.45 | loop fusion | flops 3 | bytes 18 | tf_op jit(solution)/shard_map/squeeze | solution.py:319
  7.9 0.7 %fusion.15 = (bf16[24]{0:T(256)(128)(2,1)S(1)}, bf16[24]{0:T(256)(128)(2,1)S(1)}) fusion(s32[24]{0:T(128)} %param.19), kind=kLoop, calls=%fused_computation.46 | loop fusion | flops 504 | bytes 192 | tf_op jit(solution)/shard_map/convert.2
  8.7 0.9 %pad_maximum_fusion.3 = bf16[144,512]{1,0:T(8,128)(2,1)S(1)} fusion(bf16[16,512]{1,0:T(8,128)(2,1)S(1)} %reshape.47, bf16[128,512]{1,0:T(8,128)(2,1)} %param.15), kind=kLoop, calls=%fused_computation.4 | loop fusion | flops 294912 | bytes 294912 | tf_op jit(solution)/shard_map/concatenate | solution.py:330
  9.6 2.6 %collective-permute-done = bf16[32,1024]{1,0:T(8,128)(2,1)S(1)} collective-permute-done((bf16[32,1024]{1,0:T(8,128)(2,1)S(1)}, bf16[32,1024]{1,0:T(8,128)(2,1)S(1)}, u32[]{:S(2)}, u32[]{:S(2)}) %collective-permute-start) | collective-permute-done | bytes 65568 | tf_op jit(solution)/shard_map/ppermute | solution.py:22
  12.2 2.5 %collective-permute-start.10 = (bf16[2,32,1024]{2,1,0:T(8,128)(2,1)S(1)}, bf16[2,32,1024]{2,1,0:T(8,128)(2,1)S(1)}, u32[]{:S(2)}, u32[]{:S(2)}) collective-permute-start(bf16[2,32,1024]{2,1,0:T(8,128)(2,1)S(1)} %pad_maximum_fusion.4), channel_id=1, source_target_pairs={{0,3},{1,2},{2,1},{3,0},{4,7},{5,6},{6,5},{7,4},{8,11},{9,10},{10,... | collective-permute-start | bytes 393224 | tf_op jit(solution)/shard_map/ppermute | solution.py:32
  15.8 2.9 %collective-permute-done.10 = bf16[2,32,1024]{2,1,0:T(8,128)(2,1)S(1)} collective-permute-done((bf16[2,32,1024]{2,1,0:T(8,128)(2,1)S(1)}, bf16[2,32,1024]{2,1,0:T(8,128)(2,1)S(1)}, u32[]{:S(2)}, u32[]{:S(2)}) %collective-permute-start.10) | collective-permute-done | bytes 131104 | tf_op jit(solution)/shard_map/ppermute | solution.py:32
  18.6 2.4 %collective-permute-done.9 = bf16[2,32,1024]{2,1,0:T(8,128)(2,1)S(1)} collective-permute-done((bf16[2,32,1024]{2,1,0:T(8,128)(2,1)S(1)}, bf16[2,32,1024]{2,1,0:T(8,128)(2,1)S(1)}, u32[]{:S(2)}, u32[]{:S(2)}) %collective-permute-start.9) | collective-permute-done | bytes 131104 | tf_op jit(solution)/shard_map/ppermute | solution.py:32
  21.9 1.1 %collective-permute-done.5.near_ref = bf16[128,1024]{1,0:T(8,128)(2,1)S(1)} collective-permute-done((bf16[128,1024]{1,0:T(8,128)(2,1)}, bf16[128,1024]{1,0:T(8,128)(2,1)S(1)}, u32[]{:S(2)}, u32[]{:S(2)}) %collective-permute-start.5) | collective-permute-done | bytes 262176 | tf_op jit(solution)/shard_map/ppermute | solution.py:22
  23.1 1.9 %collective-permute-start.4 = (bf16[144,512]{1,0:T(8,128)(2,1)S(1)}, bf16[144,512]{1,0:T(8,128)(2,1)S(1)}, u32[]{:S(2)}, u32[]{:S(2)}) collective-permute-start(bf16[144,512]{1,0:T(8,128)(2,1)S(1)} %pad_maximum_fusion.3), channel_id=1, source_target_pairs={{0,24},{4,28},{8,16},{12,20},{16,8},{20,12},{24,0},{28,4},{1,25},{... | collective-permute-start | bytes 442376 | tf_op jit(solution)/shard_map/ppermute | solution.py:22
  25.0 2.5 %collective-permute-start.2 = (bf16[144,512]{1,0:T(8,128)(2,1)S(1)}, bf16[144,512]{1,0:T(8,128)(2,1)S(1)}, u32[]{:S(2)}, u32[]{:S(2)}) collective-permute-start(bf16[144,512]{1,0:T(8,128)(2,1)S(1)} %pad_maximum_fusion.3), channel_id=1, source_target_pairs={{0,8},{4,12},{8,0},{12,4},{16,24},{20,28},{24,16},{28,20},{1,9},{5... | collective-permute-start | bytes 442376 | tf_op jit(solution)/shard_map/ppermute | solution.py:22
  27.5 1.5 %copy-done.2 = bf16[864,1024]{1,0:T(8,128)(2,1)S(1)} copy-done((bf16[864,1024]{1,0:T(8,128)(2,1)S(1)}, bf16[864,1024]{1,0:T(8,128)(2,1)}, u32[]{:S(2)}) %copy-start.2) | copy-done | bytes 1769496
  29.0 1.5 %copy-done.3 = bf16[864,1024]{1,0:T(8,128)(2,1)S(1)} copy-done((bf16[864,1024]{1,0:T(8,128)(2,1)S(1)}, bf16[864,1024]{1,0:T(8,128)(2,1)}, u32[]{:S(2)}) %copy-start.3) | copy-done | bytes 1769496
  30.5 2.9 %shard_map.121 = bf16[8,1024]{1,0:T(8,128)(2,1)S(1)} custom-call(bf16[864,1024]{1,0:T(8,128)(2,1)S(1)} %copy-done.2, bf16[864,1024]{1,0:T(8,128)(2,1)S(1)} %copy-done.3, bf16[128,1024]{1,0:T(8,128)(2,1)S(1)} %copy-done.1, bf16[128,1024]{1,0:T(8,128)(2,1)S(1)} %collective-permute-done.5.near_ref, bf16[128,1024]{1,0:T(8,128)(2,1)S(1)} %collective-permute-done.6.own_other_ref, ...), custom_call_target="tpu_custom_call" | custom-call | flops 1811939328 | bytes 5660672 | tf_op jit(solution)/shard_map/pallas_call | solution.py:87
  33.4 5.2 %collective-permute-done.3 = bf16[144,512]{1,0:T(8,128)(2,1)S(1)} collective-permute-done((bf16[144,512]{1,0:T(8,128)(2,1)S(1)}, bf16[144,512]{1,0:T(8,128)(2,1)S(1)}, u32[]{:S(2)}, u32[]{:S(2)}) %collective-permute-start.3) | collective-permute-done | bytes 147488 | tf_op jit(solution)/shard_map/ppermute | solution.py:22
  38.6 1.9 %collective-permute-start.14 = (bf16[8,1024]{1,0:T(8,128)(2,1)S(1)}, bf16[8,1024]{1,0:T(8,128)(2,1)S(1)}, u32[]{:S(2)}, u32[]{:S(2)}) collective-permute-start(bf16[8,1024]{1,0:T(8,128)(2,1)S(1)} %shard_map.121), channel_id=1, source_target_pairs={{0,24},{4,28},{8,16},{12,20},{16,8},{20,12},{24,0},{28,4},{1,25},{... | collective-permute-start | bytes 49160 | tf_op jit(solution)/shard_map/ppermute | solution.py:22
  40.5 2.5 %collective-permute-start.12 = (bf16[8,1024]{1,0:T(8,128)(2,1)S(1)}, bf16[8,1024]{1,0:T(8,128)(2,1)S(1)}, u32[]{:S(2)}, u32[]{:S(2)}) collective-permute-start(bf16[8,1024]{1,0:T(8,128)(2,1)S(1)} %shard_map.121), channel_id=1, source_target_pairs={{0,8},{4,12},{8,0},{12,4},{16,24},{20,28},{24,16},{28,20},{1,9},{5... | collective-permute-start | bytes 49160 | tf_op jit(solution)/shard_map/ppermute | solution.py:22
  43.1 1.0 %collective-permute-done.14 = bf16[8,1024]{1,0:T(8,128)(2,1)S(1)} collective-permute-done((bf16[8,1024]{1,0:T(8,128)(2,1)S(1)}, bf16[8,1024]{1,0:T(8,128)(2,1)S(1)}, u32[]{:S(2)}, u32[]{:S(2)}) %collective-permute-start.14) | collective-permute-done | bytes 16416 | tf_op jit(solution)/shard_map/ppermute | solution.py:22
  44.1 1.0 %collective-permute-done.13 = bf16[8,1024]{1,0:T(8,128)(2,1)S(1)} collective-permute-done((bf16[8,1024]{1,0:T(8,128)(2,1)S(1)}, bf16[8,1024]{1,0:T(8,128)(2,1)S(1)}, u32[]{:S(2)}, u32[]{:S(2)}) %collective-permute-start.13) | collective-permute-done | bytes 16416 | tf_op jit(solution)/shard_map/ppermute | solution.py:22
  45.1 1.6 %collective-permute-start.16 = (bf16[4,8,1024]{2,1,0:T(8,128)(2,1)S(1)}, bf16[4,8,1024]{2,1,0:T(8,128)(2,1)S(1)}, u32[]{:S(2)}, u32[]{:S(2)}) collective-permute-start(bf16[4,8,1024]{2,1,0:T(8,128)(2,1)S(1)} %pad_maximum_fusion.5), channel_id=1, source_target_pairs={{0,2},{1,3},{2,0},{3,1},{4,6},{5,7},{6,4},{7,5},{8,10},{9,11},{10,... | collective-permute-start | bytes 196616 | tf_op jit(solution)/shard_map/ppermute | solution.py:32
  46.7 1.5 %collective-permute-start.15 = (bf16[4,8,1024]{2,1,0:T(8,128)(2,1)S(1)}, bf16[4,8,1024]{2,1,0:T(8,128)(2,1)S(1)}, u32[]{:S(2)}, u32[]{:S(2)}) collective-permute-start(bf16[4,8,1024]{2,1,0:T(8,128)(2,1)S(1)} %pad_maximum_fusion.5), channel_id=1, source_target_pairs={{0,1},{1,0},{2,3},{3,2},{4,5},{5,4},{6,7},{7,6},{8,9},{9,8},{10,11... | collective-permute-start | bytes 196616 | tf_op jit(solution)/shard_map/ppermute | solution.py:32
  48.7 2.2 %collective-permute-done.15 = bf16[4,8,1024]{2,1,0:T(8,128)(2,1)S(1)} collective-permute-done((bf16[4,8,1024]{2,1,0:T(8,128)(2,1)S(1)}, bf16[4,8,1024]{2,1,0:T(8,128)(2,1)S(1)}, u32[]{:S(2)}, u32[]{:S(2)}) %collective-permute-start.15) | collective-permute-done | bytes 65568 | tf_op jit(solution)/shard_map/ppermute | solution.py:32
  51.0 2.3 %collective-permute-done.17 = bf16[4,8,1024]{2,1,0:T(8,128)(2,1)S(1)} collective-permute-done((bf16[4,8,1024]{2,1,0:T(8,128)(2,1)S(1)}, bf16[4,8,1024]{2,1,0:T(8,128)(2,1)S(1)}, u32[]{:S(2)}, u32[]{:S(2)}) %collective-permute-start.17) | collective-permute-done | bytes 65568 | tf_op jit(solution)/shard_map/ppermute | solution.py:32
  53.8 1.2 %collective-permute-done.18 = bf16[4,4,8,1024]{3,2,1,0:T(8,128)(2,1)S(1)} collective-permute-done((bf16[4,4,8,1024]{3,2,1,0:T(8,128)(2,1)S(1)}, bf16[4,4,8,1024]{3,2,1,0:T(8,128)(2,1)S(1)}, u32[]{:S(2)}, u32[]{:S(2)}) %collective-permute-start.18) | collective-permute-done | bytes 262176 | tf_op jit(solution)/shard_map/ppermute | solution.py:27
  56.0 2.1 %shard_map.122 = (f32[256,1024]{1,0:T(8,128)S(1)}, f32[256,1024]{1,0:T(8,128)S(1)}, f32[256,640]{1,0:T(8,128)S(1)}, f32[4,8,1280]{2,1,0:T(8,128)S(1)}, f32[1,256]{1,0:T(1,128)S(1)}) custom-call(bf16[256,1024]{1,0:T(8,128)(2,1)S(1)} %bitcast.51, bf16[4,144,512]{2,1,0:T(8,128)(2,1)S(1)} %pad_maximum_fusion.head_ref, ...), custom_call_target="tpu_custom_call" | custom-call | flops 805306368 | bytes 5676032 | tf_op jit(solution)/shard_map/pallas_call | solution.py:87
  58.1 0.8 %collective-permute-start.20 = (f32[7,1280]{1,0:T(8,128)S(1)}, f32[7,1280]{1,0:T(8,128)S(1)}, u32[]{:S(2)}, u32[]{:S(2)}) collective-permute-start(f32[7,1280]{1,0:T(8,128)S(1)} %get-tuple-element.39), channel_id=1, source_target_pairs={{0,3},{1,2},{2,1},{3,0},{4,7},{5,6},{6,5},{7,4},{8,11},{9,10},{10,... | collective-permute-start | bytes 107528 | tf_op jit(solution)/shard_map/ppermute | solution.py:32
  58.9 1.3 %collective-permute-start.21 = (f32[7,1280]{1,0:T(8,128)S(1)}, f32[7,1280]{1,0:T(8,128)S(1)}, u32[]{:S(2)}, u32[]{:S(2)}) collective-permute-start(f32[7,1280]{1,0:T(8,128)S(1)} %get-tuple-element.40), channel_id=1, source_target_pairs={{0,2},{1,3},{2,0},{3,1},{4,6},{5,7},{6,4},{7,5},{8,10},{9,11},{10,... | collective-permute-start | bytes 107528 | tf_op jit(solution)/shard_map/ppermute | solution.py:32
  60.2 1.5 %collective-permute-start.22 = (f32[7,1280]{1,0:T(8,128)S(1)}, f32[7,1280]{1,0:T(8,128)S(1)}, u32[]{:S(2)}, u32[]{:S(2)}) collective-permute-start(f32[7,1280]{1,0:T(8,128)S(1)} %get-tuple-element.41), channel_id=1, source_target_pairs={{0,1},{1,0},{2,3},{3,2},{4,5},{5,4},{6,7},{7,6},{8,9},{9,8},{10,11... | collective-permute-start | bytes 107528 | tf_op jit(solution)/shard_map/ppermute | solution.py:32
  61.6 1.7 %collective-permute-done.20 = f32[7,1280]{1,0:T(8,128)S(1)} collective-permute-done((f32[7,1280]{1,0:T(8,128)S(1)}, f32[7,1280]{1,0:T(8,128)S(1)}, u32[]{:S(2)}, u32[]{:S(2)}) %collective-permute-start.20) | collective-permute-done | bytes 35872 | tf_op jit(solution)/shard_map/ppermute | solution.py:32
  63.4 0.8 %collective-permute-done.22 = f32[7,1280]{1,0:T(8,128)S(1)} collective-permute-done((f32[7,1280]{1,0:T(8,128)S(1)}, f32[7,1280]{1,0:T(8,128)S(1)}, u32[]{:S(2)}, u32[]{:S(2)}) %collective-permute-start.22) | collective-permute-done | bytes 35872 | tf_op jit(solution)/shard_map/ppermute | solution.py:32
  64.2 1.9 %shard_map.123 = (f32[64,1024]{1,0:T(8,128)}, f32[1,6]{1,0:T(1,128)}, f32[6,512]{1,0:T(8,128)}) custom-call(f32[7,1280]{1,0:T(8,128)S(1)} %fusion.6.total_ref, f32[1,256]{1,0:T(1,128)S(1)} %slice.63.denom_ref, f32[256,1024]{1,0:T(8,128)S(1)} %get-tuple-element.29.exp_ref, f32[256,1024]{1,0:T(8,128)S(1)} %get-tuple-element.30.cos_ref, ...), custom_call_target="tpu_custom_call" | custom-call | flops 167772160 | bytes 4118552 | tf_op jit(solution)/shard_map/pallas_call | solution.py:87
  (63 shorter events, 4.1 us)
Async XLA Ops:
  0.6 20.8 %copy-start.1 = (bf16[128,1024]{1,0:T(8,128)(2,1)S(1)}, bf16[128,1024]{1,0:T(8,128)(2,1)}, u32[]{:S(2)}) copy-start(bf16[128,1024]{1,0:T(8,128)(2,1)} %own_ref.1) | copy-start | bytes 786436
  0.6 26.8 %copy-start.5 = (f32[1024]{0:T(1024)S(1)}, f32[1024]{0:T(1024)}, u32[]{:S(2)}) copy-start(f32[1024]{0:T(1024)} %param.14) | copy-start | bytes 12292
  0.7 26.8 %copy-start.4 = (f32[1024]{0:T(1024)S(1)}, f32[1024]{0:T(1024)}, u32[]{:S(2)}) copy-start(f32[1024]{0:T(1024)} %param.13) | copy-start | bytes 12292
  1.6 8.1 %collective-permute-start.1 = (bf16[32,1024]{1,0:T(8,128)(2,1)S(1)}, bf16[32,1024]{1,0:T(8,128)(2,1)S(1)}, u32[]{:S(2)}, u32[]{:S(2)}) collective-permute-start(bf16[32,1024]{1,0:T(8,128)(2,1)S(1)} %constant_dynamic-slice_fusion), channel_id=1, source_target_pairs={{0,24},{4,28},{8,16},{12,20},{16,8},{20,12},{24,0},{28,4},{1,25},{... | collective-permute-start | bytes 196616 | tf_op jit(solution)/shard_map/ppermute | solution.py:22
  6.6 5.6 %collective-permute-start = (bf16[32,1024]{1,0:T(8,128)(2,1)S(1)}, bf16[32,1024]{1,0:T(8,128)(2,1)S(1)}, u32[]{:S(2)}, u32[]{:S(2)}) collective-permute-start(bf16[32,1024]{1,0:T(8,128)(2,1)S(1)} %constant_dynamic-slice_fusion), channel_id=1, source_target_pairs={{0,16},{4,20},{8,24},{12,28},{16,0},{20,4},{24,8},{28,12},{1,17},{... | collective-permute-start | bytes 196616 | tf_op jit(solution)/shard_map/ppermute | solution.py:22
  12.2 6.4 %collective-permute-start.10 = (bf16[2,32,1024]{2,1,0:T(8,128)(2,1)S(1)}, bf16[2,32,1024]{2,1,0:T(8,128)(2,1)S(1)}, u32[]{:S(2)}, u32[]{:S(2)}) collective-permute-start(bf16[2,32,1024]{2,1,0:T(8,128)(2,1)S(1)} %pad_maximum_fusion.4), channel_id=1, source_target_pairs={{0,3},{1,2},{2,1},{3,0},{4,7},{5,6},{6,5},{7,4},{8,11},{9,10},{10,... | collective-permute-start | bytes 393224 | tf_op jit(solution)/shard_map/ppermute | solution.py:32
  14.7 6.3 %collective-permute-start.9 = (bf16[2,32,1024]{2,1,0:T(8,128)(2,1)S(1)}, bf16[2,32,1024]{2,1,0:T(8,128)(2,1)S(1)}, u32[]{:S(2)}, u32[]{:S(2)}) collective-permute-start(bf16[2,32,1024]{2,1,0:T(8,128)(2,1)S(1)} %pad_maximum_fusion.4), channel_id=1, source_target_pairs={{0,2},{1,3},{2,0},{3,1},{4,6},{5,7},{6,4},{7,5},{8,10},{9,11},{10,... | collective-permute-start | bytes 393224 | tf_op jit(solution)/shard_map/ppermute | solution.py:32
  15.2 6.1 %collective-permute-start.8 = (bf16[2,32,1024]{2,1,0:T(8,128)(2,1)S(1)}, bf16[2,32,1024]{2,1,0:T(8,128)(2,1)S(1)}, u32[]{:S(2)}, u32[]{:S(2)}) collective-permute-start(bf16[2,32,1024]{2,1,0:T(8,128)(2,1)S(1)} %pad_maximum_fusion.4), channel_id=1, source_target_pairs={{0,1},{1,0},{2,3},{3,2},{4,5},{5,4},{6,7},{7,6},{8,9},{9,8},{10,11... | collective-permute-start | bytes 393224 | tf_op jit(solution)/shard_map/ppermute | solution.py:32
  15.8 7.3 %collective-permute-start.5 = (bf16[128,1024]{1,0:T(8,128)(2,1)}, bf16[128,1024]{1,0:T(8,128)(2,1)S(1)}, u32[]{:S(2)}, u32[]{:S(2)}) collective-permute-start(bf16[128,1024]{1,0:T(8,128)(2,1)} %own_ref.1), channel_id=1, source_target_pairs={{0,8},{4,12},{8,0},{12,4},{16,24},{20,28},{24,16},{28,20},{1,9},{5... | collective-permute-start | bytes 786440 | tf_op jit(solution)/shard_map/ppermute | solution.py:22
  21.4 6.1 %collective-permute-start.11 = (bf16[4,2,32,1024]{3,2,1,0:T(8,128)(2,1)S(1)}, bf16[4,2,32,1024]{3,2,1,0:T(8,128)(2,1)S(1)}, u32[]{:S(2)}, u32[]{:S(2)}) collective-permute-start(bf16[4,2,32,1024]{3,2,1,0:T(8,128)(2,1)S(1)} %pad_maximum_fusion.1.far_ref), channel_id=1, source_target_pairs={{0,4},{4,0},{8,12},{12,8},{16,20},{20,16},{24,28},{28,24},{1,5},{5... | collective-permute-start | bytes 1572872 | tf_op jit(solution)/shard_map/ppermute | solution.py:27
  21.5 3.6 %collective-permute-start.6 = (bf16[128,1024]{1,0:T(8,128)(2,1)S(1)}, bf16[128,1024]{1,0:T(8,128)(2,1)S(1)}, u32[]{:S(2)}, u32[]{:S(2)}) collective-permute-start(bf16[128,1024]{1,0:T(8,128)(2,1)S(1)} %copy-done.1), channel_id=1, source_target_pairs={{0,4},{4,0},{8,12},{12,8},{16,20},{20,16},{24,28},{28,24},{1,5},{5... | collective-permute-start | bytes 786440 | tf_op jit(solution)/shard_map/ppermute | solution.py:27
  23.1 4.4 %collective-permute-start.7 = (bf16[128,1024]{1,0:T(8,128)(2,1)S(1)}, bf16[128,1024]{1,0:T(8,128)(2,1)S(1)}, u32[]{:S(2)}, u32[]{:S(2)}) collective-permute-start(bf16[128,1024]{1,0:T(8,128)(2,1)S(1)} %collective-permute-done.5.near_ref), channel_id=1, source_target_pairs={{0,4},{4,0},{8,12},{12,8},{16,20},{20,16},{24,28},{28,24},{1,5},{5... | collective-permute-start | bytes 786440 | tf_op jit(solution)/shard_map/ppermute | solution.py:27
  23.1 10.3 %collective-permute-start.4 = (bf16[144,512]{1,0:T(8,128)(2,1)S(1)}, bf16[144,512]{1,0:T(8,128)(2,1)S(1)}, u32[]{:S(2)}, u32[]{:S(2)}) collective-permute-start(bf16[144,512]{1,0:T(8,128)(2,1)S(1)} %pad_maximum_fusion.3), channel_id=1, source_target_pairs={{0,24},{4,28},{8,16},{12,20},{16,8},{20,12},{24,0},{28,4},{1,25},{... | collective-permute-start | bytes 442376 | tf_op jit(solution)/shard_map/ppermute | solution.py:22
  25.0 13.5 %collective-permute-start.3 = (bf16[144,512]{1,0:T(8,128)(2,1)S(1)}, bf16[144,512]{1,0:T(8,128)(2,1)S(1)}, u32[]{:S(2)}, u32[]{:S(2)}) collective-permute-start(bf16[144,512]{1,0:T(8,128)(2,1)S(1)} %pad_maximum_fusion.3), channel_id=1, source_target_pairs={{0,16},{4,20},{8,24},{12,28},{16,0},{20,4},{24,8},{28,12},{1,17},{... | collective-permute-start | bytes 442376 | tf_op jit(solution)/shard_map/ppermute | solution.py:22
  25.0 13.5 %collective-permute-start.2 = (bf16[144,512]{1,0:T(8,128)(2,1)S(1)}, bf16[144,512]{1,0:T(8,128)(2,1)S(1)}, u32[]{:S(2)}, u32[]{:S(2)}) collective-permute-start(bf16[144,512]{1,0:T(8,128)(2,1)S(1)} %pad_maximum_fusion.3), channel_id=1, source_target_pairs={{0,8},{4,12},{8,0},{12,4},{16,24},{20,28},{24,16},{28,20},{1,9},{5... | collective-permute-start | bytes 442376 | tf_op jit(solution)/shard_map/ppermute | solution.py:22
  27.5 1.5 %copy-start.2 = (bf16[864,1024]{1,0:T(8,128)(2,1)S(1)}, bf16[864,1024]{1,0:T(8,128)(2,1)}, u32[]{:S(2)}) copy-start(bf16[864,1024]{1,0:T(8,128)(2,1)} %att_ref.1) | copy-start | bytes 5308420
  29.0 1.5 %copy-start.3 = (bf16[864,1024]{1,0:T(8,128)(2,1)S(1)}, bf16[864,1024]{1,0:T(8,128)(2,1)}, u32[]{:S(2)}) copy-start(bf16[864,1024]{1,0:T(8,128)(2,1)} %stream_ref.1) | copy-start | bytes 5308420
  33.3 20.1 %copy-start = (bf16[1024,512]{1,0:T(8,128)(2,1)S(1)}, bf16[1024,512]{1,0:T(8,128)(2,1)}, u32[]{:S(2)}) copy-start(bf16[1024,512]{1,0:T(8,128)(2,1)} %weight_ref.1) | copy-start | bytes 3145732
  38.6 5.5 %collective-permute-start.14 = (bf16[8,1024]{1,0:T(8,128)(2,1)S(1)}, bf16[8,1024]{1,0:T(8,128)(2,1)S(1)}, u32[]{:S(2)}, u32[]{:S(2)}) collective-permute-start(bf16[8,1024]{1,0:T(8,128)(2,1)S(1)} %shard_map.121), channel_id=1, source_target_pairs={{0,24},{4,28},{8,16},{12,20},{16,8},{20,12},{24,0},{28,4},{1,25},{... | collective-permute-start | bytes 49160 | tf_op jit(solution)/shard_map/ppermute | solution.py:22
  40.5 4.6 %collective-permute-start.13 = (bf16[8,1024]{1,0:T(8,128)(2,1)S(1)}, bf16[8,1024]{1,0:T(8,128)(2,1)S(1)}, u32[]{:S(2)}, u32[]{:S(2)}) collective-permute-start(bf16[8,1024]{1,0:T(8,128)(2,1)S(1)} %shard_map.121), channel_id=1, source_target_pairs={{0,16},{4,20},{8,24},{12,28},{16,0},{20,4},{24,8},{28,12},{1,17},{... | collective-permute-start | bytes 49160 | tf_op jit(solution)/shard_map/ppermute | solution.py:22
  40.5 4.6 %collective-permute-start.12 = (bf16[8,1024]{1,0:T(8,128)(2,1)S(1)}, bf16[8,1024]{1,0:T(8,128)(2,1)S(1)}, u32[]{:S(2)}, u32[]{:S(2)}) collective-permute-start(bf16[8,1024]{1,0:T(8,128)(2,1)S(1)} %shard_map.121), channel_id=1, source_target_pairs={{0,8},{4,12},{8,0},{12,4},{16,24},{20,28},{24,16},{28,20},{1,9},{5... | collective-permute-start | bytes 49160 | tf_op jit(solution)/shard_map/ppermute | solution.py:22
  43.0 12.0 %collective-permute-start.19 = (bf16[4,144,512]{2,1,0:T(8,128)(2,1)S(1)}, bf16[4,144,512]{2,1,0:T(8,128)(2,1)S(1)}, u32[]{:S(2)}, u32[]{:S(2)}) collective-permute-start(bf16[4,144,512]{2,1,0:T(8,128)(2,1)S(1)} %pad_maximum_fusion.head_ref), channel_id=1, source_target_pairs={{0,4},{4,0},{8,12},{12,8},{16,20},{20,16},{24,28},{28,24},{1,5},{5... | collective-permute-start | bytes 1769480 | tf_op jit(solution)/shard_map/ppermute | solution.py:27
  45.1 5.9 %collective-permute-start.16 = (bf16[4,8,1024]{2,1,0:T(8,128)(2,1)S(1)}, bf16[4,8,1024]{2,1,0:T(8,128)(2,1)S(1)}, u32[]{:S(2)}, u32[]{:S(2)}) collective-permute-start(bf16[4,8,1024]{2,1,0:T(8,128)(2,1)S(1)} %pad_maximum_fusion.5), channel_id=1, source_target_pairs={{0,2},{1,3},{2,0},{3,1},{4,6},{5,7},{6,4},{7,5},{8,10},{9,11},{10,... | collective-permute-start | bytes 196616 | tf_op jit(solution)/shard_map/ppermute | solution.py:32
  46.7 4.3 %collective-permute-start.15 = (bf16[4,8,1024]{2,1,0:T(8,128)(2,1)S(1)}, bf16[4,8,1024]{2,1,0:T(8,128)(2,1)S(1)}, u32[]{:S(2)}, u32[]{:S(2)}) collective-permute-start(bf16[4,8,1024]{2,1,0:T(8,128)(2,1)S(1)} %pad_maximum_fusion.5), channel_id=1, source_target_pairs={{0,1},{1,0},{2,3},{3,2},{4,5},{5,4},{6,7},{7,6},{8,9},{9,8},{10,11... | collective-permute-start | bytes 196616 | tf_op jit(solution)/shard_map/ppermute | solution.py:32
  48.2 5.2 %collective-permute-start.17 = (bf16[4,8,1024]{2,1,0:T(8,128)(2,1)S(1)}, bf16[4,8,1024]{2,1,0:T(8,128)(2,1)S(1)}, u32[]{:S(2)}, u32[]{:S(2)}) collective-permute-start(bf16[4,8,1024]{2,1,0:T(8,128)(2,1)S(1)} %pad_maximum_fusion.5), channel_id=1, source_target_pairs={{0,3},{1,2},{2,1},{3,0},{4,7},{5,6},{6,5},{7,4},{8,11},{9,10},{10,... | collective-permute-start | bytes 196616 | tf_op jit(solution)/shard_map/ppermute | solution.py:32
  53.4 1.6 %collective-permute-start.18 = (bf16[4,4,8,1024]{3,2,1,0:T(8,128)(2,1)S(1)}, bf16[4,4,8,1024]{3,2,1,0:T(8,128)(2,1)S(1)}, u32[]{:S(2)}, u32[]{:S(2)}) collective-permute-start(bf16[4,4,8,1024]{3,2,1,0:T(8,128)(2,1)S(1)} %bitcast_dynamic-update-slice_fusion), channel_id=1, source_target_pairs={{0,4},{4,0},{8,12},{12,8},{16,20},{20,16},{24,28},{28,24},{1,5},{5... | collective-permute-start | bytes 786440 | tf_op jit(solution)/shard_map/ppermute | solution.py:27
  58.1 5.3 %collective-permute-start.20 = (f32[7,1280]{1,0:T(8,128)S(1)}, f32[7,1280]{1,0:T(8,128)S(1)}, u32[]{:S(2)}, u32[]{:S(2)}) collective-permute-start(f32[7,1280]{1,0:T(8,128)S(1)} %get-tuple-element.39), channel_id=1, source_target_pairs={{0,3},{1,2},{2,1},{3,0},{4,7},{5,6},{6,5},{7,4},{8,11},{9,10},{10,... | collective-permute-start | bytes 107528 | tf_op jit(solution)/shard_map/ppermute | solution.py:32
  58.9 4.5 %collective-permute-start.21 = (f32[7,1280]{1,0:T(8,128)S(1)}, f32[7,1280]{1,0:T(8,128)S(1)}, u32[]{:S(2)}, u32[]{:S(2)}) collective-permute-start(f32[7,1280]{1,0:T(8,128)S(1)} %get-tuple-element.40), channel_id=1, source_target_pairs={{0,2},{1,3},{2,0},{3,1},{4,6},{5,7},{6,4},{7,5},{8,10},{9,11},{10,... | collective-permute-start | bytes 107528 | tf_op jit(solution)/shard_map/ppermute | solution.py:32
  60.2 4.0 %collective-permute-start.22 = (f32[7,1280]{1,0:T(8,128)S(1)}, f32[7,1280]{1,0:T(8,128)S(1)}, u32[]{:S(2)}, u32[]{:S(2)}) collective-permute-start(f32[7,1280]{1,0:T(8,128)S(1)} %get-tuple-element.41), channel_id=1, source_target_pairs={{0,1},{1,0},{2,3},{3,2},{4,5},{5,4},{6,7},{7,6},{8,9},{9,8},{10,11... | collective-permute-start | bytes 107528 | tf_op jit(solution)/shard_map/ppermute | solution.py:32

commit v4 on v3

--- a/solution.py
+++ b/solution.py
@@ -11,6 +11,7 @@
 P_SIZE = 144
 BLOCK_ROWS = 128
 CORES = 2
+FACT_ROWS = 16
 
 LOGIT_SCALE = 64.0
 ANGLE_MARGIN = 0.5
@@ -27,17 +28,25 @@
     return lax.ppermute(value, "dp", [(i, i ^ 1) for i in range(count)])
 
 
+def half_swap(value):
+    n_dp, n_cls = lax.axis_size("dp"), lax.axis_size("cls")
+    pairs = [(dp * n_cls + c, dp * n_cls + (c ^ (1 << dp % CORES))) for dp in range(n_dp) for c in range(n_cls)]
+    return lax.ppermute(value, ("dp", "cls"), pairs)
+
+
 def plane_swap(value, step):
     count = lax.axis_size("cls")
     return lax.ppermute(value, "cls", [(i, i ^ step) for i in range(count)])
 
 
-def pool_kernel(att_ref, stream_ref, own_ref, near_ref, own_other_ref, near_other_ref, far_ref, far_other_ref,
-                gain_ref, shift_ref, out_ref, weight_ref, mixed_ref, pooled_ref):
+def pool_kernel(att_ref, stream_ref, own_ref, near_ref, own_other_ref, near_other_ref, far_ref, far_other_ref, gain_ref, shift_ref,
+                out_ref, weight_ref, mixed_ref, pooled_ref):
     tokens, width = stream_ref.shape
     images = tokens // P_SIZE
-    rows = own_ref.shape[0]
+    chunk = mixed_ref.shape[0]
+    pieces = range(0, tokens, chunk)
     n_cls, n_far, slice_rows, _ = far_ref.shape
+    rows = n_cls * slice_rows
     dp, cls = lax.axis_index("dp"), lax.axis_index("cls")
     z, core = dp // CORES, dp % CORES
 
@@ -54,24 +63,22 @@
             for step in range(n_cls):
                 start = (cls ^ step) * slice_rows if n_cls > 1 else 0
                 place((z ^ (k + 2)) * CORES + side, start, far[step, k])
-    per = 3 if images % 3 == 0 else 1
-    chunk = per * P_SIZE
-    for start in range(0, tokens, chunk):
-        here = pl.ds(start, chunk)
-        mixed_ref[here, :] = stream_ref[here, :].astype(jnp.float32) + jnp.dot(
-            att_ref[here, :], weight_ref[...], preferred_element_type=jnp.float32
+    step = 24
+    for k, start in enumerate(pieces):
+        mixed_ref[...] = jnp.dot(
+            att_ref[pl.ds(start, chunk), :], weight_ref[...], preferred_element_type=jnp.float32
         )
-    step = 24
-    for image in range(images):
-        total = jnp.zeros((8, width), jnp.float32)
-        for r in range(0, P_SIZE, step):
-            x = mixed_ref[pl.ds(image * P_SIZE + r, step), :]
-            centred = x - jnp.mean(x, axis=1, keepdims=True)
-            variance = jnp.mean(centred * centred, axis=1, keepdims=True)
-            scaled = centred * lax.rsqrt(variance + NORM_EPSILON)
-            total = total + jnp.sum(scaled.reshape(step // 8, 8, width), axis=0)
-        mean = jnp.sum(total, axis=0, keepdims=True) * (1.0 / P_SIZE)
-        pooled_ref[pl.ds(image, 1), :] = gain_ref[...] * mean + shift_ref[...]
+        for image in range(chunk // P_SIZE):
+            total = jnp.zeros((8, width), jnp.float32)
+            for r in range(0, P_SIZE, step):
+                at = image * P_SIZE + r
+                x = mixed_ref[pl.ds(at, step), :] + stream_ref[pl.ds(start + at, step), :].astype(jnp.float32)
+                centred = x - jnp.mean(x, axis=1, keepdims=True)
+                variance = jnp.mean(centred * centred, axis=1, keepdims=True)
+                scaled = centred * lax.rsqrt(variance + NORM_EPSILON)
+                total = total + jnp.sum(scaled.reshape(step // 8, 8, width), axis=0)
+            mean = jnp.sum(total, axis=0, keepdims=True) * (1.0 / P_SIZE)
+            pooled_ref[pl.ds(start // P_SIZE + image, 1), :] = gain_ref[...] * mean + shift_ref[...]
     if images < pooled_ref.shape[0]:
         pooled_ref[images:, :] = jnp.zeros((pooled_ref.shape[0] - images, width), jnp.float32)
     out_ref[...] = pooled_ref[...].astype(out_ref.dtype)
@@ -81,13 +88,25 @@
     return -(-images // 8) * 8
 
 
-def in_vmem(kernel, outs, scratch, mib, flops, operands):
+def after(value, *others):
+    anywhere = pl.BlockSpec(memory_space=pl.ANY)
+    return pl.pallas_call(
+        lambda *refs: None,
+        out_shape=jax.ShapeDtypeStruct(value.shape, value.dtype),
+        in_specs=[anywhere] * (1 + len(others)),
+        out_specs=anywhere,
+        input_output_aliases={0: 0},
+        compiler_params=pltpu.CompilerParams(vmem_limit_bytes=1024 * 1024),
+    )(value, *others)
+
+
+def in_vmem(kernel, outs, scratch, mib, flops, operands, in_hbm=0):
     vmem = pl.BlockSpec(memory_space=pltpu.VMEM)
     moved = sum(math.prod(x.shape) * x.dtype.itemsize for x in list(operands) + list(outs))
     return pl.pallas_call(
         kernel,
         out_shape=tuple(outs),
-        in_specs=[vmem] * len(operands),
+        in_specs=[pl.BlockSpec(memory_space=pl.ANY)] * in_hbm + [vmem] * (len(operands) - in_hbm),
         out_specs=(vmem,) * len(outs),
         scratch_shapes=scratch,
         compiler_params=pltpu.CompilerParams(vmem_limit_bytes=mib * 1024 * 1024),
@@ -101,13 +120,15 @@
 
 def pool_tokens(*operands):
     tokens, width = operands[0].shape
-    lines = padded(tokens // P_SIZE)
+    images = tokens // P_SIZE
+    lines = padded(images)
+    chunk = (3 if images % 3 == 0 else 1) * P_SIZE
     return in_vmem(
         pool_kernel,
         [jax.ShapeDtypeStruct((lines, width), jnp.bfloat16)],
         [
             pltpu.VMEM((width, width), jnp.bfloat16),
-            pltpu.VMEM((tokens, width), jnp.float32),
+            pltpu.VMEM((chunk, width), jnp.float32),
             pltpu.VMEM((lines, width), jnp.float32),
         ],
         12,
@@ -147,19 +168,47 @@
     return live, live & (column == label)
 
 
-def class_kernel(own, pooled_ref, head_ref, other_ref, image_ref, weight_ref, scale_ref,
-                 exp_ref, cos_ref, unit_ref, sums_ref, denom_ref, whole_ref, chosen_ref, group_ref):
+def class_kernel(own, head_rows, slots, group_images, base, pooled_ref, head_ref, other_ref, weight_ref, scale_ref,
+                 exp_ref, cos_ref, unit_ref, sums_ref, denom_ref, image_ref, whole_ref, chosen_ref, group_ref):
     images = pooled_ref.shape[0]
     classes, embed = weight_ref.shape
-    n_z = head_ref.shape[0]
     n_cls = sums_ref.shape[0]
-    rows = pooled_ref.shape[1] // (CORES * n_z)
     dp, cls = lax.axis_index("dp"), lax.axis_index("cls")
     z, core = dp // CORES, dp % CORES
-    for k in range(n_z):
-        for side, source in ((core, head_ref), (1 - core, other_ref)):
-            at = pl.multiple_of(((z ^ k) * CORES + side) * rows, rows)
-            whole_ref[pl.ds(at, rows), :] = source[k, :rows, :]
+    n_z = pooled_ref.shape[1] // (CORES * head_rows)
+    half = head_rows // 2
+    block = half + FACT_ROWS
+    size = group_images * n_cls
+    lines = own // n_cls
+    fact_lanes = -(-(slots + 1 + 2 * size) // 128) * 128
+    row = lax.broadcasted_iota(jnp.int32, (own, fact_lanes), 0)
+    lane = lax.broadcasted_iota(jnp.int32, (own, fact_lanes), 1)
+    image = slots + 1 + row // lines * group_images + row % lines
+    block_at = (lane == image) & (row % lines < group_images)
+    row_at = (lane == image + size) & (row % lines < group_images)
+    for side, source in ((core, head_ref), (1 - core, other_ref)):
+        mine = (cls >> side) & 1
+        for k in range(n_z):
+            for part, which in ((0, mine), (1, 1 - mine)):
+                at = pl.multiple_of(((z ^ k) * CORES + side) * head_rows + which * half, half)
+                whole_ref[pl.ds(at, half), :] = source[pl.ds((part * n_z + k) * block, half), :]
+    for which, source in enumerate((head_ref, other_ref)):
+        for k in range(n_z):
+            at = (which * n_z + k) * own - base
+            if not 0 <= at < images:
+                continue
+            facts = source[pl.ds(k * block + half, FACT_ROWS), :fact_lanes][0:1].astype(jnp.float32)
+            everywhere = jnp.broadcast_to(facts, (own, fact_lanes))
+            label = jnp.sum(
+                jnp.where(block_at, everywhere * BLOCK_ROWS, jnp.where(row_at, everywhere, 0.0)), axis=1, keepdims=True
+            ).astype(jnp.int32)
+            bits = jnp.zeros((own, 1), jnp.int32)
+            for slot in range(slots):
+                used = facts[:, slots : slots + 1] > slot
+                bits = bits + jnp.where(used, 1 << facts[:, slot : slot + 1].astype(jnp.int32), 0)
+            bits = jnp.where(row[:, :1] % lines < group_images, bits, 0)
+            image_ref[pl.ds(at, own), 0:1] = label - cls * classes
+            image_ref[pl.ds(at, own), 1:2] = bits
     embedding = jnp.dot(pooled_ref[...], whole_ref[...], preferred_element_type=jnp.float32)
     norm = jnp.sqrt(jnp.sum(embedding * embedding, axis=1, keepdims=True) + NORM_EPSILON)
     unit = embedding * (1.0 / norm)
@@ -208,18 +257,19 @@
         sums_ref[step] = group_ref[pl.ds(at, lines), :]
 
 
-def class_parts(own, n_cls, *operands):
-    pooled, head, _, _, weight, _ = operands
+def class_parts(own, n_cls, head_rows, slots, group_images, base, *operands):
+    pooled, head, _, weight, _ = operands
     images, width = pooled.shape
     classes, embed = weight.shape
     return in_vmem(
-        functools.partial(class_kernel, own),
+        functools.partial(class_kernel, own, head_rows, slots, group_images, base),
         [
             f32(images, classes),
             f32(images, classes),
             f32(images, embed + 128),
             f32(n_cls, own // n_cls, 2 * embed + 256),
             f32(1, images),
+            jax.ShapeDtypeStruct((images, 2), jnp.int32),
         ],
         [
             pltpu.VMEM((width, embed), jnp.bfloat16),
@@ -305,6 +355,7 @@
     n_dp, n_cls = lax.axis_size("dp"), lax.axis_size("cls")
     n_z = n_dp // CORES
     dp, cls = lax.axis_index("dp"), lax.axis_index("cls")
+    core = dp % CORES
     tokens, width = attended.shape
     images = tokens // P_SIZE
     size = n_cls * images
@@ -319,53 +370,50 @@
         [block_ids[0, 0], block_count[0], labels // BLOCK_ROWS, labels % BLOCK_ROWS]
     ).astype(jnp.bfloat16)
     n_facts = facts.shape[0]
-    facts = jnp.pad(facts, (0, 16 * embed - n_facts)).reshape(16, embed)
+    facts = jnp.pad(facts, (0, FACT_ROWS * embed - n_facts)).reshape(FACT_ROWS, embed)
 
     own_slice = lax.dynamic_slice_in_dim(out_proj, cls * slice_rows, slice_rows, 0)
     far = jnp.stack([z_swap(own_slice, step) for step in range(2, n_z)])
     near_from, _ = lax.optimization_barrier((out_proj, own_slice))
     near = z_swap(near_from, 1)
-    own_other = core_swap(near_from)
+    own_other = core_swap(out_proj)
+    far = after(far, own_other)
     head_rows = head_proj.shape[0]
-    head_own = jnp.concatenate([head_proj, facts], axis=0)
-    class_weight, head_own, far = lax.optimization_barrier((class_weight, head_own, far))
-    far = jnp.stack([far] + [plane_swap(far, step) for step in range(1, n_cls)])
+    half = head_rows // 2
+    head_half = lax.dynamic_slice_in_dim(head_proj, ((cls >> core) & 1) * half, half, 0)
+    head_half = jnp.concatenate([head_half, facts], axis=0)
+    from_plane = [plane_swap(far, step) for step in range(1, n_cls)]
+    head_half = after(head_half, far)
+    heads = [z_swap(head_half, step) for step in range(1, n_z)]
+    near_other = core_swap(near)
+    far = jnp.stack([far] + from_plane)
     if slice_rows % 16:
         ordered = jnp.zeros_like(far)
         for step in range(n_cls):
             ordered = lax.dynamic_update_index_in_dim(ordered, far[step], cls ^ step, 0)
         far = ordered.transpose(1, 0, 2, 3).reshape(1, n_z - 2, rows, width)
-    near_other = core_swap(near)
+    far = after(far, near_other, *heads)
     far_other = core_swap(far)
+    heads = jnp.stack(heads)
     pooled = pool_tokens(
-        attended, stream, out_proj, near, own_other, near_other, far, far_other,
-        norm_gain.reshape(1, width), norm_shift.reshape(1, width),
-    )
-
-    heads = [z_swap(head_own, step) for step in range(1, n_z)]
-    heads, pooled = lax.optimization_barrier((heads, pooled))
-    heads = jnp.stack([head_own] + heads)
-    other_heads = core_swap(heads)
-    all_facts = jnp.concatenate([heads[:, head_rows:], other_heads[:, head_rows:]], axis=0)
-    all_facts = all_facts.reshape(n_dp, 16 * embed)[:, :n_facts].astype(jnp.int32)
-
-    bits = jnp.zeros((n_dp,), jnp.int32)
-    for slot in range(slots):
-        bits = bits + jnp.where(slot < all_facts[:, slots], 1 << all_facts[:, slot], 0)
-    label = all_facts[:, slots + 1 : slots + 1 + size] * BLOCK_ROWS + all_facts[:, slots + 1 + size :]
-    label = (label - cls * classes).reshape(n_dp, n_cls, images)
-    bits = jnp.broadcast_to(bits[:, None, None], label.shape)
-    image_facts = jnp.pad(jnp.stack([label, bits], axis=-1), ((0, 0), (0, 0), (0, lines - images), (0, 0)))
-    image_facts = image_facts.reshape(-1, 2)
+        attended, stream, out_proj, near, own_other, near_other, far, far_other, norm_gain.reshape(1, width), norm_shift.reshape(1, width)
+    )
+
+    column = jnp.stack([pooled] + [z_swap(pooled, step) for step in range(1, n_z)])
+    heads = jnp.concatenate([head_half[None], heads], axis=0)
+    counterparts = half_swap(heads)
 
     scale = lax.rsqrt(
         jnp.sum(jnp.square(class_weight.astype(jnp.float32)), axis=1) + NORM_EPSILON
     )[None, :]
 
-    column = jnp.stack([pooled] + [z_swap(pooled, step) for step in range(1, n_z)])
     groups = jnp.zeros((n_z, n_cls, lines, width), pooled.dtype)
-    for step, got in [(0, column)] + [(step, plane_swap(column, step)) for step in range(1, n_cls)]:
+    from_plane = [plane_swap(column, step) for step in range(1, n_cls)]
+    for step, got in enumerate([column] + from_plane):
         groups = lax.dynamic_update_slice_in_dim(groups, got[:, None], cls ^ step, 1)
+    counterparts = after(counterparts, from_plane[0])
+    heads = jnp.concatenate([heads.reshape(-1, embed), counterparts.reshape(-1, embed)], axis=0)
+    other_heads = core_swap(heads)
     groups = jnp.concatenate([groups, core_swap(groups)], axis=0)
     pooled_all = groups.reshape(n_dp * group_lines, width)
 
@@ -373,8 +421,7 @@
     total_lines = n_dp * group_lines
     parts = [
         class_parts(
-            group_lines, n_cls, pooled_all[at : at + piece], heads, other_heads, image_facts[at : at + piece],
-            class_weight, scale,
+            group_lines, n_cls, head_rows, slots, images, at, pooled_all[at : at + piece], heads, other_heads, class_weight, scale
         )
         for at in range(0, total_lines, piece)
     ]
@@ -391,11 +438,11 @@
         total = total + plane_swap(packed(step), step)
     denominator = total[images:].reshape(1, -1)[:, :total_lines]
     share = embed // n_dp
-    for k, (exponent, cosine, unit, _, _) in enumerate(parts):
+    for k, (exponent, cosine, unit, _, _, image_facts) in enumerate(parts):
         at = k * piece
         grad, loss, embed_part = class_grad_part(
             share, images, total, denominator[:, at : at + piece], exponent, cosine, unit,
-            image_facts[at : at + piece], class_weight, scale,
+            image_facts, class_weight, scale,
         )
         if k == 0:
             class_grad, sample_loss, embed_grad = grad, loss, embed_part

time: 66.3 us -> 60.6 us (0.914)
  waiting for transfers between devices: 24.8 us -> 18.6 us
  local copies, waits for them, and re-layouts: 4.51 us -> 1.04 us
  starting transfers between devices: 25.2 us -> 28.2 us
    ppermute x9, waiting for transfers between devices: 12.6 us -> 6.17 us  [plane_swap(): return lax.ppermute(value, 'cls', [(i, i ^ step) for i in range(count)])]
    unnamed x14, local copies, waits for them, and re-layouts: 3.36 us -> 0.05 us
    ppermute x9, starting transfers between devices: 13.8 us -> 15.8 us  [z_swap(): lax.ppermute(value, 'dp', [(i, i ^ step * CORES) for i in range(count)])]
    ppermute x0 -> x1, starting transfers between devices: none -> 1.49 us  [half_swap(): return lax.ppermute(value, ('dp', 'cls'), pairs)]
    concatenate x1 -> x3, other arithmetic: 0.92 us -> 1.79 us  [the longest x1 1.02 us: per_device(): jnp.concatenate([heads.reshape(-1, embed), counterparts.reshape(-1, embed...]
    pallas_call x3 -> x7, Pallas kernels: 6.83 us -> 7.2 us  [the longest x3 7.2 us: in_vmem(): pl.pallas_call(kernel, out_shape=tuple(outs), in_specs=[pl.BlockSpec(memo...]
  transfers between devices with their start and end apart: 23 -> 24, of which waited for: 13 -> 12; matrix products, arithmetic and copies ran while one was open for 4% -> 6% of each run, Pallas kernels for 4% -> 5%
where the time goes in v4:
time: 60.6 us; the launch traced here: 60.4 us
  starting transfers between devices  28.2 us (47%)
  waiting for transfers between devices  18.6 us (31%)
  Pallas kernels  7.2 us (12%)
  other arithmetic  3.66 us (6%)
  between operations  1.61 us (3%)
  local copies, waits for them, and re-layouts  1.04 us (2%)
    ppermute x9, starting transfers between devices, z_swap(): lax.ppermute(value, 'dp', [(i, i ^ step * CORES) for i in range(count)])  15.8 us
    ppermute x9, waiting for transfers between devices, z_swap(): lax.ppermute(value, 'dp', [(i, i ^ step * CORES) for i in range(count)])  11.2 us
    ppermute x9, starting transfers between devices, plane_swap(): return lax.ppermute(value, 'cls', [(i, i ^ step) for i in range(count)])  10.7 us
    pallas_call x3, Pallas kernels, in_vmem(): pl.pallas_call(kernel, out_shape=tuple(outs), in_specs=[pl.BlockSpec(memo...  7.2 us
    ppermute x9, waiting for transfers between devices, plane_swap(): return lax.ppermute(value, 'cls', [(i, i ^ step) for i in range(count)])  6.17 us
    ppermute x1, starting transfers between devices, half_swap(): return lax.ppermute(value, ('dp', 'cls'), pairs)  1.49 us
    ppermute x5, waiting for transfers between devices, core_swap(): return lax.ppermute(value, 'dp', [(i, i ^ 1) for i in range(count)])  1.23 us
  transfers between devices with their start and end apart: 24, of which 12 were waited for; matrix products, arithmetic and copies ran while one was open for 6% of the time, Pallas kernels for 5%

profile of v4, /device:TPU:0, one launch (start us, length us, event | category | flops | bytes accessed | tf_op | source)
XLA Modules:
  0.0 60.4 jit_solution(1902048313435449128)
XLA Ops:
  0.7 0.9 %constant_dynamic-slice_fusion.1 = bf16[32,1024]{1,0:T(8,128)(2,1)S(1)} fusion(bf16[128,1024]{1,0:T(8,128)(2,1)} %own_ref.1, s32[]{:T(128)S(6)} %select_n.36), kind=kLoop, calls=%fused_computation.37 | loop fusion | bytes 131076 | tf_op jit(solution)/shard_map/dynamic_slice | solution.py:375
  1.5 5.0 %collective-permute-start.4 = (bf16[32,1024]{1,0:T(8,128)(2,1)S(1)}, bf16[32,1024]{1,0:T(8,128)(2,1)S(1)}, u32[]{:S(2)}, u32[]{:S(2)}) collective-permute-start(bf16[32,1024]{1,0:T(8,128)(2,1)S(1)} %constant_dynamic-slice_fusion.1), channel_id=1, source_target_pairs={{0,24},{4,28},{8,16},{12,20},{16,8},{20,12},{24,0},{28,4},{1,25},{... | collective-permute-start | bytes 196616 | tf_op jit(solution)/shard_map/ppermute | solution.py:23
  7.2 0.7 %fusion.15 = (bf16[24]{0:T(256)(128)(2,1)S(1)}, bf16[24]{0:T(256)(128)(2,1)S(1)}) fusion(s32[24]{0:T(128)} %param.19), kind=kLoop, calls=%fused_computation.43 | loop fusion | flops 504 | bytes 192 | tf_op jit(solution)/shard_map/convert.2
  9.2 3.1 %collective-permute-done.3 = bf16[32,1024]{1,0:T(8,128)(2,1)S(1)} collective-permute-done((bf16[32,1024]{1,0:T(8,128)(2,1)S(1)}, bf16[32,1024]{1,0:T(8,128)(2,1)S(1)}, u32[]{:S(2)}, u32[]{:S(2)}) %collective-permute-start.3) | collective-permute-done | bytes 65568 | tf_op jit(solution)/shard_map/ppermute | solution.py:23
  12.3 2.5 %collective-permute-start.7 = (bf16[2,32,1024]{2,1,0:T(8,128)(2,1)S(1)}, bf16[2,32,1024]{2,1,0:T(8,128)(2,1)S(1)}, u32[]{:S(2)}, u32[]{:S(2)}) collective-permute-start(bf16[2,32,1024]{2,1,0:T(8,128)(2,1)S(1)} %shard_map.121.refs_1_), channel_id=1, source_target_pairs={{0,3},{1,2},{2,1},{3,0},{4,7},{5,6},{6,5},{7,4},{8,11},{9,10},{10,... | collective-permute-start | bytes 393224 | tf_op jit(solution)/shard_map/ppermute | solution.py:39
  15.9 0.9 %collective-permute-done.near_ref = bf16[128,1024]{1,0:T(8,128)(2,1)S(1)} collective-permute-done((bf16[128,1024]{1,0:T(8,128)(2,1)}, bf16[128,1024]{1,0:T(8,128)(2,1)S(1)}, u32[]{:S(2)}, u32[]{:S(2)}) %collective-permute-start) | collective-permute-done | bytes 262176 | tf_op jit(solution)/shard_map/ppermute | solution.py:23
  17.0 2.7 %collective-permute-start.10 = (bf16[80,512]{1,0:T(8,128)(2,1)S(1)}, bf16[80,512]{1,0:T(8,128)(2,1)S(1)}, u32[]{:S(2)}, u32[]{:S(2)}) collective-permute-start(bf16[80,512]{1,0:T(8,128)(2,1)S(1)} %shard_map.122), channel_id=1, source_target_pairs={{0,24},{4,28},{8,16},{12,20},{16,8},{20,12},{24,0},{28,4},{1,25},{... | collective-permute-start | bytes 245768 | tf_op jit(solution)/shard_map/ppermute | solution.py:23
  19.7 1.3 %collective-permute-start.9 = (bf16[80,512]{1,0:T(8,128)(2,1)S(1)}, bf16[80,512]{1,0:T(8,128)(2,1)S(1)}, u32[]{:S(2)}, u32[]{:S(2)}) collective-permute-start(bf16[80,512]{1,0:T(8,128)(2,1)S(1)} %shard_map.122), channel_id=1, source_target_pairs={{0,16},{4,20},{8,24},{12,28},{16,0},{20,4},{24,8},{28,12},{1,17},{... | collective-permute-start | bytes 245768 | tf_op jit(solution)/shard_map/ppermute | solution.py:23
  21.1 1.7 %collective-permute-start.8 = (bf16[80,512]{1,0:T(8,128)(2,1)S(1)}, bf16[80,512]{1,0:T(8,128)(2,1)S(1)}, u32[]{:S(2)}, u32[]{:S(2)}) collective-permute-start(bf16[80,512]{1,0:T(8,128)(2,1)S(1)} %shard_map.122), channel_id=1, source_target_pairs={{0,8},{4,12},{8,0},{12,4},{16,24},{20,28},{24,16},{28,20},{1,9},{5... | collective-permute-start | bytes 245768 | tf_op jit(solution)/shard_map/ppermute | solution.py:23
  22.9 1.3 %collective-permute-done.10.refs_4_ = bf16[80,512]{1,0:T(8,128)(2,1)S(1)} collective-permute-done((bf16[80,512]{1,0:T(8,128)(2,1)S(1)}, bf16[80,512]{1,0:T(8,128)(2,1)S(1)}, u32[]{:S(2)}, u32[]{:S(2)}) %collective-permute-start.10) | collective-permute-done | bytes 81952 | tf_op jit(solution)/shard_map/ppermute | solution.py:23
  24.2 3.2 %collective-permute-done.9.refs_3_ = bf16[80,512]{1,0:T(8,128)(2,1)S(1)} collective-permute-done((bf16[80,512]{1,0:T(8,128)(2,1)S(1)}, bf16[80,512]{1,0:T(8,128)(2,1)S(1)}, u32[]{:S(2)}, u32[]{:S(2)}) %collective-permute-start.9) | collective-permute-done | bytes 81952 | tf_op jit(solution)/shard_map/ppermute | solution.py:23
  27.5 0.8 %pad_maximum_fusion.3 = bf16[4,80,512]{2,1,0:T(8,128)(2,1)} fusion(bf16[1,80,512]{2,1,0:T(8,128)(2,1)S(1)} %bitcast.53, bf16[1,80,512]{2,1,0:T(8,128)(2,1)S(1)} %bitcast.54, bf16[1,80,512]{2,1,0:T(8,128)(2,1)S(1)} %bitcast.55, bf16[1,80,512]{2,1,0:T(8,128)(2,1)S(1)} %bitcast.51), kind=kLoop, calls=%fused_computation.4 | loop fusion | flops 491520 | bytes 655360 | tf_op jit(solution)/shard_map/concatenate | solution.py:403
  28.3 1.5 %collective-permute-start.19 = (bf16[4,80,512]{2,1,0:T(8,128)(2,1)}, bf16[4,80,512]{2,1,0:T(8,128)(2,1)S(1)}, u32[]{:S(2)}, u32[]{:S(2)}) collective-permute-start(bf16[4,80,512]{2,1,0:T(8,128)(2,1)} %pad_maximum_fusion.3), channel_id=1, source_target_pairs={{0,1},{1,0},{2,3},{3,2},{4,6},{5,7},{6,4},{7,5},{8,9},{9,8},{10,11... | collective-permute-start | bytes 983048 | tf_op jit(solution)/shard_map/ppermute | solution.py:34
  29.8 2.9 %shard_map.124 = bf16[8,1024]{1,0:T(8,128)(2,1)S(1)} custom-call(bf16[864,1024]{1,0:T(8,128)(2,1)S(1)} %copy-done.3, bf16[864,1024]{1,0:T(8,128)(2,1)S(1)} %copy-done.4, bf16[128,1024]{1,0:T(8,128)(2,1)S(1)} %copy-done.2, bf16[128,1024]{1,0:T(8,128)(2,1)S(1)} %collective-permute-done.near_ref, ...), custom_call_target="tpu_custom_call" | custom-call | flops 1811939328 | bytes 5660672 | tf_op jit(solution)/shard_map/pallas_call | solution.py:106
  32.7 2.5 %collective-permute-start.14 = (bf16[8,1024]{1,0:T(8,128)(2,1)S(1)}, bf16[8,1024]{1,0:T(8,128)(2,1)S(1)}, u32[]{:S(2)}, u32[]{:S(2)}) collective-permute-start(bf16[8,1024]{1,0:T(8,128)(2,1)S(1)} %shard_map.124), channel_id=1, source_target_pairs={{0,24},{4,28},{8,16},{12,20},{16,8},{20,12},{24,0},{28,4},{1,25},{... | collective-permute-start | bytes 49160 | tf_op jit(solution)/shard_map/ppermute | solution.py:23
  35.2 2.0 %collective-permute-start.12 = (bf16[8,1024]{1,0:T(8,128)(2,1)S(1)}, bf16[8,1024]{1,0:T(8,128)(2,1)S(1)}, u32[]{:S(2)}, u32[]{:S(2)}) collective-permute-start(bf16[8,1024]{1,0:T(8,128)(2,1)S(1)} %shard_map.124), channel_id=1, source_target_pairs={{0,8},{4,12},{8,0},{12,4},{16,24},{20,28},{24,16},{28,20},{1,9},{5... | collective-permute-start | bytes 49160 | tf_op jit(solution)/shard_map/ppermute | solution.py:23
  37.2 1.1 %collective-permute-done.14 = bf16[8,1024]{1,0:T(8,128)(2,1)S(1)} collective-permute-done((bf16[8,1024]{1,0:T(8,128)(2,1)S(1)}, bf16[8,1024]{1,0:T(8,128)(2,1)S(1)}, u32[]{:S(2)}, u32[]{:S(2)}) %collective-permute-start.14) | collective-permute-done | bytes 16416 | tf_op jit(solution)/shard_map/ppermute | solution.py:23
  38.3 1.5 %collective-permute-done.13 = bf16[8,1024]{1,0:T(8,128)(2,1)S(1)} collective-permute-done((bf16[8,1024]{1,0:T(8,128)(2,1)S(1)}, bf16[8,1024]{1,0:T(8,128)(2,1)S(1)}, u32[]{:S(2)}, u32[]{:S(2)}) %collective-permute-start.13) | collective-permute-done | bytes 16416 | tf_op jit(solution)/shard_map/ppermute | solution.py:23
  39.9 1.6 %collective-permute-start.16 = (bf16[4,8,1024]{2,1,0:T(8,128)(2,1)S(1)}, bf16[4,8,1024]{2,1,0:T(8,128)(2,1)S(1)}, u32[]{:S(2)}, u32[]{:S(2)}) collective-permute-start(bf16[4,8,1024]{2,1,0:T(8,128)(2,1)S(1)} %pad_maximum_fusion.6), channel_id=1, source_target_pairs={{0,2},{1,3},{2,0},{3,1},{4,6},{5,7},{6,4},{7,5},{8,10},{9,11},{10,... | collective-permute-start | bytes 196616 | tf_op jit(solution)/shard_map/ppermute | solution.py:39
  41.5 1.1 %collective-permute-start.15 = (bf16[4,8,1024]{2,1,0:T(8,128)(2,1)S(1)}, bf16[4,8,1024]{2,1,0:T(8,128)(2,1)S(1)}, u32[]{:S(2)}, u32[]{:S(2)}) collective-permute-start(bf16[4,8,1024]{2,1,0:T(8,128)(2,1)S(1)} %pad_maximum_fusion.6), channel_id=1, source_target_pairs={{0,1},{1,0},{2,3},{3,2},{4,5},{5,4},{6,7},{7,6},{8,9},{9,8},{10,11... | collective-permute-start | bytes 196616 | tf_op jit(solution)/shard_map/ppermute | solution.py:39
  42.6 0.9 %collective-permute-start.17 = (bf16[4,8,1024]{2,1,0:T(8,128)(2,1)S(1)}, bf16[4,8,1024]{2,1,0:T(8,128)(2,1)S(1)}, u32[]{:S(2)}, u32[]{:S(2)}) collective-permute-start(bf16[4,8,1024]{2,1,0:T(8,128)(2,1)S(1)} %pad_maximum_fusion.6), channel_id=1, source_target_pairs={{0,3},{1,2},{2,1},{3,0},{4,7},{5,6},{6,5},{7,4},{8,11},{9,10},{10,... | collective-permute-start | bytes 196616 | tf_op jit(solution)/shard_map/ppermute | solution.py:39
  43.5 2.2 %collective-permute-done.15.refs_1_ = bf16[4,8,1024]{2,1,0:T(8,128)(2,1)S(1)} collective-permute-done((bf16[4,8,1024]{2,1,0:T(8,128)(2,1)S(1)}, bf16[4,8,1024]{2,1,0:T(8,128)(2,1)S(1)}, u32[]{:S(2)}, u32[]{:S(2)}) %collective-permute-start.15) | collective-permute-done | bytes 65568 | tf_op jit(solution)/shard_map/ppermute | solution.py:39
  45.7 1.0 %pad_maximum_fusion.head_ref = bf16[640,512]{1,0:T(8,128)(2,1)S(1)} fusion(bf16[320,512]{1,0:T(8,128)(2,1)S(1)} %bitcast.50, bf16[320,512]{1,0:T(8,128)(2,1)} %bitcast.27), kind=kLoop, calls=%fused_computation.1 | loop fusion | flops 1310720 | bytes 1310720 | tf_op jit(solution)/shard_map/concatenate | solution.py:415
  46.9 0.9 %collective-permute-done.17 = bf16[4,8,1024]{2,1,0:T(8,128)(2,1)S(1)} collective-permute-done((bf16[4,8,1024]{2,1,0:T(8,128)(2,1)S(1)}, bf16[4,8,1024]{2,1,0:T(8,128)(2,1)S(1)}, u32[]{:S(2)}, u32[]{:S(2)}) %collective-permute-start.17) | collective-permute-done | bytes 65568 | tf_op jit(solution)/shard_map/ppermute | solution.py:39
  48.2 1.2 %collective-permute-done.18 = bf16[4,4,8,1024]{3,2,1,0:T(8,128)(2,1)S(1)} collective-permute-done((bf16[4,4,8,1024]{3,2,1,0:T(8,128)(2,1)S(1)}, bf16[4,4,8,1024]{3,2,1,0:T(8,128)(2,1)S(1)}, u32[]{:S(2)}, u32[]{:S(2)}) %collective-permute-start.18) | collective-permute-done | bytes 262176 | tf_op jit(solution)/shard_map/ppermute | solution.py:28
  49.4 2.4 %shard_map.126 = (f32[256,1024]{1,0:T(8,128)S(1)}, f32[256,1024]{1,0:T(8,128)S(1)}, f32[256,640]{1,0:T(8,128)S(1)}, f32[4,8,1280]{2,1,0:T(8,128)S(1)}, f32[1,256]{1,0:T(1,128)S(1)}, /*index=5*/s32[256,2]{1,0:T(8,128)S(1)}) custom-call(bf16[256,1024]{1,0:T(8,128)(2,1)S(1)} %bitcast.52, bf16[640,512]{1,0:T(8,128)(2,1)S(1)} %pad_maximum_fusion.head_ref, ...), custom_call_target="tpu_custom_call" | custom-call | flops 805306368 | bytes 5807104 | tf_op jit(solution)/shard_map/pallas_call | solution.py:106
  51.9 1.1 %collective-permute-start.21 = (f32[7,1280]{1,0:T(8,128)S(1)}, f32[7,1280]{1,0:T(8,128)S(1)}, u32[]{:S(2)}, u32[]{:S(2)}) collective-permute-start(f32[7,1280]{1,0:T(8,128)S(1)} %get-tuple-element.27), channel_id=1, source_target_pairs={{0,3},{1,2},{2,1},{3,0},{4,7},{5,6},{6,5},{7,4},{8,11},{9,10},{10,... | collective-permute-start | bytes 107528 | tf_op jit(solution)/shard_map/ppermute | solution.py:39
  53.0 1.5 %collective-permute-start.22 = (f32[7,1280]{1,0:T(8,128)S(1)}, f32[7,1280]{1,0:T(8,128)S(1)}, u32[]{:S(2)}, u32[]{:S(2)}) collective-permute-start(f32[7,1280]{1,0:T(8,128)S(1)} %get-tuple-element.28), channel_id=1, source_target_pairs={{0,2},{1,3},{2,0},{3,1},{4,6},{5,7},{6,4},{7,5},{8,10},{9,11},{10,... | collective-permute-start | bytes 107528 | tf_op jit(solution)/shard_map/ppermute | solution.py:39
  54.5 1.0 %collective-permute-start.23 = (f32[7,1280]{1,0:T(8,128)S(1)}, f32[7,1280]{1,0:T(8,128)S(1)}, u32[]{:S(2)}, u32[]{:S(2)}) collective-permute-start(f32[7,1280]{1,0:T(8,128)S(1)} %get-tuple-element.29), channel_id=1, source_target_pairs={{0,1},{1,0},{2,3},{3,2},{4,5},{5,4},{6,7},{7,6},{8,9},{9,8},{10,11... | collective-permute-start | bytes 107528 | tf_op jit(solution)/shard_map/ppermute | solution.py:39
  55.5 1.7 %collective-permute-done.21 = f32[7,1280]{1,0:T(8,128)S(1)} collective-permute-done((f32[7,1280]{1,0:T(8,128)S(1)}, f32[7,1280]{1,0:T(8,128)S(1)}, u32[]{:S(2)}, u32[]{:S(2)}) %collective-permute-start.21) | collective-permute-done | bytes 35872 | tf_op jit(solution)/shard_map/ppermute | solution.py:39
  57.3 1.2 %collective-permute-done.23 = f32[7,1280]{1,0:T(8,128)S(1)} collective-permute-done((f32[7,1280]{1,0:T(8,128)S(1)}, f32[7,1280]{1,0:T(8,128)S(1)}, u32[]{:S(2)}, u32[]{:S(2)}) %collective-permute-start.23) | collective-permute-done | bytes 35872 | tf_op jit(solution)/shard_map/ppermute | solution.py:39
  58.5 1.9 %shard_map.127 = (f32[64,1024]{1,0:T(8,128)}, f32[1,6]{1,0:T(1,128)}, f32[6,512]{1,0:T(8,128)}) custom-call(f32[7,1280]{1,0:T(8,128)S(1)} %fusion.6.total_ref, f32[1,256]{1,0:T(1,128)S(1)} %slice.22.denom_ref, f32[256,1024]{1,0:T(8,128)S(1)} %get-tuple-element.16.exp_ref, f32[256,1024]{1,0:T(8,128)S(1)} %get-tuple-element.17.cos_ref, ...), custom_call_target="tpu_custom_call" | custom-call | flops 167772160 | bytes 4118552 | tf_op jit(solution)/shard_map/pallas_call | solution.py:106
  (61 shorter events, 3.5 us)
Async XLA Ops:
  0.6 8.5 %copy-start = (bf16[128,512]{1,0:T(8,128)(2,1)S(1)}, bf16[128,512]{1,0:T(8,128)(2,1)}, u32[]{:S(2)}) copy-start(bf16[128,512]{1,0:T(8,128)(2,1)} %param.15) | copy-start | bytes 393220
  1.5 7.6 %collective-permute-start.4 = (bf16[32,1024]{1,0:T(8,128)(2,1)S(1)}, bf16[32,1024]{1,0:T(8,128)(2,1)S(1)}, u32[]{:S(2)}, u32[]{:S(2)}) collective-permute-start(bf16[32,1024]{1,0:T(8,128)(2,1)S(1)} %constant_dynamic-slice_fusion.1), channel_id=1, source_target_pairs={{0,24},{4,28},{8,16},{12,20},{16,8},{20,12},{24,0},{28,4},{1,25},{... | collective-permute-start | bytes 196616 | tf_op jit(solution)/shard_map/ppermute | solution.py:23
  6.6 5.7 %collective-permute-start.3 = (bf16[32,1024]{1,0:T(8,128)(2,1)S(1)}, bf16[32,1024]{1,0:T(8,128)(2,1)S(1)}, u32[]{:S(2)}, u32[]{:S(2)}) collective-permute-start(bf16[32,1024]{1,0:T(8,128)(2,1)S(1)} %constant_dynamic-slice_fusion.1), channel_id=1, source_target_pairs={{0,16},{4,20},{8,24},{12,28},{16,0},{20,4},{24,8},{28,12},{1,17},{... | collective-permute-start | bytes 196616 | tf_op jit(solution)/shard_map/ppermute | solution.py:23
  6.6 5.7 %collective-permute-start.1 = (bf16[128,1024]{1,0:T(8,128)(2,1)}, bf16[128,1024]{1,0:T(8,128)(2,1)S(1)}, u32[]{:S(2)}, u32[]{:S(2)}) collective-permute-start(bf16[128,1024]{1,0:T(8,128)(2,1)} %own_ref.1), channel_id=1, source_target_pairs={{0,4},{4,0},{8,12},{12,8},{16,20},{20,16},{24,28},{28,24},{1,5},{5... | collective-permute-start | bytes 786440 | tf_op jit(solution)/shard_map/ppermute | solution.py:28
  6.6 10.2 %collective-permute-start = (bf16[128,1024]{1,0:T(8,128)(2,1)}, bf16[128,1024]{1,0:T(8,128)(2,1)S(1)}, u32[]{:S(2)}, u32[]{:S(2)}) collective-permute-start(bf16[128,1024]{1,0:T(8,128)(2,1)} %own_ref.1), channel_id=1, source_target_pairs={{0,8},{4,12},{8,0},{12,4},{16,24},{20,28},{24,16},{28,20},{1,9},{5... | collective-permute-start | bytes 786440 | tf_op jit(solution)/shard_map/ppermute | solution.py:23
  12.3 17.5 %copy-start.4 = (bf16[864,1024]{1,0:T(8,128)(2,1)S(1)}, bf16[864,1024]{1,0:T(8,128)(2,1)}, u32[]{:S(2)}) copy-start(bf16[864,1024]{1,0:T(8,128)(2,1)} %stream_ref.1) | copy-start | bytes 5308420
  12.3 7.4 %collective-permute-start.7 = (bf16[2,32,1024]{2,1,0:T(8,128)(2,1)S(1)}, bf16[2,32,1024]{2,1,0:T(8,128)(2,1)S(1)}, u32[]{:S(2)}, u32[]{:S(2)}) collective-permute-start(bf16[2,32,1024]{2,1,0:T(8,128)(2,1)S(1)} %shard_map.121.refs_1_), channel_id=1, source_target_pairs={{0,3},{1,2},{2,1},{3,0},{4,7},{5,6},{6,5},{7,4},{8,11},{9,10},{10,... | collective-permute-start | bytes 393224 | tf_op jit(solution)/shard_map/ppermute | solution.py:39
  14.9 6.2 %collective-permute-start.6 = (bf16[2,32,1024]{2,1,0:T(8,128)(2,1)S(1)}, bf16[2,32,1024]{2,1,0:T(8,128)(2,1)S(1)}, u32[]{:S(2)}, u32[]{:S(2)}) collective-permute-start(bf16[2,32,1024]{2,1,0:T(8,128)(2,1)S(1)} %shard_map.121.refs_1_), channel_id=1, source_target_pairs={{0,2},{1,3},{2,0},{3,1},{4,6},{5,7},{6,4},{7,5},{8,10},{9,11},{10,... | collective-permute-start | bytes 393224 | tf_op jit(solution)/shard_map/ppermute | solution.py:39
  15.4 7.4 %collective-permute-start.5 = (bf16[2,32,1024]{2,1,0:T(8,128)(2,1)S(1)}, bf16[2,32,1024]{2,1,0:T(8,128)(2,1)S(1)}, u32[]{:S(2)}, u32[]{:S(2)}) collective-permute-start(bf16[2,32,1024]{2,1,0:T(8,128)(2,1)S(1)} %shard_map.121.refs_1_), channel_id=1, source_target_pairs={{0,1},{1,0},{2,3},{3,2},{4,5},{5,4},{6,7},{7,6},{8,9},{9,8},{10,11... | collective-permute-start | bytes 393224 | tf_op jit(solution)/shard_map/ppermute | solution.py:39
  16.8 10.6 %collective-permute-start.2 = (bf16[128,1024]{1,0:T(8,128)(2,1)S(1)}, bf16[128,1024]{1,0:T(8,128)(2,1)S(1)}, u32[]{:S(2)}, u32[]{:S(2)}) collective-permute-start(bf16[128,1024]{1,0:T(8,128)(2,1)S(1)} %collective-permute-done.near_ref), channel_id=1, source_target_pairs={{0,4},{4,0},{8,12},{12,8},{16,20},{20,16},{24,28},{28,24},{1,5},{5... | collective-permute-start | bytes 786440 | tf_op jit(solution)/shard_map/ppermute | solution.py:28
  16.9 12.9 %copy-start.2 = (bf16[128,1024]{1,0:T(8,128)(2,1)S(1)}, bf16[128,1024]{1,0:T(8,128)(2,1)}, u32[]{:S(2)}) copy-start(bf16[128,1024]{1,0:T(8,128)(2,1)} %own_ref.1) | copy-start | bytes 786436
  16.9 12.9 %copy-start.3 = (bf16[864,1024]{1,0:T(8,128)(2,1)S(1)}, bf16[864,1024]{1,0:T(8,128)(2,1)}, u32[]{:S(2)}) copy-start(bf16[864,1024]{1,0:T(8,128)(2,1)} %att_ref.1) | copy-start | bytes 5308420
  16.9 12.9 %copy-start.5 = (f32[1024]{0:T(1024)S(1)}, f32[1024]{0:T(1024)}, u32[]{:S(2)}) copy-start(f32[1024]{0:T(1024)} %param.13) | copy-start | bytes 12292
  17.0 12.9 %copy-start.6 = (f32[1024]{0:T(1024)S(1)}, f32[1024]{0:T(1024)}, u32[]{:S(2)}) copy-start(f32[1024]{0:T(1024)} %param.14) | copy-start | bytes 12292
  17.0 7.2 %collective-permute-start.10 = (bf16[80,512]{1,0:T(8,128)(2,1)S(1)}, bf16[80,512]{1,0:T(8,128)(2,1)S(1)}, u32[]{:S(2)}, u32[]{:S(2)}) collective-permute-start(bf16[80,512]{1,0:T(8,128)(2,1)S(1)} %shard_map.122), channel_id=1, source_target_pairs={{0,24},{4,28},{8,16},{12,20},{16,8},{20,12},{24,0},{28,4},{1,25},{... | collective-permute-start | bytes 245768 | tf_op jit(solution)/shard_map/ppermute | solution.py:23
  19.7 7.7 %collective-permute-start.9 = (bf16[80,512]{1,0:T(8,128)(2,1)S(1)}, bf16[80,512]{1,0:T(8,128)(2,1)S(1)}, u32[]{:S(2)}, u32[]{:S(2)}) collective-permute-start(bf16[80,512]{1,0:T(8,128)(2,1)S(1)} %shard_map.122), channel_id=1, source_target_pairs={{0,16},{4,20},{8,24},{12,28},{16,0},{20,4},{24,8},{28,12},{1,17},{... | collective-permute-start | bytes 245768 | tf_op jit(solution)/shard_map/ppermute | solution.py:23
  21.1 6.3 %collective-permute-start.8 = (bf16[80,512]{1,0:T(8,128)(2,1)S(1)}, bf16[80,512]{1,0:T(8,128)(2,1)S(1)}, u32[]{:S(2)}, u32[]{:S(2)}) collective-permute-start(bf16[80,512]{1,0:T(8,128)(2,1)S(1)} %shard_map.122), channel_id=1, source_target_pairs={{0,8},{4,12},{8,0},{12,4},{16,24},{20,28},{24,16},{28,20},{1,9},{5... | collective-permute-start | bytes 245768 | tf_op jit(solution)/shard_map/ppermute | solution.py:23
  27.4 2.4 %collective-permute-start.11 = (bf16[4,2,32,1024]{3,2,1,0:T(8,128)(2,1)S(1)}, bf16[4,2,32,1024]{3,2,1,0:T(8,128)(2,1)S(1)}, u32[]{:S(2)}, u32[]{:S(2)}) collective-permute-start(bf16[4,2,32,1024]{3,2,1,0:T(8,128)(2,1)S(1)} %shard_map.123.far_ref), channel_id=1, source_target_pairs={{0,4},{4,0},{8,12},{12,8},{16,20},{20,16},{24,28},{28,24},{1,5},{5... | collective-permute-start | bytes 1572872 | tf_op jit(solution)/shard_map/ppermute | solution.py:28
  28.3 15.2 %collective-permute-start.19 = (bf16[4,80,512]{2,1,0:T(8,128)(2,1)}, bf16[4,80,512]{2,1,0:T(8,128)(2,1)S(1)}, u32[]{:S(2)}, u32[]{:S(2)}) collective-permute-start(bf16[4,80,512]{2,1,0:T(8,128)(2,1)} %pad_maximum_fusion.3), channel_id=1, source_target_pairs={{0,1},{1,0},{2,3},{3,2},{4,6},{5,7},{6,4},{7,5},{8,9},{9,8},{10,11... | collective-permute-start | bytes 983048 | tf_op jit(solution)/shard_map/ppermute | solution.py:34
  32.7 15.1 %copy-start.1 = (bf16[1024,512]{1,0:T(8,128)(2,1)S(1)}, bf16[1024,512]{1,0:T(8,128)(2,1)}, u32[]{:S(2)}) copy-start(bf16[1024,512]{1,0:T(8,128)(2,1)} %weight_ref.3) | copy-start | bytes 3145732
  32.7 5.6 %collective-permute-start.14 = (bf16[8,1024]{1,0:T(8,128)(2,1)S(1)}, bf16[8,1024]{1,0:T(8,128)(2,1)S(1)}, u32[]{:S(2)}, u32[]{:S(2)}) collective-permute-start(bf16[8,1024]{1,0:T(8,128)(2,1)S(1)} %shard_map.124), channel_id=1, source_target_pairs={{0,24},{4,28},{8,16},{12,20},{16,8},{20,12},{24,0},{28,4},{1,25},{... | collective-permute-start | bytes 49160 | tf_op jit(solution)/shard_map/ppermute | solution.py:23
  35.2 4.6 %collective-permute-start.13 = (bf16[8,1024]{1,0:T(8,128)(2,1)S(1)}, bf16[8,1024]{1,0:T(8,128)(2,1)S(1)}, u32[]{:S(2)}, u32[]{:S(2)}) collective-permute-start(bf16[8,1024]{1,0:T(8,128)(2,1)S(1)} %shard_map.124), channel_id=1, source_target_pairs={{0,16},{4,20},{8,24},{12,28},{16,0},{20,4},{24,8},{28,12},{1,17},{... | collective-permute-start | bytes 49160 | tf_op jit(solution)/shard_map/ppermute | solution.py:23
  35.2 4.6 %collective-permute-start.12 = (bf16[8,1024]{1,0:T(8,128)(2,1)S(1)}, bf16[8,1024]{1,0:T(8,128)(2,1)S(1)}, u32[]{:S(2)}, u32[]{:S(2)}) collective-permute-start(bf16[8,1024]{1,0:T(8,128)(2,1)S(1)} %shard_map.124), channel_id=1, source_target_pairs={{0,8},{4,12},{8,0},{12,4},{16,24},{20,28},{24,16},{28,20},{1,9},{5... | collective-permute-start | bytes 49160 | tf_op jit(solution)/shard_map/ppermute | solution.py:23
  39.9 7.0 %collective-permute-start.16 = (bf16[4,8,1024]{2,1,0:T(8,128)(2,1)S(1)}, bf16[4,8,1024]{2,1,0:T(8,128)(2,1)S(1)}, u32[]{:S(2)}, u32[]{:S(2)}) collective-permute-start(bf16[4,8,1024]{2,1,0:T(8,128)(2,1)S(1)} %pad_maximum_fusion.6), channel_id=1, source_target_pairs={{0,2},{1,3},{2,0},{3,1},{4,6},{5,7},{6,4},{7,5},{8,10},{9,11},{10,... | collective-permute-start | bytes 196616 | tf_op jit(solution)/shard_map/ppermute | solution.py:39
  41.5 4.3 %collective-permute-start.15 = (bf16[4,8,1024]{2,1,0:T(8,128)(2,1)S(1)}, bf16[4,8,1024]{2,1,0:T(8,128)(2,1)S(1)}, u32[]{:S(2)}, u32[]{:S(2)}) collective-permute-start(bf16[4,8,1024]{2,1,0:T(8,128)(2,1)S(1)} %pad_maximum_fusion.6), channel_id=1, source_target_pairs={{0,1},{1,0},{2,3},{3,2},{4,5},{5,4},{6,7},{7,6},{8,9},{9,8},{10,11... | collective-permute-start | bytes 196616 | tf_op jit(solution)/shard_map/ppermute | solution.py:39
  42.6 5.2 %collective-permute-start.17 = (bf16[4,8,1024]{2,1,0:T(8,128)(2,1)S(1)}, bf16[4,8,1024]{2,1,0:T(8,128)(2,1)S(1)}, u32[]{:S(2)}, u32[]{:S(2)}) collective-permute-start(bf16[4,8,1024]{2,1,0:T(8,128)(2,1)S(1)} %pad_maximum_fusion.6), channel_id=1, source_target_pairs={{0,3},{1,2},{2,1},{3,0},{4,7},{5,6},{6,5},{7,4},{8,11},{9,10},{10,... | collective-permute-start | bytes 196616 | tf_op jit(solution)/shard_map/ppermute | solution.py:39
  46.8 2.7 %collective-permute-start.20 = (bf16[640,512]{1,0:T(8,128)(2,1)S(1)}, bf16[640,512]{1,0:T(8,128)(2,1)S(1)}, u32[]{:S(2)}, u32[]{:S(2)}) collective-permute-start(bf16[640,512]{1,0:T(8,128)(2,1)S(1)} %pad_maximum_fusion.head_ref), channel_id=1, source_target_pairs={{0,4},{4,0},{8,12},{12,8},{16,20},{20,16},{24,28},{28,24},{1,5},{5... | collective-permute-start | bytes 1966088 | tf_op jit(solution)/shard_map/ppermute | solution.py:28
  47.8 1.6 %collective-permute-start.18 = (bf16[4,4,8,1024]{3,2,1,0:T(8,128)(2,1)S(1)}, bf16[4,4,8,1024]{3,2,1,0:T(8,128)(2,1)S(1)}, u32[]{:S(2)}, u32[]{:S(2)}) collective-permute-start(bf16[4,4,8,1024]{3,2,1,0:T(8,128)(2,1)S(1)} %bitcast_dynamic-update-slice_fusion), channel_id=1, source_target_pairs={{0,4},{4,0},{8,12},{12,8},{16,20},{20,16},{24,28},{28,24},{1,5},{5... | collective-permute-start | bytes 786440 | tf_op jit(solution)/shard_map/ppermute | solution.py:28
  51.9 5.2 %collective-permute-start.21 = (f32[7,1280]{1,0:T(8,128)S(1)}, f32[7,1280]{1,0:T(8,128)S(1)}, u32[]{:S(2)}, u32[]{:S(2)}) collective-permute-start(f32[7,1280]{1,0:T(8,128)S(1)} %get-tuple-element.27), channel_id=1, source_target_pairs={{0,3},{1,2},{2,1},{3,0},{4,7},{5,6},{6,5},{7,4},{8,11},{9,10},{10,... | collective-permute-start | bytes 107528 | tf_op jit(solution)/shard_map/ppermute | solution.py:39
  53.0 4.4 %collective-permute-start.22 = (f32[7,1280]{1,0:T(8,128)S(1)}, f32[7,1280]{1,0:T(8,128)S(1)}, u32[]{:S(2)}, u32[]{:S(2)}) collective-permute-start(f32[7,1280]{1,0:T(8,128)S(1)} %get-tuple-element.28), channel_id=1, source_target_pairs={{0,2},{1,3},{2,0},{3,1},{4,6},{5,7},{6,4},{7,5},{8,10},{9,11},{10,... | collective-permute-start | bytes 107528 | tf_op jit(solution)/shard_map/ppermute | solution.py:39
  54.5 4.0 %collective-permute-start.23 = (f32[7,1280]{1,0:T(8,128)S(1)}, f32[7,1280]{1,0:T(8,128)S(1)}, u32[]{:S(2)}, u32[]{:S(2)}) collective-permute-start(f32[7,1280]{1,0:T(8,128)S(1)} %get-tuple-element.29), channel_id=1, source_target_pairs={{0,1},{1,0},{2,3},{3,2},{4,5},{5,4},{6,7},{7,6},{8,9},{9,8},{10,11... | collective-permute-start | bytes 107528 | tf_op jit(solution)/shard_map/ppermute | solution.py:39

commit v5 on v4

--- a/solution.py
+++ b/solution.py
@@ -168,14 +168,12 @@
     return live, live & (column == label)
 
 
-def class_kernel(own, head_rows, slots, group_images, base, pooled_ref, head_ref, other_ref, weight_ref, scale_ref,
-                 exp_ref, cos_ref, unit_ref, sums_ref, denom_ref, image_ref, whole_ref, chosen_ref, group_ref):
-    images = pooled_ref.shape[0]
-    classes, embed = weight_ref.shape
-    n_cls = sums_ref.shape[0]
+def facts_kernel(own, slots, group_images, n_cls, classes, head_ref, other_ref, whole_ref, image_ref):
+    width = whole_ref.shape[0]
+    n_z = image_ref.shape[0] // (CORES * own)
     dp, cls = lax.axis_index("dp"), lax.axis_index("cls")
     z, core = dp // CORES, dp % CORES
-    n_z = pooled_ref.shape[1] // (CORES * head_rows)
+    head_rows = width // (CORES * n_z)
     half = head_rows // 2
     block = half + FACT_ROWS
     size = group_images * n_cls
@@ -194,9 +192,7 @@
                 whole_ref[pl.ds(at, half), :] = source[pl.ds((part * n_z + k) * block, half), :]
     for which, source in enumerate((head_ref, other_ref)):
         for k in range(n_z):
-            at = (which * n_z + k) * own - base
-            if not 0 <= at < images:
-                continue
+            at = (which * n_z + k) * own
             facts = source[pl.ds(k * block + half, FACT_ROWS), :fact_lanes][0:1].astype(jnp.float32)
             everywhere = jnp.broadcast_to(facts, (own, fact_lanes))
             label = jnp.sum(
@@ -209,6 +205,26 @@
             bits = jnp.where(row[:, :1] % lines < group_images, bits, 0)
             image_ref[pl.ds(at, own), 0:1] = label - cls * classes
             image_ref[pl.ds(at, own), 1:2] = bits
+
+
+def group_facts(own, slots, group_images, n_cls, classes, width, total, *operands):
+    embed = operands[0].shape[1]
+    return in_vmem(
+        functools.partial(facts_kernel, own, slots, group_images, n_cls, classes),
+        [jax.ShapeDtypeStruct((width, embed), jnp.bfloat16), jax.ShapeDtypeStruct((total, 2), jnp.int32)],
+        [],
+        4,
+        0,
+        operands,
+    )
+
+
+def class_kernel(own, pooled_ref, whole_ref, image_ref, weight_ref, scale_ref,
+                 exp_ref, cos_ref, unit_ref, sums_ref, denom_ref, chosen_ref, group_ref):
+    images = pooled_ref.shape[0]
+    classes, embed = weight_ref.shape
+    n_cls = sums_ref.shape[0]
+    cls = lax.axis_index("cls")
     embedding = jnp.dot(pooled_ref[...], whole_ref[...], preferred_element_type=jnp.float32)
     norm = jnp.sqrt(jnp.sum(embedding * embedding, axis=1, keepdims=True) + NORM_EPSILON)
     unit = embedding * (1.0 / norm)
@@ -257,22 +273,20 @@
         sums_ref[step] = group_ref[pl.ds(at, lines), :]
 
 
-def class_parts(own, n_cls, head_rows, slots, group_images, base, *operands):
-    pooled, head, _, weight, _ = operands
+def class_parts(own, n_cls, *operands):
+    pooled, _, _, weight, _ = operands
     images, width = pooled.shape
     classes, embed = weight.shape
     return in_vmem(
-        functools.partial(class_kernel, own, head_rows, slots, group_images, base),
+        functools.partial(class_kernel, own),
         [
             f32(images, classes),
             f32(images, classes),
             f32(images, embed + 128),
             f32(n_cls, own // n_cls, 2 * embed + 256),
             f32(1, images),
-            jax.ShapeDtypeStruct((images, 2), jnp.int32),
         ],
         [
-            pltpu.VMEM((width, embed), jnp.bfloat16),
             pltpu.VMEM((own, classes), jnp.float32),
             pltpu.VMEM((own, 2 * embed + 256), jnp.float32),
         ],
@@ -282,35 +296,69 @@
     )
 
 
-def grad_kernel(share, total_ref, denom_ref, exp_ref, cos_ref, unit_ref, image_ref, weight_ref, scale_ref,
-                grad_ref, loss_ref, embed_ref):
+def aside_kernel(share, exp_ref, cos_ref, unit_ref, image_ref, weight_ref,
+                 high_ref, low_ref, along_ref, unit_out, weight_out, marked_ref, mark_ref):
     images, classes = exp_ref.shape
-    embed = weight_ref.shape[1]
     at = lax.axis_index("dp") * share
     block = pl.ds(pl.multiple_of(at // 128 * 128, 128), 128)
     take = one_hot(share, 128, lambda row: row + at % 128)
     high, low = split(unit_ref[:, block])
     unit = over_lanes(take, high) + over_lanes(take, low)
-    weight = over_lanes(take, weight_ref[:, block])
+    unit_out[...] = unit
+    weight_out[...] = over_lanes(take, weight_ref[:, block])
+    marked = jnp.concatenate(split(unit * LOGIT_SCALE), axis=0)
+    wide = 256
+    for start in range(0, classes, wide):
+        cols = pl.ds(start, wide)
+        exponent, cosine = exp_ref[:, cols], cos_ref[:, cols]
+        _, target = masks(image_ref, start, wide)
+        high_ref[:, cols], low_ref[:, cols] = split(exponent)
+        along_ref[:, cols] = exponent * cosine
+        mark_ref[:, cols] = jnp.sum(jnp.where(target, LOGIT_SCALE * cosine, 0.0), axis=0, keepdims=True)
+        both = jnp.dot(
+            marked, jnp.where(target, 1.0, 0.0).astype(jnp.bfloat16), preferred_element_type=jnp.float32
+        )
+        marked_ref[:, cols] = both[:share] + both[share:]
+
+
+def class_grad_aside(share, *operands):
+    images, classes = operands[0].shape
+    return in_vmem(
+        functools.partial(aside_kernel, share),
+        [
+            jax.ShapeDtypeStruct((images, classes), jnp.bfloat16),
+            jax.ShapeDtypeStruct((images, classes), jnp.bfloat16),
+            f32(images, classes),
+            f32(share, images),
+            f32(share, classes),
+            f32(share, classes),
+            f32(1, classes),
+        ],
+        [],
+        5,
+        4 * images * share * classes,
+        operands,
+    )
+
+
+def grad_kernel(total_ref, denom_ref, high_ref, low_ref, along_ref, unit_share_ref, weight_share_ref, marked_ref,
+                mark_ref, scale_ref, unit_ref, grad_ref, loss_ref, embed_ref):
+    images, classes = high_ref.shape
+    share = unit_share_ref.shape[0]
+    embed = embed_ref.shape[1]
     denom = denom_ref[...]
     ratio = jnp.where(denom > 0.0, LOGIT_SCALE / denom, 0.0)
-    left = jnp.concatenate(split(unit * ratio), axis=0)
-    marked = jnp.concatenate(split(unit * LOGIT_SCALE), axis=0)
+    left = jnp.concatenate(split(unit_share_ref[...] * ratio), axis=0)
     column = jnp.broadcast_to(ratio, (128, images)).T[:, 0:1]
     dot = functools.partial(jnp.dot, preferred_element_type=jnp.float32)
     wide = 256
     for start in range(0, classes, wide):
         cols = pl.ds(start, wide)
-        exponent = exp_ref[:, cols]
-        _, target = masks(image_ref, start, wide)
-        high, low = split(exponent)
-        first = dot(left, high)
-        second = dot(marked, jnp.where(target, 1.0, 0.0).astype(jnp.bfloat16))
-        grad = first[:share] + first[share:] + dot(left[:share], low) - second[:share] - second[share:]
-        weighted = exponent * column - jnp.where(target, LOGIT_SCALE, 0.0)
-        along = jnp.sum(weighted * cos_ref[:, cols], axis=0, keepdims=True)
+        first = dot(left, high_ref[:, cols])
+        grad = first[:share] + first[share:] + dot(left[:share], low_ref[:, cols]) - marked_ref[:, cols]
+        along = jnp.sum(along_ref[:, cols] * column, axis=0, keepdims=True) - mark_ref[:, cols]
         scale = scale_ref[:, cols]
-        grad_ref[:, cols] = (grad - weight[:, start : start + wide] * (along * scale)) * scale
+        grad_ref[:, cols] = (grad - weight_share_ref[:, cols] * (along * scale)) * scale
 
     lines = padded(embed_ref.shape[0])
     own = unit_ref[pl.ds(pl.multiple_of(lax.axis_index("cls") * lines, lines), lines), :][: embed_ref.shape[0]]
@@ -327,15 +375,16 @@
     ) / own[:, embed : embed + 1]
 
 
-def class_grad_part(share, own_images, *operands):
+def class_grad_part(own_images, *operands):
     images, classes = operands[2].shape
-    embed = operands[6].shape[1]
+    share = operands[5].shape[0]
+    embed = operands[10].shape[1] - 128
     return in_vmem(
-        functools.partial(grad_kernel, share),
+        grad_kernel,
         [f32(share, classes), f32(1, own_images), f32(own_images, embed)],
         [],
-        6,
-        10 * images * share * classes,
+        5,
+        6 * images * share * classes,
         operands,
     )
 
@@ -414,16 +463,18 @@
     counterparts = after(counterparts, from_plane[0])
     heads = jnp.concatenate([heads.reshape(-1, embed), counterparts.reshape(-1, embed)], axis=0)
     other_heads = core_swap(heads)
-    groups = jnp.concatenate([groups, core_swap(groups)], axis=0)
+    total_lines = n_dp * group_lines
+    whole_head, image_facts = group_facts(
+        group_lines, slots, images, n_cls, classes, width, total_lines, heads, other_heads
+    )
+    groups = jnp.concatenate([groups, after(core_swap(groups), whole_head)], axis=0)
     pooled_all = groups.reshape(n_dp * group_lines, width)
 
     piece = group_lines * max(1, min(n_dp, 256 // group_lines))
-    total_lines = n_dp * group_lines
+    pieces = [slice(at, at + piece) for at in range(0, total_lines, piece)]
     parts = [
-        class_parts(
-            group_lines, n_cls, head_rows, slots, images, at, pooled_all[at : at + piece], heads, other_heads, class_weight, scale
-        )
-        for at in range(0, total_lines, piece)
+        class_parts(group_lines, n_cls, pooled_all[at], whole_head, image_facts[at], class_weight, scale)
+        for at in pieces
     ]
     denoms = jnp.concatenate([p[4] for p in parts], axis=1)
     sums = parts[0][3]
@@ -438,12 +489,9 @@
         total = total + plane_swap(packed(step), step)
     denominator = total[images:].reshape(1, -1)[:, :total_lines]
     share = embed // n_dp
-    for k, (exponent, cosine, unit, _, _, image_facts) in enumerate(parts):
-        at = k * piece
-        grad, loss, embed_part = class_grad_part(
-            share, images, total, denominator[:, at : at + piece], exponent, cosine, unit,
-            image_facts, class_weight, scale,
-        )
+    for k, (at, (exponent, cosine, unit, _, _)) in enumerate(zip(pieces, parts)):
+        aside = class_grad_aside(share, exponent, cosine, unit, image_facts[at], class_weight)
+        grad, loss, embed_part = class_grad_part(images, total, denominator[:, at], *aside, scale, unit)
         if k == 0:
             class_grad, sample_loss, embed_grad = grad, loss, embed_part
         else:

time: 60.6 us -> 59.5 us (0.982)
  waiting for transfers between devices: 18.6 us -> 17.4 us
    ppermute x9, waiting for transfers between devices: 6.17 us -> 5.36 us  [plane_swap(): return lax.ppermute(value, 'cls', [(i, i ^ step) for i in range(count)])]
    pallas_call x3 -> x5, Pallas kernels: 7.2 us -> 7.39 us  [in_vmem(): pl.pallas_call(kernel, out_shape=tuple(outs), in_specs=[pl.BlockSpec(memo...]
  transfers between devices with their start and end apart: 24 -> 24, of which waited for: 12 -> 12; matrix products, arithmetic and copies ran while one was open for 6% -> 6% of each run, Pallas kernels for 5% -> 7%
where the time goes in v5:
time: 59.5 us; the launch traced here: 59.3 us
  starting transfers between devices  28.2 us (47%)
  waiting for transfers between devices  17.4 us (29%)
  Pallas kernels  7.4 us (12%)
  other arithmetic  3.66 us (6%)
  between operations  1.63 us (3%)
  local copies, waits for them, and re-layouts  1.04 us (2%)
    ppermute x9, starting transfers between devices, z_swap(): lax.ppermute(value, 'dp', [(i, i ^ step * CORES) for i in range(count)])  15.8 us
    ppermute x9, waiting for transfers between devices, z_swap(): lax.ppermute(value, 'dp', [(i, i ^ step * CORES) for i in range(count)])  11.2 us
    ppermute x9, starting transfers between devices, plane_swap(): return lax.ppermute(value, 'cls', [(i, i ^ step) for i in range(count)])  10.7 us
    pallas_call x5, Pallas kernels, in_vmem(): pl.pallas_call(kernel, out_shape=tuple(outs), in_specs=[pl.BlockSpec(memo...  7.39 us
    ppermute x9, waiting for transfers between devices, plane_swap(): return lax.ppermute(value, 'cls', [(i, i ^ step) for i in range(count)])  5.36 us
    ppermute x1, starting transfers between devices, half_swap(): return lax.ppermute(value, ('dp', 'cls'), pairs)  1.49 us
  transfers between devices with their start and end apart: 24, of which 12 were waited for; matrix products, arithmetic and copies ran while one was open for 6% of the time, Pallas kernels for 7%

profile of v5, /device:TPU:0, one launch (start us, length us, event | category | flops | bytes accessed | tf_op | source)
XLA Modules:
  0.0 59.3 jit_solution(13955450592212569780)
XLA Ops:
  0.7 0.9 %constant_dynamic-slice_fusion.1 = bf16[32,1024]{1,0:T(8,128)(2,1)S(1)} fusion(bf16[128,1024]{1,0:T(8,128)(2,1)} %own_ref.1, s32[]{:T(128)S(6)} %select_n.36), kind=kLoop, calls=%fused_computation.37 | loop fusion | bytes 131076 | tf_op jit(solution)/shard_map/dynamic_slice | solution.py:424
  1.5 5.0 %collective-permute-start.4 = (bf16[32,1024]{1,0:T(8,128)(2,1)S(1)}, bf16[32,1024]{1,0:T(8,128)(2,1)S(1)}, u32[]{:S(2)}, u32[]{:S(2)}) collective-permute-start(bf16[32,1024]{1,0:T(8,128)(2,1)S(1)} %constant_dynamic-slice_fusion.1), channel_id=1, source_target_pairs={{0,24},{4,28},{8,16},{12,20},{16,8},{20,12},{24,0},{28,4},{1,25},{... | collective-permute-start | bytes 196616 | tf_op jit(solution)/shard_map/ppermute | solution.py:23
  9.2 3.1 %collective-permute-done.3 = bf16[32,1024]{1,0:T(8,128)(2,1)S(1)} collective-permute-done((bf16[32,1024]{1,0:T(8,128)(2,1)S(1)}, bf16[32,1024]{1,0:T(8,128)(2,1)S(1)}, u32[]{:S(2)}, u32[]{:S(2)}) %collective-permute-start.3) | collective-permute-done | bytes 65568 | tf_op jit(solution)/shard_map/ppermute | solution.py:23
  12.3 2.5 %collective-permute-start.7 = (bf16[2,32,1024]{2,1,0:T(8,128)(2,1)S(1)}, bf16[2,32,1024]{2,1,0:T(8,128)(2,1)S(1)}, u32[]{:S(2)}, u32[]{:S(2)}) collective-permute-start(bf16[2,32,1024]{2,1,0:T(8,128)(2,1)S(1)} %shard_map.121.refs_1_), channel_id=1, source_target_pairs={{0,3},{1,2},{2,1},{3,0},{4,7},{5,6},{6,5},{7,4},{8,11},{9,10},{10,... | collective-permute-start | bytes 393224 | tf_op jit(solution)/shard_map/ppermute | solution.py:39
  15.9 0.9 %collective-permute-done.near_ref = bf16[128,1024]{1,0:T(8,128)(2,1)S(1)} collective-permute-done((bf16[128,1024]{1,0:T(8,128)(2,1)}, bf16[128,1024]{1,0:T(8,128)(2,1)S(1)}, u32[]{:S(2)}, u32[]{:S(2)}) %collective-permute-start) | collective-permute-done | bytes 262176 | tf_op jit(solution)/shard_map/ppermute | solution.py:23
  17.0 2.7 %collective-permute-start.10 = (bf16[80,512]{1,0:T(8,128)(2,1)S(1)}, bf16[80,512]{1,0:T(8,128)(2,1)S(1)}, u32[]{:S(2)}, u32[]{:S(2)}) collective-permute-start(bf16[80,512]{1,0:T(8,128)(2,1)S(1)} %shard_map.122), channel_id=1, source_target_pairs={{0,24},{4,28},{8,16},{12,20},{16,8},{20,12},{24,0},{28,4},{1,25},{... | collective-permute-start | bytes 245768 | tf_op jit(solution)/shard_map/ppermute | solution.py:23
  19.7 1.3 %collective-permute-start.9 = (bf16[80,512]{1,0:T(8,128)(2,1)S(1)}, bf16[80,512]{1,0:T(8,128)(2,1)S(1)}, u32[]{:S(2)}, u32[]{:S(2)}) collective-permute-start(bf16[80,512]{1,0:T(8,128)(2,1)S(1)} %shard_map.122), channel_id=1, source_target_pairs={{0,16},{4,20},{8,24},{12,28},{16,0},{20,4},{24,8},{28,12},{1,17},{... | collective-permute-start | bytes 245768 | tf_op jit(solution)/shard_map/ppermute | solution.py:23
  21.1 1.7 %collective-permute-start.8 = (bf16[80,512]{1,0:T(8,128)(2,1)S(1)}, bf16[80,512]{1,0:T(8,128)(2,1)S(1)}, u32[]{:S(2)}, u32[]{:S(2)}) collective-permute-start(bf16[80,512]{1,0:T(8,128)(2,1)S(1)} %shard_map.122), channel_id=1, source_target_pairs={{0,8},{4,12},{8,0},{12,4},{16,24},{20,28},{24,16},{28,20},{1,9},{5... | collective-permute-start | bytes 245768 | tf_op jit(solution)/shard_map/ppermute | solution.py:23
  22.9 1.3 %collective-permute-done.10.refs_4_ = bf16[80,512]{1,0:T(8,128)(2,1)S(1)} collective-permute-done((bf16[80,512]{1,0:T(8,128)(2,1)S(1)}, bf16[80,512]{1,0:T(8,128)(2,1)S(1)}, u32[]{:S(2)}, u32[]{:S(2)}) %collective-permute-start.10) | collective-permute-done | bytes 81952 | tf_op jit(solution)/shard_map/ppermute | solution.py:23
  24.2 3.2 %collective-permute-done.9.refs_3_ = bf16[80,512]{1,0:T(8,128)(2,1)S(1)} collective-permute-done((bf16[80,512]{1,0:T(8,128)(2,1)S(1)}, bf16[80,512]{1,0:T(8,128)(2,1)S(1)}, u32[]{:S(2)}, u32[]{:S(2)}) %collective-permute-start.9) | collective-permute-done | bytes 81952 | tf_op jit(solution)/shard_map/ppermute | solution.py:23
  27.5 0.8 %pad_maximum_fusion.3 = bf16[4,80,512]{2,1,0:T(8,128)(2,1)} fusion(bf16[1,80,512]{2,1,0:T(8,128)(2,1)S(1)} %bitcast.51, bf16[1,80,512]{2,1,0:T(8,128)(2,1)S(1)} %bitcast.52, bf16[1,80,512]{2,1,0:T(8,128)(2,1)S(1)} %bitcast.53, bf16[1,80,512]{2,1,0:T(8,128)(2,1)S(1)} %bitcast.49), kind=kLoop, calls=%fused_computation.4 | loop fusion | flops 491520 | bytes 655360 | tf_op jit(solution)/shard_map/concatenate | solution.py:452
  28.3 1.5 %collective-permute-start.19 = (bf16[4,80,512]{2,1,0:T(8,128)(2,1)}, bf16[4,80,512]{2,1,0:T(8,128)(2,1)S(1)}, u32[]{:S(2)}, u32[]{:S(2)}) collective-permute-start(bf16[4,80,512]{2,1,0:T(8,128)(2,1)} %pad_maximum_fusion.3), channel_id=1, source_target_pairs={{0,1},{1,0},{2,3},{3,2},{4,6},{5,7},{6,4},{7,5},{8,9},{9,8},{10,11... | collective-permute-start | bytes 983048 | tf_op jit(solution)/shard_map/ppermute | solution.py:34
  29.8 2.9 %shard_map.124 = bf16[8,1024]{1,0:T(8,128)(2,1)S(1)} custom-call(bf16[864,1024]{1,0:T(8,128)(2,1)S(1)} %copy-done.3, bf16[864,1024]{1,0:T(8,128)(2,1)S(1)} %copy-done.4, bf16[128,1024]{1,0:T(8,128)(2,1)S(1)} %copy-done.2, bf16[128,1024]{1,0:T(8,128)(2,1)S(1)} %collective-permute-done.near_ref, ...), custom_call_target="tpu_custom_call" | custom-call | flops 1811939328 | bytes 5660672 | tf_op jit(solution)/shard_map/pallas_call | solution.py:106
  32.7 2.5 %collective-permute-start.14 = (bf16[8,1024]{1,0:T(8,128)(2,1)S(1)}, bf16[8,1024]{1,0:T(8,128)(2,1)S(1)}, u32[]{:S(2)}, u32[]{:S(2)}) collective-permute-start(bf16[8,1024]{1,0:T(8,128)(2,1)S(1)} %shard_map.124), channel_id=1, source_target_pairs={{0,24},{4,28},{8,16},{12,20},{16,8},{20,12},{24,0},{28,4},{1,25},{... | collective-permute-start | bytes 49160 | tf_op jit(solution)/shard_map/ppermute | solution.py:23
  35.2 2.0 %collective-permute-start.12 = (bf16[8,1024]{1,0:T(8,128)(2,1)S(1)}, bf16[8,1024]{1,0:T(8,128)(2,1)S(1)}, u32[]{:S(2)}, u32[]{:S(2)}) collective-permute-start(bf16[8,1024]{1,0:T(8,128)(2,1)S(1)} %shard_map.124), channel_id=1, source_target_pairs={{0,8},{4,12},{8,0},{12,4},{16,24},{20,28},{24,16},{28,20},{1,9},{5... | collective-permute-start | bytes 49160 | tf_op jit(solution)/shard_map/ppermute | solution.py:23
  37.2 1.1 %collective-permute-done.14 = bf16[8,1024]{1,0:T(8,128)(2,1)S(1)} collective-permute-done((bf16[8,1024]{1,0:T(8,128)(2,1)S(1)}, bf16[8,1024]{1,0:T(8,128)(2,1)S(1)}, u32[]{:S(2)}, u32[]{:S(2)}) %collective-permute-start.14) | collective-permute-done | bytes 16416 | tf_op jit(solution)/shard_map/ppermute | solution.py:23
  38.3 1.5 %collective-permute-done.13 = bf16[8,1024]{1,0:T(8,128)(2,1)S(1)} collective-permute-done((bf16[8,1024]{1,0:T(8,128)(2,1)S(1)}, bf16[8,1024]{1,0:T(8,128)(2,1)S(1)}, u32[]{:S(2)}, u32[]{:S(2)}) %collective-permute-start.13) | collective-permute-done | bytes 16416 | tf_op jit(solution)/shard_map/ppermute | solution.py:23
  39.9 1.6 %collective-permute-start.16 = (bf16[4,8,1024]{2,1,0:T(8,128)(2,1)S(1)}, bf16[4,8,1024]{2,1,0:T(8,128)(2,1)S(1)}, u32[]{:S(2)}, u32[]{:S(2)}) collective-permute-start(bf16[4,8,1024]{2,1,0:T(8,128)(2,1)S(1)} %pad_maximum_fusion.6), channel_id=1, source_target_pairs={{0,2},{1,3},{2,0},{3,1},{4,6},{5,7},{6,4},{7,5},{8,10},{9,11},{10,... | collective-permute-start | bytes 196616 | tf_op jit(solution)/shard_map/ppermute | solution.py:39
  41.5 1.1 %collective-permute-start.15 = (bf16[4,8,1024]{2,1,0:T(8,128)(2,1)S(1)}, bf16[4,8,1024]{2,1,0:T(8,128)(2,1)S(1)}, u32[]{:S(2)}, u32[]{:S(2)}) collective-permute-start(bf16[4,8,1024]{2,1,0:T(8,128)(2,1)S(1)} %pad_maximum_fusion.6), channel_id=1, source_target_pairs={{0,1},{1,0},{2,3},{3,2},{4,5},{5,4},{6,7},{7,6},{8,9},{9,8},{10,11... | collective-permute-start | bytes 196616 | tf_op jit(solution)/shard_map/ppermute | solution.py:39
  42.6 0.9 %collective-permute-start.17 = (bf16[4,8,1024]{2,1,0:T(8,128)(2,1)S(1)}, bf16[4,8,1024]{2,1,0:T(8,128)(2,1)S(1)}, u32[]{:S(2)}, u32[]{:S(2)}) collective-permute-start(bf16[4,8,1024]{2,1,0:T(8,128)(2,1)S(1)} %pad_maximum_fusion.6), channel_id=1, source_target_pairs={{0,3},{1,2},{2,1},{3,0},{4,7},{5,6},{6,5},{7,4},{8,11},{9,10},{10,... | collective-permute-start | bytes 196616 | tf_op jit(solution)/shard_map/ppermute | solution.py:39
  43.5 2.2 %collective-permute-done.15.refs_1_ = bf16[4,8,1024]{2,1,0:T(8,128)(2,1)S(1)} collective-permute-done((bf16[4,8,1024]{2,1,0:T(8,128)(2,1)S(1)}, bf16[4,8,1024]{2,1,0:T(8,128)(2,1)S(1)}, u32[]{:S(2)}, u32[]{:S(2)}) %collective-permute-start.15) | collective-permute-done | bytes 65568 | tf_op jit(solution)/shard_map/ppermute | solution.py:39
  45.7 1.0 %pad_maximum_fusion.head_ref = bf16[640,512]{1,0:T(8,128)(2,1)S(1)} fusion(bf16[320,512]{1,0:T(8,128)(2,1)S(1)} %bitcast.48, bf16[320,512]{1,0:T(8,128)(2,1)} %bitcast.25), kind=kLoop, calls=%fused_computation.1 | loop fusion | flops 1310720 | bytes 1310720 | tf_op jit(solution)/shard_map/concatenate | solution.py:464
  46.9 0.9 %collective-permute-done.17 = bf16[4,8,1024]{2,1,0:T(8,128)(2,1)S(1)} collective-permute-done((bf16[4,8,1024]{2,1,0:T(8,128)(2,1)S(1)}, bf16[4,8,1024]{2,1,0:T(8,128)(2,1)S(1)}, u32[]{:S(2)}, u32[]{:S(2)}) %collective-permute-start.17) | collective-permute-done | bytes 65568 | tf_op jit(solution)/shard_map/ppermute | solution.py:39
  48.2 0.8 %collective-permute-done.20.other_ref = bf16[640,512]{1,0:T(8,128)(2,1)S(1)} collective-permute-done((bf16[640,512]{1,0:T(8,128)(2,1)S(1)}, bf16[640,512]{1,0:T(8,128)(2,1)S(1)}, u32[]{:S(2)}, u32[]{:S(2)}) %collective-permute-start.20) | collective-permute-done | bytes 655392 | tf_op jit(solution)/shard_map/ppermute | solution.py:28
  49.6 2.0 %shard_map.128 = (f32[256,1024]{1,0:T(8,128)S(1)}, f32[256,1024]{1,0:T(8,128)S(1)}, f32[256,640]{1,0:T(8,128)S(1)}, f32[4,8,1280]{2,1,0:T(8,128)S(1)}, f32[1,256]{1,0:T(1,128)S(1)}) custom-call(bf16[256,1024]{1,0:T(8,128)(2,1)S(1)} %bitcast.50, bf16[1024,512]{1,0:T(8,128)(2,1)S(1)} %get-tuple-element.22.refs_1_.whole_ref, ...), custom_call_target="tpu_custom_call" | custom-call | flops 805306368 | bytes 5544960 | tf_op jit(solution)/shard_map/pallas_call | solution.py:106
  51.6 1.1 %collective-permute-start.21 = (f32[7,1280]{1,0:T(8,128)S(1)}, f32[7,1280]{1,0:T(8,128)S(1)}, u32[]{:S(2)}, u32[]{:S(2)}) collective-permute-start(f32[7,1280]{1,0:T(8,128)S(1)} %get-tuple-element.43), channel_id=1, source_target_pairs={{0,3},{1,2},{2,1},{3,0},{4,7},{5,6},{6,5},{7,4},{8,11},{9,10},{10,... | collective-permute-start | bytes 107528 | tf_op jit(solution)/shard_map/ppermute | solution.py:39
  52.7 1.5 %collective-permute-start.22 = (f32[7,1280]{1,0:T(8,128)S(1)}, f32[7,1280]{1,0:T(8,128)S(1)}, u32[]{:S(2)}, u32[]{:S(2)}) collective-permute-start(f32[7,1280]{1,0:T(8,128)S(1)} %get-tuple-element.44), channel_id=1, source_target_pairs={{0,2},{1,3},{2,0},{3,1},{4,6},{5,7},{6,4},{7,5},{8,10},{9,11},{10,... | collective-permute-start | bytes 107528 | tf_op jit(solution)/shard_map/ppermute | solution.py:39
  54.3 0.9 %collective-permute-start.23 = (f32[7,1280]{1,0:T(8,128)S(1)}, f32[7,1280]{1,0:T(8,128)S(1)}, u32[]{:S(2)}, u32[]{:S(2)}) collective-permute-start(f32[7,1280]{1,0:T(8,128)S(1)} %get-tuple-element.45), channel_id=1, source_target_pairs={{0,1},{1,0},{2,3},{3,2},{4,5},{5,4},{6,7},{7,6},{8,9},{9,8},{10,11... | collective-permute-start | bytes 107528 | tf_op jit(solution)/shard_map/ppermute | solution.py:39
  55.2 0.9 %shard_map.129 = (bf16[256,1024]{1,0:T(8,128)(2,1)S(1)}, bf16[256,1024]{1,0:T(8,128)(2,1)S(1)}, f32[256,1024]{1,0:T(8,128)S(1)}, f32[64,256]{1,0:T(8,128)S(1)}, ...) custom-call(f32[256,1024]{1,0:T(8,128)S(1)} %get-tuple-element.26.exp_ref, ...), custom_call_target="tpu_custom_call" | custom-call | flops 67108864 | bytes 6494208 | tf_op jit(solution)/shard_map/pallas_call | solution.py:106
  56.1 0.7 %collective-permute-done.21 = f32[7,1280]{1,0:T(8,128)S(1)} collective-permute-done((f32[7,1280]{1,0:T(8,128)S(1)}, f32[7,1280]{1,0:T(8,128)S(1)}, u32[]{:S(2)}, u32[]{:S(2)}) %collective-permute-start.21) | collective-permute-done | bytes 35872 | tf_op jit(solution)/shard_map/ppermute | solution.py:39
  57.0 1.2 %collective-permute-done.23 = f32[7,1280]{1,0:T(8,128)S(1)} collective-permute-done((f32[7,1280]{1,0:T(8,128)S(1)}, f32[7,1280]{1,0:T(8,128)S(1)}, u32[]{:S(2)}, u32[]{:S(2)}) %collective-permute-start.23) | collective-permute-done | bytes 35872 | tf_op jit(solution)/shard_map/ppermute | solution.py:39
  58.3 1.0 %shard_map.130 = (f32[64,1024]{1,0:T(8,128)}, f32[1,6]{1,0:T(1,128)}, f32[6,512]{1,0:T(8,128)}) custom-call(f32[7,1280]{1,0:T(8,128)S(1)} %fusion.6.total_ref, f32[1,256]{1,0:T(1,128)S(1)} %slice.22.denom_ref, bf16[256,1024]{1,0:T(8,128)(2,1)S(1)} %get-tuple-element.29.high_ref, bf16[256,1024]{1,0:T(8,128)(2,1)S(1)} %get-tuple-element.30.low_ref, ...), custom_call_target="tpu_custom_call" | custom-call | flops 100663296 | bytes 3661848 | tf_op jit(solution)/shard_map/pallas_call | solution.py:106
  (64 shorter events, 4.8 us)
Async XLA Ops:
  0.6 8.5 %copy-start = (bf16[128,512]{1,0:T(8,128)(2,1)S(1)}, bf16[128,512]{1,0:T(8,128)(2,1)}, u32[]{:S(2)}) copy-start(bf16[128,512]{1,0:T(8,128)(2,1)} %param.15) | copy-start | bytes 393220
  1.5 7.6 %collective-permute-start.4 = (bf16[32,1024]{1,0:T(8,128)(2,1)S(1)}, bf16[32,1024]{1,0:T(8,128)(2,1)S(1)}, u32[]{:S(2)}, u32[]{:S(2)}) collective-permute-start(bf16[32,1024]{1,0:T(8,128)(2,1)S(1)} %constant_dynamic-slice_fusion.1), channel_id=1, source_target_pairs={{0,24},{4,28},{8,16},{12,20},{16,8},{20,12},{24,0},{28,4},{1,25},{... | collective-permute-start | bytes 196616 | tf_op jit(solution)/shard_map/ppermute | solution.py:23
  6.6 5.7 %collective-permute-start.3 = (bf16[32,1024]{1,0:T(8,128)(2,1)S(1)}, bf16[32,1024]{1,0:T(8,128)(2,1)S(1)}, u32[]{:S(2)}, u32[]{:S(2)}) collective-permute-start(bf16[32,1024]{1,0:T(8,128)(2,1)S(1)} %constant_dynamic-slice_fusion.1), channel_id=1, source_target_pairs={{0,16},{4,20},{8,24},{12,28},{16,0},{20,4},{24,8},{28,12},{1,17},{... | collective-permute-start | bytes 196616 | tf_op jit(solution)/shard_map/ppermute | solution.py:23
  6.6 5.7 %collective-permute-start.1 = (bf16[128,1024]{1,0:T(8,128)(2,1)}, bf16[128,1024]{1,0:T(8,128)(2,1)S(1)}, u32[]{:S(2)}, u32[]{:S(2)}) collective-permute-start(bf16[128,1024]{1,0:T(8,128)(2,1)} %own_ref.1), channel_id=1, source_target_pairs={{0,4},{4,0},{8,12},{12,8},{16,20},{20,16},{24,28},{28,24},{1,5},{5... | collective-permute-start | bytes 786440 | tf_op jit(solution)/shard_map/ppermute | solution.py:28
  6.6 10.2 %collective-permute-start = (bf16[128,1024]{1,0:T(8,128)(2,1)}, bf16[128,1024]{1,0:T(8,128)(2,1)S(1)}, u32[]{:S(2)}, u32[]{:S(2)}) collective-permute-start(bf16[128,1024]{1,0:T(8,128)(2,1)} %own_ref.1), channel_id=1, source_target_pairs={{0,8},{4,12},{8,0},{12,4},{16,24},{20,28},{24,16},{28,20},{1,9},{5... | collective-permute-start | bytes 786440 | tf_op jit(solution)/shard_map/ppermute | solution.py:23
  12.3 17.5 %copy-start.4 = (bf16[864,1024]{1,0:T(8,128)(2,1)S(1)}, bf16[864,1024]{1,0:T(8,128)(2,1)}, u32[]{:S(2)}) copy-start(bf16[864,1024]{1,0:T(8,128)(2,1)} %stream_ref.1) | copy-start | bytes 5308420
  12.3 7.4 %collective-permute-start.7 = (bf16[2,32,1024]{2,1,0:T(8,128)(2,1)S(1)}, bf16[2,32,1024]{2,1,0:T(8,128)(2,1)S(1)}, u32[]{:S(2)}, u32[]{:S(2)}) collective-permute-start(bf16[2,32,1024]{2,1,0:T(8,128)(2,1)S(1)} %shard_map.121.refs_1_), channel_id=1, source_target_pairs={{0,3},{1,2},{2,1},{3,0},{4,7},{5,6},{6,5},{7,4},{8,11},{9,10},{10,... | collective-permute-start | bytes 393224 | tf_op jit(solution)/shard_map/ppermute | solution.py:39
  14.9 6.2 %collective-permute-start.6 = (bf16[2,32,1024]{2,1,0:T(8,128)(2,1)S(1)}, bf16[2,32,1024]{2,1,0:T(8,128)(2,1)S(1)}, u32[]{:S(2)}, u32[]{:S(2)}) collective-permute-start(bf16[2,32,1024]{2,1,0:T(8,128)(2,1)S(1)} %shard_map.121.refs_1_), channel_id=1, source_target_pairs={{0,2},{1,3},{2,0},{3,1},{4,6},{5,7},{6,4},{7,5},{8,10},{9,11},{10,... | collective-permute-start | bytes 393224 | tf_op jit(solution)/shard_map/ppermute | solution.py:39
  15.4 7.4 %collective-permute-start.5 = (bf16[2,32,1024]{2,1,0:T(8,128)(2,1)S(1)}, bf16[2,32,1024]{2,1,0:T(8,128)(2,1)S(1)}, u32[]{:S(2)}, u32[]{:S(2)}) collective-permute-start(bf16[2,32,1024]{2,1,0:T(8,128)(2,1)S(1)} %shard_map.121.refs_1_), channel_id=1, source_target_pairs={{0,1},{1,0},{2,3},{3,2},{4,5},{5,4},{6,7},{7,6},{8,9},{9,8},{10,11... | collective-permute-start | bytes 393224 | tf_op jit(solution)/shard_map/ppermute | solution.py:39
  16.8 10.6 %collective-permute-start.2 = (bf16[128,1024]{1,0:T(8,128)(2,1)S(1)}, bf16[128,1024]{1,0:T(8,128)(2,1)S(1)}, u32[]{:S(2)}, u32[]{:S(2)}) collective-permute-start(bf16[128,1024]{1,0:T(8,128)(2,1)S(1)} %collective-permute-done.near_ref), channel_id=1, source_target_pairs={{0,4},{4,0},{8,12},{12,8},{16,20},{20,16},{24,28},{28,24},{1,5},{5... | collective-permute-start | bytes 786440 | tf_op jit(solution)/shard_map/ppermute | solution.py:28
  16.9 12.9 %copy-start.2 = (bf16[128,1024]{1,0:T(8,128)(2,1)S(1)}, bf16[128,1024]{1,0:T(8,128)(2,1)}, u32[]{:S(2)}) copy-start(bf16[128,1024]{1,0:T(8,128)(2,1)} %own_ref.1) | copy-start | bytes 786436
  16.9 12.9 %copy-start.3 = (bf16[864,1024]{1,0:T(8,128)(2,1)S(1)}, bf16[864,1024]{1,0:T(8,128)(2,1)}, u32[]{:S(2)}) copy-start(bf16[864,1024]{1,0:T(8,128)(2,1)} %att_ref.1) | copy-start | bytes 5308420
  16.9 12.9 %copy-start.5 = (f32[1024]{0:T(1024)S(1)}, f32[1024]{0:T(1024)}, u32[]{:S(2)}) copy-start(f32[1024]{0:T(1024)} %param.13) | copy-start | bytes 12292
  17.0 12.9 %copy-start.6 = (f32[1024]{0:T(1024)S(1)}, f32[1024]{0:T(1024)}, u32[]{:S(2)}) copy-start(f32[1024]{0:T(1024)} %param.14) | copy-start | bytes 12292
  17.0 7.2 %collective-permute-start.10 = (bf16[80,512]{1,0:T(8,128)(2,1)S(1)}, bf16[80,512]{1,0:T(8,128)(2,1)S(1)}, u32[]{:S(2)}, u32[]{:S(2)}) collective-permute-start(bf16[80,512]{1,0:T(8,128)(2,1)S(1)} %shard_map.122), channel_id=1, source_target_pairs={{0,24},{4,28},{8,16},{12,20},{16,8},{20,12},{24,0},{28,4},{1,25},{... | collective-permute-start | bytes 245768 | tf_op jit(solution)/shard_map/ppermute | solution.py:23
  19.7 7.7 %collective-permute-start.9 = (bf16[80,512]{1,0:T(8,128)(2,1)S(1)}, bf16[80,512]{1,0:T(8,128)(2,1)S(1)}, u32[]{:S(2)}, u32[]{:S(2)}) collective-permute-start(bf16[80,512]{1,0:T(8,128)(2,1)S(1)} %shard_map.122), channel_id=1, source_target_pairs={{0,16},{4,20},{8,24},{12,28},{16,0},{20,4},{24,8},{28,12},{1,17},{... | collective-permute-start | bytes 245768 | tf_op jit(solution)/shard_map/ppermute | solution.py:23
  21.1 6.3 %collective-permute-start.8 = (bf16[80,512]{1,0:T(8,128)(2,1)S(1)}, bf16[80,512]{1,0:T(8,128)(2,1)S(1)}, u32[]{:S(2)}, u32[]{:S(2)}) collective-permute-start(bf16[80,512]{1,0:T(8,128)(2,1)S(1)} %shard_map.122), channel_id=1, source_target_pairs={{0,8},{4,12},{8,0},{12,4},{16,24},{20,28},{24,16},{28,20},{1,9},{5... | collective-permute-start | bytes 245768 | tf_op jit(solution)/shard_map/ppermute | solution.py:23
  27.4 2.4 %collective-permute-start.11 = (bf16[4,2,32,1024]{3,2,1,0:T(8,128)(2,1)S(1)}, bf16[4,2,32,1024]{3,2,1,0:T(8,128)(2,1)S(1)}, u32[]{:S(2)}, u32[]{:S(2)}) collective-permute-start(bf16[4,2,32,1024]{3,2,1,0:T(8,128)(2,1)S(1)} %shard_map.123.far_ref), channel_id=1, source_target_pairs={{0,4},{4,0},{8,12},{12,8},{16,20},{20,16},{24,28},{28,24},{1,5},{5... | collective-permute-start | bytes 1572872 | tf_op jit(solution)/shard_map/ppermute | solution.py:28
  28.3 15.2 %collective-permute-start.19 = (bf16[4,80,512]{2,1,0:T(8,128)(2,1)}, bf16[4,80,512]{2,1,0:T(8,128)(2,1)S(1)}, u32[]{:S(2)}, u32[]{:S(2)}) collective-permute-start(bf16[4,80,512]{2,1,0:T(8,128)(2,1)} %pad_maximum_fusion.3), channel_id=1, source_target_pairs={{0,1},{1,0},{2,3},{3,2},{4,6},{5,7},{6,4},{7,5},{8,9},{9,8},{10,11... | collective-permute-start | bytes 983048 | tf_op jit(solution)/shard_map/ppermute | solution.py:34
  32.7 15.1 %copy-start.1 = (bf16[1024,512]{1,0:T(8,128)(2,1)S(1)}, bf16[1024,512]{1,0:T(8,128)(2,1)}, u32[]{:S(2)}) copy-start(bf16[1024,512]{1,0:T(8,128)(2,1)} %weight_ref.3) | copy-start | bytes 3145732
  32.7 5.6 %collective-permute-start.14 = (bf16[8,1024]{1,0:T(8,128)(2,1)S(1)}, bf16[8,1024]{1,0:T(8,128)(2,1)S(1)}, u32[]{:S(2)}, u32[]{:S(2)}) collective-permute-start(bf16[8,1024]{1,0:T(8,128)(2,1)S(1)} %shard_map.124), channel_id=1, source_target_pairs={{0,24},{4,28},{8,16},{12,20},{16,8},{20,12},{24,0},{28,4},{1,25},{... | collective-permute-start | bytes 49160 | tf_op jit(solution)/shard_map/ppermute | solution.py:23
  35.2 4.6 %collective-permute-start.13 = (bf16[8,1024]{1,0:T(8,128)(2,1)S(1)}, bf16[8,1024]{1,0:T(8,128)(2,1)S(1)}, u32[]{:S(2)}, u32[]{:S(2)}) collective-permute-start(bf16[8,1024]{1,0:T(8,128)(2,1)S(1)} %shard_map.124), channel_id=1, source_target_pairs={{0,16},{4,20},{8,24},{12,28},{16,0},{20,4},{24,8},{28,12},{1,17},{... | collective-permute-start | bytes 49160 | tf_op jit(solution)/shard_map/ppermute | solution.py:23
  35.2 4.6 %collective-permute-start.12 = (bf16[8,1024]{1,0:T(8,128)(2,1)S(1)}, bf16[8,1024]{1,0:T(8,128)(2,1)S(1)}, u32[]{:S(2)}, u32[]{:S(2)}) collective-permute-start(bf16[8,1024]{1,0:T(8,128)(2,1)S(1)} %shard_map.124), channel_id=1, source_target_pairs={{0,8},{4,12},{8,0},{12,4},{16,24},{20,28},{24,16},{28,20},{1,9},{5... | collective-permute-start | bytes 49160 | tf_op jit(solution)/shard_map/ppermute | solution.py:23
  39.9 7.0 %collective-permute-start.16 = (bf16[4,8,1024]{2,1,0:T(8,128)(2,1)S(1)}, bf16[4,8,1024]{2,1,0:T(8,128)(2,1)S(1)}, u32[]{:S(2)}, u32[]{:S(2)}) collective-permute-start(bf16[4,8,1024]{2,1,0:T(8,128)(2,1)S(1)} %pad_maximum_fusion.6), channel_id=1, source_target_pairs={{0,2},{1,3},{2,0},{3,1},{4,6},{5,7},{6,4},{7,5},{8,10},{9,11},{10,... | collective-permute-start | bytes 196616 | tf_op jit(solution)/shard_map/ppermute | solution.py:39
  41.5 4.3 %collective-permute-start.15 = (bf16[4,8,1024]{2,1,0:T(8,128)(2,1)S(1)}, bf16[4,8,1024]{2,1,0:T(8,128)(2,1)S(1)}, u32[]{:S(2)}, u32[]{:S(2)}) collective-permute-start(bf16[4,8,1024]{2,1,0:T(8,128)(2,1)S(1)} %pad_maximum_fusion.6), channel_id=1, source_target_pairs={{0,1},{1,0},{2,3},{3,2},{4,5},{5,4},{6,7},{7,6},{8,9},{9,8},{10,11... | collective-permute-start | bytes 196616 | tf_op jit(solution)/shard_map/ppermute | solution.py:39
  42.6 5.2 %collective-permute-start.17 = (bf16[4,8,1024]{2,1,0:T(8,128)(2,1)S(1)}, bf16[4,8,1024]{2,1,0:T(8,128)(2,1)S(1)}, u32[]{:S(2)}, u32[]{:S(2)}) collective-permute-start(bf16[4,8,1024]{2,1,0:T(8,128)(2,1)S(1)} %pad_maximum_fusion.6), channel_id=1, source_target_pairs={{0,3},{1,2},{2,1},{3,0},{4,7},{5,6},{6,5},{7,4},{8,11},{9,10},{10,... | collective-permute-start | bytes 196616 | tf_op jit(solution)/shard_map/ppermute | solution.py:39
  46.8 2.2 %collective-permute-start.20 = (bf16[640,512]{1,0:T(8,128)(2,1)S(1)}, bf16[640,512]{1,0:T(8,128)(2,1)S(1)}, u32[]{:S(2)}, u32[]{:S(2)}) collective-permute-start(bf16[640,512]{1,0:T(8,128)(2,1)S(1)} %pad_maximum_fusion.head_ref), channel_id=1, source_target_pairs={{0,4},{4,0},{8,12},{12,8},{16,20},{20,16},{24,28},{28,24},{1,5},{5... | collective-permute-start | bytes 1966088 | tf_op jit(solution)/shard_map/ppermute | solution.py:28
  47.8 1.8 %collective-permute-start.18 = (bf16[4,4,8,1024]{3,2,1,0:T(8,128)(2,1)S(1)}, bf16[4,4,8,1024]{3,2,1,0:T(8,128)(2,1)S(1)}, u32[]{:S(2)}, u32[]{:S(2)}) collective-permute-start(bf16[4,4,8,1024]{3,2,1,0:T(8,128)(2,1)S(1)} %bitcast_dynamic-update-slice_fusion.3), channel_id=1, source_target_pairs={{0,4},{4,0},{8,12},{12,8},{16,20},{20,16},{24,28},{28,24},{1,5},{5... | collective-permute-start | bytes 786440 | tf_op jit(solution)/shard_map/ppermute | solution.py:28
  51.6 5.2 %collective-permute-start.21 = (f32[7,1280]{1,0:T(8,128)S(1)}, f32[7,1280]{1,0:T(8,128)S(1)}, u32[]{:S(2)}, u32[]{:S(2)}) collective-permute-start(f32[7,1280]{1,0:T(8,128)S(1)} %get-tuple-element.43), channel_id=1, source_target_pairs={{0,3},{1,2},{2,1},{3,0},{4,7},{5,6},{6,5},{7,4},{8,11},{9,10},{10,... | collective-permute-start | bytes 107528 | tf_op jit(solution)/shard_map/ppermute | solution.py:39
  52.7 4.3 %collective-permute-start.22 = (f32[7,1280]{1,0:T(8,128)S(1)}, f32[7,1280]{1,0:T(8,128)S(1)}, u32[]{:S(2)}, u32[]{:S(2)}) collective-permute-start(f32[7,1280]{1,0:T(8,128)S(1)} %get-tuple-element.44), channel_id=1, source_target_pairs={{0,2},{1,3},{2,0},{3,1},{4,6},{5,7},{6,4},{7,5},{8,10},{9,11},{10,... | collective-permute-start | bytes 107528 | tf_op jit(solution)/shard_map/ppermute | solution.py:39
  54.3 4.0 %collective-permute-start.23 = (f32[7,1280]{1,0:T(8,128)S(1)}, f32[7,1280]{1,0:T(8,128)S(1)}, u32[]{:S(2)}, u32[]{:S(2)}) collective-permute-start(f32[7,1280]{1,0:T(8,128)S(1)} %get-tuple-element.45), channel_id=1, source_target_pairs={{0,1},{1,0},{2,3},{3,2},{4,5},{5,4},{6,7},{7,6},{8,9},{9,8},{10,11... | collective-permute-start | bytes 107528 | tf_op jit(solution)/shard_map/ppermute | solution.py:39

commit v6 on v5

--- a/solution.py
+++ b/solution.py
@@ -441,20 +441,19 @@
         for step in range(n_cls):
             ordered = lax.dynamic_update_index_in_dim(ordered, far[step], cls ^ step, 0)
         far = ordered.transpose(1, 0, 2, 3).reshape(1, n_z - 2, rows, width)
-    far = after(far, near_other, *heads)
-    far_other = core_swap(far)
-    heads = jnp.stack(heads)
-    pooled = pool_tokens(
-        attended, stream, out_proj, near, own_other, near_other, far, far_other, norm_gain.reshape(1, width), norm_shift.reshape(1, width)
-    )
-
-    column = jnp.stack([pooled] + [z_swap(pooled, step) for step in range(1, n_z)])
-    heads = jnp.concatenate([head_half[None], heads], axis=0)
-    counterparts = half_swap(heads)
-
+    far = after(far, near_other, heads[0])
     scale = lax.rsqrt(
         jnp.sum(jnp.square(class_weight.astype(jnp.float32)), axis=1) + NORM_EPSILON
     )[None, :]
+    far_other = after(core_swap(far), scale)
+    pooled = pool_tokens(
+        attended, stream, out_proj, near, own_other, near_other, far, far_other, norm_gain.reshape(1, width), norm_shift.reshape(1, width)
+    )
+
+    column = jnp.stack([pooled] + [z_swap(pooled, step) for step in range(1, n_z)])
+    heads[0] = after(heads[0], pooled)
+    heads = jnp.stack([head_half] + heads)
+    counterparts = half_swap(heads)
 
     groups = jnp.zeros((n_z, n_cls, lines, width), pooled.dtype)
     from_plane = [plane_swap(column, step) for step in range(1, n_cls)]

time: 59.5 us -> 56.7 us (0.953)
  starting transfers between devices: 28.2 us -> 25.9 us
  other arithmetic: 3.66 us -> 1.96 us
  local copies, waits for them, and re-layouts: 1.04 us -> 2.51 us
    ppermute x9, waiting for transfers between devices: 11.2 us -> 5.35 us  [z_swap(): lax.ppermute(value, 'dp', [(i, i ^ step * CORES) for i in range(count)])]
    ppermute x9, waiting for transfers between devices: 5.36 us -> 10.8 us  [plane_swap(): return lax.ppermute(value, 'cls', [(i, i ^ step) for i in range(count)])]
    ppermute x9, starting transfers between devices: 15.8 us -> 13.6 us  [z_swap(): lax.ppermute(value, 'dp', [(i, i ^ step * CORES) for i in range(count)])]
    unnamed x14 -> x18, local copies, waits for them, and re-layouts: 0.05 us -> 1.52 us
    concatenate x1, other arithmetic: 1.02 us -> 0.04 us  [per_device(): jnp.concatenate([heads.reshape(-1, embed), counterparts.reshape(-1, embed...]
    concatenate x1 -> x0, other arithmetic: 0.77 us -> none  [per_device(): heads = jnp.concatenate([head_half[None], heads], axis=0)]
  transfers between devices with their start and end apart: 24 -> 24, of which waited for: 12 -> 15; matrix products, arithmetic and copies ran while one was open for 6% -> 3% of each run, Pallas kernels for 7% -> 8%
where the time goes in v6:
time: 56.7 us; the launch traced here: 56.6 us
  starting transfers between devices  25.9 us (46%)
  waiting for transfers between devices  17.1 us (30%)
  Pallas kernels  7.41 us (13%)
  local copies, waits for them, and re-layouts  2.51 us (4%)
  other arithmetic  1.96 us (3%)
  between operations  1.67 us (3%)
    ppermute x9, starting transfers between devices, z_swap(): lax.ppermute(value, 'dp', [(i, i ^ step * CORES) for i in range(count)])  13.6 us
    ppermute x9, waiting for transfers between devices, plane_swap(): return lax.ppermute(value, 'cls', [(i, i ^ step) for i in range(count)])  10.8 us
    ppermute x9, starting transfers between devices, plane_swap(): return lax.ppermute(value, 'cls', [(i, i ^ step) for i in range(count)])  10.7 us
    pallas_call x5, Pallas kernels, in_vmem(): pl.pallas_call(kernel, out_shape=tuple(outs), in_specs=[pl.BlockSpec(memo...  7.4 us
    ppermute x9, waiting for transfers between devices, z_swap(): lax.ppermute(value, 'dp', [(i, i ^ step * CORES) for i in range(count)])  5.35 us
    ppermute x1, starting transfers between devices, half_swap(): return lax.ppermute(value, ('dp', 'cls'), pairs)  1.56 us
    unnamed x18, local copies, waits for them, and re-layouts  1.52 us
  transfers between devices with their start and end apart: 24, of which 15 were waited for; matrix products, arithmetic and copies ran while one was open for 3% of the time, Pallas kernels for 8%

profile of v6, /device:TPU:0, one launch (start us, length us, event | category | flops | bytes accessed | tf_op | source)
XLA Modules:
  0.0 56.6 jit_solution(413254848220437288)
XLA Ops:
  0.7 0.9 %constant_dynamic-slice_fusion.1 = bf16[32,1024]{1,0:T(8,128)(2,1)S(1)} fusion(bf16[128,1024]{1,0:T(8,128)(2,1)} %own_ref.1, s32[]{:T(128)S(6)} %select_n.36), kind=kLoop, calls=%fused_computation.37 | loop fusion | bytes 131076 | tf_op jit(solution)/shard_map/dynamic_slice | solution.py:424
  1.5 5.0 %collective-permute-start.4 = (bf16[32,1024]{1,0:T(8,128)(2,1)S(1)}, bf16[32,1024]{1,0:T(8,128)(2,1)S(1)}, u32[]{:S(2)}, u32[]{:S(2)}) collective-permute-start(bf16[32,1024]{1,0:T(8,128)(2,1)S(1)} %constant_dynamic-slice_fusion.1), channel_id=1, source_target_pairs={{0,24},{4,28},{8,16},{12,20},{16,8},{20,12},{24,0},{28,4},{1,25},{... | collective-permute-start | bytes 196616 | tf_op jit(solution)/shard_map/ppermute | solution.py:23
  6.6 0.6 collective-permute-start
  7.2 0.7 %fusion.15 = (bf16[24]{0:T(256)(128)(2,1)S(1)}, bf16[24]{0:T(256)(128)(2,1)S(1)}) fusion(s32[24]{0:T(128)} %param.19), kind=kLoop, calls=%fused_computation.43 | loop fusion | flops 504 | bytes 192 | tf_op jit(solution)/shard_map/convert.2
  7.8 0.7 %convert_bitcast_fusion = bf16[3]{0:T(256)(128)(2,1)S(1)} fusion(s32[1,1,3]{2,1,0:T(1,128)} %param.17), kind=kLoop, calls=%fused_computation.42 | loop fusion | flops 3 | bytes 18 | tf_op jit(solution)/shard_map/squeeze | solution.py:419
  9.2 3.1 %collective-permute-done.3 = bf16[32,1024]{1,0:T(8,128)(2,1)S(1)} collective-permute-done((bf16[32,1024]{1,0:T(8,128)(2,1)S(1)}, bf16[32,1024]{1,0:T(8,128)(2,1)S(1)}, u32[]{:S(2)}, u32[]{:S(2)}) %collective-permute-start.3) | collective-permute-done | bytes 65568 | tf_op jit(solution)/shard_map/ppermute | solution.py:23
  12.3 2.5 %collective-permute-start.7 = (bf16[2,32,1024]{2,1,0:T(8,128)(2,1)S(1)}, bf16[2,32,1024]{2,1,0:T(8,128)(2,1)S(1)}, u32[]{:S(2)}, u32[]{:S(2)}) collective-permute-start(bf16[2,32,1024]{2,1,0:T(8,128)(2,1)S(1)} %shard_map.121.refs_1_), channel_id=1, source_target_pairs={{0,3},{1,2},{2,1},{3,0},{4,7},{5,6},{6,5},{7,4},{8,11},{9,10},{10,... | collective-permute-start | bytes 393224 | tf_op jit(solution)/shard_map/ppermute | solution.py:39
  15.9 0.9 %collective-permute-done.near_ref = bf16[128,1024]{1,0:T(8,128)(2,1)S(1)} collective-permute-done((bf16[128,1024]{1,0:T(8,128)(2,1)}, bf16[128,1024]{1,0:T(8,128)(2,1)S(1)}, u32[]{:S(2)}, u32[]{:S(2)}) %collective-permute-start) | collective-permute-done | bytes 262176 | tf_op jit(solution)/shard_map/ppermute | solution.py:23
  16.9 0.8 %collective-permute-start.8 = (bf16[80,512]{1,0:T(8,128)(2,1)S(1)}, bf16[80,512]{1,0:T(8,128)(2,1)S(1)}, u32[]{:S(2)}, u32[]{:S(2)}) collective-permute-start(bf16[80,512]{1,0:T(8,128)(2,1)S(1)} %shard_map.122), channel_id=1, source_target_pairs={{0,8},{4,12},{8,0},{12,4},{16,24},{20,28},{24,16},{28,20},{1,9},{5... | collective-permute-start | bytes 245768 | tf_op jit(solution)/shard_map/ppermute | solution.py:23
  17.7 1.1 %collective-permute-done.7 = bf16[2,32,1024]{2,1,0:T(8,128)(2,1)S(1)} collective-permute-done((bf16[2,32,1024]{2,1,0:T(8,128)(2,1)S(1)}, bf16[2,32,1024]{2,1,0:T(8,128)(2,1)S(1)}, u32[]{:S(2)}, u32[]{:S(2)}) %collective-permute-start.7) | collective-permute-done | bytes 131104 | tf_op jit(solution)/shard_map/ppermute | solution.py:39
  18.8 2.3 %collective-permute-done.6 = bf16[2,32,1024]{2,1,0:T(8,128)(2,1)S(1)} collective-permute-done((bf16[2,32,1024]{2,1,0:T(8,128)(2,1)S(1)}, bf16[2,32,1024]{2,1,0:T(8,128)(2,1)S(1)}, u32[]{:S(2)}, u32[]{:S(2)}) %collective-permute-start.6) | collective-permute-done | bytes 131104 | tf_op jit(solution)/shard_map/ppermute | solution.py:39
  22.2 2.7 %collective-permute-start.18 = (bf16[80,512]{1,0:T(8,128)(2,1)S(1)}, bf16[80,512]{1,0:T(8,128)(2,1)S(1)}, u32[]{:S(2)}, u32[]{:S(2)}) collective-permute-start(bf16[80,512]{1,0:T(8,128)(2,1)S(1)} %shard_map.122), channel_id=1, source_target_pairs={{0,24},{4,28},{8,16},{12,20},{16,8},{20,12},{24,0},{28,4},{1,25},{... | collective-permute-start | bytes 245768 | tf_op jit(solution)/shard_map/ppermute | solution.py:23
  25.0 1.5 %copy-done.4 = bf16[864,1024]{1,0:T(8,128)(2,1)S(1)} copy-done((bf16[864,1024]{1,0:T(8,128)(2,1)S(1)}, bf16[864,1024]{1,0:T(8,128)(2,1)}, u32[]{:S(2)}) %copy-start.4) | copy-done | bytes 1769496
  26.5 2.9 %shard_map.125.refs_1_ = bf16[8,1024]{1,0:T(8,128)(2,1)S(1)} custom-call(bf16[864,1024]{1,0:T(8,128)(2,1)S(1)} %copy-done.3, bf16[864,1024]{1,0:T(8,128)(2,1)S(1)} %copy-done.4, bf16[128,1024]{1,0:T(8,128)(2,1)S(1)} %copy-done.2, bf16[128,1024]{1,0:T(8,128)(2,1)S(1)} %copy-done.6, bf16[128,1024]{1,0:T(8,128)(2,1)S(1)} %collective-permute-done.1.refs_1_.own_other_ref, ...), custom_call_target="tpu_custom_call" | custom-call | flops 1811939328 | bytes 5660672 | tf_op jit(solution)/shard_map/pallas_call | solution.py:106
  29.4 2.0 %collective-permute-start.12 = (bf16[8,1024]{1,0:T(8,128)(2,1)S(1)}, bf16[8,1024]{1,0:T(8,128)(2,1)S(1)}, u32[]{:S(2)}, u32[]{:S(2)}) collective-permute-start(bf16[8,1024]{1,0:T(8,128)(2,1)S(1)} %shard_map.125.refs_1_), channel_id=1, source_target_pairs={{0,24},{4,28},{8,16},{12,20},{16,8},{20,12},{24,0},{28,4},{1,25},{... | collective-permute-start | bytes 49160 | tf_op jit(solution)/shard_map/ppermute | solution.py:23
  31.3 1.3 %collective-permute-start.11 = (bf16[8,1024]{1,0:T(8,128)(2,1)S(1)}, bf16[8,1024]{1,0:T(8,128)(2,1)S(1)}, u32[]{:S(2)}, u32[]{:S(2)}) collective-permute-start(bf16[8,1024]{1,0:T(8,128)(2,1)S(1)} %shard_map.125.refs_1_), channel_id=1, source_target_pairs={{0,16},{4,20},{8,24},{12,28},{16,0},{20,4},{24,8},{28,12},{1,17},{... | collective-permute-start | bytes 49160 | tf_op jit(solution)/shard_map/ppermute | solution.py:23
  32.6 1.2 %collective-permute-start.10 = (bf16[8,1024]{1,0:T(8,128)(2,1)S(1)}, bf16[8,1024]{1,0:T(8,128)(2,1)S(1)}, u32[]{:S(2)}, u32[]{:S(2)}) collective-permute-start(bf16[8,1024]{1,0:T(8,128)(2,1)S(1)} %shard_map.125.refs_1_), channel_id=1, source_target_pairs={{0,8},{4,12},{8,0},{12,4},{16,24},{20,28},{24,16},{28,20},{1,9},{5... | collective-permute-start | bytes 49160 | tf_op jit(solution)/shard_map/ppermute | solution.py:23
  33.9 1.6 %collective-permute-start.19 = (bf16[4,80,512]{2,1,0:T(8,128)(2,1)S(1)}, bf16[4,80,512]{2,1,0:T(8,128)(2,1)S(1)}, u32[]{:S(2)}, u32[]{:S(2)}) collective-permute-start(bf16[4,80,512]{2,1,0:T(8,128)(2,1)S(1)} %pad_maximum_fusion.3), channel_id=1, source_target_pairs={{0,1},{1,0},{2,3},{3,2},{4,6},{5,7},{6,4},{7,5},{8,9},{9,8},{10,11... | collective-permute-start | bytes 983048 | tf_op jit(solution)/shard_map/ppermute | solution.py:34
  35.4 0.5 collective-permute-done.11
  36.4 1.7 %collective-permute-start.14 = (bf16[4,8,1024]{2,1,0:T(8,128)(2,1)S(1)}, bf16[4,8,1024]{2,1,0:T(8,128)(2,1)S(1)}, u32[]{:S(2)}, u32[]{:S(2)}) collective-permute-start(bf16[4,8,1024]{2,1,0:T(8,128)(2,1)S(1)} %pad_maximum_fusion.6), channel_id=1, source_target_pairs={{0,2},{1,3},{2,0},{3,1},{4,6},{5,7},{6,4},{7,5},{8,10},{9,11},{10,... | collective-permute-start | bytes 196616 | tf_op jit(solution)/shard_map/ppermute | solution.py:39
  38.1 1.5 %collective-permute-start.13 = (bf16[4,8,1024]{2,1,0:T(8,128)(2,1)S(1)}, bf16[4,8,1024]{2,1,0:T(8,128)(2,1)S(1)}, u32[]{:S(2)}, u32[]{:S(2)}) collective-permute-start(bf16[4,8,1024]{2,1,0:T(8,128)(2,1)S(1)} %pad_maximum_fusion.6), channel_id=1, source_target_pairs={{0,1},{1,0},{2,3},{3,2},{4,5},{5,4},{6,7},{7,6},{8,9},{9,8},{10,11... | collective-permute-start | bytes 196616 | tf_op jit(solution)/shard_map/ppermute | solution.py:39
  40.0 3.2 %collective-permute-done.13.refs_1_ = bf16[4,8,1024]{2,1,0:T(8,128)(2,1)S(1)} collective-permute-done((bf16[4,8,1024]{2,1,0:T(8,128)(2,1)S(1)}, bf16[4,8,1024]{2,1,0:T(8,128)(2,1)S(1)}, u32[]{:S(2)}, u32[]{:S(2)}) %collective-permute-start.13) | collective-permute-done | bytes 65568 | tf_op jit(solution)/shard_map/ppermute | solution.py:39
  43.3 1.5 %collective-permute-done.15 = bf16[4,8,1024]{2,1,0:T(8,128)(2,1)S(1)} collective-permute-done((bf16[4,8,1024]{2,1,0:T(8,128)(2,1)S(1)}, bf16[4,8,1024]{2,1,0:T(8,128)(2,1)S(1)}, u32[]{:S(2)}, u32[]{:S(2)}) %collective-permute-start.15) | collective-permute-done | bytes 65568 | tf_op jit(solution)/shard_map/ppermute | solution.py:39
  45.4 0.6 %shard_map.128 = (bf16[1024,512]{1,0:T(8,128)(2,1)S(1)}, s32[256,2]{1,0:T(8,128)S(1)}) custom-call(bf16[640,512]{1,0:T(8,128)(2,1)S(1)} %pad_maximum_fusion.head_ref, bf16[640,512]{1,0:T(8,128)(2,1)S(1)} %collective-permute-done.20.other_ref), custom_call_target="tpu_custom_call" | custom-call | bytes 2361344 | tf_op jit(solution)/shard_map/pallas_call | solution.py:106
  46.5 2.0 %shard_map.130 = (f32[256,1024]{1,0:T(8,128)S(1)}, f32[256,1024]{1,0:T(8,128)S(1)}, f32[256,640]{1,0:T(8,128)S(1)}, f32[4,8,1280]{2,1,0:T(8,128)S(1)}, f32[1,256]{1,0:T(1,128)S(1)}) custom-call(bf16[256,1024]{1,0:T(8,128)(2,1)S(1)} %bitcast.51, bf16[1024,512]{1,0:T(8,128)(2,1)S(1)} %get-tuple-element.22.refs_1_.whole_ref, ...), custom_call_target="tpu_custom_call" | custom-call | flops 805306368 | bytes 5544960 | tf_op jit(solution)/shard_map/pallas_call | solution.py:106
  48.5 2.1 %collective-permute-start.21 = (f32[7,1280]{1,0:T(8,128)S(1)}, f32[7,1280]{1,0:T(8,128)S(1)}, u32[]{:S(2)}, u32[]{:S(2)}) collective-permute-start(f32[7,1280]{1,0:T(8,128)S(1)} %get-tuple-element.43), channel_id=1, source_target_pairs={{0,3},{1,2},{2,1},{3,0},{4,7},{5,6},{6,5},{7,4},{8,11},{9,10},{10,... | collective-permute-start | bytes 107528 | tf_op jit(solution)/shard_map/ppermute | solution.py:39
  50.6 0.9 %collective-permute-start.22 = (f32[7,1280]{1,0:T(8,128)S(1)}, f32[7,1280]{1,0:T(8,128)S(1)}, u32[]{:S(2)}, u32[]{:S(2)}) collective-permute-start(f32[7,1280]{1,0:T(8,128)S(1)} %get-tuple-element.44), channel_id=1, source_target_pairs={{0,2},{1,3},{2,0},{3,1},{4,6},{5,7},{6,4},{7,5},{8,10},{9,11},{10,... | collective-permute-start | bytes 107528 | tf_op jit(solution)/shard_map/ppermute | solution.py:39
  52.0 0.9 %shard_map.131 = (bf16[256,1024]{1,0:T(8,128)(2,1)S(1)}, bf16[256,1024]{1,0:T(8,128)(2,1)S(1)}, f32[256,1024]{1,0:T(8,128)S(1)}, f32[64,256]{1,0:T(8,128)S(1)}, ...) custom-call(f32[256,1024]{1,0:T(8,128)S(1)} %get-tuple-element.26.exp_ref, ...), custom_call_target="tpu_custom_call" | custom-call | flops 67108864 | bytes 6494208 | tf_op jit(solution)/shard_map/pallas_call | solution.py:106
  52.9 0.6 collective-permute-done.21
  53.5 1.1 %collective-permute-done.22 = f32[7,1280]{1,0:T(8,128)S(1)} collective-permute-done((f32[7,1280]{1,0:T(8,128)S(1)}, f32[7,1280]{1,0:T(8,128)S(1)}, u32[]{:S(2)}, u32[]{:S(2)}) %collective-permute-start.22) | collective-permute-done | bytes 35872 | tf_op jit(solution)/shard_map/ppermute | solution.py:39
  54.6 0.9 %collective-permute-done.23 = f32[7,1280]{1,0:T(8,128)S(1)} collective-permute-done((f32[7,1280]{1,0:T(8,128)S(1)}, f32[7,1280]{1,0:T(8,128)S(1)}, u32[]{:S(2)}, u32[]{:S(2)}) %collective-permute-start.23) | collective-permute-done | bytes 35872 | tf_op jit(solution)/shard_map/ppermute | solution.py:39
  55.5 1.0 %shard_map.132 = (f32[64,1024]{1,0:T(8,128)}, f32[1,6]{1,0:T(1,128)}, f32[6,512]{1,0:T(8,128)}) custom-call(f32[7,1280]{1,0:T(8,128)S(1)} %fusion.6.total_ref, f32[1,256]{1,0:T(1,128)S(1)} %slice.22.denom_ref, bf16[256,1024]{1,0:T(8,128)(2,1)S(1)} %get-tuple-element.29.high_ref, bf16[256,1024]{1,0:T(8,128)(2,1)S(1)} %get-tuple-element.30.low_ref, ...), custom_call_target="tpu_custom_call" | custom-call | flops 100663296 | bytes 3661848 | tf_op jit(solution)/shard_map/pallas_call | solution.py:106
  (70 shorter events, 4.9 us)
Async XLA Ops:
  0.6 8.5 %copy-start = (bf16[128,512]{1,0:T(8,128)(2,1)S(1)}, bf16[128,512]{1,0:T(8,128)(2,1)}, u32[]{:S(2)}) copy-start(bf16[128,512]{1,0:T(8,128)(2,1)} %param.15) | copy-start | bytes 393220
  1.5 7.6 %collective-permute-start.4 = (bf16[32,1024]{1,0:T(8,128)(2,1)S(1)}, bf16[32,1024]{1,0:T(8,128)(2,1)S(1)}, u32[]{:S(2)}, u32[]{:S(2)}) collective-permute-start(bf16[32,1024]{1,0:T(8,128)(2,1)S(1)} %constant_dynamic-slice_fusion.1), channel_id=1, source_target_pairs={{0,24},{4,28},{8,16},{12,20},{16,8},{20,12},{24,0},{28,4},{1,25},{... | collective-permute-start | bytes 196616 | tf_op jit(solution)/shard_map/ppermute | solution.py:23
  6.6 5.7 %collective-permute-start.3 = (bf16[32,1024]{1,0:T(8,128)(2,1)S(1)}, bf16[32,1024]{1,0:T(8,128)(2,1)S(1)}, u32[]{:S(2)}, u32[]{:S(2)}) collective-permute-start(bf16[32,1024]{1,0:T(8,128)(2,1)S(1)} %constant_dynamic-slice_fusion.1), channel_id=1, source_target_pairs={{0,16},{4,20},{8,24},{12,28},{16,0},{20,4},{24,8},{28,12},{1,17},{... | collective-permute-start | bytes 196616 | tf_op jit(solution)/shard_map/ppermute | solution.py:23
  6.6 5.7 %collective-permute-start.1 = (bf16[128,1024]{1,0:T(8,128)(2,1)}, bf16[128,1024]{1,0:T(8,128)(2,1)S(1)}, u32[]{:S(2)}, u32[]{:S(2)}) collective-permute-start(bf16[128,1024]{1,0:T(8,128)(2,1)} %own_ref.1), channel_id=1, source_target_pairs={{0,4},{4,0},{8,12},{12,8},{16,20},{20,16},{24,28},{28,24},{1,5},{5... | collective-permute-start | bytes 786440 | tf_op jit(solution)/shard_map/ppermute | solution.py:28
  6.6 10.2 %collective-permute-start = (bf16[128,1024]{1,0:T(8,128)(2,1)}, bf16[128,1024]{1,0:T(8,128)(2,1)S(1)}, u32[]{:S(2)}, u32[]{:S(2)}) collective-permute-start(bf16[128,1024]{1,0:T(8,128)(2,1)} %own_ref.1), channel_id=1, source_target_pairs={{0,8},{4,12},{8,0},{12,4},{16,24},{20,28},{24,16},{28,20},{1,9},{5... | collective-permute-start | bytes 786440 | tf_op jit(solution)/shard_map/ppermute | solution.py:23
  12.3 9.6 %copy-start.1 = (bf16[1024,512]{1,0:T(8,128)(2,1)S(1)}, bf16[1024,512]{1,0:T(8,128)(2,1)}, u32[]{:S(2)}) copy-start(bf16[1024,512]{1,0:T(8,128)(2,1)} %weight_ref.3) | copy-start | bytes 3145732
  12.3 6.4 %collective-permute-start.7 = (bf16[2,32,1024]{2,1,0:T(8,128)(2,1)S(1)}, bf16[2,32,1024]{2,1,0:T(8,128)(2,1)S(1)}, u32[]{:S(2)}, u32[]{:S(2)}) collective-permute-start(bf16[2,32,1024]{2,1,0:T(8,128)(2,1)S(1)} %shard_map.121.refs_1_), channel_id=1, source_target_pairs={{0,3},{1,2},{2,1},{3,0},{4,7},{5,6},{6,5},{7,4},{8,11},{9,10},{10,... | collective-permute-start | bytes 393224 | tf_op jit(solution)/shard_map/ppermute | solution.py:39
  14.9 6.2 %collective-permute-start.6 = (bf16[2,32,1024]{2,1,0:T(8,128)(2,1)S(1)}, bf16[2,32,1024]{2,1,0:T(8,128)(2,1)S(1)}, u32[]{:S(2)}, u32[]{:S(2)}) collective-permute-start(bf16[2,32,1024]{2,1,0:T(8,128)(2,1)S(1)} %shard_map.121.refs_1_), channel_id=1, source_target_pairs={{0,2},{1,3},{2,0},{3,1},{4,6},{5,7},{6,4},{7,5},{8,10},{9,11},{10,... | collective-permute-start | bytes 393224 | tf_op jit(solution)/shard_map/ppermute | solution.py:39
  15.4 6.0 %collective-permute-start.5 = (bf16[2,32,1024]{2,1,0:T(8,128)(2,1)S(1)}, bf16[2,32,1024]{2,1,0:T(8,128)(2,1)S(1)}, u32[]{:S(2)}, u32[]{:S(2)}) collective-permute-start(bf16[2,32,1024]{2,1,0:T(8,128)(2,1)S(1)} %shard_map.121.refs_1_), channel_id=1, source_target_pairs={{0,1},{1,0},{2,3},{3,2},{4,5},{5,4},{6,7},{7,6},{8,9},{9,8},{10,11... | collective-permute-start | bytes 393224 | tf_op jit(solution)/shard_map/ppermute | solution.py:39
  16.8 5.1 %copy-start.5 = (bf16[128,1024]{1,0:T(8,128)(2,1)}, bf16[128,1024]{1,0:T(8,128)(2,1)S(1)}, u32[]{:S(2)}) copy-start(bf16[128,1024]{1,0:T(8,128)(2,1)S(1)} %collective-permute-done.near_ref) | copy-start | bytes 786436
  16.8 5.1 %collective-permute-start.2 = (bf16[128,1024]{1,0:T(8,128)(2,1)S(1)}, bf16[128,1024]{1,0:T(8,128)(2,1)S(1)}, u32[]{:S(2)}, u32[]{:S(2)}) collective-permute-start(bf16[128,1024]{1,0:T(8,128)(2,1)S(1)} %collective-permute-done.near_ref), channel_id=1, source_target_pairs={{0,4},{4,0},{8,12},{12,8},{16,20},{20,16},{24,28},{28,24},{1,5},{5... | collective-permute-start | bytes 786440 | tf_op jit(solution)/shard_map/ppermute | solution.py:28
  16.9 4.9 %collective-permute-start.8 = (bf16[80,512]{1,0:T(8,128)(2,1)S(1)}, bf16[80,512]{1,0:T(8,128)(2,1)S(1)}, u32[]{:S(2)}, u32[]{:S(2)}) collective-permute-start(bf16[80,512]{1,0:T(8,128)(2,1)S(1)} %shard_map.122), channel_id=1, source_target_pairs={{0,8},{4,12},{8,0},{12,4},{16,24},{20,28},{24,16},{28,20},{1,9},{5... | collective-permute-start | bytes 245768 | tf_op jit(solution)/shard_map/ppermute | solution.py:23
  21.4 3.6 %copy-start.2 = (bf16[128,1024]{1,0:T(8,128)(2,1)S(1)}, bf16[128,1024]{1,0:T(8,128)(2,1)}, u32[]{:S(2)}) copy-start(bf16[128,1024]{1,0:T(8,128)(2,1)} %own_ref.1) | copy-start | bytes 786436
  21.4 3.5 %copy-start.7 = (f32[1024]{0:T(1024)S(1)}, f32[1024]{0:T(1024)}, u32[]{:S(2)}) copy-start(f32[1024]{0:T(1024)} %param.13) | copy-start | bytes 12292
  21.4 3.5 %copy-start.8 = (f32[1024]{0:T(1024)S(1)}, f32[1024]{0:T(1024)}, u32[]{:S(2)}) copy-start(f32[1024]{0:T(1024)} %param.14) | copy-start | bytes 12292
  21.9 3.1 %collective-permute-start.9 = (bf16[4,2,32,1024]{3,2,1,0:T(8,128)(2,1)S(1)}, bf16[4,2,32,1024]{3,2,1,0:T(8,128)(2,1)S(1)}, u32[]{:S(2)}, u32[]{:S(2)}) collective-permute-start(bf16[4,2,32,1024]{3,2,1,0:T(8,128)(2,1)S(1)} %shard_map.123.far_ref), channel_id=1, source_target_pairs={{0,4},{4,0},{8,12},{12,8},{16,20},{20,16},{24,28},{28,24},{1,5},{5... | collective-permute-start | bytes 1572872 | tf_op jit(solution)/shard_map/ppermute | solution.py:28
  21.9 3.1 %copy-start.3 = (bf16[864,1024]{1,0:T(8,128)(2,1)S(1)}, bf16[864,1024]{1,0:T(8,128)(2,1)}, u32[]{:S(2)}) copy-start(bf16[864,1024]{1,0:T(8,128)(2,1)} %att_ref.1) | copy-start | bytes 5308420
  21.9 3.1 %copy-start.6 = (bf16[128,1024]{1,0:T(8,128)(2,1)S(1)}, bf16[128,1024]{1,0:T(8,128)(2,1)}, u32[]{:S(2)}) copy-start(bf16[128,1024]{1,0:T(8,128)(2,1)} %copy-done.5) | copy-start | bytes 786436
  22.2 11.6 %collective-permute-start.18 = (bf16[80,512]{1,0:T(8,128)(2,1)S(1)}, bf16[80,512]{1,0:T(8,128)(2,1)S(1)}, u32[]{:S(2)}, u32[]{:S(2)}) collective-permute-start(bf16[80,512]{1,0:T(8,128)(2,1)S(1)} %shard_map.122), channel_id=1, source_target_pairs={{0,24},{4,28},{8,16},{12,20},{16,8},{20,12},{24,0},{28,4},{1,25},{... | collective-permute-start | bytes 245768 | tf_op jit(solution)/shard_map/ppermute | solution.py:23
  24.9 8.9 %collective-permute-start.17 = (bf16[80,512]{1,0:T(8,128)(2,1)S(1)}, bf16[80,512]{1,0:T(8,128)(2,1)S(1)}, u32[]{:S(2)}, u32[]{:S(2)}) collective-permute-start(bf16[80,512]{1,0:T(8,128)(2,1)S(1)} %shard_map.122), channel_id=1, source_target_pairs={{0,16},{4,20},{8,24},{12,28},{16,0},{20,4},{24,8},{28,12},{1,17},{... | collective-permute-start | bytes 245768 | tf_op jit(solution)/shard_map/ppermute | solution.py:23
  29.4 6.1 %collective-permute-start.12 = (bf16[8,1024]{1,0:T(8,128)(2,1)S(1)}, bf16[8,1024]{1,0:T(8,128)(2,1)S(1)}, u32[]{:S(2)}, u32[]{:S(2)}) collective-permute-start(bf16[8,1024]{1,0:T(8,128)(2,1)S(1)} %shard_map.125.refs_1_), channel_id=1, source_target_pairs={{0,24},{4,28},{8,16},{12,20},{16,8},{20,12},{24,0},{28,4},{1,25},{... | collective-permute-start | bytes 49160 | tf_op jit(solution)/shard_map/ppermute | solution.py:23
  31.3 4.6 %collective-permute-start.11 = (bf16[8,1024]{1,0:T(8,128)(2,1)S(1)}, bf16[8,1024]{1,0:T(8,128)(2,1)S(1)}, u32[]{:S(2)}, u32[]{:S(2)}) collective-permute-start(bf16[8,1024]{1,0:T(8,128)(2,1)S(1)} %shard_map.125.refs_1_), channel_id=1, source_target_pairs={{0,16},{4,20},{8,24},{12,28},{16,0},{20,4},{24,8},{28,12},{1,17},{... | collective-permute-start | bytes 49160 | tf_op jit(solution)/shard_map/ppermute | solution.py:23
  32.6 3.7 %collective-permute-start.10 = (bf16[8,1024]{1,0:T(8,128)(2,1)S(1)}, bf16[8,1024]{1,0:T(8,128)(2,1)S(1)}, u32[]{:S(2)}, u32[]{:S(2)}) collective-permute-start(bf16[8,1024]{1,0:T(8,128)(2,1)S(1)} %shard_map.125.refs_1_), channel_id=1, source_target_pairs={{0,8},{4,12},{8,0},{12,4},{16,24},{20,28},{24,16},{28,20},{1,9},{5... | collective-permute-start | bytes 49160 | tf_op jit(solution)/shard_map/ppermute | solution.py:23
  33.9 9.3 %collective-permute-start.19 = (bf16[4,80,512]{2,1,0:T(8,128)(2,1)S(1)}, bf16[4,80,512]{2,1,0:T(8,128)(2,1)S(1)}, u32[]{:S(2)}, u32[]{:S(2)}) collective-permute-start(bf16[4,80,512]{2,1,0:T(8,128)(2,1)S(1)} %pad_maximum_fusion.3), channel_id=1, source_target_pairs={{0,1},{1,0},{2,3},{3,2},{4,6},{5,7},{6,4},{7,5},{8,9},{9,8},{10,11... | collective-permute-start | bytes 983048 | tf_op jit(solution)/shard_map/ppermute | solution.py:34
  36.4 6.9 %collective-permute-start.14 = (bf16[4,8,1024]{2,1,0:T(8,128)(2,1)S(1)}, bf16[4,8,1024]{2,1,0:T(8,128)(2,1)S(1)}, u32[]{:S(2)}, u32[]{:S(2)}) collective-permute-start(bf16[4,8,1024]{2,1,0:T(8,128)(2,1)S(1)} %pad_maximum_fusion.6), channel_id=1, source_target_pairs={{0,2},{1,3},{2,0},{3,1},{4,6},{5,7},{6,4},{7,5},{8,10},{9,11},{10,... | collective-permute-start | bytes 196616 | tf_op jit(solution)/shard_map/ppermute | solution.py:39
  38.1 5.1 %collective-permute-start.13 = (bf16[4,8,1024]{2,1,0:T(8,128)(2,1)S(1)}, bf16[4,8,1024]{2,1,0:T(8,128)(2,1)S(1)}, u32[]{:S(2)}, u32[]{:S(2)}) collective-permute-start(bf16[4,8,1024]{2,1,0:T(8,128)(2,1)S(1)} %pad_maximum_fusion.6), channel_id=1, source_target_pairs={{0,1},{1,0},{2,3},{3,2},{4,5},{5,4},{6,7},{7,6},{8,9},{9,8},{10,11... | collective-permute-start | bytes 196616 | tf_op jit(solution)/shard_map/ppermute | solution.py:39
  39.6 5.2 %collective-permute-start.15 = (bf16[4,8,1024]{2,1,0:T(8,128)(2,1)S(1)}, bf16[4,8,1024]{2,1,0:T(8,128)(2,1)S(1)}, u32[]{:S(2)}, u32[]{:S(2)}) collective-permute-start(bf16[4,8,1024]{2,1,0:T(8,128)(2,1)S(1)} %pad_maximum_fusion.6), channel_id=1, source_target_pairs={{0,3},{1,2},{2,1},{3,0},{4,7},{5,6},{6,5},{7,4},{8,11},{9,10},{10,... | collective-permute-start | bytes 196616 | tf_op jit(solution)/shard_map/ppermute | solution.py:39
  43.2 2.2 %collective-permute-start.20 = (bf16[640,512]{1,0:T(8,128)(2,1)S(1)}, bf16[640,512]{1,0:T(8,128)(2,1)S(1)}, u32[]{:S(2)}, u32[]{:S(2)}) collective-permute-start(bf16[640,512]{1,0:T(8,128)(2,1)S(1)} %pad_maximum_fusion.head_ref), channel_id=1, source_target_pairs={{0,4},{4,0},{8,12},{12,8},{16,20},{20,16},{24,28},{28,24},{1,5},{5... | collective-permute-start | bytes 1966088 | tf_op jit(solution)/shard_map/ppermute | solution.py:28
  44.8 1.6 %collective-permute-start.16 = (bf16[4,4,8,1024]{3,2,1,0:T(8,128)(2,1)S(1)}, bf16[4,4,8,1024]{3,2,1,0:T(8,128)(2,1)S(1)}, u32[]{:S(2)}, u32[]{:S(2)}) collective-permute-start(bf16[4,4,8,1024]{3,2,1,0:T(8,128)(2,1)S(1)} %bitcast_dynamic-update-slice_fusion.3), channel_id=1, source_target_pairs={{0,4},{4,0},{8,12},{12,8},{16,20},{20,16},{24,28},{28,24},{1,5},{5... | collective-permute-start | bytes 786440 | tf_op jit(solution)/shard_map/ppermute | solution.py:28
  48.5 5.0 %collective-permute-start.21 = (f32[7,1280]{1,0:T(8,128)S(1)}, f32[7,1280]{1,0:T(8,128)S(1)}, u32[]{:S(2)}, u32[]{:S(2)}) collective-permute-start(f32[7,1280]{1,0:T(8,128)S(1)} %get-tuple-element.43), channel_id=1, source_target_pairs={{0,3},{1,2},{2,1},{3,0},{4,7},{5,6},{6,5},{7,4},{8,11},{9,10},{10,... | collective-permute-start | bytes 107528 | tf_op jit(solution)/shard_map/ppermute | solution.py:39
  50.6 4.0 %collective-permute-start.22 = (f32[7,1280]{1,0:T(8,128)S(1)}, f32[7,1280]{1,0:T(8,128)S(1)}, u32[]{:S(2)}, u32[]{:S(2)}) collective-permute-start(f32[7,1280]{1,0:T(8,128)S(1)} %get-tuple-element.44), channel_id=1, source_target_pairs={{0,2},{1,3},{2,0},{3,1},{4,6},{5,7},{6,4},{7,5},{8,10},{9,11},{10,... | collective-permute-start | bytes 107528 | tf_op jit(solution)/shard_map/ppermute | solution.py:39
  51.5 4.0 %collective-permute-start.23 = (f32[7,1280]{1,0:T(8,128)S(1)}, f32[7,1280]{1,0:T(8,128)S(1)}, u32[]{:S(2)}, u32[]{:S(2)}) collective-permute-start(f32[7,1280]{1,0:T(8,128)S(1)} %get-tuple-element.45), channel_id=1, source_target_pairs={{0,1},{1,0},{2,3},{3,2},{4,5},{5,4},{6,7},{7,6},{8,9},{9,8},{10,11... | collective-permute-start | bytes 107528 | tf_op jit(solution)/shard_map/ppermute | solution.py:39
  (1 other events, 1.5 us)

commit v7 on v6

--- a/solution.py
+++ b/solution.py
@@ -189,7 +189,8 @@
         for k in range(n_z):
             for part, which in ((0, mine), (1, 1 - mine)):
                 at = pl.multiple_of(((z ^ k) * CORES + side) * head_rows + which * half, half)
-                whole_ref[pl.ds(at, half), :] = source[pl.ds((part * n_z + k) * block, half), :]
+                start = n_z * block + k * half if part else k * block
+                whole_ref[pl.ds(at, half), :] = source[pl.ds(start, half), :]
     for which, source in enumerate((head_ref, other_ref)):
         for k in range(n_z):
             at = (which * n_z + k) * own
@@ -451,16 +452,17 @@
     )
 
     column = jnp.stack([pooled] + [z_swap(pooled, step) for step in range(1, n_z)])
-    heads[0] = after(heads[0], pooled)
+    heads = [after(rows_of, pooled) for rows_of in heads]
+    counterparts = half_swap(jnp.stack([rows_of[:half] for rows_of in heads]))
     heads = jnp.stack([head_half] + heads)
-    counterparts = half_swap(heads)
 
     groups = jnp.zeros((n_z, n_cls, lines, width), pooled.dtype)
     from_plane = [plane_swap(column, step) for step in range(1, n_cls)]
     for step, got in enumerate([column] + from_plane):
         groups = lax.dynamic_update_slice_in_dim(groups, got[:, None], cls ^ step, 1)
     counterparts = after(counterparts, from_plane[0])
-    heads = jnp.concatenate([heads.reshape(-1, embed), counterparts.reshape(-1, embed)], axis=0)
+    own_counterpart = lax.dynamic_slice_in_dim(head_proj, (1 - ((cls >> core) & 1)) * half, half, 0)
+    heads = jnp.concatenate([heads.reshape(-1, embed), own_counterpart, counterparts.reshape(-1, embed)], axis=0)
     other_heads = core_swap(heads)
     total_lines = n_dp * group_lines
     whole_head, image_facts = group_facts(

time: 56.7 us -> 56.2 us (level)
  waiting for transfers between devices: 17.1 us -> 15.6 us
  local copies, waits for them, and re-layouts: 2.51 us -> 3.89 us
    ppermute x9, waiting for transfers between devices: 10.8 us -> 9.66 us  [plane_swap(): return lax.ppermute(value, 'cls', [(i, i ^ step) for i in range(count)])]
    dynamic_slice x1, local copies, waits for them, and re-layouts: 0.01 us -> 0.89 us  [per_device(): lax.dynamic_slice_in_dim(head_proj, (1 - (cls >> core & 1)) * half, half, 0)]
    unnamed x18 -> x12, local copies, waits for them, and re-layouts: 1.52 us -> 2.05 us
  transfers between devices with their start and end apart: 24 -> 24, of which waited for: 15 -> 14; matrix products, arithmetic and copies ran while one was open for 3% -> 5% of each run, Pallas kernels for 8% -> 8%
where the time goes in v7:
time: 56.2 us; the launch traced here: 55.9 us
  starting transfers between devices  25.5 us (45%)
  waiting for transfers between devices  15.6 us (28%)
  Pallas kernels  7.37 us (13%)
  local copies, waits for them, and re-layouts  3.89 us (7%)
  other arithmetic  1.98 us (4%)
  between operations  1.65 us (3%)
    ppermute x9, starting transfers between devices, z_swap(): lax.ppermute(value, 'dp', [(i, i ^ step * CORES) for i in range(count)])  13 us
    ppermute x9, starting transfers between devices, plane_swap(): return lax.ppermute(value, 'cls', [(i, i ^ step) for i in range(count)])  10.7 us
    ppermute x9, waiting for transfers between devices, plane_swap(): return lax.ppermute(value, 'cls', [(i, i ^ step) for i in range(count)])  9.66 us
    pallas_call x5, Pallas kernels, in_vmem(): pl.pallas_call(kernel, out_shape=tuple(outs), in_specs=[pl.BlockSpec(memo...  7.36 us
    ppermute x9, waiting for transfers between devices, z_swap(): lax.ppermute(value, 'dp', [(i, i ^ step * CORES) for i in range(count)])  4.99 us
    unnamed x12, local copies, waits for them, and re-layouts  2.05 us
    ppermute x1, starting transfers between devices, half_swap(): return lax.ppermute(value, ('dp', 'cls'), pairs)  1.56 us
  transfers between devices with their start and end apart: 24, of which 14 were waited for; matrix products, arithmetic and copies ran while one was open for 5% of the time, Pallas kernels for 8%

profile of v7, /device:TPU:0, one launch (start us, length us, event | category | flops | bytes accessed | tf_op | source)
XLA Modules:
  0.0 55.9 jit_solution(10234560764442488597)
XLA Ops:
  0.6 0.8 %constant_dynamic-slice_fusion.2 = bf16[32,1024]{1,0:T(8,128)(2,1)S(1)} fusion(bf16[128,1024]{1,0:T(8,128)(2,1)} %own_ref.1, s32[]{:T(128)S(6)} %select_n.39), kind=kLoop, calls=%fused_computation.42 | loop fusion | bytes 131076 | tf_op jit(solution)/shard_map/dynamic_slice | solution.py:425
  1.5 5.0 %collective-permute-start.4 = (bf16[32,1024]{1,0:T(8,128)(2,1)S(1)}, bf16[32,1024]{1,0:T(8,128)(2,1)S(1)}, u32[]{:S(2)}, u32[]{:S(2)}) collective-permute-start(bf16[32,1024]{1,0:T(8,128)(2,1)S(1)} %constant_dynamic-slice_fusion.2), channel_id=1, source_target_pairs={{0,24},{4,28},{8,16},{12,20},{16,8},{20,12},{24,0},{28,4},{1,25},{... | collective-permute-start | bytes 196616 | tf_op jit(solution)/shard_map/ppermute | solution.py:23
  7.1 0.7 %fusion.15 = (bf16[24]{0:T(256)(128)(2,1)S(1)}, bf16[24]{0:T(256)(128)(2,1)S(1)}) fusion(s32[24]{0:T(128)} %param.19), kind=kLoop, calls=%fused_computation.48 | loop fusion | flops 504 | bytes 192 | tf_op jit(solution)/shard_map/convert.2
  9.1 0.9 %constant_dynamic-slice_fusion = (bf16[64,512]{1,0:T(8,128)(2,1)S(1)}, bf16[64,512]{1,0:T(8,128)(2,1)S(1)}) fusion(bf16[128,512]{1,0:T(8,128)(2,1)} %param.15, s32[]{:T(128)S(6)} %select_n.48, s32[]{:T(128)S(6)} %select_n.41), kind=kLoop, calls=%fused_computation.40 | loop fusion | bytes 262152 | tf_op jit(solution)/shard_map/dynamic_slice | solution.py:464
  10.0 2.3 %collective-permute-done.3 = bf16[32,1024]{1,0:T(8,128)(2,1)S(1)} collective-permute-done((bf16[32,1024]{1,0:T(8,128)(2,1)S(1)}, bf16[32,1024]{1,0:T(8,128)(2,1)S(1)}, u32[]{:S(2)}, u32[]{:S(2)}) %collective-permute-start.3) | collective-permute-done | bytes 65568 | tf_op jit(solution)/shard_map/ppermute | solution.py:23
  12.3 2.5 %collective-permute-start.7 = (bf16[2,32,1024]{2,1,0:T(8,128)(2,1)S(1)}, bf16[2,32,1024]{2,1,0:T(8,128)(2,1)S(1)}, u32[]{:S(2)}, u32[]{:S(2)}) collective-permute-start(bf16[2,32,1024]{2,1,0:T(8,128)(2,1)S(1)} %shard_map.121.refs_1_), channel_id=1, source_target_pairs={{0,3},{1,2},{2,1},{3,0},{4,7},{5,6},{6,5},{7,4},{8,11},{9,10},{10,... | collective-permute-start | bytes 393224 | tf_op jit(solution)/shard_map/ppermute | solution.py:39
  15.8 0.9 %collective-permute-done.near_ref = bf16[128,1024]{1,0:T(8,128)(2,1)S(1)} collective-permute-done((bf16[128,1024]{1,0:T(8,128)(2,1)}, bf16[128,1024]{1,0:T(8,128)(2,1)S(1)}, u32[]{:S(2)}, u32[]{:S(2)}) %collective-permute-start) | collective-permute-done | bytes 262176 | tf_op jit(solution)/shard_map/ppermute | solution.py:23
  16.9 0.8 %collective-permute-start.8 = (bf16[80,512]{1,0:T(8,128)(2,1)S(1)}, bf16[80,512]{1,0:T(8,128)(2,1)S(1)}, u32[]{:S(2)}, u32[]{:S(2)}) collective-permute-start(bf16[80,512]{1,0:T(8,128)(2,1)S(1)} %shard_map.122), channel_id=1, source_target_pairs={{0,8},{4,12},{8,0},{12,4},{16,24},{20,28},{24,16},{28,20},{1,9},{5... | collective-permute-start | bytes 245768 | tf_op jit(solution)/shard_map/ppermute | solution.py:23
  17.6 1.1 %collective-permute-done.7 = bf16[2,32,1024]{2,1,0:T(8,128)(2,1)S(1)} collective-permute-done((bf16[2,32,1024]{2,1,0:T(8,128)(2,1)S(1)}, bf16[2,32,1024]{2,1,0:T(8,128)(2,1)S(1)}, u32[]{:S(2)}, u32[]{:S(2)}) %collective-permute-start.7) | collective-permute-done | bytes 131104 | tf_op jit(solution)/shard_map/ppermute | solution.py:39
  18.7 2.3 %collective-permute-done.6 = bf16[2,32,1024]{2,1,0:T(8,128)(2,1)S(1)} collective-permute-done((bf16[2,32,1024]{2,1,0:T(8,128)(2,1)S(1)}, bf16[2,32,1024]{2,1,0:T(8,128)(2,1)S(1)}, u32[]{:S(2)}, u32[]{:S(2)}) %collective-permute-start.6) | collective-permute-done | bytes 131104 | tf_op jit(solution)/shard_map/ppermute | solution.py:39
  22.8 2.2 %collective-permute-start.18 = (bf16[80,512]{1,0:T(8,128)(2,1)S(1)}, bf16[80,512]{1,0:T(8,128)(2,1)S(1)}, u32[]{:S(2)}, u32[]{:S(2)}) collective-permute-start(bf16[80,512]{1,0:T(8,128)(2,1)S(1)} %shard_map.122), channel_id=1, source_target_pairs={{0,24},{4,28},{8,16},{12,20},{16,8},{20,12},{24,0},{28,4},{1,25},{... | collective-permute-start | bytes 245768 | tf_op jit(solution)/shard_map/ppermute | solution.py:23
  25.0 1.5 %copy-done.3 = bf16[864,1024]{1,0:T(8,128)(2,1)S(1)} copy-done((bf16[864,1024]{1,0:T(8,128)(2,1)S(1)}, bf16[864,1024]{1,0:T(8,128)(2,1)}, u32[]{:S(2)}) %copy-start.3) | copy-done | bytes 1769496
  26.5 2.9 %shard_map.125.refs_1_ = bf16[8,1024]{1,0:T(8,128)(2,1)S(1)} custom-call(bf16[864,1024]{1,0:T(8,128)(2,1)S(1)} %copy-done.2, bf16[864,1024]{1,0:T(8,128)(2,1)S(1)} %copy-done.3, bf16[128,1024]{1,0:T(8,128)(2,1)S(1)} %copy-done.1, bf16[128,1024]{1,0:T(8,128)(2,1)S(1)} %collective-permute-done.near_ref, ...), custom_call_target="tpu_custom_call" | custom-call | flops 1811939328 | bytes 5660672 | tf_op jit(solution)/shard_map/pallas_call | solution.py:106
  29.4 2.0 %collective-permute-start.12 = (bf16[8,1024]{1,0:T(8,128)(2,1)S(1)}, bf16[8,1024]{1,0:T(8,128)(2,1)S(1)}, u32[]{:S(2)}, u32[]{:S(2)}) collective-permute-start(bf16[8,1024]{1,0:T(8,128)(2,1)S(1)} %shard_map.125.refs_1_), channel_id=1, source_target_pairs={{0,24},{4,28},{8,16},{12,20},{16,8},{20,12},{24,0},{28,4},{1,25},{... | collective-permute-start | bytes 49160 | tf_op jit(solution)/shard_map/ppermute | solution.py:23
  31.4 1.8 %collective-permute-start.11 = (bf16[8,1024]{1,0:T(8,128)(2,1)S(1)}, bf16[8,1024]{1,0:T(8,128)(2,1)S(1)}, u32[]{:S(2)}, u32[]{:S(2)}) collective-permute-start(bf16[8,1024]{1,0:T(8,128)(2,1)S(1)} %shard_map.125.refs_1_), channel_id=1, source_target_pairs={{0,16},{4,20},{8,24},{12,28},{16,0},{20,4},{24,8},{28,12},{1,17},{... | collective-permute-start | bytes 49160 | tf_op jit(solution)/shard_map/ppermute | solution.py:23
  33.2 0.7 %collective-permute-start.10 = (bf16[8,1024]{1,0:T(8,128)(2,1)S(1)}, bf16[8,1024]{1,0:T(8,128)(2,1)S(1)}, u32[]{:S(2)}, u32[]{:S(2)}) collective-permute-start(bf16[8,1024]{1,0:T(8,128)(2,1)S(1)} %shard_map.125.refs_1_), channel_id=1, source_target_pairs={{0,8},{4,12},{8,0},{12,4},{16,24},{20,28},{24,16},{28,20},{1,9},{5... | collective-permute-start | bytes 49160 | tf_op jit(solution)/shard_map/ppermute | solution.py:23
  33.9 1.6 %collective-permute-start.19 = (bf16[3,64,512]{2,1,0:T(8,128)(2,1)S(1)}, bf16[3,64,512]{2,1,0:T(8,128)(2,1)S(1)}, u32[]{:S(2)}, u32[]{:S(2)}) collective-permute-start(bf16[3,64,512]{2,1,0:T(8,128)(2,1)S(1)} %pad_maximum_fusion.4), channel_id=1, source_target_pairs={{0,1},{1,0},{2,3},{3,2},{4,6},{5,7},{6,4},{7,5},{8,9},{9,8},{10,11... | collective-permute-start | bytes 589832 | tf_op jit(solution)/shard_map/ppermute | solution.py:34
  36.0 0.9 %collective-permute-done.10 = bf16[8,1024]{1,0:T(8,128)(2,1)S(1)} collective-permute-done((bf16[8,1024]{1,0:T(8,128)(2,1)S(1)}, bf16[8,1024]{1,0:T(8,128)(2,1)S(1)}, u32[]{:S(2)}, u32[]{:S(2)}) %collective-permute-start.10) | collective-permute-done | bytes 16416 | tf_op jit(solution)/shard_map/ppermute | solution.py:23
  36.9 1.5 %collective-permute-start.14 = (bf16[4,8,1024]{2,1,0:T(8,128)(2,1)S(1)}, bf16[4,8,1024]{2,1,0:T(8,128)(2,1)S(1)}, u32[]{:S(2)}, u32[]{:S(2)}) collective-permute-start(bf16[4,8,1024]{2,1,0:T(8,128)(2,1)S(1)} %pad_maximum_fusion.7), channel_id=1, source_target_pairs={{0,2},{1,3},{2,0},{3,1},{4,6},{5,7},{6,4},{7,5},{8,10},{9,11},{10,... | collective-permute-start | bytes 196616 | tf_op jit(solution)/shard_map/ppermute | solution.py:39
  38.5 1.1 %collective-permute-start.13 = (bf16[4,8,1024]{2,1,0:T(8,128)(2,1)S(1)}, bf16[4,8,1024]{2,1,0:T(8,128)(2,1)S(1)}, u32[]{:S(2)}, u32[]{:S(2)}) collective-permute-start(bf16[4,8,1024]{2,1,0:T(8,128)(2,1)S(1)} %pad_maximum_fusion.7), channel_id=1, source_target_pairs={{0,1},{1,0},{2,3},{3,2},{4,5},{5,4},{6,7},{7,6},{8,9},{9,8},{10,11... | collective-permute-start | bytes 196616 | tf_op jit(solution)/shard_map/ppermute | solution.py:39
  39.6 0.9 %collective-permute-start.15 = (bf16[4,8,1024]{2,1,0:T(8,128)(2,1)S(1)}, bf16[4,8,1024]{2,1,0:T(8,128)(2,1)S(1)}, u32[]{:S(2)}, u32[]{:S(2)}) collective-permute-start(bf16[4,8,1024]{2,1,0:T(8,128)(2,1)S(1)} %pad_maximum_fusion.7), channel_id=1, source_target_pairs={{0,3},{1,2},{2,1},{3,0},{4,7},{5,6},{6,5},{7,4},{8,11},{9,10},{10,... | collective-permute-start | bytes 196616 | tf_op jit(solution)/shard_map/ppermute | solution.py:39
  40.5 2.2 %collective-permute-done.13.refs_1_ = bf16[4,8,1024]{2,1,0:T(8,128)(2,1)S(1)} collective-permute-done((bf16[4,8,1024]{2,1,0:T(8,128)(2,1)S(1)}, bf16[4,8,1024]{2,1,0:T(8,128)(2,1)S(1)}, u32[]{:S(2)}, u32[]{:S(2)}) %collective-permute-start.13) | collective-permute-done | bytes 65568 | tf_op jit(solution)/shard_map/ppermute | solution.py:39
  42.9 1.8 %collective-permute-done.15 = bf16[4,8,1024]{2,1,0:T(8,128)(2,1)S(1)} collective-permute-done((bf16[4,8,1024]{2,1,0:T(8,128)(2,1)S(1)}, bf16[4,8,1024]{2,1,0:T(8,128)(2,1)S(1)}, u32[]{:S(2)}, u32[]{:S(2)}) %collective-permute-start.15) | collective-permute-done | bytes 65568 | tf_op jit(solution)/shard_map/ppermute | solution.py:39
  45.5 0.9 %collective-permute-done.16.refs_0_ = bf16[4,4,8,1024]{3,2,1,0:T(8,128)(2,1)S(1)} collective-permute-done((bf16[4,4,8,1024]{3,2,1,0:T(8,128)(2,1)S(1)}, bf16[4,4,8,1024]{3,2,1,0:T(8,128)(2,1)S(1)}, u32[]{:S(2)}, u32[]{:S(2)}) %collective-permute-start.16) | collective-permute-done | bytes 262176 | tf_op jit(solution)/shard_map/ppermute | solution.py:28
  46.4 2.0 %shard_map.132 = (f32[256,1024]{1,0:T(8,128)S(1)}, f32[256,1024]{1,0:T(8,128)S(1)}, f32[256,640]{1,0:T(8,128)S(1)}, f32[4,8,1280]{2,1,0:T(8,128)S(1)}, f32[1,256]{1,0:T(1,128)S(1)}) custom-call(bf16[256,1024]{1,0:T(8,128)(2,1)S(1)} %bitcast.59, bf16[1024,512]{1,0:T(8,128)(2,1)S(1)} %get-tuple-element.22.refs_1_.whole_ref, ...), custom_call_target="tpu_custom_call" | custom-call | flops 805306368 | bytes 5544960 | tf_op jit(solution)/shard_map/pallas_call | solution.py:106
  48.4 1.0 %collective-permute-start.21 = (f32[7,1280]{1,0:T(8,128)S(1)}, f32[7,1280]{1,0:T(8,128)S(1)}, u32[]{:S(2)}, u32[]{:S(2)}) collective-permute-start(f32[7,1280]{1,0:T(8,128)S(1)} %get-tuple-element.45), channel_id=1, source_target_pairs={{0,3},{1,2},{2,1},{3,0},{4,7},{5,6},{6,5},{7,4},{8,11},{9,10},{10,... | collective-permute-start | bytes 107528 | tf_op jit(solution)/shard_map/ppermute | solution.py:39
  49.4 1.5 %collective-permute-start.22 = (f32[7,1280]{1,0:T(8,128)S(1)}, f32[7,1280]{1,0:T(8,128)S(1)}, u32[]{:S(2)}, u32[]{:S(2)}) collective-permute-start(f32[7,1280]{1,0:T(8,128)S(1)} %get-tuple-element.46), channel_id=1, source_target_pairs={{0,2},{1,3},{2,0},{3,1},{4,6},{5,7},{6,4},{7,5},{8,10},{9,11},{10,... | collective-permute-start | bytes 107528 | tf_op jit(solution)/shard_map/ppermute | solution.py:39
  50.9 1.1 %collective-permute-start.23 = (f32[7,1280]{1,0:T(8,128)S(1)}, f32[7,1280]{1,0:T(8,128)S(1)}, u32[]{:S(2)}, u32[]{:S(2)}) collective-permute-start(f32[7,1280]{1,0:T(8,128)S(1)} %get-tuple-element.47), channel_id=1, source_target_pairs={{0,1},{1,0},{2,3},{3,2},{4,5},{5,4},{6,7},{7,6},{8,9},{9,8},{10,11... | collective-permute-start | bytes 107528 | tf_op jit(solution)/shard_map/ppermute | solution.py:39
  52.0 0.9 %shard_map.133 = (bf16[256,1024]{1,0:T(8,128)(2,1)S(1)}, bf16[256,1024]{1,0:T(8,128)(2,1)S(1)}, f32[256,1024]{1,0:T(8,128)S(1)}, f32[64,256]{1,0:T(8,128)S(1)}, ...) custom-call(f32[256,1024]{1,0:T(8,128)S(1)} %get-tuple-element.26.exp_ref, ...), custom_call_target="tpu_custom_call" | custom-call | flops 67108864 | bytes 6494208 | tf_op jit(solution)/shard_map/pallas_call | solution.py:106
  52.8 0.9 %collective-permute-done.21 = f32[7,1280]{1,0:T(8,128)S(1)} collective-permute-done((f32[7,1280]{1,0:T(8,128)S(1)}, f32[7,1280]{1,0:T(8,128)S(1)}, u32[]{:S(2)}, u32[]{:S(2)}) %collective-permute-start.21) | collective-permute-done | bytes 35872 | tf_op jit(solution)/shard_map/ppermute | solution.py:39
  53.8 1.0 %collective-permute-done.23 = f32[7,1280]{1,0:T(8,128)S(1)} collective-permute-done((f32[7,1280]{1,0:T(8,128)S(1)}, f32[7,1280]{1,0:T(8,128)S(1)}, u32[]{:S(2)}, u32[]{:S(2)}) %collective-permute-start.23) | collective-permute-done | bytes 35872 | tf_op jit(solution)/shard_map/ppermute | solution.py:39
  54.9 1.0 %shard_map.134 = (f32[64,1024]{1,0:T(8,128)}, f32[1,6]{1,0:T(1,128)}, f32[6,512]{1,0:T(8,128)}) custom-call(f32[7,1280]{1,0:T(8,128)S(1)} %fusion.6.total_ref, f32[1,256]{1,0:T(1,128)S(1)} %slice.37.denom_ref, bf16[256,1024]{1,0:T(8,128)(2,1)S(1)} %get-tuple-element.29.high_ref, bf16[256,1024]{1,0:T(8,128)(2,1)S(1)} %get-tuple-element.30.low_ref, ...), custom_call_target="tpu_custom_call" | custom-call | flops 100663296 | bytes 3661848 | tf_op jit(solution)/shard_map/pallas_call | solution.py:106
  (70 shorter events, 5.8 us)
Async XLA Ops:
  1.5 8.5 %collective-permute-start.4 = (bf16[32,1024]{1,0:T(8,128)(2,1)S(1)}, bf16[32,1024]{1,0:T(8,128)(2,1)S(1)}, u32[]{:S(2)}, u32[]{:S(2)}) collective-permute-start(bf16[32,1024]{1,0:T(8,128)(2,1)S(1)} %constant_dynamic-slice_fusion.2), channel_id=1, source_target_pairs={{0,24},{4,28},{8,16},{12,20},{16,8},{20,12},{24,0},{28,4},{1,25},{... | collective-permute-start | bytes 196616 | tf_op jit(solution)/shard_map/ppermute | solution.py:23
  6.5 5.7 %collective-permute-start.3 = (bf16[32,1024]{1,0:T(8,128)(2,1)S(1)}, bf16[32,1024]{1,0:T(8,128)(2,1)S(1)}, u32[]{:S(2)}, u32[]{:S(2)}) collective-permute-start(bf16[32,1024]{1,0:T(8,128)(2,1)S(1)} %constant_dynamic-slice_fusion.2), channel_id=1, source_target_pairs={{0,16},{4,20},{8,24},{12,28},{16,0},{20,4},{24,8},{28,12},{1,17},{... | collective-permute-start | bytes 196616 | tf_op jit(solution)/shard_map/ppermute | solution.py:23
  6.5 5.7 %collective-permute-start.1 = (bf16[128,1024]{1,0:T(8,128)(2,1)}, bf16[128,1024]{1,0:T(8,128)(2,1)S(1)}, u32[]{:S(2)}, u32[]{:S(2)}) collective-permute-start(bf16[128,1024]{1,0:T(8,128)(2,1)} %own_ref.1), channel_id=1, source_target_pairs={{0,4},{4,0},{8,12},{12,8},{16,20},{20,16},{24,28},{28,24},{1,5},{5... | collective-permute-start | bytes 786440 | tf_op jit(solution)/shard_map/ppermute | solution.py:28
  6.5 10.2 %collective-permute-start = (bf16[128,1024]{1,0:T(8,128)(2,1)}, bf16[128,1024]{1,0:T(8,128)(2,1)S(1)}, u32[]{:S(2)}, u32[]{:S(2)}) collective-permute-start(bf16[128,1024]{1,0:T(8,128)(2,1)} %own_ref.1), channel_id=1, source_target_pairs={{0,8},{4,12},{8,0},{12,4},{16,24},{20,28},{24,16},{28,20},{1,9},{5... | collective-permute-start | bytes 786440 | tf_op jit(solution)/shard_map/ppermute | solution.py:23
  12.3 6.4 %collective-permute-start.7 = (bf16[2,32,1024]{2,1,0:T(8,128)(2,1)S(1)}, bf16[2,32,1024]{2,1,0:T(8,128)(2,1)S(1)}, u32[]{:S(2)}, u32[]{:S(2)}) collective-permute-start(bf16[2,32,1024]{2,1,0:T(8,128)(2,1)S(1)} %shard_map.121.refs_1_), channel_id=1, source_target_pairs={{0,3},{1,2},{2,1},{3,0},{4,7},{5,6},{6,5},{7,4},{8,11},{9,10},{10,... | collective-permute-start | bytes 393224 | tf_op jit(solution)/shard_map/ppermute | solution.py:39
  14.8 6.2 %collective-permute-start.6 = (bf16[2,32,1024]{2,1,0:T(8,128)(2,1)S(1)}, bf16[2,32,1024]{2,1,0:T(8,128)(2,1)S(1)}, u32[]{:S(2)}, u32[]{:S(2)}) collective-permute-start(bf16[2,32,1024]{2,1,0:T(8,128)(2,1)S(1)} %shard_map.121.refs_1_), channel_id=1, source_target_pairs={{0,2},{1,3},{2,0},{3,1},{4,6},{5,7},{6,4},{7,5},{8,10},{9,11},{10,... | collective-permute-start | bytes 393224 | tf_op jit(solution)/shard_map/ppermute | solution.py:39
  15.3 6.0 %collective-permute-start.5 = (bf16[2,32,1024]{2,1,0:T(8,128)(2,1)S(1)}, bf16[2,32,1024]{2,1,0:T(8,128)(2,1)S(1)}, u32[]{:S(2)}, u32[]{:S(2)}) collective-permute-start(bf16[2,32,1024]{2,1,0:T(8,128)(2,1)S(1)} %shard_map.121.refs_1_), channel_id=1, source_target_pairs={{0,1},{1,0},{2,3},{3,2},{4,5},{5,4},{6,7},{7,6},{8,9},{9,8},{10,11... | collective-permute-start | bytes 393224 | tf_op jit(solution)/shard_map/ppermute | solution.py:39
  16.7 5.1 %collective-permute-start.2 = (bf16[128,1024]{1,0:T(8,128)(2,1)S(1)}, bf16[128,1024]{1,0:T(8,128)(2,1)S(1)}, u32[]{:S(2)}, u32[]{:S(2)}) collective-permute-start(bf16[128,1024]{1,0:T(8,128)(2,1)S(1)} %collective-permute-done.near_ref), channel_id=1, source_target_pairs={{0,4},{4,0},{8,12},{12,8},{16,20},{20,16},{24,28},{28,24},{1,5},{5... | collective-permute-start | bytes 786440 | tf_op jit(solution)/shard_map/ppermute | solution.py:28
  16.9 4.9 %collective-permute-start.8 = (bf16[80,512]{1,0:T(8,128)(2,1)S(1)}, bf16[80,512]{1,0:T(8,128)(2,1)S(1)}, u32[]{:S(2)}, u32[]{:S(2)}) collective-permute-start(bf16[80,512]{1,0:T(8,128)(2,1)S(1)} %shard_map.122), channel_id=1, source_target_pairs={{0,8},{4,12},{8,0},{12,4},{16,24},{20,28},{24,16},{28,20},{1,9},{5... | collective-permute-start | bytes 245768 | tf_op jit(solution)/shard_map/ppermute | solution.py:23
  21.3 1.2 %copy-start = (bf16[1024,512]{1,0:T(8,128)(2,1)S(1)}, bf16[1024,512]{1,0:T(8,128)(2,1)}, u32[]{:S(2)}) copy-start(bf16[1024,512]{1,0:T(8,128)(2,1)} %weight_ref.3) | copy-start | bytes 3145732
  21.8 3.2 %copy-start.1 = (bf16[128,1024]{1,0:T(8,128)(2,1)S(1)}, bf16[128,1024]{1,0:T(8,128)(2,1)}, u32[]{:S(2)}) copy-start(bf16[128,1024]{1,0:T(8,128)(2,1)} %own_ref.1) | copy-start | bytes 786436
  21.8 3.2 %copy-start.4 = (f32[1024]{0:T(1024)S(1)}, f32[1024]{0:T(1024)}, u32[]{:S(2)}) copy-start(f32[1024]{0:T(1024)} %param.13) | copy-start | bytes 12292
  21.8 3.2 %copy-start.5 = (f32[1024]{0:T(1024)S(1)}, f32[1024]{0:T(1024)}, u32[]{:S(2)}) copy-start(f32[1024]{0:T(1024)} %param.14) | copy-start | bytes 12292
  21.8 3.1 %collective-permute-start.9 = (bf16[4,2,32,1024]{3,2,1,0:T(8,128)(2,1)S(1)}, bf16[4,2,32,1024]{3,2,1,0:T(8,128)(2,1)S(1)}, u32[]{:S(2)}, u32[]{:S(2)}) collective-permute-start(bf16[4,2,32,1024]{3,2,1,0:T(8,128)(2,1)S(1)} %shard_map.123.far_ref), channel_id=1, source_target_pairs={{0,4},{4,0},{8,12},{12,8},{16,20},{20,16},{24,28},{28,24},{1,5},{5... | collective-permute-start | bytes 1572872 | tf_op jit(solution)/shard_map/ppermute | solution.py:28
  22.5 2.5 %copy-start.2 = (bf16[864,1024]{1,0:T(8,128)(2,1)S(1)}, bf16[864,1024]{1,0:T(8,128)(2,1)}, u32[]{:S(2)}) copy-start(bf16[864,1024]{1,0:T(8,128)(2,1)} %att_ref.1) | copy-start | bytes 5308420
  22.8 11.1 %collective-permute-start.18 = (bf16[80,512]{1,0:T(8,128)(2,1)S(1)}, bf16[80,512]{1,0:T(8,128)(2,1)S(1)}, u32[]{:S(2)}, u32[]{:S(2)}) collective-permute-start(bf16[80,512]{1,0:T(8,128)(2,1)S(1)} %shard_map.122), channel_id=1, source_target_pairs={{0,24},{4,28},{8,16},{12,20},{16,8},{20,12},{24,0},{28,4},{1,25},{... | collective-permute-start | bytes 245768 | tf_op jit(solution)/shard_map/ppermute | solution.py:23
  25.0 8.9 %collective-permute-start.17 = (bf16[80,512]{1,0:T(8,128)(2,1)S(1)}, bf16[80,512]{1,0:T(8,128)(2,1)S(1)}, u32[]{:S(2)}, u32[]{:S(2)}) collective-permute-start(bf16[80,512]{1,0:T(8,128)(2,1)S(1)} %shard_map.122), channel_id=1, source_target_pairs={{0,16},{4,20},{8,24},{12,28},{16,0},{20,4},{24,8},{28,12},{1,17},{... | collective-permute-start | bytes 245768 | tf_op jit(solution)/shard_map/ppermute | solution.py:23
  25.0 1.5 %copy-start.3 = (bf16[864,1024]{1,0:T(8,128)(2,1)S(1)}, bf16[864,1024]{1,0:T(8,128)(2,1)}, u32[]{:S(2)}) copy-start(bf16[864,1024]{1,0:T(8,128)(2,1)} %stream_ref.1) | copy-start | bytes 5308420
  29.4 6.2 %collective-permute-start.12 = (bf16[8,1024]{1,0:T(8,128)(2,1)S(1)}, bf16[8,1024]{1,0:T(8,128)(2,1)S(1)}, u32[]{:S(2)}, u32[]{:S(2)}) collective-permute-start(bf16[8,1024]{1,0:T(8,128)(2,1)S(1)} %shard_map.125.refs_1_), channel_id=1, source_target_pairs={{0,24},{4,28},{8,16},{12,20},{16,8},{20,12},{24,0},{28,4},{1,25},{... | collective-permute-start | bytes 49160 | tf_op jit(solution)/shard_map/ppermute | solution.py:23
  31.4 4.6 %collective-permute-start.11 = (bf16[8,1024]{1,0:T(8,128)(2,1)S(1)}, bf16[8,1024]{1,0:T(8,128)(2,1)S(1)}, u32[]{:S(2)}, u32[]{:S(2)}) collective-permute-start(bf16[8,1024]{1,0:T(8,128)(2,1)S(1)} %shard_map.125.refs_1_), channel_id=1, source_target_pairs={{0,16},{4,20},{8,24},{12,28},{16,0},{20,4},{24,8},{28,12},{1,17},{... | collective-permute-start | bytes 49160 | tf_op jit(solution)/shard_map/ppermute | solution.py:23
  33.2 3.7 %collective-permute-start.10 = (bf16[8,1024]{1,0:T(8,128)(2,1)S(1)}, bf16[8,1024]{1,0:T(8,128)(2,1)S(1)}, u32[]{:S(2)}, u32[]{:S(2)}) collective-permute-start(bf16[8,1024]{1,0:T(8,128)(2,1)S(1)} %shard_map.125.refs_1_), channel_id=1, source_target_pairs={{0,8},{4,12},{8,0},{12,4},{16,24},{20,28},{24,16},{28,20},{1,9},{5... | collective-permute-start | bytes 49160 | tf_op jit(solution)/shard_map/ppermute | solution.py:23
  33.9 8.8 %collective-permute-start.19 = (bf16[3,64,512]{2,1,0:T(8,128)(2,1)S(1)}, bf16[3,64,512]{2,1,0:T(8,128)(2,1)S(1)}, u32[]{:S(2)}, u32[]{:S(2)}) collective-permute-start(bf16[3,64,512]{2,1,0:T(8,128)(2,1)S(1)} %pad_maximum_fusion.4), channel_id=1, source_target_pairs={{0,1},{1,0},{2,3},{3,2},{4,6},{5,7},{6,4},{7,5},{8,9},{9,8},{10,11... | collective-permute-start | bytes 589832 | tf_op jit(solution)/shard_map/ppermute | solution.py:34
  36.9 6.0 %collective-permute-start.14 = (bf16[4,8,1024]{2,1,0:T(8,128)(2,1)S(1)}, bf16[4,8,1024]{2,1,0:T(8,128)(2,1)S(1)}, u32[]{:S(2)}, u32[]{:S(2)}) collective-permute-start(bf16[4,8,1024]{2,1,0:T(8,128)(2,1)S(1)} %pad_maximum_fusion.7), channel_id=1, source_target_pairs={{0,2},{1,3},{2,0},{3,1},{4,6},{5,7},{6,4},{7,5},{8,10},{9,11},{10,... | collective-permute-start | bytes 196616 | tf_op jit(solution)/shard_map/ppermute | solution.py:39
  38.5 4.3 %collective-permute-start.13 = (bf16[4,8,1024]{2,1,0:T(8,128)(2,1)S(1)}, bf16[4,8,1024]{2,1,0:T(8,128)(2,1)S(1)}, u32[]{:S(2)}, u32[]{:S(2)}) collective-permute-start(bf16[4,8,1024]{2,1,0:T(8,128)(2,1)S(1)} %pad_maximum_fusion.7), channel_id=1, source_target_pairs={{0,1},{1,0},{2,3},{3,2},{4,5},{5,4},{6,7},{7,6},{8,9},{9,8},{10,11... | collective-permute-start | bytes 196616 | tf_op jit(solution)/shard_map/ppermute | solution.py:39
  39.6 5.2 %collective-permute-start.15 = (bf16[4,8,1024]{2,1,0:T(8,128)(2,1)S(1)}, bf16[4,8,1024]{2,1,0:T(8,128)(2,1)S(1)}, u32[]{:S(2)}, u32[]{:S(2)}) collective-permute-start(bf16[4,8,1024]{2,1,0:T(8,128)(2,1)S(1)} %pad_maximum_fusion.7), channel_id=1, source_target_pairs={{0,3},{1,2},{2,1},{3,0},{4,7},{5,6},{6,5},{7,4},{8,11},{9,10},{10,... | collective-permute-start | bytes 196616 | tf_op jit(solution)/shard_map/ppermute | solution.py:39
  42.8 2.1 %collective-permute-start.20 = (bf16[576,512]{1,0:T(8,128)(2,1)S(1)}, bf16[576,512]{1,0:T(8,128)(2,1)S(1)}, u32[]{:S(2)}, u32[]{:S(2)}) collective-permute-start(bf16[576,512]{1,0:T(8,128)(2,1)S(1)} %pad_maximum_fusion.head_ref), channel_id=1, source_target_pairs={{0,4},{4,0},{8,12},{12,8},{16,20},{20,16},{24,28},{28,24},{1,5},{5... | collective-permute-start | bytes 1769480 | tf_op jit(solution)/shard_map/ppermute | solution.py:28
  44.8 1.6 %collective-permute-start.16 = (bf16[4,4,8,1024]{3,2,1,0:T(8,128)(2,1)S(1)}, bf16[4,4,8,1024]{3,2,1,0:T(8,128)(2,1)S(1)}, u32[]{:S(2)}, u32[]{:S(2)}) collective-permute-start(bf16[4,4,8,1024]{3,2,1,0:T(8,128)(2,1)S(1)} %bitcast_dynamic-update-slice_fusion.3), channel_id=1, source_target_pairs={{0,4},{4,0},{8,12},{12,8},{16,20},{20,16},{24,28},{28,24},{1,5},{5... | collective-permute-start | bytes 786440 | tf_op jit(solution)/shard_map/ppermute | solution.py:28
  48.4 5.3 %collective-permute-start.21 = (f32[7,1280]{1,0:T(8,128)S(1)}, f32[7,1280]{1,0:T(8,128)S(1)}, u32[]{:S(2)}, u32[]{:S(2)}) collective-permute-start(f32[7,1280]{1,0:T(8,128)S(1)} %get-tuple-element.45), channel_id=1, source_target_pairs={{0,3},{1,2},{2,1},{3,0},{4,7},{5,6},{6,5},{7,4},{8,11},{9,10},{10,... | collective-permute-start | bytes 107528 | tf_op jit(solution)/shard_map/ppermute | solution.py:39
  49.4 4.4 %collective-permute-start.22 = (f32[7,1280]{1,0:T(8,128)S(1)}, f32[7,1280]{1,0:T(8,128)S(1)}, u32[]{:S(2)}, u32[]{:S(2)}) collective-permute-start(f32[7,1280]{1,0:T(8,128)S(1)} %get-tuple-element.46), channel_id=1, source_target_pairs={{0,2},{1,3},{2,0},{3,1},{4,6},{5,7},{6,4},{7,5},{8,10},{9,11},{10,... | collective-permute-start | bytes 107528 | tf_op jit(solution)/shard_map/ppermute | solution.py:39
  50.9 4.0 %collective-permute-start.23 = (f32[7,1280]{1,0:T(8,128)S(1)}, f32[7,1280]{1,0:T(8,128)S(1)}, u32[]{:S(2)}, u32[]{:S(2)}) collective-permute-start(f32[7,1280]{1,0:T(8,128)S(1)} %get-tuple-element.47), channel_id=1, source_target_pairs={{0,1},{1,0},{2,3},{3,2},{4,5},{5,4},{6,7},{7,6},{8,9},{9,8},{10,11... | collective-permute-start | bytes 107528 | tf_op jit(solution)/shard_map/ppermute | solution.py:39

commit v8 on v7

--- a/solution.py
+++ b/solution.py
@@ -262,8 +262,11 @@
         [
             sums[:own] + sums[own : 2 * own],
             sums[2 * own : 3 * own] + sums[3 * own :],
-            jnp.broadcast_to(denom[:own], (own, 128)),
-            jnp.broadcast_to(jnp.sum(picked, axis=1, keepdims=True), (own, 128)),
+            jnp.where(
+                lax.broadcasted_iota(jnp.int32, (own, 128), 1) < 64,
+                denom[:own],
+                jnp.sum(picked, axis=1, keepdims=True),
+            ),
         ],
         axis=1,
     )
@@ -284,12 +287,12 @@
             f32(images, classes),
             f32(images, classes),
             f32(images, embed + 128),
-            f32(n_cls, own // n_cls, 2 * embed + 256),
+            f32(n_cls, own // n_cls, 2 * embed + 128),
             f32(1, images),
         ],
         [
             pltpu.VMEM((own, classes), jnp.float32),
-            pltpu.VMEM((own, 2 * embed + 256), jnp.float32),
+            pltpu.VMEM((own, 2 * embed + 128), jnp.float32),
         ],
         6,
         6 * images * embed * classes,
@@ -365,7 +368,7 @@
     own = unit_ref[pl.ds(pl.multiple_of(lax.axis_index("cls") * lines, lines), lines), :][: embed_ref.shape[0]]
     total = total_ref[: embed_ref.shape[0], :]
     weighted, picked = total[:, :embed], total[:, embed : 2 * embed]
-    own_denom, target_logit = total[:, 2 * embed : 2 * embed + 1], total[:, 2 * embed + 128 : 2 * embed + 129]
+    own_denom, target_logit = total[:, 2 * embed : 2 * embed + 1], total[:, 2 * embed + 64 : 2 * embed + 65]
     loss = jnp.broadcast_to(jnp.log(own_denom) - target_logit, (loss_ref.shape[1], 128))
     loss = jnp.concatenate([loss, jnp.zeros((128 - loss_ref.shape[1], 128), jnp.float32)], axis=0)
     loss_ref[...] = loss.T[0:1, : loss_ref.shape[1]]

time: 56.2 us -> 56.2 us (level)
  no operation moved by 1% of the time
where the time goes in v8:
time: 56.2 us; the launch traced here: 55.9 us
  starting transfers between devices  25.5 us (45%)
  waiting for transfers between devices  15.5 us (28%)
  Pallas kernels  7.38 us (13%)
  local copies, waits for them, and re-layouts  3.89 us (7%)
  other arithmetic  1.98 us (4%)
  between operations  1.65 us (3%)
    ppermute x9, starting transfers between devices, z_swap(): lax.ppermute(value, 'dp', [(i, i ^ step * CORES) for i in range(count)])  13 us
    ppermute x9, starting transfers between devices, plane_swap(): return lax.ppermute(value, 'cls', [(i, i ^ step) for i in range(count)])  10.7 us
    ppermute x9, waiting for transfers between devices, plane_swap(): return lax.ppermute(value, 'cls', [(i, i ^ step) for i in range(count)])  9.62 us
    pallas_call x5, Pallas kernels, in_vmem(): pl.pallas_call(kernel, out_shape=tuple(outs), in_specs=[pl.BlockSpec(memo...  7.37 us
    ppermute x9, waiting for transfers between devices, z_swap(): lax.ppermute(value, 'dp', [(i, i ^ step * CORES) for i in range(count)])  4.99 us
    unnamed x12, local copies, waits for them, and re-layouts  2.05 us
    ppermute x1, starting transfers between devices, half_swap(): return lax.ppermute(value, ('dp', 'cls'), pairs)  1.56 us
  transfers between devices with their start and end apart: 24, of which 14 were waited for; matrix products, arithmetic and copies ran while one was open for 5% of the time, Pallas kernels for 8%

profile of v8, /device:TPU:0, one launch (start us, length us, event | category | flops | bytes accessed | tf_op | source)
XLA Modules:
  0.0 55.9 jit_solution(16467488141937503805)
XLA Ops:
  0.6 0.8 %constant_dynamic-slice_fusion.2 = bf16[32,1024]{1,0:T(8,128)(2,1)S(1)} fusion(bf16[128,1024]{1,0:T(8,128)(2,1)} %own_ref.1, s32[]{:T(128)S(6)} %select_n.39), kind=kLoop, calls=%fused_computation.42 | loop fusion | bytes 131076 | tf_op jit(solution)/shard_map/dynamic_slice | solution.py:428
  1.5 5.0 %collective-permute-start.4 = (bf16[32,1024]{1,0:T(8,128)(2,1)S(1)}, bf16[32,1024]{1,0:T(8,128)(2,1)S(1)}, u32[]{:S(2)}, u32[]{:S(2)}) collective-permute-start(bf16[32,1024]{1,0:T(8,128)(2,1)S(1)} %constant_dynamic-slice_fusion.2), channel_id=1, source_target_pairs={{0,24},{4,28},{8,16},{12,20},{16,8},{20,12},{24,0},{28,4},{1,25},{... | collective-permute-start | bytes 196616 | tf_op jit(solution)/shard_map/ppermute | solution.py:23
  7.1 0.7 %fusion.15 = (bf16[24]{0:T(256)(128)(2,1)S(1)}, bf16[24]{0:T(256)(128)(2,1)S(1)}) fusion(s32[24]{0:T(128)} %param.19), kind=kLoop, calls=%fused_computation.48 | loop fusion | flops 504 | bytes 192 | tf_op jit(solution)/shard_map/convert.2
  9.1 0.9 %constant_dynamic-slice_fusion = (bf16[64,512]{1,0:T(8,128)(2,1)S(1)}, bf16[64,512]{1,0:T(8,128)(2,1)S(1)}) fusion(bf16[128,512]{1,0:T(8,128)(2,1)} %param.15, s32[]{:T(128)S(6)} %select_n.48, s32[]{:T(128)S(6)} %select_n.41), kind=kLoop, calls=%fused_computation.40 | loop fusion | bytes 262152 | tf_op jit(solution)/shard_map/dynamic_slice | solution.py:467
  10.0 2.3 %collective-permute-done.3 = bf16[32,1024]{1,0:T(8,128)(2,1)S(1)} collective-permute-done((bf16[32,1024]{1,0:T(8,128)(2,1)S(1)}, bf16[32,1024]{1,0:T(8,128)(2,1)S(1)}, u32[]{:S(2)}, u32[]{:S(2)}) %collective-permute-start.3) | collective-permute-done | bytes 65568 | tf_op jit(solution)/shard_map/ppermute | solution.py:23
  12.3 2.5 %collective-permute-start.7 = (bf16[2,32,1024]{2,1,0:T(8,128)(2,1)S(1)}, bf16[2,32,1024]{2,1,0:T(8,128)(2,1)S(1)}, u32[]{:S(2)}, u32[]{:S(2)}) collective-permute-start(bf16[2,32,1024]{2,1,0:T(8,128)(2,1)S(1)} %shard_map.121.refs_1_), channel_id=1, source_target_pairs={{0,3},{1,2},{2,1},{3,0},{4,7},{5,6},{6,5},{7,4},{8,11},{9,10},{10,... | collective-permute-start | bytes 393224 | tf_op jit(solution)/shard_map/ppermute | solution.py:39
  15.8 0.9 %collective-permute-done.near_ref = bf16[128,1024]{1,0:T(8,128)(2,1)S(1)} collective-permute-done((bf16[128,1024]{1,0:T(8,128)(2,1)}, bf16[128,1024]{1,0:T(8,128)(2,1)S(1)}, u32[]{:S(2)}, u32[]{:S(2)}) %collective-permute-start) | collective-permute-done | bytes 262176 | tf_op jit(solution)/shard_map/ppermute | solution.py:23
  16.9 0.8 %collective-permute-start.8 = (bf16[80,512]{1,0:T(8,128)(2,1)S(1)}, bf16[80,512]{1,0:T(8,128)(2,1)S(1)}, u32[]{:S(2)}, u32[]{:S(2)}) collective-permute-start(bf16[80,512]{1,0:T(8,128)(2,1)S(1)} %shard_map.122), channel_id=1, source_target_pairs={{0,8},{4,12},{8,0},{12,4},{16,24},{20,28},{24,16},{28,20},{1,9},{5... | collective-permute-start | bytes 245768 | tf_op jit(solution)/shard_map/ppermute | solution.py:23
  17.6 1.1 %collective-permute-done.7 = bf16[2,32,1024]{2,1,0:T(8,128)(2,1)S(1)} collective-permute-done((bf16[2,32,1024]{2,1,0:T(8,128)(2,1)S(1)}, bf16[2,32,1024]{2,1,0:T(8,128)(2,1)S(1)}, u32[]{:S(2)}, u32[]{:S(2)}) %collective-permute-start.7) | collective-permute-done | bytes 131104 | tf_op jit(solution)/shard_map/ppermute | solution.py:39
  18.7 2.3 %collective-permute-done.6 = bf16[2,32,1024]{2,1,0:T(8,128)(2,1)S(1)} collective-permute-done((bf16[2,32,1024]{2,1,0:T(8,128)(2,1)S(1)}, bf16[2,32,1024]{2,1,0:T(8,128)(2,1)S(1)}, u32[]{:S(2)}, u32[]{:S(2)}) %collective-permute-start.6) | collective-permute-done | bytes 131104 | tf_op jit(solution)/shard_map/ppermute | solution.py:39
  22.8 2.2 %collective-permute-start.18 = (bf16[80,512]{1,0:T(8,128)(2,1)S(1)}, bf16[80,512]{1,0:T(8,128)(2,1)S(1)}, u32[]{:S(2)}, u32[]{:S(2)}) collective-permute-start(bf16[80,512]{1,0:T(8,128)(2,1)S(1)} %shard_map.122), channel_id=1, source_target_pairs={{0,24},{4,28},{8,16},{12,20},{16,8},{20,12},{24,0},{28,4},{1,25},{... | collective-permute-start | bytes 245768 | tf_op jit(solution)/shard_map/ppermute | solution.py:23
  25.0 1.5 %copy-done.3 = bf16[864,1024]{1,0:T(8,128)(2,1)S(1)} copy-done((bf16[864,1024]{1,0:T(8,128)(2,1)S(1)}, bf16[864,1024]{1,0:T(8,128)(2,1)}, u32[]{:S(2)}) %copy-start.3) | copy-done | bytes 1769496
  26.5 2.9 %shard_map.125.refs_1_ = bf16[8,1024]{1,0:T(8,128)(2,1)S(1)} custom-call(bf16[864,1024]{1,0:T(8,128)(2,1)S(1)} %copy-done.2, bf16[864,1024]{1,0:T(8,128)(2,1)S(1)} %copy-done.3, bf16[128,1024]{1,0:T(8,128)(2,1)S(1)} %copy-done.1, bf16[128,1024]{1,0:T(8,128)(2,1)S(1)} %collective-permute-done.near_ref, ...), custom_call_target="tpu_custom_call" | custom-call | flops 1811939328 | bytes 5660672 | tf_op jit(solution)/shard_map/pallas_call | solution.py:106
  29.4 2.0 %collective-permute-start.12 = (bf16[8,1024]{1,0:T(8,128)(2,1)S(1)}, bf16[8,1024]{1,0:T(8,128)(2,1)S(1)}, u32[]{:S(2)}, u32[]{:S(2)}) collective-permute-start(bf16[8,1024]{1,0:T(8,128)(2,1)S(1)} %shard_map.125.refs_1_), channel_id=1, source_target_pairs={{0,24},{4,28},{8,16},{12,20},{16,8},{20,12},{24,0},{28,4},{1,25},{... | collective-permute-start | bytes 49160 | tf_op jit(solution)/shard_map/ppermute | solution.py:23
  31.4 1.8 %collective-permute-start.11 = (bf16[8,1024]{1,0:T(8,128)(2,1)S(1)}, bf16[8,1024]{1,0:T(8,128)(2,1)S(1)}, u32[]{:S(2)}, u32[]{:S(2)}) collective-permute-start(bf16[8,1024]{1,0:T(8,128)(2,1)S(1)} %shard_map.125.refs_1_), channel_id=1, source_target_pairs={{0,16},{4,20},{8,24},{12,28},{16,0},{20,4},{24,8},{28,12},{1,17},{... | collective-permute-start | bytes 49160 | tf_op jit(solution)/shard_map/ppermute | solution.py:23
  33.2 0.7 %collective-permute-start.10 = (bf16[8,1024]{1,0:T(8,128)(2,1)S(1)}, bf16[8,1024]{1,0:T(8,128)(2,1)S(1)}, u32[]{:S(2)}, u32[]{:S(2)}) collective-permute-start(bf16[8,1024]{1,0:T(8,128)(2,1)S(1)} %shard_map.125.refs_1_), channel_id=1, source_target_pairs={{0,8},{4,12},{8,0},{12,4},{16,24},{20,28},{24,16},{28,20},{1,9},{5... | collective-permute-start | bytes 49160 | tf_op jit(solution)/shard_map/ppermute | solution.py:23
  33.9 1.6 %collective-permute-start.19 = (bf16[3,64,512]{2,1,0:T(8,128)(2,1)S(1)}, bf16[3,64,512]{2,1,0:T(8,128)(2,1)S(1)}, u32[]{:S(2)}, u32[]{:S(2)}) collective-permute-start(bf16[3,64,512]{2,1,0:T(8,128)(2,1)S(1)} %pad_maximum_fusion.4), channel_id=1, source_target_pairs={{0,1},{1,0},{2,3},{3,2},{4,6},{5,7},{6,4},{7,5},{8,9},{9,8},{10,11... | collective-permute-start | bytes 589832 | tf_op jit(solution)/shard_map/ppermute | solution.py:34
  36.0 0.9 %collective-permute-done.10 = bf16[8,1024]{1,0:T(8,128)(2,1)S(1)} collective-permute-done((bf16[8,1024]{1,0:T(8,128)(2,1)S(1)}, bf16[8,1024]{1,0:T(8,128)(2,1)S(1)}, u32[]{:S(2)}, u32[]{:S(2)}) %collective-permute-start.10) | collective-permute-done | bytes 16416 | tf_op jit(solution)/shard_map/ppermute | solution.py:23
  36.9 1.5 %collective-permute-start.14 = (bf16[4,8,1024]{2,1,0:T(8,128)(2,1)S(1)}, bf16[4,8,1024]{2,1,0:T(8,128)(2,1)S(1)}, u32[]{:S(2)}, u32[]{:S(2)}) collective-permute-start(bf16[4,8,1024]{2,1,0:T(8,128)(2,1)S(1)} %pad_maximum_fusion.7), channel_id=1, source_target_pairs={{0,2},{1,3},{2,0},{3,1},{4,6},{5,7},{6,4},{7,5},{8,10},{9,11},{10,... | collective-permute-start | bytes 196616 | tf_op jit(solution)/shard_map/ppermute | solution.py:39
  38.5 1.1 %collective-permute-start.13 = (bf16[4,8,1024]{2,1,0:T(8,128)(2,1)S(1)}, bf16[4,8,1024]{2,1,0:T(8,128)(2,1)S(1)}, u32[]{:S(2)}, u32[]{:S(2)}) collective-permute-start(bf16[4,8,1024]{2,1,0:T(8,128)(2,1)S(1)} %pad_maximum_fusion.7), channel_id=1, source_target_pairs={{0,1},{1,0},{2,3},{3,2},{4,5},{5,4},{6,7},{7,6},{8,9},{9,8},{10,11... | collective-permute-start | bytes 196616 | tf_op jit(solution)/shard_map/ppermute | solution.py:39
  39.6 0.9 %collective-permute-start.15 = (bf16[4,8,1024]{2,1,0:T(8,128)(2,1)S(1)}, bf16[4,8,1024]{2,1,0:T(8,128)(2,1)S(1)}, u32[]{:S(2)}, u32[]{:S(2)}) collective-permute-start(bf16[4,8,1024]{2,1,0:T(8,128)(2,1)S(1)} %pad_maximum_fusion.7), channel_id=1, source_target_pairs={{0,3},{1,2},{2,1},{3,0},{4,7},{5,6},{6,5},{7,4},{8,11},{9,10},{10,... | collective-permute-start | bytes 196616 | tf_op jit(solution)/shard_map/ppermute | solution.py:39
  40.5 2.2 %collective-permute-done.13.refs_1_ = bf16[4,8,1024]{2,1,0:T(8,128)(2,1)S(1)} collective-permute-done((bf16[4,8,1024]{2,1,0:T(8,128)(2,1)S(1)}, bf16[4,8,1024]{2,1,0:T(8,128)(2,1)S(1)}, u32[]{:S(2)}, u32[]{:S(2)}) %collective-permute-start.13) | collective-permute-done | bytes 65568 | tf_op jit(solution)/shard_map/ppermute | solution.py:39
  42.9 1.8 %collective-permute-done.15 = bf16[4,8,1024]{2,1,0:T(8,128)(2,1)S(1)} collective-permute-done((bf16[4,8,1024]{2,1,0:T(8,128)(2,1)S(1)}, bf16[4,8,1024]{2,1,0:T(8,128)(2,1)S(1)}, u32[]{:S(2)}, u32[]{:S(2)}) %collective-permute-start.15) | collective-permute-done | bytes 65568 | tf_op jit(solution)/shard_map/ppermute | solution.py:39
  45.5 0.9 %collective-permute-done.16.refs_0_ = bf16[4,4,8,1024]{3,2,1,0:T(8,128)(2,1)S(1)} collective-permute-done((bf16[4,4,8,1024]{3,2,1,0:T(8,128)(2,1)S(1)}, bf16[4,4,8,1024]{3,2,1,0:T(8,128)(2,1)S(1)}, u32[]{:S(2)}, u32[]{:S(2)}) %collective-permute-start.16) | collective-permute-done | bytes 262176 | tf_op jit(solution)/shard_map/ppermute | solution.py:28
  46.4 2.0 %shard_map.132 = (f32[256,1024]{1,0:T(8,128)S(1)}, f32[256,1024]{1,0:T(8,128)S(1)}, f32[256,640]{1,0:T(8,128)S(1)}, f32[4,8,1152]{2,1,0:T(8,128)S(1)}, f32[1,256]{1,0:T(1,128)S(1)}) custom-call(bf16[256,1024]{1,0:T(8,128)(2,1)S(1)} %bitcast.59, bf16[1024,512]{1,0:T(8,128)(2,1)S(1)} %get-tuple-element.22.refs_1_.whole_ref, ...), custom_call_target="tpu_custom_call" | custom-call | flops 805306368 | bytes 5528576 | tf_op jit(solution)/shard_map/pallas_call | solution.py:106
  48.4 1.0 %collective-permute-start.21 = (f32[7,1152]{1,0:T(8,128)S(1)}, f32[7,1152]{1,0:T(8,128)S(1)}, u32[]{:S(2)}, u32[]{:S(2)}) collective-permute-start(f32[7,1152]{1,0:T(8,128)S(1)} %get-tuple-element.45), channel_id=1, source_target_pairs={{0,3},{1,2},{2,1},{3,0},{4,7},{5,6},{6,5},{7,4},{8,11},{9,10},{10,... | collective-permute-start | bytes 96776 | tf_op jit(solution)/shard_map/ppermute | solution.py:39
  49.4 1.5 %collective-permute-start.22 = (f32[7,1152]{1,0:T(8,128)S(1)}, f32[7,1152]{1,0:T(8,128)S(1)}, u32[]{:S(2)}, u32[]{:S(2)}) collective-permute-start(f32[7,1152]{1,0:T(8,128)S(1)} %get-tuple-element.46), channel_id=1, source_target_pairs={{0,2},{1,3},{2,0},{3,1},{4,6},{5,7},{6,4},{7,5},{8,10},{9,11},{10,... | collective-permute-start | bytes 96776 | tf_op jit(solution)/shard_map/ppermute | solution.py:39
  50.9 1.1 %collective-permute-start.23 = (f32[7,1152]{1,0:T(8,128)S(1)}, f32[7,1152]{1,0:T(8,128)S(1)}, u32[]{:S(2)}, u32[]{:S(2)}) collective-permute-start(f32[7,1152]{1,0:T(8,128)S(1)} %get-tuple-element.47), channel_id=1, source_target_pairs={{0,1},{1,0},{2,3},{3,2},{4,5},{5,4},{6,7},{7,6},{8,9},{9,8},{10,11... | collective-permute-start | bytes 96776 | tf_op jit(solution)/shard_map/ppermute | solution.py:39
  52.0 0.9 %shard_map.133 = (bf16[256,1024]{1,0:T(8,128)(2,1)S(1)}, bf16[256,1024]{1,0:T(8,128)(2,1)S(1)}, f32[256,1024]{1,0:T(8,128)S(1)}, f32[64,256]{1,0:T(8,128)S(1)}, ...) custom-call(f32[256,1024]{1,0:T(8,128)S(1)} %get-tuple-element.26.exp_ref, ...), custom_call_target="tpu_custom_call" | custom-call | flops 67108864 | bytes 6494208 | tf_op jit(solution)/shard_map/pallas_call | solution.py:106
  52.8 0.8 %collective-permute-done.21 = f32[7,1152]{1,0:T(8,128)S(1)} collective-permute-done((f32[7,1152]{1,0:T(8,128)S(1)}, f32[7,1152]{1,0:T(8,128)S(1)}, u32[]{:S(2)}, u32[]{:S(2)}) %collective-permute-start.21) | collective-permute-done | bytes 32288 | tf_op jit(solution)/shard_map/ppermute | solution.py:39
  53.7 1.1 %collective-permute-done.23 = f32[7,1152]{1,0:T(8,128)S(1)} collective-permute-done((f32[7,1152]{1,0:T(8,128)S(1)}, f32[7,1152]{1,0:T(8,128)S(1)}, u32[]{:S(2)}, u32[]{:S(2)}) %collective-permute-start.23) | collective-permute-done | bytes 32288 | tf_op jit(solution)/shard_map/ppermute | solution.py:39
  54.8 1.0 %shard_map.134 = (f32[64,1024]{1,0:T(8,128)}, f32[1,6]{1,0:T(1,128)}, f32[6,512]{1,0:T(8,128)}) custom-call(f32[7,1152]{1,0:T(8,128)S(1)} %fusion.6.total_ref, f32[1,256]{1,0:T(1,128)S(1)} %slice.37.denom_ref, bf16[256,1024]{1,0:T(8,128)(2,1)S(1)} %get-tuple-element.29.high_ref, bf16[256,1024]{1,0:T(8,128)(2,1)S(1)} %get-tuple-element.30.low_ref, ...), custom_call_target="tpu_custom_call" | custom-call | flops 100663296 | bytes 3658264 | tf_op jit(solution)/shard_map/pallas_call | solution.py:106
  (70 shorter events, 5.7 us)
Async XLA Ops:
  1.5 8.5 %collective-permute-start.4 = (bf16[32,1024]{1,0:T(8,128)(2,1)S(1)}, bf16[32,1024]{1,0:T(8,128)(2,1)S(1)}, u32[]{:S(2)}, u32[]{:S(2)}) collective-permute-start(bf16[32,1024]{1,0:T(8,128)(2,1)S(1)} %constant_dynamic-slice_fusion.2), channel_id=1, source_target_pairs={{0,24},{4,28},{8,16},{12,20},{16,8},{20,12},{24,0},{28,4},{1,25},{... | collective-permute-start | bytes 196616 | tf_op jit(solution)/shard_map/ppermute | solution.py:23
  6.5 5.7 %collective-permute-start.3 = (bf16[32,1024]{1,0:T(8,128)(2,1)S(1)}, bf16[32,1024]{1,0:T(8,128)(2,1)S(1)}, u32[]{:S(2)}, u32[]{:S(2)}) collective-permute-start(bf16[32,1024]{1,0:T(8,128)(2,1)S(1)} %constant_dynamic-slice_fusion.2), channel_id=1, source_target_pairs={{0,16},{4,20},{8,24},{12,28},{16,0},{20,4},{24,8},{28,12},{1,17},{... | collective-permute-start | bytes 196616 | tf_op jit(solution)/shard_map/ppermute | solution.py:23
  6.5 5.7 %collective-permute-start.1 = (bf16[128,1024]{1,0:T(8,128)(2,1)}, bf16[128,1024]{1,0:T(8,128)(2,1)S(1)}, u32[]{:S(2)}, u32[]{:S(2)}) collective-permute-start(bf16[128,1024]{1,0:T(8,128)(2,1)} %own_ref.1), channel_id=1, source_target_pairs={{0,4},{4,0},{8,12},{12,8},{16,20},{20,16},{24,28},{28,24},{1,5},{5... | collective-permute-start | bytes 786440 | tf_op jit(solution)/shard_map/ppermute | solution.py:28
  6.5 10.2 %collective-permute-start = (bf16[128,1024]{1,0:T(8,128)(2,1)}, bf16[128,1024]{1,0:T(8,128)(2,1)S(1)}, u32[]{:S(2)}, u32[]{:S(2)}) collective-permute-start(bf16[128,1024]{1,0:T(8,128)(2,1)} %own_ref.1), channel_id=1, source_target_pairs={{0,8},{4,12},{8,0},{12,4},{16,24},{20,28},{24,16},{28,20},{1,9},{5... | collective-permute-start | bytes 786440 | tf_op jit(solution)/shard_map/ppermute | solution.py:23
  12.3 6.4 %collective-permute-start.7 = (bf16[2,32,1024]{2,1,0:T(8,128)(2,1)S(1)}, bf16[2,32,1024]{2,1,0:T(8,128)(2,1)S(1)}, u32[]{:S(2)}, u32[]{:S(2)}) collective-permute-start(bf16[2,32,1024]{2,1,0:T(8,128)(2,1)S(1)} %shard_map.121.refs_1_), channel_id=1, source_target_pairs={{0,3},{1,2},{2,1},{3,0},{4,7},{5,6},{6,5},{7,4},{8,11},{9,10},{10,... | collective-permute-start | bytes 393224 | tf_op jit(solution)/shard_map/ppermute | solution.py:39
  14.8 6.2 %collective-permute-start.6 = (bf16[2,32,1024]{2,1,0:T(8,128)(2,1)S(1)}, bf16[2,32,1024]{2,1,0:T(8,128)(2,1)S(1)}, u32[]{:S(2)}, u32[]{:S(2)}) collective-permute-start(bf16[2,32,1024]{2,1,0:T(8,128)(2,1)S(1)} %shard_map.121.refs_1_), channel_id=1, source_target_pairs={{0,2},{1,3},{2,0},{3,1},{4,6},{5,7},{6,4},{7,5},{8,10},{9,11},{10,... | collective-permute-start | bytes 393224 | tf_op jit(solution)/shard_map/ppermute | solution.py:39
  15.3 6.0 %collective-permute-start.5 = (bf16[2,32,1024]{2,1,0:T(8,128)(2,1)S(1)}, bf16[2,32,1024]{2,1,0:T(8,128)(2,1)S(1)}, u32[]{:S(2)}, u32[]{:S(2)}) collective-permute-start(bf16[2,32,1024]{2,1,0:T(8,128)(2,1)S(1)} %shard_map.121.refs_1_), channel_id=1, source_target_pairs={{0,1},{1,0},{2,3},{3,2},{4,5},{5,4},{6,7},{7,6},{8,9},{9,8},{10,11... | collective-permute-start | bytes 393224 | tf_op jit(solution)/shard_map/ppermute | solution.py:39
  16.7 5.1 %collective-permute-start.2 = (bf16[128,1024]{1,0:T(8,128)(2,1)S(1)}, bf16[128,1024]{1,0:T(8,128)(2,1)S(1)}, u32[]{:S(2)}, u32[]{:S(2)}) collective-permute-start(bf16[128,1024]{1,0:T(8,128)(2,1)S(1)} %collective-permute-done.near_ref), channel_id=1, source_target_pairs={{0,4},{4,0},{8,12},{12,8},{16,20},{20,16},{24,28},{28,24},{1,5},{5... | collective-permute-start | bytes 786440 | tf_op jit(solution)/shard_map/ppermute | solution.py:28
  16.9 4.9 %collective-permute-start.8 = (bf16[80,512]{1,0:T(8,128)(2,1)S(1)}, bf16[80,512]{1,0:T(8,128)(2,1)S(1)}, u32[]{:S(2)}, u32[]{:S(2)}) collective-permute-start(bf16[80,512]{1,0:T(8,128)(2,1)S(1)} %shard_map.122), channel_id=1, source_target_pairs={{0,8},{4,12},{8,0},{12,4},{16,24},{20,28},{24,16},{28,20},{1,9},{5... | collective-permute-start | bytes 245768 | tf_op jit(solution)/shard_map/ppermute | solution.py:23
  21.3 1.2 %copy-start = (bf16[1024,512]{1,0:T(8,128)(2,1)S(1)}, bf16[1024,512]{1,0:T(8,128)(2,1)}, u32[]{:S(2)}) copy-start(bf16[1024,512]{1,0:T(8,128)(2,1)} %weight_ref.3) | copy-start | bytes 3145732
  21.8 3.2 %copy-start.1 = (bf16[128,1024]{1,0:T(8,128)(2,1)S(1)}, bf16[128,1024]{1,0:T(8,128)(2,1)}, u32[]{:S(2)}) copy-start(bf16[128,1024]{1,0:T(8,128)(2,1)} %own_ref.1) | copy-start | bytes 786436
  21.8 3.2 %copy-start.4 = (f32[1024]{0:T(1024)S(1)}, f32[1024]{0:T(1024)}, u32[]{:S(2)}) copy-start(f32[1024]{0:T(1024)} %param.13) | copy-start | bytes 12292
  21.8 3.2 %copy-start.5 = (f32[1024]{0:T(1024)S(1)}, f32[1024]{0:T(1024)}, u32[]{:S(2)}) copy-start(f32[1024]{0:T(1024)} %param.14) | copy-start | bytes 12292
  21.8 3.1 %collective-permute-start.9 = (bf16[4,2,32,1024]{3,2,1,0:T(8,128)(2,1)S(1)}, bf16[4,2,32,1024]{3,2,1,0:T(8,128)(2,1)S(1)}, u32[]{:S(2)}, u32[]{:S(2)}) collective-permute-start(bf16[4,2,32,1024]{3,2,1,0:T(8,128)(2,1)S(1)} %shard_map.123.far_ref), channel_id=1, source_target_pairs={{0,4},{4,0},{8,12},{12,8},{16,20},{20,16},{24,28},{28,24},{1,5},{5... | collective-permute-start | bytes 1572872 | tf_op jit(solution)/shard_map/ppermute | solution.py:28
  22.5 2.5 %copy-start.2 = (bf16[864,1024]{1,0:T(8,128)(2,1)S(1)}, bf16[864,1024]{1,0:T(8,128)(2,1)}, u32[]{:S(2)}) copy-start(bf16[864,1024]{1,0:T(8,128)(2,1)} %att_ref.1) | copy-start | bytes 5308420
  22.8 11.1 %collective-permute-start.18 = (bf16[80,512]{1,0:T(8,128)(2,1)S(1)}, bf16[80,512]{1,0:T(8,128)(2,1)S(1)}, u32[]{:S(2)}, u32[]{:S(2)}) collective-permute-start(bf16[80,512]{1,0:T(8,128)(2,1)S(1)} %shard_map.122), channel_id=1, source_target_pairs={{0,24},{4,28},{8,16},{12,20},{16,8},{20,12},{24,0},{28,4},{1,25},{... | collective-permute-start | bytes 245768 | tf_op jit(solution)/shard_map/ppermute | solution.py:23
  25.0 8.9 %collective-permute-start.17 = (bf16[80,512]{1,0:T(8,128)(2,1)S(1)}, bf16[80,512]{1,0:T(8,128)(2,1)S(1)}, u32[]{:S(2)}, u32[]{:S(2)}) collective-permute-start(bf16[80,512]{1,0:T(8,128)(2,1)S(1)} %shard_map.122), channel_id=1, source_target_pairs={{0,16},{4,20},{8,24},{12,28},{16,0},{20,4},{24,8},{28,12},{1,17},{... | collective-permute-start | bytes 245768 | tf_op jit(solution)/shard_map/ppermute | solution.py:23
  25.0 1.5 %copy-start.3 = (bf16[864,1024]{1,0:T(8,128)(2,1)S(1)}, bf16[864,1024]{1,0:T(8,128)(2,1)}, u32[]{:S(2)}) copy-start(bf16[864,1024]{1,0:T(8,128)(2,1)} %stream_ref.1) | copy-start | bytes 5308420
  29.4 6.2 %collective-permute-start.12 = (bf16[8,1024]{1,0:T(8,128)(2,1)S(1)}, bf16[8,1024]{1,0:T(8,128)(2,1)S(1)}, u32[]{:S(2)}, u32[]{:S(2)}) collective-permute-start(bf16[8,1024]{1,0:T(8,128)(2,1)S(1)} %shard_map.125.refs_1_), channel_id=1, source_target_pairs={{0,24},{4,28},{8,16},{12,20},{16,8},{20,12},{24,0},{28,4},{1,25},{... | collective-permute-start | bytes 49160 | tf_op jit(solution)/shard_map/ppermute | solution.py:23
  31.4 4.6 %collective-permute-start.11 = (bf16[8,1024]{1,0:T(8,128)(2,1)S(1)}, bf16[8,1024]{1,0:T(8,128)(2,1)S(1)}, u32[]{:S(2)}, u32[]{:S(2)}) collective-permute-start(bf16[8,1024]{1,0:T(8,128)(2,1)S(1)} %shard_map.125.refs_1_), channel_id=1, source_target_pairs={{0,16},{4,20},{8,24},{12,28},{16,0},{20,4},{24,8},{28,12},{1,17},{... | collective-permute-start | bytes 49160 | tf_op jit(solution)/shard_map/ppermute | solution.py:23
  33.2 3.7 %collective-permute-start.10 = (bf16[8,1024]{1,0:T(8,128)(2,1)S(1)}, bf16[8,1024]{1,0:T(8,128)(2,1)S(1)}, u32[]{:S(2)}, u32[]{:S(2)}) collective-permute-start(bf16[8,1024]{1,0:T(8,128)(2,1)S(1)} %shard_map.125.refs_1_), channel_id=1, source_target_pairs={{0,8},{4,12},{8,0},{12,4},{16,24},{20,28},{24,16},{28,20},{1,9},{5... | collective-permute-start | bytes 49160 | tf_op jit(solution)/shard_map/ppermute | solution.py:23
  33.9 8.8 %collective-permute-start.19 = (bf16[3,64,512]{2,1,0:T(8,128)(2,1)S(1)}, bf16[3,64,512]{2,1,0:T(8,128)(2,1)S(1)}, u32[]{:S(2)}, u32[]{:S(2)}) collective-permute-start(bf16[3,64,512]{2,1,0:T(8,128)(2,1)S(1)} %pad_maximum_fusion.4), channel_id=1, source_target_pairs={{0,1},{1,0},{2,3},{3,2},{4,6},{5,7},{6,4},{7,5},{8,9},{9,8},{10,11... | collective-permute-start | bytes 589832 | tf_op jit(solution)/shard_map/ppermute | solution.py:34
  36.9 6.0 %collective-permute-start.14 = (bf16[4,8,1024]{2,1,0:T(8,128)(2,1)S(1)}, bf16[4,8,1024]{2,1,0:T(8,128)(2,1)S(1)}, u32[]{:S(2)}, u32[]{:S(2)}) collective-permute-start(bf16[4,8,1024]{2,1,0:T(8,128)(2,1)S(1)} %pad_maximum_fusion.7), channel_id=1, source_target_pairs={{0,2},{1,3},{2,0},{3,1},{4,6},{5,7},{6,4},{7,5},{8,10},{9,11},{10,... | collective-permute-start | bytes 196616 | tf_op jit(solution)/shard_map/ppermute | solution.py:39
  38.5 4.3 %collective-permute-start.13 = (bf16[4,8,1024]{2,1,0:T(8,128)(2,1)S(1)}, bf16[4,8,1024]{2,1,0:T(8,128)(2,1)S(1)}, u32[]{:S(2)}, u32[]{:S(2)}) collective-permute-start(bf16[4,8,1024]{2,1,0:T(8,128)(2,1)S(1)} %pad_maximum_fusion.7), channel_id=1, source_target_pairs={{0,1},{1,0},{2,3},{3,2},{4,5},{5,4},{6,7},{7,6},{8,9},{9,8},{10,11... | collective-permute-start | bytes 196616 | tf_op jit(solution)/shard_map/ppermute | solution.py:39
  39.6 5.2 %collective-permute-start.15 = (bf16[4,8,1024]{2,1,0:T(8,128)(2,1)S(1)}, bf16[4,8,1024]{2,1,0:T(8,128)(2,1)S(1)}, u32[]{:S(2)}, u32[]{:S(2)}) collective-permute-start(bf16[4,8,1024]{2,1,0:T(8,128)(2,1)S(1)} %pad_maximum_fusion.7), channel_id=1, source_target_pairs={{0,3},{1,2},{2,1},{3,0},{4,7},{5,6},{6,5},{7,4},{8,11},{9,10},{10,... | collective-permute-start | bytes 196616 | tf_op jit(solution)/shard_map/ppermute | solution.py:39
  42.8 2.1 %collective-permute-start.20 = (bf16[576,512]{1,0:T(8,128)(2,1)S(1)}, bf16[576,512]{1,0:T(8,128)(2,1)S(1)}, u32[]{:S(2)}, u32[]{:S(2)}) collective-permute-start(bf16[576,512]{1,0:T(8,128)(2,1)S(1)} %pad_maximum_fusion.head_ref), channel_id=1, source_target_pairs={{0,4},{4,0},{8,12},{12,8},{16,20},{20,16},{24,28},{28,24},{1,5},{5... | collective-permute-start | bytes 1769480 | tf_op jit(solution)/shard_map/ppermute | solution.py:28
  44.8 1.6 %collective-permute-start.16 = (bf16[4,4,8,1024]{3,2,1,0:T(8,128)(2,1)S(1)}, bf16[4,4,8,1024]{3,2,1,0:T(8,128)(2,1)S(1)}, u32[]{:S(2)}, u32[]{:S(2)}) collective-permute-start(bf16[4,4,8,1024]{3,2,1,0:T(8,128)(2,1)S(1)} %bitcast_dynamic-update-slice_fusion.3), channel_id=1, source_target_pairs={{0,4},{4,0},{8,12},{12,8},{16,20},{20,16},{24,28},{28,24},{1,5},{5... | collective-permute-start | bytes 786440 | tf_op jit(solution)/shard_map/ppermute | solution.py:28
  48.4 5.2 %collective-permute-start.21 = (f32[7,1152]{1,0:T(8,128)S(1)}, f32[7,1152]{1,0:T(8,128)S(1)}, u32[]{:S(2)}, u32[]{:S(2)}) collective-permute-start(f32[7,1152]{1,0:T(8,128)S(1)} %get-tuple-element.45), channel_id=1, source_target_pairs={{0,3},{1,2},{2,1},{3,0},{4,7},{5,6},{6,5},{7,4},{8,11},{9,10},{10,... | collective-permute-start | bytes 96776 | tf_op jit(solution)/shard_map/ppermute | solution.py:39
  49.4 4.4 %collective-permute-start.22 = (f32[7,1152]{1,0:T(8,128)S(1)}, f32[7,1152]{1,0:T(8,128)S(1)}, u32[]{:S(2)}, u32[]{:S(2)}) collective-permute-start(f32[7,1152]{1,0:T(8,128)S(1)} %get-tuple-element.46), channel_id=1, source_target_pairs={{0,2},{1,3},{2,0},{3,1},{4,6},{5,7},{6,4},{7,5},{8,10},{9,11},{10,... | collective-permute-start | bytes 96776 | tf_op jit(solution)/shard_map/ppermute | solution.py:39
  50.9 4.0 %collective-permute-start.23 = (f32[7,1152]{1,0:T(8,128)S(1)}, f32[7,1152]{1,0:T(8,128)S(1)}, u32[]{:S(2)}, u32[]{:S(2)}) collective-permute-start(f32[7,1152]{1,0:T(8,128)S(1)} %get-tuple-element.47), channel_id=1, source_target_pairs={{0,1},{1,0},{2,3},{3,2},{4,5},{5,4},{6,7},{7,6},{8,9},{9,8},{10,11... | collective-permute-start | bytes 96776 | tf_op jit(solution)/shard_map/ppermute | solution.py:39
